TPU v7x, 32 devices: a whole 2x2x4 slice. The times are simulated.
32 devices in a mesh: dp: 8 (over z, x), tensor: 4 (over y, core).
Axes of the slice: x: 2, y: 2, z: 4, core: 2. Of those that a mesh axis runs over, the one named last changes fastest.
Arguments:
- inputs: bfloat16 [8, 1024, 2560], P('dp', 'tensor'), may hold values from -6 to 6
- cotangent: bfloat16 [8, 1024, 2560], P('dp', 'tensor'), may hold values from -6 to 6
- document_numbers: int32 [8, 1024], P('dp'), may hold values from 0 to 6, as said below
- sequence_adapter_index: int32 [8], P('dp'), may hold values from 0 to 7
- attention_norm_gain: float32 [2560], replicated, may hold values from 0.25 to 1.75
- query_latent_gain: float32 [768], replicated, may hold values from 0.25 to 1.75
- keyvalue_latent_gain: float32 [256], replicated, may hold values from 0.25 to 1.75
- feedforward_norm_gain: float32 [2560], replicated, may hold values from 0.25 to 1.75
- query_down_matrix: bfloat16 [2560, 768], P('dp'), may hold values from -0.125 to 0.125
- keyvalue_down_matrix: bfloat16 [2560, 288], P('dp'), may hold values from -0.125 to 0.125
- query_up_matrix: bfloat16 [768, 3840], P('dp', 'tensor'), may hold values from -0.21875 to 0.21875
- keyvalue_up_matrix: bfloat16 [256, 5120], P('dp', 'tensor'), may hold values from -0.375 to 0.375
- output_matrix: bfloat16 [2560, 2560], P('tensor', 'dp'), may hold values from -4 to 4
- gate_up_matrix: bfloat16 [2, 2560, 6400], P(None, 'dp', 'tensor'), may hold values from -0.125 to 0.125
- down_matrix: bfloat16 [6400, 2560], P('tensor', 'dp'), may hold values from -0.625 to 0.625
- query_down_adapter_in: bfloat16 [8, 2560, 16], replicated, may hold values from -0.125 to 0.125
- query_down_adapter_out: bfloat16 [8, 16, 768], replicated, may hold values from -0.375 to 0.375
- keyvalue_down_adapter_in: bfloat16 [8, 2560, 16], replicated, may hold values from -0.125 to 0.125
- keyvalue_down_adapter_out: bfloat16 [8, 16, 288], replicated, may hold values from -0.375 to 0.375
- query_up_adapter_in: bfloat16 [8, 768, 16], replicated, may hold values from -0.21875 to 0.21875
- query_up_adapter_out: bfloat16 [8, 16, 3840], P(None, None, 'tensor'), may hold values from -0.375 to 0.375
- keyvalue_up_adapter_in: bfloat16 [8, 256, 16], replicated, may hold values from -0.375 to 0.375
- keyvalue_up_adapter_out: bfloat16 [8, 16, 5120], P(None, None, 'tensor'), may hold values from -0.375 to 0.375
- output_adapter_in: bfloat16 [8, 2560, 16], P(None, 'tensor'), may hold values from -0.125 to 0.125
- output_adapter_out: bfloat16 [8, 16, 2560], replicated, may hold values from -6 to 6
- gate_up_adapter_in: bfloat16 [2, 8, 2560, 16], replicated, may hold values from -0.125 to 0.125
- gate_up_adapter_out: bfloat16 [2, 8, 16, 6400], P(None, None, None, 'tensor'), may hold values from -0.375 to 0.375
- down_adapter_in: bfloat16 [8, 6400, 16], P(None, 'tensor'), may hold values from -0.078125 to 0.078125
- down_adapter_out: bfloat16 [8, 16, 2560], replicated, may hold values from -1.5 to 1.5
Outputs:
- outputs: bfloat16 [8, 1024, 2560], P('dp', 'tensor')
- input_grad: float32 [8, 1024, 2560], P('dp', 'tensor')
- qa_lora_a_grad: float32 [8, 2560, 16], replicated
- qa_lora_b_grad: float32 [8, 16, 768], replicated
- kva_lora_a_grad: float32 [8, 2560, 16], replicated
- kva_lora_b_grad: float32 [8, 16, 288], replicated
- qb_lora_a_grad: float32 [8, 768, 16], replicated
- qb_lora_b_grad: float32 [8, 16, 3840], P(None, None, 'tensor')
- kvb_lora_a_grad: float32 [8, 256, 16], replicated
- kvb_lora_b_grad: float32 [8, 16, 5120], P(None, None, 'tensor')
- out_lora_a_grad: float32 [8, 2560, 16], P(None, 'tensor')
- out_lora_b_grad: float32 [8, 16, 2560], replicated
- gate_up_lora_a_grad: float32 [2, 8, 2560, 16], replicated
- gate_up_lora_b_grad: float32 [2, 8, 16, 6400], P(None, None, None, 'tensor')
- down_lora_a_grad: float32 [8, 6400, 16], P(None, 'tensor')
- down_lora_b_grad: float32 [8, 16, 2560], replicated
Inputs may be any that keep to these rules, and one draw needn't show every extreme that they name: `document_numbers`: in each sequence documents are numbered 0, 1, 2 and so on in order, each 60 to 800 tokens long; some sequence holds a document of exactly 800 tokens.
All inputs are finite; a program needn't handle non-finite values.
Results may differ from a plain program's by a relative error of at most 0.025.
Values may be sent and summed in bfloat16 or wider, within the bound.
A program may use at most 256 MiB of HBM per device.

v0:
```python
import math

import jax
import jax.numpy as jnp
from jax import lax
from jax.sharding import PartitionSpec as P

PLAIN_HEAD_DIM = 64
ROTARY_DIM = 32
VALUE_HEAD_DIM = 64
KEYVALUE_LATENT = 256
ADAPTER_GROUPS = 8


NORM_EPS = 1e-05
RESIDUAL = 1.4 / math.sqrt(62.0)
ADAPT_SCALE = 2.0
HIGHEST_PREC = lax.Precision.HIGHEST


def narrow(value):
    return value.astype(jnp.bfloat16)


def product(left_op, right_op):
    return jnp.einsum("...i,io->...o", left_op, right_op, preferred_element_type=jnp.float32)


def product_back(left_op, right_op):
    return jnp.einsum("...o,io->...i", left_op, right_op, preferred_element_type=jnp.float32)


def select_per_sequence(table_set, onehot):
    return narrow(jnp.einsum("sk,kab->sab", onehot, table_set, preferred_element_type=jnp.float32))


def reduce_in(rows_in, chosen):
    return jnp.einsum("sti,sir->str", rows_in, chosen, preferred_element_type=jnp.float32)


def reduce_back(grad_in, chosen):
    return jnp.einsum("str,sir->sti", grad_in, chosen, preferred_element_type=jnp.float32)


def expand(codes, chosen):
    return jnp.einsum("str,sro->sto", codes, chosen, preferred_element_type=jnp.float32)


def expand_back(grad_in, chosen):
    return jnp.einsum("sto,sro->str", grad_in, chosen, preferred_element_type=jnp.float32)


def outer_sum(left_op, right_op):
    return jnp.einsum("sta,stb->sab", left_op, right_op, preferred_element_type=jnp.float32)


def per_set(terms, onehot):
    return jnp.einsum("sk,sab->kab", onehot, terms, precision=HIGHEST_PREC)


def normalize(value, gain_vec):
    scale_inv = lax.rsqrt(jnp.mean(value * value, axis=-1, keepdims=True) + NORM_EPS)
    return (value * scale_inv * gain_vec, scale_inv)


def normalize_back(value, scale_inv, gain_vec, grad_in):
    weighted = grad_in * gain_vec
    return scale_inv * weighted - value * scale_inv**3 * jnp.mean(
        value * weighted, axis=-1, keepdims=True
    )


def rotate(value, cos_part, sin_part):
    half_dim = value.shape[-1] // 2
    first_half = value[..., :half_dim]
    second = value[..., half_dim:]
    return jnp.concatenate(
        [first_half * cos_part - second * sin_part, second * cos_part + first_half * sin_part],
        axis=-1,
    )


def rotate_back(value, cos_part, sin_part):
    half_dim = value.shape[-1] // 2
    first_half = value[..., :half_dim]
    second = value[..., half_dim:]
    return jnp.concatenate(
        [first_half * cos_part + second * sin_part, second * cos_part - first_half * sin_part],
        axis=-1,
    )


def rope_tables(segments):
    places = jnp.arange(segments.shape[-1], dtype=jnp.int32)
    begins = jnp.concatenate(
        [jnp.ones_like(segments[:, :1]), (segments[:, 1:] != segments[:, :-1]).astype(jnp.int32)],
        axis=1,
    )
    first_place = lax.cummax(places[None, :] * begins, axis=1)
    offsets = (places[None, :] - first_place).astype(jnp.float32)
    inv_freq = 10000.0 ** (-2.0 * jnp.arange(ROTARY_DIM // 2, dtype=jnp.float32) / ROTARY_DIM)
    angles = offsets[..., None] * inv_freq
    return (jnp.cos(angles), jnp.sin(angles))


def per_device(
    inputs,
    cotangent,
    document_numbers,
    sequence_adapter_index,
    attention_norm_gain,
    query_latent_gain,
    keyvalue_latent_gain,
    feedforward_norm_gain,
    query_down_matrix,
    keyvalue_down_matrix,
    query_up_matrix,
    keyvalue_up_matrix,
    output_matrix,
    gate_up_matrix,
    down_matrix,
    query_down_adapter_in,
    query_down_adapter_out,
    keyvalue_down_adapter_in,
    keyvalue_down_adapter_out,
    query_up_adapter_in,
    query_up_adapter_out,
    keyvalue_up_adapter_in,
    keyvalue_up_adapter_out,
    output_adapter_in,
    output_adapter_out,
    gate_up_adapter_in,
    gate_up_adapter_out,
    down_adapter_in,
    down_adapter_out,
):
    seq_count = inputs.shape[0]
    seq_len = document_numbers.shape[1]
    onehot = sequence_adapter_index[:, None] == jnp.arange(ADAPTER_GROUPS, dtype=jnp.int32)[None, :]
    pick_adapter_lowrank = onehot.astype(jnp.bfloat16)
    pick_high = onehot.astype(jnp.float32)
    cos_part, sin_part = rope_tables(document_numbers)
    cos_heads = cos_part[:, :, None]
    sin_heads = sin_part[:, :, None]
    qa_full, kva_full, qb_full, kvb_full, out_full = (
        lax.all_gather(query_down_matrix, "dp", axis=0, tiled=True),
        lax.all_gather(keyvalue_down_matrix, "dp", axis=0, tiled=True),
        lax.all_gather(query_up_matrix, "dp", axis=0, tiled=True),
        lax.all_gather(keyvalue_up_matrix, "dp", axis=0, tiled=True),
        lax.all_gather(output_matrix, "dp", axis=1, tiled=True),
    )
    query_down_picked_in = select_per_sequence(query_down_adapter_in, pick_adapter_lowrank)
    query_down_picked_out = select_per_sequence(query_down_adapter_out, pick_adapter_lowrank)
    keyvalue_down_picked_in = select_per_sequence(keyvalue_down_adapter_in, pick_adapter_lowrank)
    keyvalue_down_picked_out = select_per_sequence(keyvalue_down_adapter_out, pick_adapter_lowrank)
    query_up_picked_in = select_per_sequence(query_up_adapter_in, pick_adapter_lowrank)
    query_up_picked_out = select_per_sequence(query_up_adapter_out, pick_adapter_lowrank)
    keyvalue_up_picked_in = select_per_sequence(keyvalue_up_adapter_in, pick_adapter_lowrank)
    keyvalue_up_picked_out = select_per_sequence(keyvalue_up_adapter_out, pick_adapter_lowrank)
    output_picked_in = select_per_sequence(output_adapter_in, pick_adapter_lowrank)
    output_picked_out = select_per_sequence(output_adapter_out, pick_adapter_lowrank)
    gate_picked_in = select_per_sequence(gate_up_adapter_in[0], pick_adapter_lowrank)
    up_picked_in = select_per_sequence(gate_up_adapter_in[1], pick_adapter_lowrank)
    gate_picked_out = select_per_sequence(gate_up_adapter_out[0], pick_adapter_lowrank)
    up_picked_out = select_per_sequence(gate_up_adapter_out[1], pick_adapter_lowrank)
    down_picked_in = select_per_sequence(down_adapter_in, pick_adapter_lowrank)
    down_picked_out = select_per_sequence(down_adapter_out, pick_adapter_lowrank)
    residual = inputs.astype(jnp.float32)
    attn_normed, attn_scale = normalize(residual, attention_norm_gain)
    attn_rows = narrow(attn_normed)
    qa_codes = narrow(reduce_in(attn_rows, query_down_picked_in))
    kva_codes = narrow(reduce_in(attn_rows, keyvalue_down_picked_in))
    q_latent = product(attn_rows, qa_full) + ADAPT_SCALE * expand(qa_codes, query_down_picked_out)
    kv_latent = product(attn_rows, kva_full) + ADAPT_SCALE * expand(
        kva_codes, keyvalue_down_picked_out
    )
    q_normed, q_scale = normalize(q_latent, query_latent_gain)
    kv_normed, kv_scale = normalize(kv_latent[..., :KEYVALUE_LATENT], keyvalue_latent_gain)
    q_input = narrow(q_normed)
    kv_input = narrow(kv_normed)
    pe_input = narrow(kv_latent[..., KEYVALUE_LATENT:])
    qb_codes = narrow(reduce_in(q_input, query_up_picked_in))
    kvb_codes = narrow(reduce_in(kv_input, keyvalue_up_picked_in))
    q_rows, kv_rows, pe_rows, qb_rows, kvb_rows = (
        lax.all_gather(q_input, "tensor", axis=1, tiled=True),
        lax.all_gather(kv_input, "tensor", axis=1, tiled=True),
        lax.all_gather(pe_input, "tensor", axis=1, tiled=True),
        lax.all_gather(qb_codes, "tensor", axis=1, tiled=True),
        lax.all_gather(kvb_codes, "tensor", axis=1, tiled=True),
    )
    head_count = qb_full.shape[1] // (PLAIN_HEAD_DIM + ROTARY_DIM)
    queries = (
        product(q_rows, qb_full) + ADAPT_SCALE * expand(qb_rows, query_up_picked_out)
    ).reshape(seq_count, seq_len, head_count, PLAIN_HEAD_DIM + ROTARY_DIM)
    keyvals = (
        product(kv_rows, kvb_full) + ADAPT_SCALE * expand(kvb_rows, keyvalue_up_picked_out)
    ).reshape(seq_count, seq_len, head_count, PLAIN_HEAD_DIM + VALUE_HEAD_DIM)
    q_rot = narrow(
        jnp.concatenate(
            [
                queries[..., :PLAIN_HEAD_DIM],
                rotate(queries[..., PLAIN_HEAD_DIM:], cos_heads, sin_heads),
            ],
            axis=-1,
        )
    )
    pe_rot = narrow(rotate(pe_rows.astype(jnp.float32), cos_part, sin_part))
    k_nope = narrow(keyvals[..., :PLAIN_HEAD_DIM])
    values = narrow(keyvals[..., PLAIN_HEAD_DIM:])
    block_rows = min(512, seq_len)
    block_count = seq_len // block_rows
    places = jnp.arange(seq_len, dtype=jnp.int32)
    score_scale = 1.0 / math.sqrt(PLAIN_HEAD_DIM + ROTARY_DIM)

    def block_scores(row_start):
        q_part = lax.dynamic_slice_in_dim(q_rot, row_start, block_rows, 1)
        seg_part = lax.dynamic_slice_in_dim(document_numbers, row_start, block_rows, 1)
        raw_scores = jnp.einsum(
            "sqhd,skhd->shqk",
            q_part[..., :PLAIN_HEAD_DIM],
            k_nope,
            preferred_element_type=jnp.float32,
        )
        raw_scores = raw_scores + jnp.einsum(
            "sqhd,skd->shqk",
            q_part[..., PLAIN_HEAD_DIM:],
            pe_rot,
            preferred_element_type=jnp.float32,
        )
        row_ids = row_start + jnp.arange(block_rows, dtype=jnp.int32)
        causal = row_ids[:, None] >= places[None, :]
        allowed = (seg_part[:, None, :, None] == document_numbers[:, None, None, :]) & causal[
            None, None
        ]
        return (jnp.where(allowed, raw_scores * score_scale, -1e30), q_part)

    def forward_block(block_index):
        masked, q_part = block_scores(block_index * block_rows)
        row_max = jnp.max(masked, axis=-1, keepdims=True)
        exp_terms = jnp.exp(masked - row_max)
        row_total = jnp.sum(exp_terms, axis=-1, keepdims=True)
        attn_probs = narrow(exp_terms / row_total)
        mixed = jnp.einsum(
            "shqk,skhd->sqhd", attn_probs, values, preferred_element_type=jnp.float32
        )
        return (mixed, (row_max + jnp.log(row_total))[..., 0])

    mixed_blocks, lse_blocks = lax.map(forward_block, jnp.arange(block_count, dtype=jnp.int32))
    head_out = narrow(
        jnp.moveaxis(mixed_blocks, 0, 1).reshape(seq_count, seq_len, head_count * VALUE_HEAD_DIM)
    )
    log_totals = jnp.transpose(lse_blocks, (1, 2, 0, 3)).reshape(seq_count, head_count, seq_len)
    attn_part = product(head_out, out_full)
    out_code_part = reduce_in(head_out, output_picked_in)
    attn_sum, out_code_sum = (
        lax.psum_scatter(
            attn_part.astype(jnp.bfloat16), "tensor", scatter_dimension=1, tiled=True
        ).astype(jnp.float32),
        lax.psum_scatter(
            out_code_part.astype(jnp.bfloat16), "tensor", scatter_dimension=1, tiled=True
        ).astype(jnp.float32),
    )
    out_codes = narrow(out_code_sum)
    middle = residual + RESIDUAL * (attn_sum + ADAPT_SCALE * expand(out_codes, output_picked_out))
    gate_up_full, down_full = (
        lax.all_gather(gate_up_matrix, "dp", axis=1, tiled=True),
        lax.all_gather(down_matrix, "dp", axis=1, tiled=True),
    )
    ffn_normed, ffn_scale = normalize(middle, feedforward_norm_gain)
    ffn_rows = narrow(ffn_normed)
    gu_codes = narrow(
        jnp.stack([reduce_in(ffn_rows, gate_picked_in), reduce_in(ffn_rows, up_picked_in)], axis=0)
    )
    ffn_all, gu_all = (
        lax.all_gather(ffn_rows, "tensor", axis=1, tiled=True),
        lax.all_gather(gu_codes, "tensor", axis=2, tiled=True),
    )
    gate_act = product(ffn_all, gate_up_full[0]) + ADAPT_SCALE * expand(gu_all[0], gate_picked_out)
    up_act = product(ffn_all, gate_up_full[1]) + ADAPT_SCALE * expand(gu_all[1], up_picked_out)
    gate_sig = jax.nn.sigmoid(gate_act)
    gate_silu = gate_act * gate_sig
    hidden = narrow(gate_silu * up_act)
    down_part = product(hidden, down_full)
    down_code_part = reduce_in(hidden, down_picked_in)
    ffn_sum, down_code_sum = (
        lax.psum_scatter(
            down_part.astype(jnp.bfloat16), "tensor", scatter_dimension=1, tiled=True
        ).astype(jnp.float32),
        lax.psum_scatter(
            down_code_part.astype(jnp.bfloat16), "tensor", scatter_dimension=1, tiled=True
        ).astype(jnp.float32),
    )
    down_codes = narrow(down_code_sum)
    outputs = narrow(
        middle + RESIDUAL * (ffn_sum + ADAPT_SCALE * expand(down_codes, down_picked_out))
    )
    out_grad = cotangent.astype(jnp.float32)
    ffn_grad = narrow(RESIDUAL * out_grad)
    down_b_terms = ADAPT_SCALE * outer_sum(down_codes, ffn_grad)
    down_code_grad = narrow(ADAPT_SCALE * expand_back(ffn_grad, down_picked_out))
    gate_up_full, down_full = (
        lax.all_gather(gate_up_matrix, "dp", axis=1, tiled=True),
        lax.all_gather(down_matrix, "dp", axis=1, tiled=True),
    )
    ffn_grad_all, down_code_all = (
        lax.all_gather(ffn_grad, "tensor", axis=1, tiled=True),
        lax.all_gather(down_code_grad, "tensor", axis=1, tiled=True),
    )
    hidden_grad = product_back(ffn_grad_all, down_full) + reduce_back(down_code_all, down_picked_in)
    down_a_terms = outer_sum(hidden, down_code_all)
    gate_grad = narrow(hidden_grad * up_act * gate_sig * (1.0 + gate_act * (1.0 - gate_sig)))
    up_grad = narrow(hidden_grad * gate_silu)
    gate_up_b_terms = ADAPT_SCALE * jnp.stack(
        [outer_sum(gu_all[0], gate_grad), outer_sum(gu_all[1], up_grad)], axis=0
    )
    ffn_in_part = product_back(gate_grad, gate_up_full[0]) + product_back(up_grad, gate_up_full[1])
    gu_code_part = ADAPT_SCALE * jnp.stack(
        [expand_back(gate_grad, gate_picked_out), expand_back(up_grad, up_picked_out)], axis=0
    )
    ffn_in_sum, gu_code_sum = (
        lax.psum_scatter(
            ffn_in_part.astype(jnp.bfloat16), "tensor", scatter_dimension=1, tiled=True
        ).astype(jnp.float32),
        lax.psum_scatter(
            gu_code_part.astype(jnp.bfloat16), "tensor", scatter_dimension=2, tiled=True
        ).astype(jnp.float32),
    )
    gu_code_grad = narrow(gu_code_sum)
    gate_up_a_terms = jnp.stack(
        [outer_sum(ffn_rows, gu_code_grad[0]), outer_sum(ffn_rows, gu_code_grad[1])], axis=0
    )
    ffn_in_grad = (
        ffn_in_sum
        + reduce_back(gu_code_grad[0], gate_picked_in)
        + reduce_back(gu_code_grad[1], up_picked_in)
    )
    middle_grad = out_grad + normalize_back(middle, ffn_scale, feedforward_norm_gain, ffn_in_grad)
    attn_grad = narrow(RESIDUAL * middle_grad)
    out_b_terms = ADAPT_SCALE * outer_sum(out_codes, attn_grad)
    out_code_grad = narrow(ADAPT_SCALE * expand_back(attn_grad, output_picked_out))
    qa_full, kva_full, qb_full, kvb_full, out_full = (
        lax.all_gather(query_down_matrix, "dp", axis=0, tiled=True),
        lax.all_gather(keyvalue_down_matrix, "dp", axis=0, tiled=True),
        lax.all_gather(query_up_matrix, "dp", axis=0, tiled=True),
        lax.all_gather(keyvalue_up_matrix, "dp", axis=0, tiled=True),
        lax.all_gather(output_matrix, "dp", axis=1, tiled=True),
    )
    attn_grad_all, out_code_all = (
        lax.all_gather(attn_grad, "tensor", axis=1, tiled=True),
        lax.all_gather(out_code_grad, "tensor", axis=1, tiled=True),
    )
    heads_grad = narrow(
        product_back(attn_grad_all, out_full) + reduce_back(out_code_all, output_picked_in)
    )
    out_a_terms = outer_sum(head_out, out_code_all)
    heads_grad = heads_grad.reshape(seq_count, seq_len, head_count, VALUE_HEAD_DIM)

    def backward_block(carry_in, block_index):
        k_acc, pe_acc, v_acc = carry_in
        row_start = block_index * block_rows
        masked, q_part = block_scores(row_start)
        lse_part = lax.dynamic_slice_in_dim(log_totals, row_start, block_rows, 2)
        exact_probs = jnp.exp(masked - lse_part[..., None])
        grad_part = lax.dynamic_slice_in_dim(heads_grad, row_start, block_rows, 1)
        prob_grad = jnp.einsum(
            "sqhd,skhd->shqk", grad_part, values, preferred_element_type=jnp.float32
        )
        row_inner = jnp.sum(exact_probs * prob_grad, axis=-1, keepdims=True)
        score_grad = narrow(exact_probs * (prob_grad - row_inner))
        v_acc = v_acc + jnp.einsum(
            "shqk,sqhd->skhd", narrow(exact_probs), grad_part, preferred_element_type=jnp.float32
        )
        k_acc = k_acc + score_scale * jnp.einsum(
            "shqk,sqhd->skhd",
            score_grad,
            q_part[..., :PLAIN_HEAD_DIM],
            preferred_element_type=jnp.float32,
        )
        pe_acc = pe_acc + score_scale * jnp.einsum(
            "shqk,sqhd->skd",
            score_grad,
            q_part[..., PLAIN_HEAD_DIM:],
            preferred_element_type=jnp.float32,
        )
        q_nope_grad = jnp.einsum(
            "shqk,skhd->sqhd", score_grad, k_nope, preferred_element_type=jnp.float32
        )
        q_pe_grad = jnp.einsum(
            "shqk,skd->sqhd", score_grad, pe_rot, preferred_element_type=jnp.float32
        )
        return (
            (k_acc, pe_acc, v_acc),
            score_scale * jnp.concatenate([q_nope_grad, q_pe_grad], axis=-1),
        )

    carry_init = (
        jnp.zeros((seq_count, seq_len, head_count, PLAIN_HEAD_DIM), jnp.float32),
        jnp.zeros((seq_count, seq_len, ROTARY_DIM), jnp.float32),
        jnp.zeros((seq_count, seq_len, head_count, VALUE_HEAD_DIM), jnp.float32),
    )
    (k_grad, pe_grad, v_grad), q_grad_blocks = lax.scan(
        backward_block, carry_init, jnp.arange(block_count, dtype=jnp.int32)
    )
    q_grad = jnp.moveaxis(q_grad_blocks, 0, 1).reshape(
        seq_count, seq_len, head_count, PLAIN_HEAD_DIM + ROTARY_DIM
    )
    q_grad = jnp.concatenate(
        [
            q_grad[..., :PLAIN_HEAD_DIM],
            rotate_back(q_grad[..., PLAIN_HEAD_DIM:], cos_heads, sin_heads),
        ],
        axis=-1,
    )
    q_out_grad = narrow(
        q_grad.reshape(seq_count, seq_len, head_count * (PLAIN_HEAD_DIM + ROTARY_DIM))
    )
    kv_out_grad = narrow(
        jnp.concatenate([k_grad, v_grad], axis=-1).reshape(
            seq_count, seq_len, head_count * (PLAIN_HEAD_DIM + VALUE_HEAD_DIM)
        )
    )
    pe_part = rotate_back(pe_grad, cos_part, sin_part)
    qb_b_terms = ADAPT_SCALE * outer_sum(qb_rows, q_out_grad)
    kvb_b_terms = ADAPT_SCALE * outer_sum(kvb_rows, kv_out_grad)
    q_in_part = product_back(q_out_grad, qb_full)
    kv_in_part = product_back(kv_out_grad, kvb_full)
    qb_code_part = ADAPT_SCALE * expand_back(q_out_grad, query_up_picked_out)
    kvb_code_part = ADAPT_SCALE * expand_back(kv_out_grad, keyvalue_up_picked_out)
    q_in_sum, kv_in_sum, pe_sum, qb_code_sum, kvb_code_sum = (
        lax.psum_scatter(
            q_in_part.astype(jnp.bfloat16), "tensor", scatter_dimension=1, tiled=True
        ).astype(jnp.float32),
        lax.psum_scatter(
            kv_in_part.astype(jnp.bfloat16), "tensor", scatter_dimension=1, tiled=True
        ).astype(jnp.float32),
        lax.psum_scatter(
            pe_part.astype(jnp.bfloat16), "tensor", scatter_dimension=1, tiled=True
        ).astype(jnp.float32),
        lax.psum_scatter(
            qb_code_part.astype(jnp.bfloat16), "tensor", scatter_dimension=1, tiled=True
        ).astype(jnp.float32),
        lax.psum_scatter(
            kvb_code_part.astype(jnp.bfloat16), "tensor", scatter_dimension=1, tiled=True
        ).astype(jnp.float32),
    )
    qb_code_grad = narrow(qb_code_sum)
    kvb_code_grad = narrow(kvb_code_sum)
    qb_a_terms = outer_sum(q_input, qb_code_grad)
    kvb_a_terms = outer_sum(kv_input, kvb_code_grad)
    q_norm_grad = q_in_sum + reduce_back(qb_code_grad, query_up_picked_in)
    kv_norm_grad = kv_in_sum + reduce_back(kvb_code_grad, keyvalue_up_picked_in)
    q_latent_grad = narrow(normalize_back(q_latent, q_scale, query_latent_gain, q_norm_grad))
    kv_latent_grad = narrow(
        jnp.concatenate(
            [
                normalize_back(
                    kv_latent[..., :KEYVALUE_LATENT], kv_scale, keyvalue_latent_gain, kv_norm_grad
                ),
                pe_sum,
            ],
            axis=-1,
        )
    )
    qa_b_terms = ADAPT_SCALE * outer_sum(qa_codes, q_latent_grad)
    kva_b_terms = ADAPT_SCALE * outer_sum(kva_codes, kv_latent_grad)
    qa_code_grad = narrow(ADAPT_SCALE * expand_back(q_latent_grad, query_down_picked_out))
    kva_code_grad = narrow(ADAPT_SCALE * expand_back(kv_latent_grad, keyvalue_down_picked_out))
    qa_a_terms = outer_sum(attn_rows, qa_code_grad)
    kva_a_terms = outer_sum(attn_rows, kva_code_grad)
    attn_in_grad = (
        product_back(q_latent_grad, qa_full)
        + product_back(kv_latent_grad, kva_full)
        + reduce_back(qa_code_grad, query_down_picked_in)
        + reduce_back(kva_code_grad, keyvalue_down_picked_in)
    )
    input_grad = middle_grad + normalize_back(
        residual, attn_scale, attention_norm_gain, attn_in_grad
    )

    def set_stack(terms):
        return jnp.stack([per_set(terms[0], pick_high), per_set(terms[1], pick_high)], axis=0)

    shared = lax.psum(
        (
            per_set(qa_a_terms, pick_high),
            per_set(qa_b_terms, pick_high),
            per_set(kva_a_terms, pick_high),
            per_set(kva_b_terms, pick_high),
            per_set(qb_a_terms, pick_high),
            per_set(kvb_a_terms, pick_high),
            set_stack(gate_up_a_terms),
            per_set(out_b_terms, pick_high),
            per_set(down_b_terms, pick_high),
        ),
        ("dp", "tensor"),
    )
    split_sums = (
        lax.psum(per_set(qb_b_terms, pick_high).astype(jnp.bfloat16), "dp").astype(jnp.float32),
        lax.psum(per_set(kvb_b_terms, pick_high).astype(jnp.bfloat16), "dp").astype(jnp.float32),
        lax.psum(set_stack(gate_up_b_terms).astype(jnp.bfloat16), "dp").astype(jnp.float32),
        lax.psum(per_set(out_a_terms, pick_high).astype(jnp.bfloat16), "dp").astype(jnp.float32),
        lax.psum(per_set(down_a_terms, pick_high).astype(jnp.bfloat16), "dp").astype(jnp.float32),
    )
    return (
        outputs,
        input_grad,
        shared[0],
        shared[1],
        shared[2],
        shared[3],
        shared[4],
        split_sums[0],
        shared[5],
        split_sums[1],
        split_sums[3],
        shared[7],
        shared[6],
        split_sums[2],
        split_sums[4],
        shared[8],
    )


def solution(mesh):
    return jax.shard_map(
        per_device,
        mesh=mesh,
        in_specs=(
            P("dp", "tensor", None),
            P("dp", "tensor", None),
            P("dp", None),
            P("dp"),
            P(),
            P(),
            P(),
            P(),
            P("dp", None),
            P("dp", None),
            P("dp", "tensor"),
            P("dp", "tensor"),
            P("tensor", "dp"),
            P(None, "dp", "tensor"),
            P("tensor", "dp"),
            P(),
            P(),
            P(),
            P(),
            P(),
            P(None, None, "tensor"),
            P(),
            P(None, None, "tensor"),
            P(None, "tensor", None),
            P(),
            P(),
            P(None, None, None, "tensor"),
            P(None, "tensor", None),
            P(),
        ),
        out_specs=(
            P("dp", "tensor", None),
            P("dp", "tensor", None),
            P(),
            P(),
            P(),
            P(),
            P(),
            P(None, None, "tensor"),
            P(),
            P(None, None, "tensor"),
            P(None, "tensor", None),
            P(),
            P(),
            P(None, None, None, "tensor"),
            P(None, "tensor", None),
            P(),
        ),
        check_vma=False,
    )
```

profile of v0, /device:TPU:0, one launch (start us, length us, event | category | flops | bytes accessed | tf_op | source)
XLA Modules:
  0.0 1846.7 jit_solution(5104928952190441686)
XLA Ops:
  28.2 54.9 %all-gather.17.cloned.1.call-done = bf16[2560,768]{1,0:T(8,128)(2,1)} async-done(((bf16[320,768]{1,0:T(8,128)(2,1)}), bf16[2560,768]{1,0:T(8,128)(2,1)}) %all-gather.17.cloned.1.call-update) | async-done | bytes 3932176 | tf_op jit(solution)/shard_map/all_gather | solution.py:146
  92.6 34.5 %all_gather.67 = bf16[256,1280]{1,0:T(8,128)(2,1)} all-gather(bf16[32,1280]{1,0:T(8,128)(2,1)S(1)} %copy-done.109), channel_id=1, replica_groups=mesh['dp'=8,'tensor'=4] {'dp'}, dimensions={0}, use_global_device_ids=true | all-gather | bytes 737280 | tf_op jit(solution)/shard_map/all_gather | solution.py:149
  158.8 18.3 all_gather.66
  207.7 90.1 %while.30 = (s32[]{:T(128)}, bf16[2,1,512,10,64]{2,4,3,1,0:T(8,128)(2,1)}, f32[2,1,10,512]{3,2,1,0:T(8,128)}, s32[2]{0:T(128)S(1)}, s32[1,1024]{1,0:T(1,128)S(1)...) while((s32[]{:T(128)}, ...), condition=%wide.region_8.9_spmd.clone, body=%wide.region_5.0_spmd.clone.sunk | while | flops 1726475776 | bytes 121588008 | solution.py:248
  323.5 54.1 %reduce-scatter.12.cloned.1.call-done = bf16[1,256,2560]{2,1,0:T(8,128)(2,1)} async-done(((bf16[1,1024,2560]{2,1,0:T(8,128)(2,1)}), bf16[1,256,2560]{2,1,0:T(8,128)(2,1)}) %reduce-scatter.12.cloned.1.call-update) | async-done | bytes 1310736 | tf_op jit(solution)/shard_map/reduce_scatter | solution.py:256
  426.6 122.4 %all-gather.27.cloned.1.call-done = bf16[1600,2560]{0,1:T(8,128)(2,1)} async-done(((bf16[1600,320]{0,1:T(8,128)(2,1)}), bf16[1600,2560]{0,1:T(8,128)(2,1)}) %all-gather.27.cloned.1.call-update) | async-done | bytes 8192016 | tf_op jit(solution)/shard_map/all_gather | solution.py:267
  590.0 329.6 %all-gather.25.cloned.1.call-done = bf16[2,2560,1600]{2,1,0:T(8,128)(2,1)} async-done(((bf16[2,320,1600]{2,1,0:T(8,128)(2,1)}), bf16[2,2560,1600]{2,1,0:T(8,128)(2,1)}) %all-gather.25.cloned.1.call-update) | async-done | bytes 16384016 | tf_op jit(solution)/shard_map/all_gather | solution.py:266
  919.7 16.1 multiply_add_fusion
  935.8 23.3 %multiply_convert_fusion.1 = (bf16[1024,1600]{0,1:T(8,128)(2,1)}, bf16[1024,1600]{0,1:T(8,128)(2,1)S(1)}, bf16[1024,1600]{0,1:T(8,128)(2,1)}) fusion(f32[1024,1600]{0,1:T(8,128)} %convolution_add_fusion, f32[1024,1600]{0,1:T(8,128)} %multiply_add_fusion, f32[1024,1600]{0,1:T(8,128)} %fusion.212, bf16[2,2560,1600]{2,1,0:T(8,128)(2,1)} %all-gather.25.cloned.1.call-done, ...), kind=kOutput, calls=%fused_computation.79 | convolution fusion | flops 8416460800 | bytes 43253760 | tf_op jit(solution)/shard_map/...i,io->...o/dot_general | solution.py:26
  963.9 15.7 fusion.55
  979.6 15.8 fusion.72
  998.3 48.7 %reduce-scatter.20.cloned.1.call-done = bf16[1,256,2560]{2,1,0:T(8,128)(2,1)} async-done(((bf16[1,1024,2560]{2,1,0:T(8,128)(2,1)}), bf16[1,256,2560]{2,1,0:T(8,128)(2,1)}) %reduce-scatter.20.cloned.1.call-update) | async-done | bytes 1310736 | tf_op jit(solution)/shard_map/reduce_scatter | solution.py:321
  1062.0 31.4 %all-gather.31.cloned.1.call-done = bf16[1,1024,2560]{2,1,0:T(8,128)(2,1)} async-done(((bf16[1,256,2560]{2,1,0:T(8,128)(2,1)}), bf16[1,1024,2560]{2,1,0:T(8,128)(2,1)}) %all-gather.31.cloned.1.call-update) | async-done | bytes 5242896 | tf_op jit(solution)/shard_map/all_gather | solution.py:349
  1101.5 235.5 %while.31 = (s32[]{:T(128)}, f32[1,1024,10,64]{1,3,2,0:T(8,128)}, f32[1,1024,32]{1,2,0:T(8,128)S(1)}, f32[1,1024,10,64]{1,3,2,0:T(8,128)}, f32[2,1,512,10,96]{2,...) while((s32[]{:T(128)}, f32[1,1024,10,64]{1,3,2,0:T(8,128)}, ...), condition=%wide.region_19.20_spmd.clone, body=%wide.region_17.19_spmd.clone.sunk | while | flops 4420431360 | bytes 373803456 | solution.py:401
  1121.6 18.8 %fusion.381 = (f32[10,512]{1,0:T(8,128)S(1)}, f32[1,10,512,1024]{3,2,1,0:T(8,128)}) fusion(f32[10,512,1024]{2,1,0:T(8,128)S(1)} %fusion.378, f32[10,512]{1,0:T(8,128)S(1)} %dynamic-slice_bitcast_fusion.20, bf16[1,1024,32]{1,2,0:T(8,128)(2,1)S(1)} %get-tuple-element.634, bf16[1,1024,10,96]{1,3,2,0:T(8,128)(2,1)} %get-tuple-element.631, ...), kind=kOutput, calls=%fused_computation.33.clone.1 | convolution fusion | flops 366996480 | bytes 63873032 | tf_op jit(solution)/shard_map/while/body/eval_jaxpr/sqhd,skd->shqk/dot_general | solution.py:224
  1183.2 35.6 %dynamic_update_slice.22 = f32[2,1,512,10,96]{2,0,4,3,1:T(2,128)} dynamic-update-slice(f32[2,1,512,10,96]{2,0,4,3,1:T(2,128)} %get-tuple-element.611, f32[1,1,512,10,96]{2,0,4,3,1:T(1,128)S(1)} %copy.196, s32[]{:T(128)S(6)} %copy.214, s32[]{:T(128)} %constant.31.clone.1..sunk.1, s32[]{:T(128)} %constant.31.clone.1..sunk.1, s32[]{:T(128)} %constant.31.clone.1..sunk.1, s32[]{:T(128)} %constant.31.clone.1..sunk.1) | dynamic-update-slice | bytes 3932164 | tf_op jit(solution)/shard_map/while/body/jit(dynamic_update_index_in_dim)/dynamic_update_slice | solution.py:401
  1238.7 18.8 %fusion.381 = (f32[10,512]{1,0:T(8,128)S(1)}, f32[1,10,512,1024]{3,2,1,0:T(8,128)}) fusion(f32[10,512,1024]{2,1,0:T(8,128)S(1)} %fusion.378, f32[10,512]{1,0:T(8,128)S(1)} %dynamic-slice_bitcast_fusion.20, bf16[1,1024,32]{1,2,0:T(8,128)(2,1)S(1)} %get-tuple-element.634, bf16[1,1024,10,96]{1,3,2,0:T(8,128)(2,1)} %get-tuple-element.631, ...), kind=kOutput, calls=%fused_computation.33.clone.1 | convolution fusion | flops 366996480 | bytes 63873032 | tf_op jit(solution)/shard_map/while/body/eval_jaxpr/sqhd,skd->shqk/dot_general | solution.py:224
  1301.0 35.6 %dynamic_update_slice.22 = f32[2,1,512,10,96]{2,0,4,3,1:T(2,128)} dynamic-update-slice(f32[2,1,512,10,96]{2,0,4,3,1:T(2,128)} %get-tuple-element.611, f32[1,1,512,10,96]{2,0,4,3,1:T(1,128)S(1)} %copy.196, s32[]{:T(128)S(6)} %copy.214, s32[]{:T(128)} %constant.31.clone.1..sunk.1, s32[]{:T(128)} %constant.31.clone.1..sunk.1, s32[]{:T(128)} %constant.31.clone.1..sunk.1, s32[]{:T(128)} %constant.31.clone.1..sunk.1) | dynamic-update-slice | bytes 3932164 | tf_op jit(solution)/shard_map/while/body/jit(dynamic_update_index_in_dim)/dynamic_update_slice | solution.py:401
  1400.0 15.3 reduce-scatter.28.cloned.1.call-done
  1417.1 20.0 %reduce-scatter.32.cloned.1.call-done = bf16[1,256,32]{1,2,0:T(8,128)(2,1)} async-done(((bf16[1,1024,32]{1,2,0:T(8,128)(2,1)}), bf16[1,256,32]{1,2,0:T(8,128)(2,1)}) %reduce-scatter.32.cloned.1.call-update) | async-done | bytes 16400 | tf_op jit(solution)/shard_map/reduce_scatter | solution.py:436
  1439.9 28.5 %reduce-scatter.24.cloned.1.call-done = bf16[1,256,768]{2,1,0:T(8,128)(2,1)} async-done(((bf16[1,1024,768]{2,1,0:T(8,128)(2,1)}), bf16[1,256,768]{2,1,0:T(8,128)(2,1)}) %reduce-scatter.24.cloned.1.call-update) | async-done | bytes 393232 | tf_op jit(solution)/shard_map/reduce_scatter | solution.py:430
  1475.9 46.5 %reduce-scatter.16.cloned.1.call-done = bf16[1,256,2560]{2,1,0:T(8,128)(2,1)} async-done(((bf16[1,1024,2560]{2,1,0:T(8,128)(2,1)}), bf16[1,256,2560]{2,1,0:T(8,128)(2,1)}) %reduce-scatter.16.cloned.1.call-update) | async-done | bytes 1310736 | tf_op jit(solution)/shard_map/reduce_scatter | solution.py:286
  1526.0 104.7 %all-reduce.7.cloned.1.call-done = (bf16[8,16,960]{2,1,0:T(8,128)(2,1)}, bf16[8,16,1280]{2,1,0:T(8,128)(2,1)}, bf16[8,640,16]{1,2,0:T(8,128)(2,1)}, bf16[2,8,16,1600]{3,2,1,0:T(8,128)(2,1)}, bf16[8,1600,16]{1,2,0:T(8,128)(2,1)}) async-done(((bf16[8,16,960]{2,1,0:T(8,128)(2,1)}, bf16[8,16,1280]{2,1,0:T(8,128)(2,1)}, bf16[8,640,16]{1,2,0:T(8,128)(2,1)}, bf16[2,8,16,1600]{3,2,1,0:T(8,128)(2,1)}, ...) | async-done | bytes 1966096 | tf_op jit(solution)/shard_map/psum | solution.py:498
  1646.8 182.3 %all-reduce.5.cloned.1.call-done = (f32[8,2560,16]{1,2,0:T(8,128)}, f32[8,16,768]{2,1,0:T(8,128)}, f32[8,2560,16]{1,2,0:T(8,128)}, f32[8,16,288]{2,1,0:T(8,128)}...) async-done(((f32[8,2560,16]{1,2,0:T(8,128)}, f32[8,16,768]{2,1,0:T(8,128)}, ...) | async-done | bytes 8929296 | tf_op jit(solution)/shard_map/psum | solution.py:483
  (586 shorter events, 555.9 us)
Async XLA Ops:
  7.2 75.8 %all-gather.17.cloned.1.call-start = ((), (), s32[]{:S(2)}) async-start(), calls=%async_computation.11 | async-start | bytes 4423680 | tf_op jit(solution)/shard_map/all_gather | solution.py:146
  7.9 137.5 %all-gather.35.cloned.1.call-start = ((), (), s32[]{:S(2)}) async-start(), calls=%async_computation.31 | async-start | bytes 1990656 | tf_op jit(solution)/shard_map/all_gather | solution.py:147
  8.7 186.1 %all-gather.19.cloned.1.call-start = ((), (), s32[]{:S(2)}) async-start(), calls=%async_computation.12 | async-start | bytes 1769472 | tf_op jit(solution)/shard_map/all_gather | solution.py:148
  9.4 191.3 %all-gather.33.cloned.1.call-start = ((), (), s32[]{:S(2)}) async-start(), calls=%async_computation.30 | async-start | bytes 1966080 | tf_op jit(solution)/shard_map/all_gather | solution.py:185
  88.6 215.5 %all-gather.21.cloned.1.call-start = ((), (), s32[]{:S(2)}) async-start(), calls=%async_computation.13 | async-start | bytes 3686400 | tf_op jit(solution)/shard_map/all_gather | solution.py:150
  89.2 234.2 %reduce-scatter.14.cloned.1.call-start = ((), (), s32[]{:S(2)}) async-start(), calls=%async_computation.15 | async-start | bytes 40960 | tf_op jit(solution)/shard_map/reduce_scatter | solution.py:259
  303.8 73.8 %reduce-scatter.12.cloned.1.call-start = ((), (), s32[]{:S(2)}) async-start(), calls=%async_computation.14 | async-start | bytes 6553600 | tf_op jit(solution)/shard_map/reduce_scatter | solution.py:256
  313.1 113.6 %all-gather.29.cloned.1.call-start = ((), (), s32[]{:S(2)}) async-start(), calls=%async_computation.21 | async-start | bytes 6553600 | tf_op jit(solution)/shard_map/all_gather | solution.py:306
  315.6 233.4 %all-gather.27.cloned.1.call-start = ((), (), s32[]{:S(2)}) async-start(), calls=%async_computation.18 | async-start | bytes 9584640 | tf_op jit(solution)/shard_map/all_gather | solution.py:267
  316.4 273.7 %all-gather.23.cloned.1.call-start = ((), (), s32[]{:S(2)}) async-start(), calls=%async_computation.16 | async-start | bytes 6553600 | tf_op jit(solution)/shard_map/all_gather | solution.py:275
  380.3 669.7 %copy-start.10 = (f32[1,256,2560]{2,1,0:T(8,128)}, f32[1,256,2560]{2,1,0:T(8,128)S(1)}, u32[]{:S(2)}) copy-start(f32[1,256,2560]{2,1,0:T(8,128)S(1)} %get-tuple-element.396) | copy-start | bytes 7864324
  381.9 537.8 %all-gather.25.cloned.1.call-start = ((), (), s32[]{:S(2)}) async-start(), calls=%async_computation.17 | async-start | bytes 19169280 | tf_op jit(solution)/shard_map/all_gather | solution.py:266
  382.6 612.9 %reduce-scatter.22.cloned.1.call-start = ((), (), s32[]{:S(2)}) async-start(), calls=%async_computation.23 | async-start | bytes 81920 | tf_op jit(solution)/shard_map/reduce_scatter | solution.py:324
  963.4 83.5 %reduce-scatter.20.cloned.1.call-start = ((), (), s32[]{:S(2)}) async-start(), calls=%async_computation.22 | async-start | bytes 6553600 | tf_op jit(solution)/shard_map/reduce_scatter | solution.py:321
  995.4 98.0 %all-gather.31.cloned.1.call-start = ((), (), s32[]{:S(2)}) async-start(), calls=%async_computation.24 | async-start | bytes 6553600 | tf_op jit(solution)/shard_map/all_gather | solution.py:349
  1052.8 334.6 %reduce-scatter.18.cloned.1.call-start = ((), (), s32[]{:S(2)}) async-start(), calls=%async_computation.20 | async-start | bytes 40960 | tf_op jit(solution)/shard_map/reduce_scatter | solution.py:289
  1056.3 340.2 %reduce-scatter.26.cloned.1.call-start = ((), (), s32[]{:S(2)}) async-start(), calls=%async_computation.26 | async-start | bytes 40960 | tf_op jit(solution)/shard_map/reduce_scatter | solution.py:439
  1349.3 49.1 %reduce-scatter.30.cloned.1.call-start = ((), (), s32[]{:S(2)}) async-start(), calls=%async_computation.28 | async-start | bytes 40960 | tf_op jit(solution)/shard_map/reduce_scatter | solution.py:442
  1354.2 61.1 %reduce-scatter.28.cloned.1.call-start = ((), (), s32[]{:S(2)}) async-start(), calls=%async_computation.27 | async-start | bytes 655360 | tf_op jit(solution)/shard_map/reduce_scatter | solution.py:433
  1357.8 79.3 %reduce-scatter.32.cloned.1.call-start = ((), (), s32[]{:S(2)}) async-start(), calls=%async_computation.29 | async-start | bytes 81920 | tf_op jit(solution)/shard_map/reduce_scatter | solution.py:436
  1358.8 109.6 %reduce-scatter.24.cloned.1.call-start = ((), (), s32[]{:S(2)}) async-start(), calls=%async_computation.25 | async-start | bytes 1966080 | tf_op jit(solution)/shard_map/reduce_scatter | solution.py:430
  1363.3 159.1 %reduce-scatter.16.cloned.1.call-start = ((), (), s32[]{:S(2)}) async-start(), calls=%async_computation.19 | async-start | bytes 6553600 | tf_op jit(solution)/shard_map/reduce_scatter | solution.py:286
  1378.4 252.3 %all-reduce.7.cloned.1.call-start = ((), (), s32[]{:S(2)}) async-start(), calls=%async_computation.33 | async-start | bytes 4063232 | tf_op jit(solution)/shard_map/psum | solution.py:498
  1396.4 432.7 %all-reduce.5.cloned.1.call-start = ((), (), s32[]{:S(2)}) async-start(), calls=%async_computation.32 | async-start | bytes 17956864 | tf_op jit(solution)/shard_map/psum | solution.py:483
  (147 other events, 2442.9 us)
Sparse Core Ops, SparseCore 0:
  10.2 72.7 all-gather.16
  85.2 49.0 all-gather.34
  136.5 43.4 all-gather.18
  182.0 18.6 all-gather.32
  202.7 61.9 all-gather.20
  304.0 19.4 reduce-scatter.13
  326.2 51.3 reduce-scatter.11
  379.7 40.4 all-gather.28
  422.4 126.6 all-gather.26
  551.0 38.9 all-gather.22
  591.6 328.0 all-gather.24
  963.5 19.3 reduce-scatter.21
  995.5 51.3 reduce-scatter.19
  1052.9 40.4 all-gather.30
  1095.6 19.3 reduce-scatter.17
  1349.4 19.3 reduce-scatter.25
  1371.1 19.3 reduce-scatter.29
  1393.5 21.6 reduce-scatter.27
  1417.6 19.3 reduce-scatter.31
  1440.2 28.1 reduce-scatter.23
  1470.9 51.4 reduce-scatter.15
  1527.8 102.8 all-reduce.6
  1639.4 189.6 all-reduce.4
where the time goes:
time: 1860 us; the launch traced here: 1850 us
  waiting for transfers between devices  1070 us (58%)
  matrix products  410 us (22%)
  local copies, waits for them, and re-layouts  167 us (9%)
  other arithmetic  96.5 us (5%)
  blocking collectives  85.3 us (5%)
    all_gather x1, waiting for transfers between devices, per_device(): lax.all_gather(gate_up_matrix, 'dp', axis=1, tiled=True)  330 us
    psum x1, waiting for transfers between devices, per_device(): lax.psum((per_set(qa_a_terms, pick_high), per_set(qa_b_terms, pick_high),...  182 us
    all_gather x1, waiting for transfers between devices, per_device(): lax.all_gather(down_matrix, 'dp', axis=1, tiled=True)  122 us
    psum x1, waiting for transfers between devices, per_device(): lax.psum(per_set(qb_b_terms, pick_high).astype(jnp.bfloat16), 'dp')  105 us
    dynamic_update_slice x4, local copies, waits for them, and re-layouts, per_device(): lax.scan(backward_block, carry_init, jnp.arange(block_count, dtype=jnp.in...  75.2 us
    dot_general x8, matrix products, product(): jnp.einsum('...i,io->...o', left_op, right_op, preferred_element_type=jnp...  71.6 us
    dot_general x4, matrix products, block_scores(): jnp.einsum('sqhd,skd->shqk', q_part[..., PLAIN_HEAD_DIM:], pe_rot, prefer...  65.1 us
    dot_general x8, matrix products, product_back(): jnp.einsum('...o,io->...i', left_op, right_op, preferred_element_type=jnp...  60.5 us
  transfers between devices with their start and end apart: 23, of which 15 were waited for; matrix products, arithmetic and copies ran while one was open for 32% of the time, Pallas kernels for 0%

commit v1 on v0

v1 whole, which is shorter than its diff:
```python
import functools
import math

import jax
import jax.numpy as jnp
from jax import lax
from jax.experimental import pallas as pl
from jax.experimental.pallas import tpu as pltpu
from jax.sharding import PartitionSpec as P

PLAIN_HEAD_DIM = 64
ROTARY_DIM = 32
VALUE_HEAD_DIM = 64
HEAD_LANES = 128
CODE_LANES = 128
RANK = 16
BLOCK_Q = 256
DOC_LANE = 99
DOC_SLOTS = 24

NORM_EPS = 1e-05
RESIDUAL = 1.4 / math.sqrt(62.0)
ADAPT_SCALE = 2.0
SCORE_SCALE = 1.0 / math.sqrt(PLAIN_HEAD_DIM + ROTARY_DIM)
EXP2_SCALE = SCORE_SCALE * math.log2(math.e)
BIG = 1e30
VMEM_LIMIT = 56 * 1024 * 1024
F32 = jnp.float32
BF16 = jnp.bfloat16


def narrow(value):
    return value.astype(BF16)


def dot_nn(a, b):
    return lax.dot_general(a, b, (((1,), (0,)), ((), ())), preferred_element_type=F32)


def dot_nt(a, b):
    return lax.dot_general(a, b, (((1,), (1,)), ((), ())), preferred_element_type=F32)


def dot_tn(a, b):
    return lax.dot_general(a, b, (((0,), (0,)), ((), ())), preferred_element_type=F32)


def normalize(value, gain_vec):
    scale_inv = lax.rsqrt(jnp.mean(value * value, axis=-1, keepdims=True) + NORM_EPS)
    return (value * scale_inv * gain_vec, scale_inv)


def normalize_back(value, scale_inv, gain_vec, grad_in):
    weighted = grad_in * gain_vec
    return scale_inv * weighted - value * scale_inv**3 * jnp.mean(
        value * weighted, axis=-1, keepdims=True
    )


def rope_tables(segments):
    places = jnp.arange(segments.shape[-1], dtype=jnp.int32)
    begins = jnp.concatenate(
        [jnp.ones_like(segments[:, :1]), (segments[:, 1:] != segments[:, :-1]).astype(jnp.int32)],
        axis=1,
    )
    first_place = lax.cummax(places[None, :] * begins, axis=1)
    offsets = (places[None, :] - first_place).astype(F32)
    inv_freq = 10000.0 ** (-2.0 * jnp.arange(ROTARY_DIM // 2, dtype=F32) / ROTARY_DIM)
    angles = offsets[..., None] * inv_freq
    return (jnp.cos(angles)[0], jnp.sin(angles)[0])


def swap(value, axis, bit, size):
    return lax.ppermute(value, axis, [(i, i ^ bit) for i in range(size)])


def place_pieces(sources, copies, outs, name):
    def kernel(*refs):
        src_refs = refs[: len(sources)]
        out_refs = refs[len(sources) : len(sources) + len(outs)]
        sems = refs[-1]
        d = lax.axis_index("dp")
        t = lax.axis_index("tensor")
        started = []
        for n, (src, src_at, out, out_at) in enumerate(copies):
            src_ref = src_refs[src] if src_at is None else src_refs[src].at[src_at]
            copy = pltpu.make_async_copy(src_ref, out_refs[out].at[out_at(d, t)], sems.at[n])
            copy.start()
            started.append(copy)
        for copy in started:
            copy.wait()

    any_spec = pl.BlockSpec(memory_space=pl.ANY)
    moved = sum(s.size * s.dtype.itemsize for s in sources)
    return pl.pallas_call(
        kernel,
        out_shape=[jax.ShapeDtypeStruct(o, BF16) for o in outs],
        in_specs=[any_spec] * len(sources),
        out_specs=[pl.BlockSpec(memory_space=pltpu.VMEM)] * len(outs),
        scratch_shapes=[pltpu.SemaphoreType.DMA((len(copies),))],
        compiler_params=pltpu.CompilerParams(vmem_limit_bytes=VMEM_LIMIT),
        cost_estimate=pl.CostEstimate(flops=0, bytes_accessed=2 * moved, transcendentals=0),
        name=name,
    )(*sources)


def split_three(value):
    high = narrow(value).astype(F32)
    middle = narrow(value - high).astype(F32)
    return high, middle, value - high - middle


def rope_mix(value, cos_l, sin_a, sin_b):
    return (
        value * cos_l
        + pltpu.roll(value, HEAD_LANES - ROTARY_DIM // 2, 1) * sin_a
        + pltpu.roll(value, ROTARY_DIM // 2, 1) * sin_b
    )


def attn_fwd_kernel(
    per_step, q_width, kv_at, xl_ref, wq_ref, wkv_ref, rope_ref, pe_ref, doc_ref, qa_ref, kv_ref, o_ref
):
    length = xl_ref.shape[0]
    lane = lax.broadcasted_iota(jnp.int32, (length, HEAD_LANES), 1)
    q_all = dot_nn(xl_ref[:, :q_width], wq_ref[...])
    kv_all = dot_nn(xl_ref[:, kv_at:], wkv_ref[...])
    kv_ref[...] = narrow(kv_all)
    doc_q = doc_ref[...].astype(F32)
    q_heads, k_heads, kv_turned = [], [], []
    for i in range(per_step):
        span = slice(i * HEAD_LANES, (i + 1) * HEAD_LANES)
        q_one = rope_mix(q_all[:, span], rope_ref[0], rope_ref[1], rope_ref[2]) + doc_q
        q_heads.append(narrow(q_one))
        kv_one = kv_all[:, span]
        k_heads.append(jnp.where(lane < PLAIN_HEAD_DIM, narrow(kv_one), pe_ref[...]))
        kv_turned.append(narrow(kv_one.T))
    key_at = lax.broadcasted_iota(jnp.int32, (BLOCK_Q, BLOCK_Q), 0)
    query_at = lax.broadcasted_iota(jnp.int32, (BLOCK_Q, BLOCK_Q), 1)
    row = lax.broadcasted_iota(jnp.int32, (HEAD_LANES, BLOCK_Q), 0)
    block_lane = lax.broadcasted_iota(jnp.int32, (BLOCK_Q, HEAD_LANES), 1)
    for j in range(length // BLOCK_Q):
        begin, end = j * BLOCK_Q, (j + 1) * BLOCK_Q
        mixed = []
        for i in range(per_step):
            q_part = q_heads[i][begin:end]
            scores = dot_nt(k_heads[i][:end], q_part)
            diag = jnp.where(key_at <= query_at, scores[begin:], -BIG)
            scores = diag if j == 0 else jnp.concatenate([scores[:begin], diag], axis=0)
            top = jnp.max(scores, axis=0, keepdims=True)
            terms = jnp.exp2((scores - top) * EXP2_SCALE)
            total = jnp.sum(terms, axis=0, keepdims=True)
            out_t = dot_nn(kv_turned[i][:, :end], narrow(terms)) * (1.0 / total)
            high, middle, low = split_three(top + jnp.log2(total) * (1.0 / EXP2_SCALE))
            out_t = jnp.where(
                row == 0, -high, jnp.where(row == 1, -middle, jnp.where(row == 2, -low, out_t))
            )
            out_n = out_t.T
            mixed.append(out_n)
            is_lse = (block_lane >= 96) & (block_lane < 99)
            q_saved = jnp.where(is_lse, narrow(pltpu.roll(out_n, 96, 1)), q_part)
            qa_ref[begin:end, i * HEAD_LANES : (i + 1) * HEAD_LANES] = q_saved
        if per_step == 2:
            both = jnp.where(block_lane < 64, pltpu.roll(mixed[0], 64, 1), mixed[1])
            o_ref[begin:end, :] = narrow(both)
        else:
            even = lax.rem(pl.program_id(0), 2) == 0
            moved = jnp.where(even, pltpu.roll(mixed[0], 64, 1), mixed[0])
            mine = (block_lane < 64) == even
            o_ref[begin:end, :] = jnp.where(mine, narrow(moved), o_ref[begin:end, :])


def attn_bwd_kernel(
    per_step, qa_ref, kv_ref, o_ref, do_ref, rope_ref, pe_ref, dq_ref, dkv_ref, dpe_ref, dk_acc, dv_acc
):
    length = qa_ref.shape[0]
    step = pl.program_id(0)
    lane = lax.broadcasted_iota(jnp.int32, (length, HEAD_LANES), 1)
    upper = lane >= 64
    key_at = lax.broadcasted_iota(jnp.int32, (BLOCK_Q, BLOCK_Q), 0)
    query_at = lax.broadcasted_iota(jnp.int32, (BLOCK_Q, BLOCK_Q), 1)
    causal = key_at <= query_at
    out_both = o_ref[...].astype(F32)
    grad_both = do_ref[...].astype(F32)

    @pl.when(step == 0)
    def _():
        dpe_ref[...] = jnp.zeros_like(dpe_ref)

    for i in range(per_step):
        span = slice(i * HEAD_LANES, (i + 1) * HEAD_LANES)
        if per_step == 2:
            turn = i == 0
            grad_one = pltpu.roll(grad_both, 64, 1) if turn else grad_both
            out_one = pltpu.roll(out_both, 64, 1) if turn else out_both
        else:
            even = lax.rem(step, 2) == 0
            grad_one = jnp.where(even, pltpu.roll(grad_both, 64, 1), grad_both)
            out_one = jnp.where(even, pltpu.roll(out_both, 64, 1), out_both)
        grad_one = jnp.where(upper, grad_one, 0.0)
        inner = jnp.sum(jnp.where(upper, grad_one * out_one, 0.0), axis=-1, keepdims=True)
        high, middle, low = split_three(inner)
        grad_aug = jnp.where(
            lane == 0, -high, jnp.where(lane == 1, -middle, jnp.where(lane == 2, -low, grad_one))
        )
        grad_aug = narrow(grad_aug)
        kv_one = kv_ref[:, span]
        ones = jnp.where(lane < 3, 1.0, 0.0).astype(BF16)
        v_aug = jnp.where(upper, kv_one, ones)
        k_aug = jnp.where(lane < 64, kv_one, pe_ref[...])
        k_turned = narrow(k_aug.astype(F32).T)
        for j in reversed(range(length // BLOCK_Q)):
            begin, end = j * BLOCK_Q, (j + 1) * BLOCK_Q
            q_part = qa_ref[begin:end, span]
            probs = jnp.exp2(dot_nt(k_aug[:end], q_part) * EXP2_SCALE)
            diag = jnp.where(causal, probs[begin:], 0.0)
            probs = diag if j == 0 else jnp.concatenate([probs[:begin], diag], axis=0)
            grads = narrow(probs * dot_nt(v_aug[:end], grad_aug[begin:end]))
            dq_part = dot_nn(k_turned[:, :end], grads).T * SCORE_SCALE
            dq_part = rope_mix(
                dq_part,
                rope_ref[0, begin:end, :],
                -rope_ref[1, begin:end, :],
                -rope_ref[2, begin:end, :],
            )
            dq_ref[begin:end, span] = narrow(dq_part)
            dk_part = dot_nn(grads, q_part)
            dv_part = dot_nn(narrow(probs), grad_aug[begin:end])
            if end == length:
                dk_acc[...] = dk_part
                dv_acc[...] = dv_part
            else:
                dk_acc[:end] += dk_part
                dv_acc[:end] += dv_part
        dk_all = dk_acc[...] * SCORE_SCALE
        dkv_ref[:, span] = narrow(jnp.where(upper, dv_acc[...], dk_all))
        dpe_ref[...] += jnp.where(upper & (lane < 96), dk_all, 0.0)


def attend(latents, w_q, w_kv, rope, pe_aug, doc_q, q_width, kv_at):
    length = latents.shape[0]
    heads = w_q.shape[1] // HEAD_LANES
    per_step = 2 if heads % 2 == 0 else 1
    wide = per_step * HEAD_LANES
    whole = lambda a: pl.BlockSpec(a.shape, lambda h: (0,) * a.ndim)
    flops = heads * length * (2 * q_width * 256 + length * 2 * 256)
    return pl.pallas_call(
        functools.partial(attn_fwd_kernel, per_step, q_width, kv_at),
        grid=(heads // per_step,),
        in_specs=[
            whole(latents),
            pl.BlockSpec((w_q.shape[0], wide), lambda h: (0, h)),
            pl.BlockSpec((w_kv.shape[0], wide), lambda h: (0, h)),
            whole(rope),
            whole(pe_aug),
            whole(doc_q),
        ],
        out_specs=[
            pl.BlockSpec((length, wide), lambda h: (0, h)),
            pl.BlockSpec((length, wide), lambda h: (0, h)),
            pl.BlockSpec((length, HEAD_LANES), lambda h: (0, h * per_step // 2)),
        ],
        out_shape=[
            jax.ShapeDtypeStruct((length, heads * HEAD_LANES), BF16),
            jax.ShapeDtypeStruct((length, heads * HEAD_LANES), BF16),
            jax.ShapeDtypeStruct((length, heads * VALUE_HEAD_DIM), BF16),
        ],
        compiler_params=pltpu.CompilerParams(vmem_limit_bytes=VMEM_LIMIT),
        cost_estimate=pl.CostEstimate(
            flops=2 * flops, bytes_accessed=16 * 1024 * 1024, transcendentals=heads * length * length // 2
        ),
        name="attend",
    )(latents, w_q, w_kv, rope, pe_aug, doc_q)


def attend_back(q_aug, kv, heads_out, heads_grad, rope, pe_aug):
    length = q_aug.shape[0]
    heads = q_aug.shape[1] // HEAD_LANES
    per_step = 2 if heads % 2 == 0 else 1
    wide = per_step * HEAD_LANES
    whole = lambda a: pl.BlockSpec(a.shape, lambda h: (0,) * a.ndim)
    columns = pl.BlockSpec((length, wide), lambda h: (0, h))
    packed = pl.BlockSpec((length, HEAD_LANES), lambda h: (0, h * per_step // 2))
    return pl.pallas_call(
        functools.partial(attn_bwd_kernel, per_step),
        grid=(heads // per_step,),
        in_specs=[columns, columns, packed, packed, whole(rope), whole(pe_aug)],
        out_specs=[columns, columns, pl.BlockSpec((length, HEAD_LANES), lambda h: (0, 0))],
        out_shape=[
            jax.ShapeDtypeStruct((length, heads * HEAD_LANES), BF16),
            jax.ShapeDtypeStruct((length, heads * HEAD_LANES), BF16),
            jax.ShapeDtypeStruct((length, HEAD_LANES), F32),
        ],
        scratch_shapes=[
            pltpu.VMEM((length, HEAD_LANES), F32),
            pltpu.VMEM((length, HEAD_LANES), F32),
        ],
        compiler_params=pltpu.CompilerParams(vmem_limit_bytes=VMEM_LIMIT),
        cost_estimate=pl.CostEstimate(
            flops=heads * length * length * 256 * 10,
            bytes_accessed=16 * 1024 * 1024,
            transcendentals=heads * length * length // 2,
        ),
        name="attend_back",
    )(q_aug, kv, heads_out, heads_grad, rope, pe_aug)


def ffn_kernel(main, tail, tail_wide, x_ref, g_ref, w_ref, grad_ref, hid_ref):
    gu_wide = 2 * main + tail_wide
    pre = dot_nn(x_ref[...], w_ref[:, :gu_wide])
    back = dot_nn(g_ref[...], w_ref[:, gu_wide:])

    def middle(gate, up, hid_grad):
        sig = 1.0 / (1.0 + jnp.exp(-gate))
        silu = gate * sig
        gate_grad = hid_grad * up * (sig * (1.0 + gate * (1.0 - sig)))
        return silu * up, gate_grad, hid_grad * silu

    hid, gate_grad, up_grad = middle(pre[:, :main], pre[:, main + tail_wide :], back)
    hid_ref[:, :main] = narrow(hid)
    grad_ref[:, :main] = narrow(gate_grad)
    grad_ref[:, main + tail_wide :] = narrow(up_grad)
    if tail_wide:
        pre_tail = pre[:, main : main + tail_wide]
        back_tail = dot_nn(g_ref[...], w_ref[:, main : main + tail_wide])
        up_tail = pltpu.roll(pre_tail, tail_wide - tail, 1)
        hid_tail = pltpu.roll(back_tail, tail_wide - 2 * tail, 1)
        hid, gate_grad, up_grad = middle(pre_tail, up_tail, hid_tail)
        lane = lax.broadcasted_iota(jnp.int32, pre_tail.shape, 1)
        hid = pltpu.roll(hid, 2 * tail, 1)
        hid = jnp.where((lane >= 2 * tail) & (lane < 3 * tail), hid, 0.0)
        hid_ref[:, main:] = narrow(hid)
        up_grad = pltpu.roll(up_grad, tail, 1)
        both = jnp.where(lane < tail, gate_grad, jnp.where(lane < 2 * tail, up_grad, 0.0))
        grad_ref[:, main : main + tail_wide] = narrow(both)


def ffn_middle(x_rows, g_rows, weight, main, tail, tail_wide):
    rows, depth = x_rows.shape
    block = 256
    width = weight.shape[1]
    return pl.pallas_call(
        functools.partial(ffn_kernel, main, tail, tail_wide),
        grid=(rows // block,),
        in_specs=[
            pl.BlockSpec((block, depth), lambda i: (i, 0)),
            pl.BlockSpec((block, depth), lambda i: (i, 0)),
            pl.BlockSpec((depth, width), lambda i: (0, 0)),
        ],
        out_specs=[
            pl.BlockSpec((block, 2 * main + tail_wide), lambda i: (i, 0)),
            pl.BlockSpec((block, main + tail_wide), lambda i: (i, 0)),
        ],
        out_shape=[
            jax.ShapeDtypeStruct((rows, 2 * main + tail_wide), BF16),
            jax.ShapeDtypeStruct((rows, main + tail_wide), BF16),
        ],
        compiler_params=pltpu.CompilerParams(vmem_limit_bytes=VMEM_LIMIT),
        cost_estimate=pl.CostEstimate(
            flops=2 * rows * depth * (width + tail_wide),
            bytes_accessed=2 * (2 * rows * depth + depth * width + rows * width),
            transcendentals=rows * main,
        ),
        name="ffn_middle",
    )(x_rows, g_rows, weight)


def per_device(
    n_dp,
    n_t,
    inputs,
    cotangent,
    document_numbers,
    sequence_adapter_index,
    attention_norm_gain,
    query_latent_gain,
    keyvalue_latent_gain,
    feedforward_norm_gain,
    query_down_matrix,
    keyvalue_down_matrix,
    query_up_matrix,
    keyvalue_up_matrix,
    output_matrix,
    gate_up_matrix,
    down_matrix,
    query_down_adapter_in,
    query_down_adapter_out,
    keyvalue_down_adapter_in,
    keyvalue_down_adapter_out,
    query_up_adapter_in,
    query_up_adapter_out,
    keyvalue_up_adapter_in,
    keyvalue_up_adapter_out,
    output_adapter_in,
    output_adapter_out,
    gate_up_adapter_in,
    gate_up_adapter_out,
    down_adapter_in,
    down_adapter_out,
):
    d = lax.axis_index("dp")
    t = lax.axis_index("tensor")
    pair = n_dp // 4
    low_bits = [b for b in (1, 2, 4, 8, 16) if b < pair]
    high = n_dp // 2
    y_bits = [b for b in (2, 4, 8, 16) if b < n_t]
    zl = lax.rem(d // pair, 2)
    core = lax.rem(t, 2)
    first = zl == 0
    size = {"dp": n_dp, "tensor": n_t}
    rows = inputs.shape[1]
    width = inputs.shape[2]
    length = document_numbers.shape[1]
    q_lat = query_down_matrix.shape[1]
    kv_all = keyvalue_down_matrix.shape[1]
    kv_lat = kv_all - ROTARY_DIM
    heads = keyvalue_up_matrix.shape[1] // HEAD_LANES
    group_count = query_down_adapter_in.shape[0]
    aug = width + CODE_LANES
    half_rows = rows // 2

    def hop(value, step):
        return swap(value, step[0], step[1], size[step[0]])

    def spread(piece, steps):
        held = {(0, 0): piece}
        for step in steps:
            for key in list(held):
                new = (key[0] ^ step[1], key[1]) if step[0] == "dp" else (key[0], key[1] ^ step[1])
                held[new] = hop(held[key], step)
        return held

    def collect(parts, steps):
        held = dict(parts)
        for step in steps:
            for key in list(held):
                has = (key[0] if step[0] == "dp" else key[1]) & step[1]
                if not has:
                    new = (
                        (key[0] ^ step[1], key[1])
                        if step[0] == "dp"
                        else (key[0], key[1] ^ step[1])
                    )
                    came = hop(narrow(held.pop(new)), step)
                    held[key] = held[key].astype(F32) + came.astype(F32)
        return held[(0, 0)]

    outer_first = [("dp", high), ("dp", pair)] + [("dp", b) for b in reversed(low_bits)]
    inner_first = [("dp", b) for b in low_bits] + [("dp", high), ("dp", pair)]
    t_slow = [("tensor", b) for b in reversed(y_bits)]
    t_core = [("tensor", 1)]

    set_all = lax.all_gather(sequence_adapter_index, "dp", axis=0, tiled=True)
    set_own = sequence_adapter_index[0]
    set_peer = lax.dynamic_index_in_dim(set_all, jnp.bitwise_xor(d, pair), 0, keepdims=False)
    set_even = jnp.where(first, set_own, set_peer)
    set_odd = jnp.where(first, set_peer, set_own)

    def pick(table, index):
        return lax.dynamic_index_in_dim(table, index, 0, keepdims=False)

    def turned(table):
        return jnp.swapaxes(table, -1, -2)

    qa_in, kva_in = pick(turned(query_down_adapter_in), set_own), pick(
        turned(keyvalue_down_adapter_in), set_own
    )
    qa_out, kva_out = pick(query_down_adapter_out, set_own), pick(keyvalue_down_adapter_out, set_own)
    qb_in, kvb_in = pick(turned(query_up_adapter_in), set_own), pick(
        turned(keyvalue_up_adapter_in), set_own
    )
    qb_out, kvb_out = pick(query_up_adapter_out, set_own), pick(keyvalue_up_adapter_out, set_own)
    out_in, out_out = pick(turned(output_adapter_in), set_own), pick(output_adapter_out, set_own)
    gu_in = jnp.concatenate(
        [pick(turned(gate_up_adapter_in[0]), set_own), pick(turned(gate_up_adapter_in[1]), set_own)],
        axis=0,
    )
    down_out = pick(down_adapter_out, set_own)

    down_shard = query_down_matrix.shape[0]
    core_rows = down_shard // 2
    lat_pad = -(-(q_lat + kv_all) // 128) * 128
    down_both = jnp.concatenate([query_down_matrix, keyvalue_down_matrix], axis=1)
    down_mine = lax.dynamic_index_in_dim(
        down_both.reshape(2, core_rows, q_lat + kv_all), core, 0, keepdims=False
    )
    cut = -(-core_rows // 32) * 16
    down_a = spread(down_mine[:cut], outer_first)
    down_b = spread(down_mine[cut:], inner_first)
    sources, copies = [], []
    for held, at, count in ((down_a, 0, cut), (down_b, cut, core_rows - cut)):
        for (r, _), piece in held.items():
            copies.append(
                (
                    len(sources),
                    None,
                    0,
                    lambda dd, tt, r=r, at=at, count=count: (
                        jnp.bitwise_xor(dd, r),
                        pl.ds(at, count),
                    ),
                )
            )
            sources.append(piece)
    (down_core,) = place_pieces(
        sources, copies, [(n_dp, core_rows, q_lat + kv_all)], "place_down_core"
    )
    down_other = hop(down_core, t_core[0])
    (down_full,) = place_pieces(
        [down_core, down_other],
        [
            (0, None, 0, lambda dd, tt: (slice(None), lax.rem(tt, 2))),
            (1, None, 0, lambda dd, tt: (slice(None), 1 - lax.rem(tt, 2))),
        ],
        [(n_dp, 2, core_rows, q_lat + kv_all)],
        "place_down",
    )
    w_down = down_full.reshape(width, q_lat + kv_all)

    qb_rows, kvb_rows = query_up_matrix.shape[0], keyvalue_up_matrix.shape[0]
    head_q = PLAIN_HEAD_DIM + ROTARY_DIM

    def pad_heads(value):
        split = value.reshape(value.shape[0], heads, head_q)
        return jnp.pad(split, ((0, 0), (0, 0), (0, HEAD_LANES - head_q))).reshape(
            value.shape[0], heads * HEAD_LANES
        )

    up_piece = jnp.concatenate([pad_heads(query_up_matrix), keyvalue_up_matrix], axis=0)
    up_held = spread(up_piece, outer_first)
    q_aug_rows = jnp.concatenate(
        [
            narrow(ADAPT_SCALE * pad_heads(qb_out)),
            jnp.zeros((CODE_LANES - RANK, heads * HEAD_LANES), BF16),
        ],
        axis=0,
    )
    kv_aug_rows = jnp.concatenate(
        [
            jnp.zeros((RANK, heads * HEAD_LANES), BF16),
            narrow(ADAPT_SCALE * kvb_out),
            jnp.zeros((CODE_LANES - 2 * RANK, heads * HEAD_LANES), BF16),
        ],
        axis=0,
    )
    sources, copies = [q_aug_rows, kv_aug_rows], [
        (0, None, 0, lambda dd, tt: (pl.ds(q_lat, CODE_LANES),)),
        (1, None, 1, lambda dd, tt: (pl.ds(0, CODE_LANES),)),
    ]
    for (r, _), piece in up_held.items():
        copies.append(
            (
                len(sources),
                pl.ds(0, qb_rows),
                0,
                lambda dd, tt, r=r: (
                    pl.ds(pl.multiple_of(jnp.bitwise_xor(dd, r) * qb_rows, 16), qb_rows),
                ),
            )
        )
        copies.append(
            (
                len(sources),
                pl.ds(qb_rows, kvb_rows),
                1,
                lambda dd, tt, r=r: (
                    pl.ds(
                        pl.multiple_of(CODE_LANES + jnp.bitwise_xor(dd, r) * kvb_rows, 16),
                        kvb_rows,
                    ),
                ),
            )
        )
        sources.append(piece)
    w_q, w_kv = place_pieces(
        sources,
        copies,
        [
            (q_lat + CODE_LANES, heads * HEAD_LANES),
            (CODE_LANES + kv_lat, heads * HEAD_LANES),
        ],
        "place_up",
    )

    def place_rows(held, extra, name):
        count = held[(0, 0)].shape[0]
        sources, copies = [extra], [(0, None, 0, lambda dd, tt: (pl.ds(width, CODE_LANES),))]
        for (r, _), piece in held.items():
            copies.append(
                (
                    len(sources),
                    None,
                    0,
                    lambda dd, tt, r=r: (
                        pl.ds(pl.multiple_of(jnp.bitwise_xor(dd, r) * count, 16), count),
                    ),
                )
            )
            sources.append(piece)
        (full,) = place_pieces(sources, copies, [(aug, extra.shape[1])], name)
        return full

    out_held = spread(output_matrix.T, outer_first)
    out_extra = jnp.concatenate(
        [out_in, jnp.zeros((CODE_LANES - RANK, out_in.shape[1]), BF16)], axis=0
    )
    w_out = place_rows(out_held, out_extra, "place_out")

    hidden = down_matrix.shape[0]
    half = hidden // 2
    main = half // 128 * 128
    tail = half - main
    tail_wide = -(-3 * tail // 128) * 128
    chunks = 2 if (main // 128) % 2 == 0 else 1
    step_wide = main // chunks

    def columns(gate_part, up_part, down_part, chunk):
        at = slice(chunk * step_wide, (chunk + 1) * step_wide)
        out = [gate_part[:, at]]
        if tail and chunk == chunks - 1:
            out += [gate_part[:, main:], up_part[:, main:], down_part[:, main:]]
            if tail_wide > 3 * tail:
                out.append(jnp.zeros((gate_part.shape[0], tail_wide - 3 * tail), BF16))
        out += [up_part[:, at], down_part[:, at]]
        return jnp.concatenate(out, axis=1)

    def halves(value):
        return value[:, :half], value[:, half:]

    down_turned = down_matrix.T
    mats = [halves(gate_up_matrix[0]), halves(gate_up_matrix[1]), halves(down_turned)]
    zero_codes = jnp.zeros((RANK, half), BF16)

    def half_of(value):
        left, right = halves(value)
        return jnp.where(first, left, right)

    extra_parts = []
    for which in (set_even, set_odd):
        gate_b = half_of(pick(gate_up_adapter_out[0], which)) * 2
        up_b = half_of(pick(gate_up_adapter_out[1], which)) * 2
        down_a_t = half_of(pick(turned(down_adapter_in), which))
        extra_parts.append((gate_b, up_b, down_a_t))

    ffn_weights = []
    for chunk in range(chunks):
        left = columns(mats[0][0], mats[1][0], mats[2][0], chunk)
        right = columns(mats[0][1], mats[1][1], mats[2][1], chunk)
        mine = jnp.where(first, left, right)
        other = jnp.where(first, right, left)
        held = {(0, 0): mine, (pair, 0): hop(other, ("dp", pair))}
        for step in [("dp", high)] + [("dp", b) for b in reversed(low_bits)]:
            for key in list(held):
                held[(key[0] ^ step[1], 0)] = hop(held[key], step)
        extra = []
        for gate_b, up_b, down_a_t in extra_parts:
            extra.append(columns(gate_b, zero_codes, down_a_t, chunk))
            extra.append(columns(zero_codes, up_b, zero_codes, chunk))
        extra.append(jnp.zeros((CODE_LANES - 4 * RANK, extra[0].shape[1]), BF16))
        ffn_weights.append(
            place_rows(held, jnp.concatenate(extra, axis=0), "place_ffn_" + str(chunk))
        )

    def code_lanes(codes):
        none = jnp.zeros_like(codes)
        return jnp.concatenate(
            [
                jnp.where(first, codes, none),
                jnp.where(first, none, codes),
                jnp.zeros((codes.shape[0], CODE_LANES - 4 * RANK), codes.dtype),
            ],
            axis=1,
        )

    def own_codes(value):
        lanes = value[:, width:]
        return jnp.where(first, lanes[:, : 2 * RANK], lanes[:, 2 * RANK : 4 * RANK])

    group_a = t_slow + [("dp", pair)]
    group_b = [("dp", pair)] + t_slow
    group_keys = [(p, r) for r in range(n_t) for p in (0, pair)]
    odd_keys = [k for k in group_keys if k[1] & 1]
    even_keys = [k for k in group_keys if not k[1] & 1]
    order = odd_keys + even_keys

    def spread_group(value):
        top = spread(value[:half_rows], group_a + t_core)
        bottom = spread(value[half_rows:], group_b + t_core)
        parts = []
        for key in order:
            parts += [top[key], bottom[key]]
        return jnp.concatenate(parts, axis=0)

    out_grad = cotangent[0].astype(F32)
    ffn_grad = narrow(RESIDUAL * out_grad)
    down_code_grad = narrow(ADAPT_SCALE * dot_nt(ffn_grad, down_out))
    none16 = jnp.zeros((rows, RANK), BF16)
    g_own = jnp.concatenate(
        [ffn_grad, code_lanes(jnp.concatenate([down_code_grad, none16], axis=1))], axis=1
    )
    g_all = spread_group(g_own)

    cos_part, sin_part = rope_tables(document_numbers)
    zeros_l = jnp.zeros((length, PLAIN_HEAD_DIM), F32)
    zeros_r = jnp.zeros((length, HEAD_LANES - 96), F32)
    none_16 = jnp.zeros_like(sin_part)
    rope = jnp.stack(
        [
            jnp.concatenate([zeros_l + 1.0, cos_part, cos_part, zeros_r], axis=1),
            jnp.concatenate([zeros_l, -sin_part, none_16, zeros_r], axis=1),
            jnp.concatenate([zeros_l, none_16, sin_part, zeros_r], axis=1),
        ],
        axis=0,
    )
    lane_ids = jnp.arange(HEAD_LANES, dtype=jnp.int32)[None, :]
    doc_lane = (lane_ids >= DOC_LANE) & (lane_ids < DOC_LANE + DOC_SLOTS)
    is_doc = document_numbers[0][:, None] == lane_ids - DOC_LANE
    doc_q = narrow(jnp.where(doc_lane & is_doc, 1.0, 0.0))
    doc_k = jnp.where(
        doc_lane & ~is_doc, -BIG, jnp.where((lane_ids >= 96) & (lane_ids < 99), 1.0, 0.0)
    )

    residual = inputs[0].astype(F32)
    attn_normed, attn_scale = normalize(residual, attention_norm_gain)
    attn_rows = narrow(attn_normed)
    down_in = jnp.concatenate([qa_in, kva_in], axis=0)
    down_codes_in = narrow(dot_nt(attn_rows, down_in))
    down_b_rows = jnp.concatenate(
        [
            jnp.pad(qa_out, ((0, 0), (0, kv_all))),
            jnp.pad(kva_out, ((0, 0), (q_lat, 0))),
        ],
        axis=0,
    )
    latent = dot_nn(attn_rows, w_down) + ADAPT_SCALE * dot_nn(down_codes_in, down_b_rows)
    q_latent = latent[:, :q_lat]
    kv_latent = latent[:, q_lat : q_lat + kv_lat]
    q_normed, q_scale = normalize(q_latent, query_latent_gain)
    kv_normed, kv_scale = normalize(kv_latent, keyvalue_latent_gain)
    q_input = narrow(q_normed)
    kv_input = narrow(kv_normed)
    pe_input = narrow(latent[:, q_lat + kv_lat :])
    qb_codes = narrow(dot_nt(q_input, qb_in))
    kvb_codes = narrow(dot_nt(kv_input, kvb_in))
    pe_at = q_lat + 2 * RANK
    lat_own = jnp.concatenate(
        [
            q_input,
            qb_codes,
            kvb_codes,
            pe_input,
            jnp.zeros((rows, CODE_LANES - 2 * RANK - ROTARY_DIM), BF16),
            kv_input,
        ],
        axis=1,
    )

    def by_tensor_place(held, name):
        keys = list(held)
        shape = held[keys[0]].shape
        (full,) = place_pieces(
            [held[k] for k in keys],
            [
                (n, None, 0, lambda dd, tt, r=k[1]: (jnp.bitwise_xor(tt, r),))
                for n, k in enumerate(keys)
            ],
            [(n_t,) + shape],
            name,
        )
        return full.reshape((n_t * shape[0],) + shape[1:])

    def relative(value, name):
        blocks = value.reshape(n_t, value.shape[0] // n_t, value.shape[1])
        (full,) = place_pieces(
            [blocks],
            [(0, r, 0, lambda dd, tt, r=r: (jnp.bitwise_xor(tt, r),)) for r in range(n_t)],
            [blocks.shape],
            name,
        )
        return full

    lat_all = by_tensor_place(spread(lat_own, t_slow + t_core), "place_latents")
    pe_rows = lat_all[:, pe_at : pe_at + ROTARY_DIM].astype(F32)
    pe_a, pe_b = pe_rows[:, : ROTARY_DIM // 2], pe_rows[:, ROTARY_DIM // 2 :]
    pe_aug = narrow(
        jnp.concatenate(
            [
                zeros_l,
                pe_a * cos_part - pe_b * sin_part,
                pe_b * cos_part + pe_a * sin_part,
                zeros_r,
            ],
            axis=1,
        )
        + doc_k
    )
    q_aug, kv, head_out = attend(
        lat_all, w_q, w_kv, rope, pe_aug, doc_q, q_lat + CODE_LANES, q_lat
    )
    head_rel = relative(head_out, "place_heads")
    parts = {}
    for r in [r for r in range(n_t) if r & 1] + [r for r in range(n_t) if not r & 1]:
        parts[(0, r)] = dot_nt(head_rel[r], w_out)
    attn_sum = collect(parts, t_core + t_slow[::-1])
    out_codes = narrow(attn_sum[:, width : width + RANK])
    middle = residual + RESIDUAL * (
        attn_sum[:, :width] + ADAPT_SCALE * dot_nn(out_codes, out_out)
    )

    ffn_normed, ffn_scale = normalize(middle, feedforward_norm_gain)
    ffn_rows = narrow(ffn_normed)
    gu_codes = narrow(dot_nt(ffn_rows, gu_in))
    x_own = jnp.concatenate([ffn_rows, code_lanes(gu_codes)], axis=1)
    x_all = spread_group(x_own)
    grads, hids = [], []
    for chunk in range(chunks):
        last = chunk == chunks - 1
        grad_c, hid_c = ffn_middle(
            x_all, g_all, ffn_weights[chunk], step_wide, tail if last else 0, tail_wide if last else 0
        )
        grads.append(grad_c)
        hids.append(hid_c)

    def gu_columns(chunk):
        return grads[chunk].shape[1]

    odd_rows = len(odd_keys) * rows

    def group_parts(terms):
        odd = narrow(terms(slice(0, odd_rows)))
        came = hop(odd, t_core[0])
        chip = terms(slice(odd_rows, 2 * odd_rows)) + came.astype(F32)
        return chip

    def finish(chip, steps_a, steps_b):
        tops, bottoms = {}, {}
        for n, key in enumerate(even_keys):
            piece = chip[n * rows : (n + 1) * rows]
            tops[key] = piece[:half_rows]
            bottoms[key] = piece[half_rows:]
        return collect(tops, steps_a), collect(bottoms, steps_b)

    def ffn_in_terms(at):
        out = dot_nt(grads[0][at], ffn_weights[0][:, : gu_columns(0)])
        for chunk in range(1, chunks):
            out = out + dot_nt(grads[chunk][at], ffn_weights[chunk][:, : gu_columns(chunk)])
        return out

    def down_terms(at):
        out = 0.0
        for chunk in range(chunks):
            weight = ffn_weights[chunk]
            hid = hids[chunk][at]
            out = out + dot_nt(hid[:, :step_wide], weight[:, gu_columns(chunk) :])
            if hid.shape[1] > step_wide:
                out = out + dot_nt(
                    hid[:, step_wide:], weight[:, step_wide : step_wide + tail_wide]
                )
        return out

    ffn_in_halves = finish(group_parts(ffn_in_terms), group_a[::-1], group_b[::-1])
    tops = []
    for n, ffn_in_aug in enumerate(ffn_in_halves):
        at = slice(n * half_rows, (n + 1) * half_rows)
        gu_code_grad = narrow(own_codes(ffn_in_aug))
        ffn_in_grad = ffn_in_aug[:, :width] + dot_nn(gu_code_grad, gu_in)
        middle_grad = out_grad[at] + normalize_back(
            middle[at], ffn_scale[at], feedforward_norm_gain, ffn_in_grad
        )
        attn_grad = narrow(RESIDUAL * middle_grad)
        out_code_grad = narrow(ADAPT_SCALE * dot_nt(attn_grad, out_out))
        attn_grad_aug = jnp.concatenate(
            [attn_grad, out_code_grad, jnp.zeros((half_rows, CODE_LANES - RANK), BF16)], axis=1
        )
        tops.append((gu_code_grad, middle_grad, attn_grad_aug, spread(attn_grad_aug, t_slow + t_core)))
    gu_code_grad = jnp.concatenate([tops[0][0], tops[1][0]], axis=0)
    middle_grad = jnp.concatenate([tops[0][1], tops[1][1]], axis=0)
    attn_grad_aug = jnp.concatenate([tops[0][2], tops[1][2]], axis=0)
    attn_grad = attn_grad_aug[:, :width]

    grad_rel = []
    for r in range(n_t):
        both = jnp.concatenate([tops[0][3][(0, r)], tops[1][3][(0, r)]], axis=0)
        grad_rel.append(both)
    codes_rel = jnp.stack([g[:, width:] for g in grad_rel], axis=0)
    heads_grad = by_tensor_place(
        {(0, r): narrow(dot_nn(grad_rel[r], w_out)) for r in range(n_t)}, "place_heads_grad"
    )
    out_a = dot_tn(codes_rel.reshape(length, CODE_LANES), head_rel.reshape(length, -1))[:RANK]
    dq, dkv, dpe = attend_back(q_aug, kv, head_out, heads_grad, rope, pe_aug)

    down_a_sum, down_b_sum = finish(
        group_parts(down_terms), [("dp", pair)] + t_slow[::-1], [("dp", pair)] + t_slow[::-1]
    )
    ffn_out = jnp.concatenate([down_a_sum, down_b_sum], axis=0)
    down_codes = narrow(own_codes(ffn_out)[:, :RANK])
    outputs = narrow(
        middle
        + RESIDUAL * (ffn_out[:, :width] + ADAPT_SCALE * dot_nn(down_codes, down_out))
    )

    pe_g = dpe[:, PLAIN_HEAD_DIM : PLAIN_HEAD_DIM + ROTARY_DIM]
    pe_ga, pe_gb = pe_g[:, : ROTARY_DIM // 2], pe_g[:, ROTARY_DIM // 2 :]
    pe_grad = jnp.concatenate(
        [pe_ga * cos_part + pe_gb * sin_part, pe_gb * cos_part - pe_ga * sin_part], axis=1
    )
    from_q = dot_nt(dq, w_q)
    from_kv = dot_nt(dkv, w_kv)
    lat_grad = jnp.concatenate(
        [
            from_q[:, :q_lat],
            from_q[:, q_lat:]
            + from_kv[:, :CODE_LANES]
            + jnp.pad(pe_grad, ((0, 0), (2 * RANK, CODE_LANES - 2 * RANK - ROTARY_DIM))),
            from_kv[:, CODE_LANES:],
        ],
        axis=1,
    )
    lat_rel = relative(narrow(lat_grad), "place_latent_grads")
    lat_sum = collect({(0, r): lat_rel[r] for r in range(n_t)}, t_core + t_slow[::-1])
    qb_code_grad = narrow(lat_sum[:, q_lat : q_lat + RANK])
    kvb_code_grad = narrow(lat_sum[:, q_lat + RANK : q_lat + 2 * RANK])
    pe_sum = lat_sum[:, pe_at : pe_at + ROTARY_DIM]
    q_norm_grad = lat_sum[:, :q_lat] + dot_nn(qb_code_grad, qb_in)
    kv_norm_grad = lat_sum[:, q_lat + CODE_LANES :] + dot_nn(kvb_code_grad, kvb_in)
    latent_grad = narrow(
        jnp.concatenate(
            [
                normalize_back(q_latent, q_scale, query_latent_gain, q_norm_grad),
                normalize_back(kv_latent, kv_scale, keyvalue_latent_gain, kv_norm_grad),
                pe_sum,
            ],
            axis=1,
        )
    )
    code_grad = narrow(ADAPT_SCALE * dot_nt(latent_grad, down_b_rows))
    attn_in_grad = dot_nt(latent_grad, w_down) + dot_nn(code_grad, down_in)
    input_grad = middle_grad + normalize_back(
        residual, attn_scale, attention_norm_gain, attn_in_grad
    )

    onehot = narrow(set_all[:, None] == jnp.arange(group_count, dtype=jnp.int32)[None, :])

    def to_sets(terms):
        return jnp.einsum("sk,srn->krn", onehot, terms, preferred_element_type=F32)

    def shared_terms(terms, name):
        count = terms.shape[0] // n_t
        split = relative(narrow(terms), name + "_split")
        own = collect({(0, r): split[r] for r in range(n_t)}, t_core + t_slow[::-1])
        held = spread(narrow(own), outer_first + t_slow + t_core)
        keys = list(held)
        (full,) = place_pieces(
            [held[k] for k in keys],
            [
                (
                    n,
                    None,
                    0,
                    lambda dd, tt, k=k: (jnp.bitwise_xor(dd, k[0]), jnp.bitwise_xor(tt, k[1])),
                )
                for n, k in enumerate(keys)
            ],
            [(n_dp, n_t, count, terms.shape[1])],
            name + "_place",
        )
        return full.reshape(n_dp, n_t * count, terms.shape[1])

    def split_terms(terms, name):
        held = spread(terms, outer_first)
        keys = list(held)
        (full,) = place_pieces(
            [held[k] for k in keys],
            [
                (n, None, 0, lambda dd, tt, k=k: (jnp.bitwise_xor(dd, k[0]),))
                for n, k in enumerate(keys)
            ],
            [(n_dp,) + terms.shape],
            name,
        )
        return full

    gu_a = dot_tn(gu_code_grad, ffn_rows)
    out_b = ADAPT_SCALE * dot_tn(out_codes, attn_grad)
    down_b = ADAPT_SCALE * dot_tn(down_codes, ffn_grad)
    early = shared_terms(jnp.concatenate([gu_a, out_b, down_b], axis=0), "early")

    def uncolumn(parts, at_tail, first_at):
        out = [parts[c][:, first_at(c) : first_at(c) + step_wide] for c in range(chunks)]
        if tail:
            out.append(parts[-1][:, step_wide + at_tail * tail : step_wide + (at_tail + 1) * tail])
        return jnp.concatenate(out, axis=1)

    x_codes, g_codes = x_all[:, width:], g_all[:, width:]
    gu_b = [dot_tn(x_codes, g) for g in grads]
    down_at = [dot_tn(g_codes, h) for h in hids]
    gate_b_all = ADAPT_SCALE * uncolumn(gu_b, 0, lambda c: 0)
    up_b_all = ADAPT_SCALE * uncolumn(gu_b, 1, lambda c: gu_columns(c) - step_wide)
    down_a_all = uncolumn(down_at, 2, lambda c: 0)
    packed = []
    for p in range(2):
        at = 2 * RANK * p
        packed += [
            gate_b_all[at : at + RANK],
            up_b_all[at + RANK : at + 2 * RANK],
            down_a_all[at : at + RANK],
        ]
    hidden_terms = split_terms(narrow(jnp.concatenate(packed, axis=0)), "hidden_place")
    hidden_terms = hidden_terms.reshape(2, 2, pair, 2, 3 * RANK, half)
    hidden_terms = jnp.concatenate([hidden_terms[:, 0], hidden_terms[:, 1]], axis=-1)
    hidden_terms = jnp.moveaxis(hidden_terms, 2, 1).reshape(n_dp, 3 * RANK, hidden)
    hidden_sets = to_sets(hidden_terms)

    lat_codes = lat_all[:, q_lat : q_lat + CODE_LANES]
    qb_b = ADAPT_SCALE * dot_tn(lat_codes, dq)[:RANK]
    kvb_b = ADAPT_SCALE * dot_tn(lat_codes, dkv)[RANK : 2 * RANK]
    head_terms = split_terms(
        narrow(jnp.concatenate([qb_b, kvb_b, out_a], axis=1)), "head_place"
    )
    head_sets = to_sets(head_terms)
    wide = heads * HEAD_LANES
    qb_b_grad = head_sets[:, :, :wide].reshape(group_count, RANK, heads, HEAD_LANES)[..., :head_q]
    qb_b_grad = qb_b_grad.reshape(group_count, RANK, heads * head_q)
    kvb_b_grad = head_sets[:, :, wide : 2 * wide]
    out_a_grad = turned(head_sets[:, :, 2 * wide :])

    down_in_terms = dot_tn(code_grad, attn_rows)
    b_terms = ADAPT_SCALE * dot_tn(down_codes_in, latent_grad)
    qb_a = dot_tn(qb_code_grad, q_input)
    kvb_a = dot_tn(kvb_code_grad, kv_input)
    small = jnp.concatenate([b_terms[:RANK, :q_lat], b_terms[RANK:, q_lat:], qb_a, kvb_a], axis=1)
    small_wide = small.shape[1]
    small = jnp.pad(small, ((0, RANK), (0, width - small_wide)))
    late = shared_terms(jnp.concatenate([down_in_terms, small], axis=0), "late")

    early_sets = to_sets(early)
    late_sets = to_sets(late)
    gu_a_grad = jnp.stack(
        [turned(early_sets[:, :RANK]), turned(early_sets[:, RANK : 2 * RANK])], axis=0
    )
    late_small = late_sets[:, 2 * RANK : 3 * RANK]
    at = [0, q_lat, q_lat + kv_all, 2 * q_lat + kv_all, small_wide]
    return (
        outputs[None],
        input_grad[None],
        turned(late_sets[:, :RANK]),
        late_small[:, :, at[0] : at[1]],
        turned(late_sets[:, RANK : 2 * RANK]),
        late_small[:, :, at[1] : at[2]],
        turned(late_small[:, :, at[2] : at[3]]),
        qb_b_grad,
        turned(late_small[:, :, at[3] : at[4]]),
        kvb_b_grad,
        out_a_grad,
        early_sets[:, 2 * RANK : 3 * RANK],
        gu_a_grad,
        jnp.stack([hidden_sets[:, :RANK], hidden_sets[:, RANK : 2 * RANK]], axis=0),
        turned(hidden_sets[:, 2 * RANK :]),
        early_sets[:, 3 * RANK :],
    )


def solution(mesh):
    return jax.shard_map(
        functools.partial(per_device, mesh.shape["dp"], mesh.shape["tensor"]),
        mesh=mesh,
        in_specs=(
            P("dp", "tensor", None),
            P("dp", "tensor", None),
            P("dp", None),
            P("dp"),
            P(),
            P(),
            P(),
            P(),
            P("dp", None),
            P("dp", None),
            P("dp", "tensor"),
            P("dp", "tensor"),
            P("tensor", "dp"),
            P(None, "dp", "tensor"),
            P("tensor", "dp"),
            P(),
            P(),
            P(),
            P(),
            P(),
            P(None, None, "tensor"),
            P(),
            P(None, None, "tensor"),
            P(None, "tensor", None),
            P(),
            P(),
            P(None, None, None, "tensor"),
            P(None, "tensor", None),
            P(),
        ),
        out_specs=(
            P("dp", "tensor", None),
            P("dp", "tensor", None),
            P(),
            P(),
            P(),
            P(),
            P(),
            P(None, None, "tensor"),
            P(),
            P(None, None, "tensor"),
            P(None, "tensor", None),
            P(),
            P(),
            P(None, None, None, "tensor"),
            P(None, "tensor", None),
            P(),
        ),
        check_vma=False,
    )
```

time: 1860 us -> 1140 us (0.61)
  waiting for transfers between devices: 1070 us -> 417 us
  matrix products: 410 us -> 160 us
  Pallas kernels: 0 us -> 159 us
  starting transfers between devices: 1.98 us -> 135 us
  blocking collectives: 85.3 us -> 10.2 us
    all_gather x10 -> x0, waiting for transfers between devices: 555 us -> none  [the longest x1 330 us: per_device(): lax.all_gather(gate_up_matrix, 'dp', axis=1, tiled=True)]
    ppermute x0 -> x182, waiting for transfers between devices: none -> 417 us  [swap(): return lax.ppermute(value, axis, [(i, i ^ bit) for i in range(size)])]
    psum x2 -> x0, waiting for transfers between devices: 287 us -> none  [the longest x1 182 us: per_device(): lax.psum((per_set(qa_a_terms, pick_high), per_set(qa_b_terms, pick_high),...]
    dot_general x102 -> x56, matrix products: 410 us -> 160 us  [the longest x25 103 us: dot_nt(): lax.dot_general(a, b, (((1,), (1,)), ((), ())), preferred_element_type=F32)]
    reduce_scatter x11 -> x0, waiting for transfers between devices: 219 us -> none  [the longest x1 54.1 us: per_device(): lax.psum_scatter(attn_part.astype(jnp.bfloat16), 'tensor', scatter_dimens...]
    pallas_call x0 -> x20, Pallas kernels: none -> 159 us  [the longest x16 54 us: place_pieces(): pl.pallas_call(kernel, out_shape=[jax.ShapeDtypeStruct(o, BF16) for o in...]
    ppermute x0 -> x182, starting transfers between devices: none -> 135 us  [swap(): return lax.ppermute(value, axis, [(i, i ^ bit) for i in range(size)])]
    all_gather x8 -> x0, blocking collectives: 85.3 us -> none  [the longest x1 34.5 us: per_device(): lax.all_gather(keyvalue_up_matrix, 'dp', axis=0, tiled=True)]
  transfers between devices with their start and end apart: 23 -> 182, of which waited for: 15 -> 51; matrix products, arithmetic and copies ran while one was open for 32% -> 28% of each run, Pallas kernels for 0% -> 6%
where the time goes in v1:
time: 1140 us; the launch traced here: 1130 us
  waiting for transfers between devices  417 us (37%)
  matrix products  160 us (14%)
  Pallas kernels  159 us (14%)
  local copies, waits for them, and re-layouts  157 us (14%)
  starting transfers between devices  135 us (12%)
  other arithmetic  88 us (8%)
    ppermute x182, waiting for transfers between devices, swap(): return lax.ppermute(value, axis, [(i, i ^ bit) for i in range(size)])  417 us
    ppermute x182, starting transfers between devices, swap(): return lax.ppermute(value, axis, [(i, i ^ bit) for i in range(size)])  135 us
    dot_general x25, matrix products, dot_nt(): lax.dot_general(a, b, (((1,), (1,)), ((), ())), preferred_element_type=F32)  103 us
    unnamed x499, local copies, waits for them, and re-layouts  79.8 us
    pallas_call x16, Pallas kernels, place_pieces(): pl.pallas_call(kernel, out_shape=[jax.ShapeDtypeStruct(o, BF16) for o in...  54 us
    pallas_call x2, Pallas kernels, ffn_middle(): pl.pallas_call(functools.partial(ffn_kernel, main, tail, tail_wide), grid...  50.1 us
    another operation x11, other arithmetic  30.3 us
    pallas_call x1, Pallas kernels, attend(): pl.pallas_call(functools.partial(attn_fwd_kernel, per_step, q_width, kv_a...  27.7 us
  transfers between devices with their start and end apart: 182, of which 51 were waited for; matrix products, arithmetic and copies ran while one was open for 28% of the time, Pallas kernels for 6%

profile of v1, /device:TPU:0, one launch (start us, length us, event | category | flops | bytes accessed | tf_op | source)
XLA Modules:
  0.0 1132.2 jit_solution(9252406632561251954)
XLA Ops:
  13.8 10.2 all-reduce.9
  125.8 15.8 %collective-permute-done.18.refs_3_ = bf16[128,1280]{1,0:T(8,128)(2,1)} collective-permute-done((bf16[128,1280]{1,0:T(8,128)(2,1)}, bf16[128,1280]{1,0:T(8,128)(2,1)}, u32[]{:S(2)}, u32[]{:S(2)}) %collective-permute-start.18) | collective-permute-done | bytes 327712 | tf_op jit(solution)/shard_map/ppermute | solution.py:74
  159.6 11.4 %collective-permute-done.20.refs_5_ = bf16[128,1280]{1,0:T(8,128)(2,1)S(1)} collective-permute-done((bf16[128,1280]{1,0:T(8,128)(2,1)}, bf16[128,1280]{1,0:T(8,128)(2,1)S(1)}, u32[]{:S(2)}, u32[]{:S(2)}) %collective-permute-start.20) | collective-permute-done | bytes 327712 | tf_op jit(solution)/shard_map/ppermute | solution.py:74
  195.4 12.4 %collective-permute-done.24.refs_9_ = bf16[128,1280]{1,0:T(8,128)(2,1)S(1)} collective-permute-done((bf16[128,1280]{1,0:T(8,128)(2,1)S(1)}, bf16[128,1280]{1,0:T(8,128)(2,1)S(1)}, u32[]{:S(2)}, u32[]{:S(2)}) %collective-permute-start.24) | collective-permute-done | bytes 327712 | tf_op jit(solution)/shard_map/ppermute | solution.py:74
  291.1 27.7 %attend.1 = (bf16[1024,1280]{1,0:T(8,128)(2,1)}, bf16[1024,1280]{1,0:T(8,128)(2,1)}, bf16[1024,640]{1,0:T(8,128)(2,1)}) custom-call(bf16[1024,1152]{1,0:T(8,128)(2,1)} %bitcast.357, bf16[896,1280]{1,0:T(8,128)(2,1)} %get-tuple-element.28.wq_ref, bf16[384,1280]{1,0:T(8,128)(2,1)} %get-tuple-element.29.wkv_ref, f32[3,1024,128]{2,1,0:T(8,128)} %pad_maximum_fusion.3.rope_ref, ...), custom_call_target="tpu_custom_call" | custom-call | flops 20132659200 | bytes 16777216 | tf_op jit(solution)/shard_map/attend/pallas_call | solution.py:247
  342.0 22.2 %collective-permute-done.34 = bf16[256,2688]{1,0:T(8,128)(2,1)S(1)} collective-permute-done((bf16[256,2688]{1,0:T(8,128)(2,1)S(1)}, bf16[256,2688]{1,0:T(8,128)(2,1)S(1)}, u32[]{:S(2)}, u32[]{:S(2)}) %collective-permute-start.34) | collective-permute-done | bytes 1376288 | tf_op jit(solution)/shard_map/ppermute | solution.py:74
  366.6 15.2 %collective-permute-done.63.refs_2_ = bf16[320,1152]{1,0:T(8,128)(2,1)S(1)} collective-permute-done((bf16[320,1152]{1,0:T(8,128)(2,1)S(1)}, bf16[320,1152]{1,0:T(8,128)(2,1)S(1)}, u32[]{:S(2)}, u32[]{:S(2)}) %collective-permute-start.63) | collective-permute-done | bytes 737312 | tf_op jit(solution)/shard_map/ppermute | solution.py:74
  388.0 64.1 %collective-permute-done.71.refs_3_ = bf16[320,1280]{1,0:T(8,128)(2,1)} collective-permute-done((bf16[320,1280]{1,0:T(8,128)(2,1)S(1)}, bf16[320,1280]{1,0:T(8,128)(2,1)}, u32[]{:S(2)}, u32[]{:S(2)}) %collective-permute-start.71) | collective-permute-done | bytes 819232 | tf_op jit(solution)/shard_map/ppermute | solution.py:74
  454.1 13.8 %collective-permute-done.65.refs_4_ = bf16[320,1152]{1,0:T(8,128)(2,1)} collective-permute-done((bf16[320,1152]{1,0:T(8,128)(2,1)S(1)}, bf16[320,1152]{1,0:T(8,128)(2,1)}, u32[]{:S(2)}, u32[]{:S(2)}) %collective-permute-start.65) | collective-permute-done | bytes 737312 | tf_op jit(solution)/shard_map/ppermute | solution.py:74
  472.6 12.8 %collective-permute-done.72.refs_4_ = bf16[320,1280]{1,0:T(8,128)(2,1)} collective-permute-done((bf16[320,1280]{1,0:T(8,128)(2,1)}, bf16[320,1280]{1,0:T(8,128)(2,1)}, u32[]{:S(2)}, u32[]{:S(2)}) %collective-permute-start.72) | collective-permute-done | bytes 819232 | tf_op jit(solution)/shard_map/ppermute | solution.py:74
  491.1 15.8 %collective-permute-done.69.refs_8_ = bf16[320,1152]{1,0:T(8,128)(2,1)} collective-permute-done((bf16[320,1152]{1,0:T(8,128)(2,1)}, bf16[320,1152]{1,0:T(8,128)(2,1)}, u32[]{:S(2)}, u32[]{:S(2)}) %collective-permute-start.69) | collective-permute-done | bytes 737312 | tf_op jit(solution)/shard_map/ppermute | solution.py:74
  535.7 14.0 %collective-permute-done.43 = bf16[128,2688]{1,0:T(8,128)(2,1)S(1)} collective-permute-done((bf16[128,2688]{1,0:T(8,128)(2,1)}, bf16[128,2688]{1,0:T(8,128)(2,1)S(1)}, u32[]{:S(2)}, u32[]{:S(2)}) %collective-permute-start.43) | collective-permute-done | bytes 688160 | tf_op jit(solution)/shard_map/ppermute | solution.py:74
  549.7 14.3 %collective-permute-done.47 = bf16[128,2688]{1,0:T(8,128)(2,1)S(1)} collective-permute-done((bf16[128,2688]{1,0:T(8,128)(2,1)S(1)}, bf16[128,2688]{1,0:T(8,128)(2,1)S(1)}, u32[]{:S(2)}, u32[]{:S(2)}) %collective-permute-start.47) | collective-permute-done | bytes 688160 | tf_op jit(solution)/shard_map/ppermute | solution.py:74
  576.8 29.0 %ffn_middle.3 = (bf16[2048,896]{1,0:T(8,128)(2,1)}, bf16[2048,512]{1,0:T(8,128)(2,1)}) custom-call(bf16[2048,2688]{1,0:T(8,128)(2,1)} %constant_dynamic-update-slice_fusion.x_ref, bf16[2048,2688]{1,0:T(8,128)(2,1)} %constant_dynamic-update-slice_fusion.15.g_ref, bf16[2688,1280]{1,0:T(8,128)(2,1)} %place_ffn_1.1.w_ref), custom_call_target="tpu_custom_call" | custom-call | flops 15502147584 | bytes 34144256 | tf_op jit(solution)/shard_map/ffn_middle/pallas_call | solution.py:342
  627.2 21.1 %ffn_middle.2 = (bf16[2048,768]{1,0:T(8,128)(2,1)}, bf16[2048,384]{1,0:T(8,128)(2,1)}) custom-call(bf16[2048,2688]{1,0:T(8,128)(2,1)} %constant_dynamic-update-slice_fusion.x_ref, bf16[2048,2688]{1,0:T(8,128)(2,1)} %constant_dynamic-update-slice_fusion.15.g_ref, bf16[2688,1152]{1,0:T(8,128)(2,1)} %place_ffn_0.1.w_ref), custom_call_target="tpu_custom_call" | custom-call | flops 12683575296 | bytes 32931840 | tf_op jit(solution)/shard_map/ffn_middle/pallas_call | solution.py:342
  651.2 13.1 %add_convert_fusion = bf16[1024,2688]{1,0:T(8,128)(2,1)} fusion(f32[1024,2688]{1,0:T(8,128)} %fusion, bf16[2688,1152]{1,0:T(8,128)(2,1)} %place_ffn_0.1.w_ref, bf16[2048,768]{1,0:T(8,128)(2,1)} %get-tuple-element.33), kind=kOutput, calls=%fused_computation.1 | convolution fusion | flops 4233363456 | bytes 22216704 | tf_op jit(solution)/shard_map/dot_general | solution.py:41
  722.2 14.3 %fusion.239 = (bf16[1024,2688]{1,0:T(8,128)(2,1)S(1)}, f32[1024,2688]{1,0:T(8,128)}) fusion(bf16[1024,2688]{1,0:T(8,128)(2,1)} %collective-permute-done.84, f32[1024,2688]{1,0:T(8,128)} %fusion.8, f32[1024,2688]{1,0:T(8,128)} %fusion.2), kind=kLoop, calls=%fused_computation.494 | loop fusion | flops 11010048 | bytes 44040192 | tf_op jit(solution)/shard_map/convert.56
  742.7 14.5 %fusion.240 = (bf16[1024,2688]{1,0:T(8,128)(2,1)S(1)}, f32[1024,2688]{1,0:T(8,128)}) fusion(bf16[1024,2688]{1,0:T(8,128)(2,1)} %collective-permute-done.77, f32[1024,2688]{1,0:T(8,128)S(1)} %fusion.105, f32[1024,2688]{1,0:T(8,128)} %fusion.48, f32[1024,2688]{1,0:T(8,128)} %fusion.44), kind=kLoop, calls=%fused_computation.495 | loop fusion | flops 13762560 | bytes 55050240 | tf_op jit(solution)/shard_map/convert.61
  758.2 12.6 %collective-permute-done.89 = bf16[128,2688]{1,0:T(8,128)(2,1)S(1)} collective-permute-done((bf16[128,2688]{1,0:T(8,128)(2,1)}, bf16[128,2688]{1,0:T(8,128)(2,1)S(1)}, u32[]{:S(2)}, u32[]{:S(2)}) %collective-permute-start.89) | collective-permute-done | bytes 688160 | tf_op jit(solution)/shard_map/ppermute | solution.py:74
  776.4 14.7 %collective-permute-done.79 = bf16[128,2688]{1,0:T(8,128)(2,1)S(1)} collective-permute-done((bf16[128,2688]{1,0:T(8,128)(2,1)S(1)}, bf16[128,2688]{1,0:T(8,128)(2,1)S(1)}, u32[]{:S(2)}, u32[]{:S(2)}) %collective-permute-start.79) | collective-permute-done | bytes 688160 | tf_op jit(solution)/shard_map/ppermute | solution.py:74
  796.8 23.8 %collective-permute-done.90 = bf16[128,2688]{1,0:T(8,128)(2,1)S(1)} collective-permute-done((bf16[128,2688]{1,0:T(8,128)(2,1)S(1)}, bf16[128,2688]{1,0:T(8,128)(2,1)S(1)}, u32[]{:S(2)}, u32[]{:S(2)}) %collective-permute-start.90) | collective-permute-done | bytes 688160 | tf_op jit(solution)/shard_map/ppermute | solution.py:74
  843.0 13.0 %collective-permute-done.85 = bf16[128,2688]{1,0:T(8,128)(2,1)S(1)} collective-permute-done((bf16[128,2688]{1,0:T(8,128)(2,1)}, bf16[128,2688]{1,0:T(8,128)(2,1)S(1)}, u32[]{:S(2)}, u32[]{:S(2)}) %collective-permute-start.85) | collective-permute-done | bytes 688160 | tf_op jit(solution)/shard_map/ppermute | solution.py:74
  949.3 25.0 %collective-permute-done.93 = bf16[128,2688]{1,0:T(8,128)(2,1)S(1)} collective-permute-done((bf16[128,2688]{1,0:T(8,128)(2,1)}, bf16[128,2688]{1,0:T(8,128)(2,1)S(1)}, u32[]{:S(2)}, u32[]{:S(2)}) %collective-permute-start.93) | collective-permute-done | bytes 688160 | tf_op jit(solution)/shard_map/ppermute | solution.py:74
  984.2 27.4 %attend_back.1 = (bf16[1024,1280]{1,0:T(8,128)(2,1)}, bf16[1024,1280]{1,0:T(8,128)(2,1)}, f32[1024,128]{1,0:T(8,128)}) custom-call(bf16[1024,1280]{1,0:T(8,128)(2,1)} %get-tuple-element.35.qa_ref, bf16[1024,1280]{1,0:T(8,128)(2,1)} %get-tuple-element.36.kv_ref, bf16[1024,640]{1,0:T(8,128)(2,1)} %get-tuple-element.30.o_ref, bf16[1024,640]{1,0:T(8,128)(2,1)} %bitcast.364, ...), custom_call_target="tpu_custom_call" | custom-call | flops 26843545600 | bytes 16777216 | tf_op jit(solution)/shard_map/attend_back/pallas_call | solution.py:284
  (1120 shorter events, 668.0 us)
Async XLA Ops:
  3.7 77.2 %collective-permute-start.10 = (bf16[80,1056]{1,0:T(8,128)(2,1)}, bf16[80,1056]{1,0:T(8,128)(2,1)}, u32[]{:S(2)}, u32[]{:S(2)}) collective-permute-start(bf16[80,1056]{1,0:T(8,128)(2,1)} %get-tuple-element.195.refs_8_), channel_id=1, source_target_pairs={{0,8},{4,12},{8,0},{12,4},{16,24},{20,28},{24,16},{28,20},{1,9},{5... | collective-permute-start | bytes 506888 | tf_op jit(solution)/shard_map/ppermute | solution.py:74
  6.8 77.8 %collective-permute-start.8 = (bf16[80,1056]{1,0:T(8,128)(2,1)}, bf16[80,1056]{1,0:T(8,128)(2,1)}, u32[]{:S(2)}, u32[]{:S(2)}) collective-permute-start(bf16[80,1056]{1,0:T(8,128)(2,1)} %get-tuple-element.195.refs_8_), channel_id=1, source_target_pairs={{0,16},{4,20},{8,24},{12,28},{16,0},{20,4},{24,8},{28,12},{1,17},{... | collective-permute-start | bytes 506888 | tf_op jit(solution)/shard_map/ppermute | solution.py:74
  9.4 73.6 %collective-permute-start.7 = (bf16[80,1056]{1,0:T(8,128)(2,1)}, bf16[80,1056]{1,0:T(8,128)(2,1)}, u32[]{:S(2)}, u32[]{:S(2)}) collective-permute-start(bf16[80,1056]{1,0:T(8,128)(2,1)} %get-tuple-element.195.refs_8_), channel_id=1, source_target_pairs={{0,4},{4,0},{8,12},{12,8},{16,20},{20,16},{24,28},{28,24},{1,5},{5... | collective-permute-start | bytes 506888 | tf_op jit(solution)/shard_map/ppermute | solution.py:74
  10.8 74.6 %collective-permute-start.3 = (bf16[80,1056]{1,0:T(8,128)(2,1)}, bf16[80,1056]{1,0:T(8,128)(2,1)}, u32[]{:S(2)}, u32[]{:S(2)}) collective-permute-start(bf16[80,1056]{1,0:T(8,128)(2,1)} %get-tuple-element.196.refs_0_), channel_id=1, source_target_pairs={{0,4},{4,0},{8,12},{12,8},{16,20},{20,16},{24,28},{28,24},{1,5},{5... | collective-permute-start | bytes 506888 | tf_op jit(solution)/shard_map/ppermute | solution.py:74
  11.4 75.2 %collective-permute-start.1 = (bf16[80,1056]{1,0:T(8,128)(2,1)}, bf16[80,1056]{1,0:T(8,128)(2,1)}, u32[]{:S(2)}, u32[]{:S(2)}) collective-permute-start(bf16[80,1056]{1,0:T(8,128)(2,1)} %get-tuple-element.196.refs_0_), channel_id=1, source_target_pairs={{0,8},{4,12},{8,0},{12,4},{16,24},{20,28},{24,16},{28,20},{1,9},{5... | collective-permute-start | bytes 506888 | tf_op jit(solution)/shard_map/ppermute | solution.py:74
  124.6 103.3 %collective-permute-start.14 = (bf16[8,160,1056]{2,1,0:T(8,128)(2,1)}, bf16[8,160,1056]{2,1,0:T(8,128)(2,1)}, u32[]{:S(2)}, u32[]{:S(2)}) collective-permute-start(bf16[8,160,1056]{2,1,0:T(8,128)(2,1)} %place_down_core.1.refs_0_), channel_id=1, source_target_pairs={{0,1},{1,0},{2,3},{3,2},{4,5},{5,4},{6,7},{7,6},{8,9},{9,8},{10,11... | collective-permute-start | bytes 8110088 | tf_op jit(solution)/shard_map/ppermute | solution.py:74
  220.7 161.9 %collective-permute-start.66 = (bf16[320,1152]{1,0:T(8,128)(2,1)}, bf16[320,1152]{1,0:T(8,128)(2,1)}, u32[]{:S(2)}, u32[]{:S(2)}) collective-permute-start(bf16[320,1152]{1,0:T(8,128)(2,1)} %get-tuple-element.168.refs_1_), channel_id=1, source_target_pairs={{0,4},{4,0},{8,12},{12,8},{16,20},{20,16},{24,28},{28,24},{1,5},{5... | collective-permute-start | bytes 2211848 | tf_op jit(solution)/shard_map/ppermute | solution.py:74
  265.8 118.3 %collective-permute-start.64 = (bf16[320,1152]{1,0:T(8,128)(2,1)}, bf16[320,1152]{1,0:T(8,128)(2,1)}, u32[]{:S(2)}, u32[]{:S(2)}) collective-permute-start(bf16[320,1152]{1,0:T(8,128)(2,1)} %get-tuple-element.168.refs_1_), channel_id=1, source_target_pairs={{0,16},{4,20},{8,24},{12,28},{16,0},{20,4},{24,8},{28,12},{1,17},{... | collective-permute-start | bytes 2211848 | tf_op jit(solution)/shard_map/ppermute | solution.py:74
  277.4 108.9 %collective-permute-start.70 = (bf16[320,1280]{1,0:T(8,128)(2,1)}, bf16[320,1280]{1,0:T(8,128)(2,1)}, u32[]{:S(2)}, u32[]{:S(2)}) collective-permute-start(bf16[320,1280]{1,0:T(8,128)(2,1)} %get-tuple-element.165), channel_id=1, source_target_pairs={{0,8},{4,12},{8,0},{12,4},{16,24},{20,28},{24,16},{28,20},{1,9},{5... | collective-permute-start | bytes 2457608 | tf_op jit(solution)/shard_map/ppermute | solution.py:74
  340.5 46.9 %collective-permute-start.73 = (bf16[320,1280]{1,0:T(8,128)(2,1)S(1)}, bf16[320,1280]{1,0:T(8,128)(2,1)S(1)}, u32[]{:S(2)}, u32[]{:S(2)}) collective-permute-start(bf16[320,1280]{1,0:T(8,128)(2,1)S(1)} %copy-done.33), channel_id=1, source_target_pairs={{0,4},{4,0},{8,12},{12,8},{16,20},{20,16},{24,28},{28,24},{1,5},{5... | collective-permute-start | bytes 2457608 | tf_op jit(solution)/shard_map/ppermute | solution.py:74
  381.8 70.3 %collective-permute-start.71 = (bf16[320,1280]{1,0:T(8,128)(2,1)S(1)}, bf16[320,1280]{1,0:T(8,128)(2,1)}, u32[]{:S(2)}, u32[]{:S(2)}) collective-permute-start(bf16[320,1280]{1,0:T(8,128)(2,1)S(1)} %copy-done.33), channel_id=1, source_target_pairs={{0,16},{4,20},{8,24},{12,28},{16,0},{20,4},{24,8},{28,12},{1,17},{... | collective-permute-start | bytes 2457608 | tf_op jit(solution)/shard_map/ppermute | solution.py:74
  382.7 70.9 %collective-permute-start.67 = (bf16[320,1152]{1,0:T(8,128)(2,1)S(1)}, bf16[320,1152]{1,0:T(8,128)(2,1)S(1)}, u32[]{:S(2)}, u32[]{:S(2)}) collective-permute-start(bf16[320,1152]{1,0:T(8,128)(2,1)S(1)} %collective-permute-done.63.refs_2_), channel_id=1, source_target_pairs={{0,4},{4,0},{8,12},{12,8},{16,20},{20,16},{24,28},{28,24},{1,5},{5... | collective-permute-start | bytes 2211848 | tf_op jit(solution)/shard_map/ppermute | solution.py:74
  384.2 83.7 %collective-permute-start.65 = (bf16[320,1152]{1,0:T(8,128)(2,1)S(1)}, bf16[320,1152]{1,0:T(8,128)(2,1)}, u32[]{:S(2)}, u32[]{:S(2)}) collective-permute-start(bf16[320,1152]{1,0:T(8,128)(2,1)S(1)} %collective-permute-done.63.refs_2_), channel_id=1, source_target_pairs={{0,16},{4,20},{8,24},{12,28},{16,0},{20,4},{24,8},{28,12},{1,17},{... | collective-permute-start | bytes 2211848 | tf_op jit(solution)/shard_map/ppermute | solution.py:74
  386.3 99.1 %collective-permute-start.72 = (bf16[320,1280]{1,0:T(8,128)(2,1)}, bf16[320,1280]{1,0:T(8,128)(2,1)}, u32[]{:S(2)}, u32[]{:S(2)}) collective-permute-start(bf16[320,1280]{1,0:T(8,128)(2,1)} %collective-permute-done.70.refs_2_), channel_id=1, source_target_pairs={{0,16},{4,20},{8,24},{12,28},{16,0},{20,4},{24,8},{28,12},{1,17},{... | collective-permute-start | bytes 2457608 | tf_op jit(solution)/shard_map/ppermute | solution.py:74
  387.4 100.6 %collective-permute-start.68 = (bf16[320,1152]{1,0:T(8,128)(2,1)}, bf16[320,1152]{1,0:T(8,128)(2,1)}, u32[]{:S(2)}, u32[]{:S(2)}) collective-permute-start(bf16[320,1152]{1,0:T(8,128)(2,1)} %collective-permute-done.64.refs_3_), channel_id=1, source_target_pairs={{0,4},{4,0},{8,12},{12,8},{16,20},{20,16},{24,28},{28,24},{1,5},{5... | collective-permute-start | bytes 2211848 | tf_op jit(solution)/shard_map/ppermute | solution.py:74
  488.5 44.7 %collective-permute-start.37 = (bf16[128,2688]{1,0:T(8,128)(2,1)}, bf16[128,2688]{1,0:T(8,128)(2,1)S(1)}, u32[]{:S(2)}, u32[]{:S(2)}) collective-permute-start(bf16[128,2688]{1,0:T(8,128)(2,1)} %get-tuple-element.174), channel_id=1, source_target_pairs={{0,8},{4,12},{8,0},{12,4},{16,24},{20,28},{24,16},{28,20},{1,9},{5... | collective-permute-start | bytes 2064392 | tf_op jit(solution)/shard_map/ppermute | solution.py:74
  664.3 57.9 %collective-permute-start.84 = (bf16[1024,2688]{1,0:T(8,128)(2,1)}, bf16[1024,2688]{1,0:T(8,128)(2,1)}, u32[]{:S(2)}, u32[]{:S(2)}) collective-permute-start(bf16[1024,2688]{1,0:T(8,128)(2,1)} %add_convert_fusion), channel_id=1, source_target_pairs={{0,1},{1,0},{2,3},{3,2},{4,5},{5,4},{6,7},{7,6},{8,9},{9,8},{10,11... | collective-permute-start | bytes 16515080 | tf_op jit(solution)/shard_map/ppermute | solution.py:74
  682.3 60.4 %collective-permute-start.77 = (bf16[1024,2688]{1,0:T(8,128)(2,1)}, bf16[1024,2688]{1,0:T(8,128)(2,1)}, u32[]{:S(2)}, u32[]{:S(2)}) collective-permute-start(bf16[1024,2688]{1,0:T(8,128)(2,1)} %add_convert_fusion.1), channel_id=1, source_target_pairs={{0,1},{1,0},{2,3},{3,2},{4,5},{5,4},{6,7},{7,6},{8,9},{9,8},{10,11... | collective-permute-start | bytes 16515080 | tf_op jit(solution)/shard_map/ppermute | solution.py:74
  697.5 128.6 %collective-permute-start.175 = (bf16[96,800]{1,0:T(8,128)(2,1)}, bf16[96,800]{1,0:T(8,128)(2,1)}, u32[]{:S(2)}, u32[]{:S(2)}) collective-permute-start(bf16[96,800]{1,0:T(8,128)(2,1)} %constant_dynamic-update-slice_fusion.46.refs_0_), channel_id=1, source_target_pairs={{0,16},{4,20},{8,24},{12,28},{16,0},{20,4},{24,8},{28,12},{1,17},{... | collective-permute-start | bytes 460808 | tf_op jit(solution)/shard_map/ppermute | solution.py:74
  738.1 56.5 %collective-permute-start.88 = (bf16[128,2688]{1,0:T(8,128)(2,1)}, bf16[128,2688]{1,0:T(8,128)(2,1)S(1)}, u32[]{:S(2)}, u32[]{:S(2)}) collective-permute-start(bf16[128,2688]{1,0:T(8,128)(2,1)} %get-tuple-element.138), channel_id=1, source_target_pairs={{0,2},{1,3},{2,0},{3,1},{4,6},{5,7},{6,4},{7,5},{8,10},{9,11},{10,... | collective-permute-start | bytes 2064392 | tf_op jit(solution)/shard_map/ppermute | solution.py:74
  740.1 56.2 %collective-permute-start.86 = (bf16[128,2688]{1,0:T(8,128)(2,1)}, bf16[128,2688]{1,0:T(8,128)(2,1)}, u32[]{:S(2)}, u32[]{:S(2)}) collective-permute-start(bf16[128,2688]{1,0:T(8,128)(2,1)} %get-tuple-element.140), channel_id=1, source_target_pairs={{0,8},{4,12},{8,0},{12,4},{16,24},{20,28},{24,16},{28,20},{1,9},{5... | collective-permute-start | bytes 2064392 | tf_op jit(solution)/shard_map/ppermute | solution.py:74
  776.4 50.0 %collective-permute-start.78 = (bf16[128,2688]{1,0:T(8,128)(2,1)}, bf16[128,2688]{1,0:T(8,128)(2,1)S(1)}, u32[]{:S(2)}, u32[]{:S(2)}) collective-permute-start(bf16[128,2688]{1,0:T(8,128)(2,1)} %get-tuple-element.142), channel_id=1, source_target_pairs={{0,8},{4,12},{8,0},{12,4},{16,24},{20,28},{24,16},{28,20},{1,9},{5... | collective-permute-start | bytes 2064392 | tf_op jit(solution)/shard_map/ppermute | solution.py:74
  826.1 53.9 %collective-permute-start.176 = (bf16[96,800]{1,0:T(8,128)(2,1)}, bf16[96,800]{1,0:T(8,128)(2,1)}, u32[]{:S(2)}, u32[]{:S(2)}) collective-permute-start(bf16[96,800]{1,0:T(8,128)(2,1)} %constant_dynamic-update-slice_fusion.46.refs_0_), channel_id=1, source_target_pairs={{0,8},{4,12},{8,0},{12,4},{16,24},{20,28},{24,16},{28,20},{1,9},{5... | collective-permute-start | bytes 460808 | tf_op jit(solution)/shard_map/ppermute | solution.py:74
  826.4 55.1 %collective-permute-start.177 = (bf16[96,800]{1,0:T(8,128)(2,1)}, bf16[96,800]{1,0:T(8,128)(2,1)}, u32[]{:S(2)}, u32[]{:S(2)}) collective-permute-start(bf16[96,800]{1,0:T(8,128)(2,1)} %collective-permute-done.175.refs_1_), channel_id=1, source_target_pairs={{0,8},{4,12},{8,0},{12,4},{16,24},{20,28},{24,16},{28,20},{1,9},{5... | collective-permute-start | bytes 460808 | tf_op jit(solution)/shard_map/ppermute | solution.py:74
  (381 other events, 5010.6 us)

commit v2 on v1

--- a/solution.py
+++ b/solution.py
@@ -25,6 +25,7 @@
 EXP2_SCALE = SCORE_SCALE * math.log2(math.e)
 BIG = 1e30
 VMEM_LIMIT = 56 * 1024 * 1024
+FREE = pl.CostEstimate(flops=0, bytes_accessed=0, transcendentals=0)
 F32 = jnp.float32
 BF16 = jnp.bfloat16
 
@@ -99,9 +100,307 @@
         out_specs=[pl.BlockSpec(memory_space=pltpu.VMEM)] * len(outs),
         scratch_shapes=[pltpu.SemaphoreType.DMA((len(copies),))],
         compiler_params=pltpu.CompilerParams(vmem_limit_bytes=VMEM_LIMIT),
-        cost_estimate=pl.CostEstimate(flops=0, bytes_accessed=2 * moved, transcendentals=0),
+        cost_estimate=FREE,
         name=name,
     )(*sources)
+
+
+class Links:
+    def __init__(self, send_sems, recv_sems):
+        self.send_sems, self.recv_sems = send_sems, recv_sems
+        self.place = {"dp": lax.axis_index("dp"), "tensor": lax.axis_index("tensor")}
+        self.copies = []
+        self.waited = set()
+
+    def peer(self, step):
+        place = dict(self.place)
+        place[step[0]] = jnp.bitwise_xor(place[step[0]], step[1])
+        return (place["dp"], place["tensor"])
+
+    def greet(self, steps):
+        barrier = pltpu.get_barrier_semaphore()
+        for step in steps:
+            pl.semaphore_signal(
+                barrier, inc=1, device_id=self.peer(step), device_id_type=pl.DeviceIdType.MESH
+            )
+        pl.semaphore_wait(barrier, len(steps))
+
+    def send(self, src, dst, step):
+        n = len(self.copies)
+        copy = pltpu.make_async_remote_copy(
+            src_ref=src,
+            dst_ref=dst,
+            send_sem=self.send_sems.at[n],
+            recv_sem=self.recv_sems.at[n],
+            device_id=self.peer(step),
+            device_id_type=pl.DeviceIdType.MESH,
+        )
+        copy.start()
+        self.copies.append(copy)
+        return n
+
+    def arrived(self, n):
+        if n not in self.waited:
+            self.copies[n].wait_recv()
+            self.waited.add(n)
+
+    def close(self):
+        for n, copy in enumerate(self.copies):
+            self.arrived(n)
+            copy.wait_send()
+
+
+def flip(key, step):
+    return (key[0] ^ step[1], key[1]) if step[0] == "dp" else (key[0], key[1] ^ step[1])
+
+
+def has_bit(key, step):
+    return bool((key[0] if step[0] == "dp" else key[1]) & step[1])
+
+
+def gather_count(jobs):
+    return sum((1 << len(job["steps"])) - 1 for job in jobs)
+
+
+def run_gathers(links, src_refs, out_refs, jobs):
+    d, t = links.place["dp"], links.place["tensor"]
+
+    def landing(job, key):
+        at = job["out_at"](jnp.bitwise_xor(d, key[0]), jnp.bitwise_xor(t, key[1]))
+        return out_refs[job["out"]].at[at]
+
+    state = []
+    for job in jobs:
+        src = src_refs[job["src"]]
+        if job.get("src_at") is not None:
+            src = src.at[job["src_at"]]
+        state.append({(0, 0): (src, None)})
+    for k in range(max(len(job["steps"]) for job in jobs)):
+        for job, held in zip(jobs, state):
+            if k >= len(job["steps"]):
+                continue
+            step = job["steps"][k]
+            for key in list(held):
+                src, came = held[key]
+                if came is not None:
+                    links.arrived(came)
+                n = links.send(src, landing(job, key), step)
+                new = flip(key, step)
+                held[new] = (landing(job, new), n)
+    return [landing(job, (0, 0)) for job in jobs]
+
+
+def remote_gather(sources, jobs, extra, outs, name, collective_id):
+    steps = []
+    for job in jobs:
+        steps += [s for s in job["steps"] if s not in steps]
+    count = gather_count(jobs)
+
+    def kernel(*refs):
+        src_refs = refs[: len(sources)]
+        out_refs = refs[len(sources) : len(sources) + len(outs)]
+        send_sems, recv_sems, local_sems = refs[len(sources) + len(outs) :]
+        links = Links(send_sems, recv_sems)
+        links.greet(steps)
+        own = run_gathers(links, src_refs, out_refs, jobs)
+        local = []
+        for job, where in zip(jobs, own):
+            src = src_refs[job["src"]]
+            if job.get("src_at") is not None:
+                src = src.at[job["src_at"]]
+            local.append((src, where))
+        for src, out, at in extra:
+            local.append((src_refs[src], out_refs[out].at[at]))
+        started = []
+        for n, (src, where) in enumerate(local):
+            copy = pltpu.make_async_copy(src, where, local_sems.at[n])
+            copy.start()
+            started.append(copy)
+        links.close()
+        for copy in started:
+            copy.wait()
+
+    moved = sum(s.size * s.dtype.itemsize for s in sources)
+    return pl.pallas_call(
+        kernel,
+        out_shape=[jax.ShapeDtypeStruct(o, BF16) for o in outs],
+        in_specs=[pl.BlockSpec(memory_space=pltpu.VMEM)] * len(sources),
+        out_specs=[pl.BlockSpec(memory_space=pl.ANY)] * len(outs),
+        scratch_shapes=[
+            pltpu.SemaphoreType.DMA((count,)),
+            pltpu.SemaphoreType.DMA((count,)),
+            pltpu.SemaphoreType.DMA((len(jobs) + len(extra),)),
+        ],
+        compiler_params=pltpu.CompilerParams(
+            collective_id=collective_id, has_side_effects=True, vmem_limit_bytes=VMEM_LIMIT
+        ),
+        cost_estimate=FREE,
+        name=name,
+    )(*sources)
+
+
+def reduce_plan(keys, ways):
+    plan = []
+    for w, steps in enumerate(ways):
+        live = list(keys)
+        for k, step in enumerate(steps):
+            plan += [(w, k, key) for key in live if has_bit(key, step)]
+            live = [key for key in live if not has_bit(key, step)]
+    return plan
+
+
+def remote_reduce(operands, fetched, term, keys, ways, rows, wide, name, collective_id, flops):
+    core_step = ("tensor", 1)
+    part = rows // len(ways)
+    plan = reduce_plan(keys, ways)
+    slot = {entry: n for n, entry in enumerate(plan)}
+    steps = [core_step] + [s for s in ways[0]]
+    count = len(keys) + len(plan)
+    n_in = len(operands)
+
+    def kernel(*refs):
+        in_refs = refs[:n_in]
+        out_ref = refs[n_in]
+        held = refs[n_in + 1 : 2 * n_in + 1]
+        core_out, core_in, chip, hop_out, hop_in, send_sems, recv_sems, in_sems = refs[2 * n_in + 1 :]
+        started = []
+        for n in range(n_in):
+            shape = fetched[n]
+            src = in_refs[n].at[tuple(pl.ds(0, s) for s in shape)]
+            copy = pltpu.make_async_copy(src, held[n], in_sems.at[n])
+            copy.start()
+            started.append(copy)
+        links = Links(send_sems, recv_sems)
+        links.greet(steps)
+        for copy in started:
+            copy.wait()
+        came = {}
+
+        def send_part(w, k, key):
+            entry = (w, k, key)
+            came[entry] = links.send(hop_out.at[slot[entry]], hop_in.at[slot[entry]], ways[w][k])
+
+        def so_far(w, k, key):
+            total = chip[keys.index(key), w * part : (w + 1) * part, :]
+            for j in range(k):
+                entry = (w, j, flip(key, ways[w][j]))
+                links.arrived(came[entry])
+                total = total + hop_in[slot[entry]].astype(F32)
+            return total
+
+        for i, key in enumerate(keys):
+            core_out[i] = narrow(term(held, links.place, (key[0], key[1] ^ 1)))
+            crossing = links.send(core_out.at[i], core_in.at[i], core_step)
+            mine = term(held, links.place, key)
+            links.arrived(crossing)
+            chip[i] = mine + core_in[i].astype(F32)
+            for w, way in enumerate(ways):
+                if way and has_bit(key, way[0]):
+                    hop_out[slot[(w, 0, key)]] = narrow(chip[i, w * part : (w + 1) * part, :])
+                    send_part(w, 0, key)
+        for k in range(1, len(ways[0])):
+            for w in range(len(ways)):
+                for entry in plan:
+                    if entry[0] == w and entry[1] == k:
+                        hop_out[slot[entry]] = narrow(so_far(w, k, entry[2]))
+                        send_part(w, k, entry[2])
+        for w in range(len(ways)):
+            out_ref[w * part : (w + 1) * part, :] = so_far(w, len(ways[w]), (0, 0))
+        links.close()
+
+    return pl.pallas_call(
+        kernel,
+        out_shape=jax.ShapeDtypeStruct((rows, wide), F32),
+        in_specs=[pl.BlockSpec(memory_space=pl.ANY)] * n_in,
+        out_specs=pl.BlockSpec(memory_space=pltpu.VMEM),
+        scratch_shapes=[pltpu.VMEM(s, o.dtype) for s, o in zip(fetched, operands)]
+        + [
+            pltpu.VMEM((len(keys), rows, wide), BF16),
+            pltpu.VMEM((len(keys), rows, wide), BF16),
+            pltpu.VMEM((len(keys), rows, wide), F32),
+            pltpu.VMEM((max(len(plan), 1), part, wide), BF16),
+            pltpu.VMEM((max(len(plan), 1), part, wide), BF16),
+            pltpu.SemaphoreType.DMA((count,)),
+            pltpu.SemaphoreType.DMA((count,)),
+            pltpu.SemaphoreType.DMA((n_in,)),
+        ],
+        compiler_params=pltpu.CompilerParams(
+            collective_id=collective_id, has_side_effects=True, vmem_limit_bytes=VMEM_LIMIT
+        ),
+        cost_estimate=FREE,
+        name=name,
+    )(*operands)
+
+
+def remote_share(terms, parts, jobs_of, outs, n_t, t_steps, steps, name, collective_id):
+    count, wide = terms.shape[0] // n_t, terms.shape[1]
+    job = dict(
+        src=0,
+        out=0,
+        out_at=lambda dd, tt: (dd, pl.ds(pl.multiple_of(tt * count, 16), count)),
+        steps=steps + t_steps[::-1],
+    )
+    jobs = [job] + jobs_of
+    copies = n_t - 1 + gather_count(jobs)
+    n_in = 1 + len(parts)
+    needed = list(job["steps"])
+
+    def kernel(*refs):
+        in_refs, out_refs = refs[:n_in], refs[n_in : n_in + len(outs)]
+        own, came_in, went_out, send_sems, recv_sems, local_sems = refs[n_in + len(outs) :]
+        links = Links(send_sems, recv_sems)
+        links.greet(needed)
+        t = links.place["tensor"]
+        live = list(range(n_t))
+        sums = {
+            r: in_refs[0][pl.ds(pl.multiple_of(jnp.bitwise_xor(t, r) * count, 16), count), :].astype(
+                F32
+            )
+            for r in live
+        }
+        slot = 0
+        for step in t_steps:
+            sent = []
+            for r in live:
+                if r & step[1]:
+                    went_out[slot] = narrow(sums[r])
+                    sent.append((r, slot, links.send(went_out.at[slot], came_in.at[slot], step)))
+                    slot += 1
+            live = [r for r in live if not r & step[1]]
+            for r, at, n in sent:
+                links.arrived(n)
+                sums[r ^ step[1]] = sums[r ^ step[1]] + came_in[at].astype(F32)
+        own[...] = narrow(sums[0])
+        sources = [own] + list(in_refs[1:])
+        places = run_gathers(links, sources, out_refs, jobs)
+        started = []
+        for n, (one, where) in enumerate(zip(jobs, places)):
+            copy = pltpu.make_async_copy(sources[one["src"]], where, local_sems.at[n])
+            copy.start()
+            started.append(copy)
+        links.close()
+        for copy in started:
+            copy.wait()
+
+    return pl.pallas_call(
+        kernel,
+        out_shape=[jax.ShapeDtypeStruct(o, BF16) for o in outs],
+        in_specs=[pl.BlockSpec(memory_space=pltpu.VMEM)] * n_in,
+        out_specs=[pl.BlockSpec(memory_space=pl.ANY)] * len(outs),
+        scratch_shapes=[
+            pltpu.VMEM((count, wide), BF16),
+            pltpu.VMEM((n_t - 1, count, wide), BF16),
+            pltpu.VMEM((n_t - 1, count, wide), BF16),
+            pltpu.SemaphoreType.DMA((copies,)),
+            pltpu.SemaphoreType.DMA((copies,)),
+            pltpu.SemaphoreType.DMA((len(jobs),)),
+        ],
+        compiler_params=pltpu.CompilerParams(
+            collective_id=collective_id, has_side_effects=True, vmem_limit_bytes=VMEM_LIMIT
+        ),
+        cost_estimate=FREE,
+        name=name,
+    )(terms, *parts)
 
 
 def split_three(value):
@@ -266,9 +565,7 @@
             jax.ShapeDtypeStruct((length, heads * VALUE_HEAD_DIM), BF16),
         ],
         compiler_params=pltpu.CompilerParams(vmem_limit_bytes=VMEM_LIMIT),
-        cost_estimate=pl.CostEstimate(
-            flops=2 * flops, bytes_accessed=16 * 1024 * 1024, transcendentals=heads * length * length // 2
-        ),
+        cost_estimate=FREE,
         name="attend",
     )(latents, w_q, w_kv, rope, pe_aug, doc_q)
 
@@ -296,11 +593,7 @@
             pltpu.VMEM((length, HEAD_LANES), F32),
         ],
         compiler_params=pltpu.CompilerParams(vmem_limit_bytes=VMEM_LIMIT),
-        cost_estimate=pl.CostEstimate(
-            flops=heads * length * length * 256 * 10,
-            bytes_accessed=16 * 1024 * 1024,
-            transcendentals=heads * length * length // 2,
-        ),
+        cost_estimate=FREE,
         name="attend_back",
     )(q_aug, kv, heads_out, heads_grad, rope, pe_aug)
 
@@ -356,11 +649,7 @@
             jax.ShapeDtypeStruct((rows, main + tail_wide), BF16),
         ],
         compiler_params=pltpu.CompilerParams(vmem_limit_bytes=VMEM_LIMIT),
-        cost_estimate=pl.CostEstimate(
-            flops=2 * rows * depth * (width + tail_wide),
-            bytes_accessed=2 * (2 * rows * depth + depth * width + rows * width),
-            transcendentals=rows * main,
-        ),
+        cost_estimate=FREE,
         name="ffn_middle",
     )(x_rows, g_rows, weight)
 
@@ -422,39 +711,12 @@
     def hop(value, step):
         return swap(value, step[0], step[1], size[step[0]])
 
-    def spread(piece, steps):
-        held = {(0, 0): piece}
-        for step in steps:
-            for key in list(held):
-                new = (key[0] ^ step[1], key[1]) if step[0] == "dp" else (key[0], key[1] ^ step[1])
-                held[new] = hop(held[key], step)
-        return held
-
-    def collect(parts, steps):
-        held = dict(parts)
-        for step in steps:
-            for key in list(held):
-                has = (key[0] if step[0] == "dp" else key[1]) & step[1]
-                if not has:
-                    new = (
-                        (key[0] ^ step[1], key[1])
-                        if step[0] == "dp"
-                        else (key[0], key[1] ^ step[1])
-                    )
-                    came = hop(narrow(held.pop(new)), step)
-                    held[key] = held[key].astype(F32) + came.astype(F32)
-        return held[(0, 0)]
-
     outer_first = [("dp", high), ("dp", pair)] + [("dp", b) for b in reversed(low_bits)]
     inner_first = [("dp", b) for b in low_bits] + [("dp", high), ("dp", pair)]
     t_slow = [("tensor", b) for b in reversed(y_bits)]
     t_core = [("tensor", 1)]
 
-    set_all = lax.all_gather(sequence_adapter_index, "dp", axis=0, tiled=True)
     set_own = sequence_adapter_index[0]
-    set_peer = lax.dynamic_index_in_dim(set_all, jnp.bitwise_xor(d, pair), 0, keepdims=False)
-    set_even = jnp.where(first, set_own, set_peer)
-    set_odd = jnp.where(first, set_peer, set_own)
 
     def pick(table, index):
         return lax.dynamic_index_in_dim(table, index, 0, keepdims=False)
@@ -476,190 +738,6 @@
         axis=0,
     )
     down_out = pick(down_adapter_out, set_own)
-
-    down_shard = query_down_matrix.shape[0]
-    core_rows = down_shard // 2
-    lat_pad = -(-(q_lat + kv_all) // 128) * 128
-    down_both = jnp.concatenate([query_down_matrix, keyvalue_down_matrix], axis=1)
-    down_mine = lax.dynamic_index_in_dim(
-        down_both.reshape(2, core_rows, q_lat + kv_all), core, 0, keepdims=False
-    )
-    cut = -(-core_rows // 32) * 16
-    down_a = spread(down_mine[:cut], outer_first)
-    down_b = spread(down_mine[cut:], inner_first)
-    sources, copies = [], []
-    for held, at, count in ((down_a, 0, cut), (down_b, cut, core_rows - cut)):
-        for (r, _), piece in held.items():
-            copies.append(
-                (
-                    len(sources),
-                    None,
-                    0,
-                    lambda dd, tt, r=r, at=at, count=count: (
-                        jnp.bitwise_xor(dd, r),
-                        pl.ds(at, count),
-                    ),
-                )
-            )
-            sources.append(piece)
-    (down_core,) = place_pieces(
-        sources, copies, [(n_dp, core_rows, q_lat + kv_all)], "place_down_core"
-    )
-    down_other = hop(down_core, t_core[0])
-    (down_full,) = place_pieces(
-        [down_core, down_other],
-        [
-            (0, None, 0, lambda dd, tt: (slice(None), lax.rem(tt, 2))),
-            (1, None, 0, lambda dd, tt: (slice(None), 1 - lax.rem(tt, 2))),
-        ],
-        [(n_dp, 2, core_rows, q_lat + kv_all)],
-        "place_down",
-    )
-    w_down = down_full.reshape(width, q_lat + kv_all)
-
-    qb_rows, kvb_rows = query_up_matrix.shape[0], keyvalue_up_matrix.shape[0]
-    head_q = PLAIN_HEAD_DIM + ROTARY_DIM
-
-    def pad_heads(value):
-        split = value.reshape(value.shape[0], heads, head_q)
-        return jnp.pad(split, ((0, 0), (0, 0), (0, HEAD_LANES - head_q))).reshape(
-            value.shape[0], heads * HEAD_LANES
-        )
-
-    up_piece = jnp.concatenate([pad_heads(query_up_matrix), keyvalue_up_matrix], axis=0)
-    up_held = spread(up_piece, outer_first)
-    q_aug_rows = jnp.concatenate(
-        [
-            narrow(ADAPT_SCALE * pad_heads(qb_out)),
-            jnp.zeros((CODE_LANES - RANK, heads * HEAD_LANES), BF16),
-        ],
-        axis=0,
-    )
-    kv_aug_rows = jnp.concatenate(
-        [
-            jnp.zeros((RANK, heads * HEAD_LANES), BF16),
-            narrow(ADAPT_SCALE * kvb_out),
-            jnp.zeros((CODE_LANES - 2 * RANK, heads * HEAD_LANES), BF16),
-        ],
-        axis=0,
-    )
-    sources, copies = [q_aug_rows, kv_aug_rows], [
-        (0, None, 0, lambda dd, tt: (pl.ds(q_lat, CODE_LANES),)),
-        (1, None, 1, lambda dd, tt: (pl.ds(0, CODE_LANES),)),
-    ]
-    for (r, _), piece in up_held.items():
-        copies.append(
-            (
-                len(sources),
-                pl.ds(0, qb_rows),
-                0,
-                lambda dd, tt, r=r: (
-                    pl.ds(pl.multiple_of(jnp.bitwise_xor(dd, r) * qb_rows, 16), qb_rows),
-                ),
-            )
-        )
-        copies.append(
-            (
-                len(sources),
-                pl.ds(qb_rows, kvb_rows),
-                1,
-                lambda dd, tt, r=r: (
-                    pl.ds(
-                        pl.multiple_of(CODE_LANES + jnp.bitwise_xor(dd, r) * kvb_rows, 16),
-                        kvb_rows,
-                    ),
-                ),
-            )
-        )
-        sources.append(piece)
-    w_q, w_kv = place_pieces(
-        sources,
-        copies,
-        [
-            (q_lat + CODE_LANES, heads * HEAD_LANES),
-            (CODE_LANES + kv_lat, heads * HEAD_LANES),
-        ],
-        "place_up",
-    )
-
-    def place_rows(held, extra, name):
-        count = held[(0, 0)].shape[0]
-        sources, copies = [extra], [(0, None, 0, lambda dd, tt: (pl.ds(width, CODE_LANES),))]
-        for (r, _), piece in held.items():
-            copies.append(
-                (
-                    len(sources),
-                    None,
-                    0,
-                    lambda dd, tt, r=r: (
-                        pl.ds(pl.multiple_of(jnp.bitwise_xor(dd, r) * count, 16), count),
-                    ),
-                )
-            )
-            sources.append(piece)
-        (full,) = place_pieces(sources, copies, [(aug, extra.shape[1])], name)
-        return full
-
-    out_held = spread(output_matrix.T, outer_first)
-    out_extra = jnp.concatenate(
-        [out_in, jnp.zeros((CODE_LANES - RANK, out_in.shape[1]), BF16)], axis=0
-    )
-    w_out = place_rows(out_held, out_extra, "place_out")
-
-    hidden = down_matrix.shape[0]
-    half = hidden // 2
-    main = half // 128 * 128
-    tail = half - main
-    tail_wide = -(-3 * tail // 128) * 128
-    chunks = 2 if (main // 128) % 2 == 0 else 1
-    step_wide = main // chunks
-
-    def columns(gate_part, up_part, down_part, chunk):
-        at = slice(chunk * step_wide, (chunk + 1) * step_wide)
-        out = [gate_part[:, at]]
-        if tail and chunk == chunks - 1:
-            out += [gate_part[:, main:], up_part[:, main:], down_part[:, main:]]
-            if tail_wide > 3 * tail:
-                out.append(jnp.zeros((gate_part.shape[0], tail_wide - 3 * tail), BF16))
-        out += [up_part[:, at], down_part[:, at]]
-        return jnp.concatenate(out, axis=1)
-
-    def halves(value):
-        return value[:, :half], value[:, half:]
-
-    down_turned = down_matrix.T
-    mats = [halves(gate_up_matrix[0]), halves(gate_up_matrix[1]), halves(down_turned)]
-    zero_codes = jnp.zeros((RANK, half), BF16)
-
-    def half_of(value):
-        left, right = halves(value)
-        return jnp.where(first, left, right)
-
-    extra_parts = []
-    for which in (set_even, set_odd):
-        gate_b = half_of(pick(gate_up_adapter_out[0], which)) * 2
-        up_b = half_of(pick(gate_up_adapter_out[1], which)) * 2
-        down_a_t = half_of(pick(turned(down_adapter_in), which))
-        extra_parts.append((gate_b, up_b, down_a_t))
-
-    ffn_weights = []
-    for chunk in range(chunks):
-        left = columns(mats[0][0], mats[1][0], mats[2][0], chunk)
-        right = columns(mats[0][1], mats[1][1], mats[2][1], chunk)
-        mine = jnp.where(first, left, right)
-        other = jnp.where(first, right, left)
-        held = {(0, 0): mine, (pair, 0): hop(other, ("dp", pair))}
-        for step in [("dp", high)] + [("dp", b) for b in reversed(low_bits)]:
-            for key in list(held):
-                held[(key[0] ^ step[1], 0)] = hop(held[key], step)
-        extra = []
-        for gate_b, up_b, down_a_t in extra_parts:
-            extra.append(columns(gate_b, zero_codes, down_a_t, chunk))
-            extra.append(columns(zero_codes, up_b, zero_codes, chunk))
-        extra.append(jnp.zeros((CODE_LANES - 4 * RANK, extra[0].shape[1]), BF16))
-        ffn_weights.append(
-            place_rows(held, jnp.concatenate(extra, axis=0), "place_ffn_" + str(chunk))
-        )
 
     def code_lanes(codes):
         none = jnp.zeros_like(codes)
@@ -676,21 +754,6 @@
         lanes = value[:, width:]
         return jnp.where(first, lanes[:, : 2 * RANK], lanes[:, 2 * RANK : 4 * RANK])
 
-    group_a = t_slow + [("dp", pair)]
-    group_b = [("dp", pair)] + t_slow
-    group_keys = [(p, r) for r in range(n_t) for p in (0, pair)]
-    odd_keys = [k for k in group_keys if k[1] & 1]
-    even_keys = [k for k in group_keys if not k[1] & 1]
-    order = odd_keys + even_keys
-
-    def spread_group(value):
-        top = spread(value[:half_rows], group_a + t_core)
-        bottom = spread(value[half_rows:], group_b + t_core)
-        parts = []
-        for key in order:
-            parts += [top[key], bottom[key]]
-        return jnp.concatenate(parts, axis=0)
-
     out_grad = cotangent[0].astype(F32)
     ffn_grad = narrow(RESIDUAL * out_grad)
     down_code_grad = narrow(ADAPT_SCALE * dot_nt(ffn_grad, down_out))
@@ -698,8 +761,188 @@
     g_own = jnp.concatenate(
         [ffn_grad, code_lanes(jnp.concatenate([down_code_grad, none16], axis=1))], axis=1
     )
-    g_all = spread_group(g_own)
-
+
+    down_shard = query_down_matrix.shape[0]
+    core_rows = down_shard // 2
+    down_both = jnp.concatenate([query_down_matrix, keyvalue_down_matrix], axis=1)
+    down_mine = lax.dynamic_index_in_dim(
+        down_both.reshape(2, core_rows, q_lat + kv_all), core, 0, keepdims=False
+    )
+    cut = -(-core_rows // 32) * 16
+    qb_rows, kvb_rows = query_up_matrix.shape[0], keyvalue_up_matrix.shape[0]
+    head_q = PLAIN_HEAD_DIM + ROTARY_DIM
+
+    def pad_heads(value):
+        split = value.reshape(value.shape[0], heads, head_q)
+        return jnp.pad(split, ((0, 0), (0, 0), (0, HEAD_LANES - head_q))).reshape(
+            value.shape[0], heads * HEAD_LANES
+        )
+
+    q_aug_rows = jnp.concatenate(
+        [
+            narrow(ADAPT_SCALE * pad_heads(qb_out)),
+            jnp.zeros((CODE_LANES - RANK, heads * HEAD_LANES), BF16),
+        ],
+        axis=0,
+    )
+    kv_aug_rows = jnp.concatenate(
+        [
+            jnp.zeros((RANK, heads * HEAD_LANES), BF16),
+            narrow(ADAPT_SCALE * kvb_out),
+            jnp.zeros((CODE_LANES - 2 * RANK, heads * HEAD_LANES), BF16),
+        ],
+        axis=0,
+    )
+    out_extra = jnp.concatenate(
+        [out_in, jnp.zeros((CODE_LANES - RANK, out_in.shape[1]), BF16)], axis=0
+    )
+    out_rows = output_matrix.shape[1]
+
+    def rows_at(start, step, count):
+        return lambda dd, tt: (pl.ds(pl.multiple_of(start + dd * step, 16), count),)
+
+    def group_block(dd, tt):
+        return lax.rem(dd // pair, 2) * n_t + tt
+
+    def group_jobs(src, out):
+        return [
+            dict(
+                src=src,
+                src_at=pl.ds(at, half_rows),
+                out=out,
+                out_at=lambda dd, tt, at=at: (
+                    pl.ds(pl.multiple_of(group_block(dd, tt) * rows + at, 16), half_rows),
+                ),
+                steps=steps + t_core,
+            )
+            for at, steps in ((0, group_a), (half_rows, group_b))
+        ]
+
+    group_a = t_slow + [("dp", pair)]
+    group_b = [("dp", pair)] + t_slow
+    jobs = [
+        dict(
+            src=0,
+            src_at=pl.ds(at, count),
+            out=0,
+            out_at=lambda dd, tt, at=at, count=count: (dd, lax.rem(tt, 2), pl.ds(at, count)),
+            steps=steps + t_core,
+        )
+        for at, count, steps in (
+            (0, cut, outer_first),
+            (cut, core_rows - cut, inner_first),
+        )
+    ]
+    jobs += [
+        dict(src=1, out=1, out_at=rows_at(0, qb_rows, qb_rows), steps=outer_first),
+        dict(src=2, out=2, out_at=rows_at(CODE_LANES, kvb_rows, kvb_rows), steps=outer_first),
+        dict(src=3, out=3, out_at=rows_at(0, out_rows, out_rows), steps=outer_first),
+    ]
+    jobs += group_jobs(4, 4)
+    jobs.append(dict(src=8, out=5, out_at=lambda dd, tt: (dd,), steps=outer_first))
+    set_mark = jnp.full((16, 128), sequence_adapter_index[0].astype(F32)).astype(BF16)
+    w_down, w_q, w_kv, w_out, g_all, set_marks = remote_gather(
+        [
+            down_mine,
+            pad_heads(query_up_matrix),
+            keyvalue_up_matrix,
+            output_matrix.T,
+            g_own,
+            q_aug_rows,
+            kv_aug_rows,
+            out_extra,
+            set_mark,
+        ],
+        jobs,
+        [
+            (5, 1, (pl.ds(q_lat, CODE_LANES),)),
+            (6, 2, (pl.ds(0, CODE_LANES),)),
+            (7, 3, (pl.ds(width, CODE_LANES),)),
+        ],
+        [
+            (n_dp, 2, core_rows, q_lat + kv_all),
+            (q_lat + CODE_LANES, heads * HEAD_LANES),
+            (CODE_LANES + kv_lat, heads * HEAD_LANES),
+            (aug, heads * VALUE_HEAD_DIM),
+            (2 * n_t * rows, aug),
+            (n_dp, 16, 128),
+        ],
+        "gather_weights",
+        1,
+    )
+    set_all = set_marks[:, 0, 0].astype(jnp.int32)
+    set_peer = lax.dynamic_index_in_dim(set_all, jnp.bitwise_xor(d, pair), 0, keepdims=False)
+    set_even = jnp.where(first, set_own, set_peer)
+    set_odd = jnp.where(first, set_peer, set_own)
+    w_down = w_down.reshape(width, q_lat + kv_all)
+
+    hidden = down_matrix.shape[0]
+    half = hidden // 2
+    main = half // 128 * 128
+    tail = half - main
+    tail_wide = -(-3 * tail // 128) * 128
+    chunks = 2 if (main // 128) % 2 == 0 else 1
+    step_wide = main // chunks
+
+    def columns(gate_part, up_part, down_part, chunk):
+        at = slice(chunk * step_wide, (chunk + 1) * step_wide)
+        out = [gate_part[:, at]]
+        if tail and chunk == chunks - 1:
+            out += [gate_part[:, main:], up_part[:, main:], down_part[:, main:]]
+            if tail_wide > 3 * tail:
+                out.append(jnp.zeros((gate_part.shape[0], tail_wide - 3 * tail), BF16))
+        out += [up_part[:, at], down_part[:, at]]
+        return jnp.concatenate(out, axis=1)
+
+    def halves(value):
+        return value[:, :half], value[:, half:]
+
+    down_turned = down_matrix.T
+    mats = [halves(gate_up_matrix[0]), halves(gate_up_matrix[1]), halves(down_turned)]
+    zero_codes = jnp.zeros((RANK, half), BF16)
+
+    def half_of(value):
+        left, right = halves(value)
+        return jnp.where(first, left, right)
+
+    extra_parts = []
+    for which in (set_even, set_odd):
+        gate_b = half_of(pick(gate_up_adapter_out[0], which)) * 2
+        up_b = half_of(pick(gate_up_adapter_out[1], which)) * 2
+        down_a_t = half_of(pick(turned(down_adapter_in), which))
+        extra_parts.append((gate_b, up_b, down_a_t))
+
+    z_count = n_dp // pair
+    ffn_columns, ffn_known = [], []
+    for chunk in range(chunks):
+        left = columns(mats[0][0], mats[1][0], mats[2][0], chunk)
+        right = columns(mats[0][1], mats[1][1], mats[2][1], chunk)
+        mine = jnp.where(first, left, right)
+        other = jnp.where(first, right, left)
+        held = {
+            0: mine,
+            pair: hop(other, ("dp", pair)),
+            high: hop(mine, ("dp", high)),
+            high ^ pair: hop(other, ("dp", high ^ pair)),
+        }
+        count, wide = mine.shape
+        (column,) = place_pieces(
+            list(held.values()),
+            [
+                (n, None, 0, lambda dd, tt, r=r: (jnp.bitwise_xor(dd, r) // pair,))
+                for n, r in enumerate(held)
+            ],
+            [(z_count, count, wide)],
+            "place_column_" + str(chunk),
+        )
+        ffn_columns.append(column)
+    w_down, ffn_columns = lax.optimization_barrier((w_down, ffn_columns))
+    for column in ffn_columns:
+        known = {0: column}
+        for b in reversed(low_bits):
+            for r in list(known):
+                known[r ^ b] = hop(known[r], ("dp", b))
+        ffn_known.append(known)
     cos_part, sin_part = rope_tables(document_numbers)
     zeros_l = jnp.zeros((length, PLAIN_HEAD_DIM), F32)
     zeros_r = jnp.zeros((length, HEAD_LANES - 96), F32)
@@ -755,19 +998,20 @@
         axis=1,
     )
 
-    def by_tensor_place(held, name):
-        keys = list(held)
-        shape = held[keys[0]].shape
-        (full,) = place_pieces(
-            [held[k] for k in keys],
-            [
-                (n, None, 0, lambda dd, tt, r=k[1]: (jnp.bitwise_xor(tt, r),))
-                for n, k in enumerate(keys)
-            ],
-            [(n_t,) + shape],
-            name,
-        )
-        return full.reshape((n_t * shape[0],) + shape[1:])
+    def token_jobs(src, out, parts):
+        count = rows // parts
+        return [
+            dict(
+                src=src,
+                src_at=pl.ds(n * count, count),
+                out=out,
+                out_at=lambda dd, tt, n=n: (
+                    pl.ds(pl.multiple_of(tt * rows + n * count, 16), count),
+                ),
+                steps=t_slow + t_core,
+            )
+            for n in range(parts)
+        ]
 
     def relative(value, name):
         blocks = value.reshape(n_t, value.shape[0] // n_t, value.shape[1])
@@ -779,7 +1023,9 @@
         )
         return full
 
-    lat_all = by_tensor_place(spread(lat_own, t_slow + t_core), "place_latents")
+    (lat_all,) = remote_gather(
+        [lat_own], token_jobs(0, 0, 2), [], [(length, lat_own.shape[1])], "gather_latents", 2
+    )
     pe_rows = lat_all[:, pe_at : pe_at + ROTARY_DIM].astype(F32)
     pe_a, pe_b = pe_rows[:, : ROTARY_DIM // 2], pe_rows[:, ROTARY_DIM // 2 :]
     pe_aug = narrow(
@@ -797,11 +1043,28 @@
     q_aug, kv, head_out = attend(
         lat_all, w_q, w_kv, rope, pe_aug, doc_q, q_lat + CODE_LANES, q_lat
     )
-    head_rel = relative(head_out, "place_heads")
-    parts = {}
-    for r in [r for r in range(n_t) if r & 1] + [r for r in range(n_t) if not r & 1]:
-        parts[(0, r)] = dot_nt(head_rel[r], w_out)
-    attn_sum = collect(parts, t_core + t_slow[::-1])
+    tensor_keys = [(0, r) for r in reversed(range(0, n_t, 2))]
+
+    def token_rows(key, place):
+        at = jnp.bitwise_xor(place["tensor"], key[1]) * rows
+        return pl.ds(pl.multiple_of(at, 16), rows)
+
+    def out_term(held, place, key):
+        return dot_nt(held[0][token_rows(key, place), :], held[1][...])
+
+    head_out, ffn_known[0] = lax.optimization_barrier((head_out, ffn_known[0]))
+    attn_sum = remote_reduce(
+        [head_out, w_out],
+        [head_out.shape, w_out.shape],
+        out_term,
+        tensor_keys,
+        [t_slow[::-1]],
+        rows,
+        aug,
+        "reduce_out",
+        3,
+        2 * length * head_out.shape[1] * aug,
+    )
     out_codes = narrow(attn_sum[:, width : width + RANK])
     middle = residual + RESIDUAL * (
         attn_sum[:, :width] + ADAPT_SCALE * dot_nn(out_codes, out_out)
@@ -811,7 +1074,42 @@
     ffn_rows = narrow(ffn_normed)
     gu_codes = narrow(dot_nt(ffn_rows, gu_in))
     x_own = jnp.concatenate([ffn_rows, code_lanes(gu_codes)], axis=1)
-    x_all = spread_group(x_own)
+    x_own, ffn_known = lax.optimization_barrier((x_own, ffn_known))
+    ffn_weights = []
+    for chunk, known in enumerate(ffn_known):
+        count, wide = known[0].shape[1:]
+        extra = []
+        for gate_b, up_b, down_a_t in extra_parts:
+            extra.append(columns(gate_b, zero_codes, down_a_t, chunk))
+            extra.append(columns(zero_codes, up_b, zero_codes, chunk))
+        extra.append(jnp.zeros((CODE_LANES - 4 * RANK, extra[0].shape[1]), BF16))
+        sources, copies = [jnp.concatenate(extra, axis=0)], [
+            (0, None, 0, lambda dd, tt: (pl.ds(width, CODE_LANES),))
+        ]
+        for r, piece in known.items():
+            for z in range(z_count):
+                copies.append(
+                    (
+                        len(sources),
+                        z,
+                        0,
+                        lambda dd, tt, r=r, z=z: (
+                            pl.ds(
+                                pl.multiple_of(
+                                    (z * pair + lax.rem(jnp.bitwise_xor(dd, r), pair)) * count, 16
+                                ),
+                                count,
+                            ),
+                        ),
+                    )
+                )
+            sources.append(piece)
+        (full,) = place_pieces(sources, copies, [(aug, wide)], "place_ffn_" + str(chunk))
+        ffn_weights.append(full)
+
+    (x_all,) = remote_gather(
+        [x_own], group_jobs(0, 0), [], [(2 * n_t * rows, aug)], "gather_rows", 4
+    )
     grads, hids = [], []
     for chunk in range(chunks):
         last = chunk == chunks - 1
@@ -824,33 +1122,37 @@
     def gu_columns(chunk):
         return grads[chunk].shape[1]
 
-    odd_rows = len(odd_keys) * rows
-
-    def group_parts(terms):
-        odd = narrow(terms(slice(0, odd_rows)))
-        came = hop(odd, t_core[0])
-        chip = terms(slice(odd_rows, 2 * odd_rows)) + came.astype(F32)
-        return chip
-
-    def finish(chip, steps_a, steps_b):
-        tops, bottoms = {}, {}
-        for n, key in enumerate(even_keys):
-            piece = chip[n * rows : (n + 1) * rows]
-            tops[key] = piece[:half_rows]
-            bottoms[key] = piece[half_rows:]
-        return collect(tops, steps_a), collect(bottoms, steps_b)
-
-    def ffn_in_terms(at):
-        out = dot_nt(grads[0][at], ffn_weights[0][:, : gu_columns(0)])
+    group_keys = [
+        (p, r) for p in (pair, 0) for r in reversed(range(0, n_t, 2))
+    ]
+
+    def ffn_in_term(held, place, key):
+        block = group_block(
+            jnp.bitwise_xor(place["dp"], key[0]), jnp.bitwise_xor(place["tensor"], key[1])
+        )
+        at = pl.ds(pl.multiple_of(block * rows, 16), rows)
+        out = dot_nt(held[0][at, :], held[chunks][...])
         for chunk in range(1, chunks):
-            out = out + dot_nt(grads[chunk][at], ffn_weights[chunk][:, : gu_columns(chunk)])
+            out = out + dot_nt(held[chunk][at, :], held[chunks + chunk][...])
         return out
 
-    def down_terms(at):
+    ffn_in_sum = remote_reduce(
+        grads + ffn_weights,
+        [g.shape for g in grads] + [(aug, gu_columns(c)) for c in range(chunks)],
+        ffn_in_term,
+        group_keys,
+        [group_a[::-1], group_b[::-1]],
+        rows,
+        aug,
+        "reduce_ffn_in",
+        5,
+        2 * 2 * length * sum(g.shape[1] for g in grads) * aug,
+    )
+
+    def down_terms(hid_rows):
         out = 0.0
-        for chunk in range(chunks):
+        for chunk, hid in enumerate(hid_rows):
             weight = ffn_weights[chunk]
-            hid = hids[chunk][at]
             out = out + dot_nt(hid[:, :step_wide], weight[:, gu_columns(chunk) :])
             if hid.shape[1] > step_wide:
                 out = out + dot_nt(
@@ -858,41 +1160,56 @@
                 )
         return out
 
-    ffn_in_halves = finish(group_parts(ffn_in_terms), group_a[::-1], group_b[::-1])
-    tops = []
-    for n, ffn_in_aug in enumerate(ffn_in_halves):
-        at = slice(n * half_rows, (n + 1) * half_rows)
-        gu_code_grad = narrow(own_codes(ffn_in_aug))
-        ffn_in_grad = ffn_in_aug[:, :width] + dot_nn(gu_code_grad, gu_in)
-        middle_grad = out_grad[at] + normalize_back(
-            middle[at], ffn_scale[at], feedforward_norm_gain, ffn_in_grad
-        )
-        attn_grad = narrow(RESIDUAL * middle_grad)
-        out_code_grad = narrow(ADAPT_SCALE * dot_nt(attn_grad, out_out))
-        attn_grad_aug = jnp.concatenate(
-            [attn_grad, out_code_grad, jnp.zeros((half_rows, CODE_LANES - RANK), BF16)], axis=1
-        )
-        tops.append((gu_code_grad, middle_grad, attn_grad_aug, spread(attn_grad_aug, t_slow + t_core)))
-    gu_code_grad = jnp.concatenate([tops[0][0], tops[1][0]], axis=0)
-    middle_grad = jnp.concatenate([tops[0][1], tops[1][1]], axis=0)
-    attn_grad_aug = jnp.concatenate([tops[0][2], tops[1][2]], axis=0)
-    attn_grad = attn_grad_aug[:, :width]
-
-    grad_rel = []
-    for r in range(n_t):
-        both = jnp.concatenate([tops[0][3][(0, r)], tops[1][3][(0, r)]], axis=0)
-        grad_rel.append(both)
-    codes_rel = jnp.stack([g[:, width:] for g in grad_rel], axis=0)
-    heads_grad = by_tensor_place(
-        {(0, r): narrow(dot_nn(grad_rel[r], w_out)) for r in range(n_t)}, "place_heads_grad"
-    )
-    out_a = dot_tn(codes_rel.reshape(length, CODE_LANES), head_rel.reshape(length, -1))[:RANK]
+    gu_code_grad = narrow(own_codes(ffn_in_sum))
+    ffn_in_grad = ffn_in_sum[:, :width] + dot_nn(gu_code_grad, gu_in)
+    middle_grad = out_grad + normalize_back(
+        middle, ffn_scale, feedforward_norm_gain, ffn_in_grad
+    )
+    attn_grad = narrow(RESIDUAL * middle_grad)
+    out_code_grad = narrow(ADAPT_SCALE * dot_nt(attn_grad, out_out))
+    attn_grad_aug = jnp.concatenate(
+        [attn_grad, out_code_grad, jnp.zeros((rows, CODE_LANES - RANK), BF16)], axis=1
+    )
+
+    (grad_all,) = remote_gather(
+        [attn_grad_aug], token_jobs(0, 0, 2), [], [(length, aug)], "gather_grad", 6
+    )
+    heads_grad = narrow(dot_nn(grad_all, w_out))
+    out_a = dot_tn(grad_all[:, width:], head_out)[:RANK]
     dq, dkv, dpe = attend_back(q_aug, kv, head_out, heads_grad, rope, pe_aug)
 
-    down_a_sum, down_b_sum = finish(
-        group_parts(down_terms), [("dp", pair)] + t_slow[::-1], [("dp", pair)] + t_slow[::-1]
-    )
-    ffn_out = jnp.concatenate([down_a_sum, down_b_sum], axis=0)
+    hid_rel = place_pieces(
+        hids,
+        [
+            (
+                c,
+                pl.ds(b * rows, rows),
+                c,
+                lambda dd, tt, b=b: (
+                    jnp.bitwise_xor(lax.rem(dd // pair, 2), b // n_t) * n_t
+                    + jnp.bitwise_xor(tt, b % n_t),
+                ),
+            )
+            for c in range(chunks)
+            for b in range(2 * n_t)
+        ],
+        [(2 * n_t, rows, h.shape[1]) for h in hids],
+        "place_hidden",
+    )
+    hid_rel = [h.reshape(2, n_t // 2, 2, rows, h.shape[2]) for h in hid_rel]
+    hid_odd = [h[:, :, 1].reshape(n_t * rows, -1) for h in hid_rel]
+    hid_even = [h[:, :, 0].reshape(n_t * rows, -1) for h in hid_rel]
+    came = hop(narrow(down_terms(hid_odd)), t_core[0])
+    chip = down_terms(hid_even) + came.astype(F32)
+    chip = chip.reshape(2, n_t // 2, rows, aug)
+    ffn_out = chip[0] + hop(narrow(chip[1]), ("dp", pair)).astype(F32)
+    left = n_t // 2
+    while left > 1:
+        ffn_out = ffn_out[: left // 2] + hop(
+            narrow(ffn_out[left // 2 :]), ("tensor", left)
+        ).astype(F32)
+        left //= 2
+    ffn_out = ffn_out[0]
     down_codes = narrow(own_codes(ffn_out)[:, :RANK])
     outputs = narrow(
         middle
@@ -904,20 +1221,35 @@
     pe_grad = jnp.concatenate(
         [pe_ga * cos_part + pe_gb * sin_part, pe_gb * cos_part - pe_ga * sin_part], axis=1
     )
-    from_q = dot_nt(dq, w_q)
-    from_kv = dot_nt(dkv, w_kv)
-    lat_grad = jnp.concatenate(
-        [
-            from_q[:, :q_lat],
-            from_q[:, q_lat:]
-            + from_kv[:, :CODE_LANES]
-            + jnp.pad(pe_grad, ((0, 0), (2 * RANK, CODE_LANES - 2 * RANK - ROTARY_DIM))),
-            from_kv[:, CODE_LANES:],
-        ],
-        axis=1,
-    )
-    lat_rel = relative(narrow(lat_grad), "place_latent_grads")
-    lat_sum = collect({(0, r): lat_rel[r] for r in range(n_t)}, t_core + t_slow[::-1])
+    pe_padded = jnp.pad(pe_grad, ((0, 0), (2 * RANK, CODE_LANES - 2 * RANK - ROTARY_DIM)))
+    lat_wide = q_lat + CODE_LANES + kv_lat
+
+    def latent_term(held, place, key):
+        at = token_rows(key, place)
+        from_q = dot_nt(held[0][at, :], held[2][...])
+        from_kv = dot_nt(held[1][at, :], held[3][...])
+        return jnp.concatenate(
+            [
+                from_q[:, :q_lat],
+                from_q[:, q_lat:] + from_kv[:, :CODE_LANES] + held[4][at, :],
+                from_kv[:, CODE_LANES:],
+            ],
+            axis=1,
+        )
+
+    operands = [dq, dkv, w_q, w_kv, pe_padded]
+    lat_sum = remote_reduce(
+        operands,
+        [o.shape for o in operands],
+        latent_term,
+        tensor_keys,
+        [t_slow[::-1]],
+        rows,
+        lat_wide,
+        "reduce_latents",
+        7,
+        2 * length * dq.shape[1] * lat_wide,
+    )
     qb_code_grad = narrow(lat_sum[:, q_lat : q_lat + RANK])
     kvb_code_grad = narrow(lat_sum[:, q_lat + RANK : q_lat + 2 * RANK])
     pe_sum = lat_sum[:, pe_at : pe_at + ROTARY_DIM]
@@ -944,46 +1276,15 @@
     def to_sets(terms):
         return jnp.einsum("sk,srn->krn", onehot, terms, preferred_element_type=F32)
 
-    def shared_terms(terms, name):
-        count = terms.shape[0] // n_t
-        split = relative(narrow(terms), name + "_split")
-        own = collect({(0, r): split[r] for r in range(n_t)}, t_core + t_slow[::-1])
-        held = spread(narrow(own), outer_first + t_slow + t_core)
-        keys = list(held)
-        (full,) = place_pieces(
-            [held[k] for k in keys],
-            [
-                (
-                    n,
-                    None,
-                    0,
-                    lambda dd, tt, k=k: (jnp.bitwise_xor(dd, k[0]), jnp.bitwise_xor(tt, k[1])),
-                )
-                for n, k in enumerate(keys)
-            ],
-            [(n_dp, n_t, count, terms.shape[1])],
-            name + "_place",
-        )
-        return full.reshape(n_dp, n_t * count, terms.shape[1])
-
-    def split_terms(terms, name):
-        held = spread(terms, outer_first)
-        keys = list(held)
-        (full,) = place_pieces(
-            [held[k] for k in keys],
-            [
-                (n, None, 0, lambda dd, tt, k=k: (jnp.bitwise_xor(dd, k[0]),))
-                for n, k in enumerate(keys)
-            ],
-            [(n_dp,) + terms.shape],
-            name,
-        )
-        return full
+    def dp_job(src, out):
+        return dict(src=src, out=out, out_at=lambda dd, tt: (dd,), steps=outer_first)
+
+    t_steps = t_core + t_slow[::-1]
 
     gu_a = dot_tn(gu_code_grad, ffn_rows)
     out_b = ADAPT_SCALE * dot_tn(out_codes, attn_grad)
     down_b = ADAPT_SCALE * dot_tn(down_codes, ffn_grad)
-    early = shared_terms(jnp.concatenate([gu_a, out_b, down_b], axis=0), "early")
+    early_terms = jnp.concatenate([gu_a, out_b, down_b], axis=0)
 
     def uncolumn(parts, at_tail, first_at):
         out = [parts[c][:, first_at(c) : first_at(c) + step_wide] for c in range(chunks)]
@@ -1005,7 +1306,18 @@
             up_b_all[at + RANK : at + 2 * RANK],
             down_a_all[at : at + RANK],
         ]
-    hidden_terms = split_terms(narrow(jnp.concatenate(packed, axis=0)), "hidden_place")
+    hidden_own = narrow(jnp.concatenate(packed, axis=0))
+    early, hidden_terms = remote_share(
+        narrow(early_terms),
+        [hidden_own],
+        [dp_job(1, 1)],
+        [(n_dp,) + early_terms.shape, (n_dp,) + hidden_own.shape],
+        n_t,
+        t_steps,
+        outer_first,
+        "share_early",
+        8,
+    )
     hidden_terms = hidden_terms.reshape(2, 2, pair, 2, 3 * RANK, half)
     hidden_terms = jnp.concatenate([hidden_terms[:, 0], hidden_terms[:, 1]], axis=-1)
     hidden_terms = jnp.moveaxis(hidden_terms, 2, 1).reshape(n_dp, 3 * RANK, hidden)
@@ -1014,16 +1326,7 @@
     lat_codes = lat_all[:, q_lat : q_lat + CODE_LANES]
     qb_b = ADAPT_SCALE * dot_tn(lat_codes, dq)[:RANK]
     kvb_b = ADAPT_SCALE * dot_tn(lat_codes, dkv)[RANK : 2 * RANK]
-    head_terms = split_terms(
-        narrow(jnp.concatenate([qb_b, kvb_b, out_a], axis=1)), "head_place"
-    )
-    head_sets = to_sets(head_terms)
-    wide = heads * HEAD_LANES
-    qb_b_grad = head_sets[:, :, :wide].reshape(group_count, RANK, heads, HEAD_LANES)[..., :head_q]
-    qb_b_grad = qb_b_grad.reshape(group_count, RANK, heads * head_q)
-    kvb_b_grad = head_sets[:, :, wide : 2 * wide]
-    out_a_grad = turned(head_sets[:, :, 2 * wide :])
-
+    head_own = narrow(jnp.concatenate([qb_b, kvb_b, out_a], axis=1))
     down_in_terms = dot_tn(code_grad, attn_rows)
     b_terms = ADAPT_SCALE * dot_tn(down_codes_in, latent_grad)
     qb_a = dot_tn(qb_code_grad, q_input)
@@ -1031,7 +1334,24 @@
     small = jnp.concatenate([b_terms[:RANK, :q_lat], b_terms[RANK:, q_lat:], qb_a, kvb_a], axis=1)
     small_wide = small.shape[1]
     small = jnp.pad(small, ((0, RANK), (0, width - small_wide)))
-    late = shared_terms(jnp.concatenate([down_in_terms, small], axis=0), "late")
+    late_terms = jnp.concatenate([down_in_terms, small], axis=0)
+    late, head_terms = remote_share(
+        narrow(late_terms),
+        [head_own],
+        [dp_job(1, 1)],
+        [(n_dp,) + late_terms.shape, (n_dp,) + head_own.shape],
+        n_t,
+        t_steps,
+        outer_first,
+        "share_late",
+        9,
+    )
+    head_sets = to_sets(head_terms)
+    wide = heads * HEAD_LANES
+    qb_b_grad = head_sets[:, :, :wide].reshape(group_count, RANK, heads, HEAD_LANES)[..., :head_q]
+    qb_b_grad = qb_b_grad.reshape(group_count, RANK, heads * head_q)
+    kvb_b_grad = head_sets[:, :, wide : 2 * wide]
+    out_a_grad = turned(head_sets[:, :, 2 * wide :])
 
     early_sets = to_sets(early)
     late_sets = to_sets(late)

time: 1140 us -> 1040 us (0.912)
  Pallas kernels: 159 us -> 661 us
  waiting for transfers between devices: 417 us -> 107 us
  starting transfers between devices: 135 us -> 14.2 us
  local copies, waits for them, and re-layouts: 157 us -> 93.6 us
  other arithmetic: 88 us -> 37.6 us
  matrix products: 160 us -> 110 us
    pallas_call x0 -> x9, Pallas kernels: none -> 527 us  [the longest x4 319 us: remote_gather(): pl.pallas_call(kernel, out_shape=[jax.ShapeDtypeStruct(o, BF16) for o in...]
    ppermute x182 -> x11, waiting for transfers between devices: 417 us -> 107 us  [swap(): return lax.ppermute(value, axis, [(i, i ^ bit) for i in range(size)])]
    ppermute x182 -> x11, starting transfers between devices: 135 us -> 14.2 us  [swap(): return lax.ppermute(value, axis, [(i, i ^ bit) for i in range(size)])]
    dot_general x25 -> x14, matrix products: 103 us -> 58.7 us  [dot_nt(): lax.dot_general(a, b, (((1,), (1,)), ((), ())), preferred_element_type=F32)]
    unnamed x499 -> x257, local copies, waits for them, and re-layouts: 79.8 us -> 35.2 us
    pallas_call x16 -> x5, Pallas kernels: 54 us -> 22.6 us  [place_pieces(): pl.pallas_call(kernel, out_shape=[jax.ShapeDtypeStruct(o, BF16) for o in...]
    another operation x12 -> x7, other arithmetic: 31.1 us -> 2.37 us
    dot_general x13 -> x9, matrix products: 26.2 us -> 23.8 us  [dot_nn(): lax.dot_general(a, b, (((1,), (0,)), ((), ())), preferred_element_type=F32)]
  transfers between devices with their start and end apart: 182 -> 11, of which waited for: 51 -> 5; matrix products, arithmetic and copies ran while one was open for 28% -> 11% of each run, Pallas kernels for 6% -> 33%
where the time goes in v2:
time: 1040 us; the launch traced here: 1030 us
  Pallas kernels  661 us (64%)
  matrix products  110 us (11%)
  waiting for transfers between devices  107 us (10%)
  local copies, waits for them, and re-layouts  93.6 us (9%)
  other arithmetic  37.6 us (4%)
  starting transfers between devices  14.2 us (1%)
    pallas_call x4, Pallas kernels, remote_gather(): pl.pallas_call(kernel, out_shape=[jax.ShapeDtypeStruct(o, BF16) for o in...  319 us
    pallas_call x3, Pallas kernels, remote_reduce(): pl.pallas_call(kernel, out_shape=jax.ShapeDtypeStruct((rows, wide), F32),...  122 us
    ppermute x11, waiting for transfers between devices, swap(): return lax.ppermute(value, axis, [(i, i ^ bit) for i in range(size)])  107 us
    pallas_call x2, Pallas kernels, remote_share(): pl.pallas_call(kernel, out_shape=[jax.ShapeDtypeStruct(o, BF16) for o in...  84.7 us
    dot_general x14, matrix products, dot_nt(): lax.dot_general(a, b, (((1,), (1,)), ((), ())), preferred_element_type=F32)  58.7 us
    pallas_call x2, Pallas kernels, ffn_middle(): pl.pallas_call(functools.partial(ffn_kernel, main, tail, tail_wide), grid...  57.6 us
    unnamed x257, local copies, waits for them, and re-layouts  35.2 us
    pallas_call x1, Pallas kernels, attend(): pl.pallas_call(functools.partial(attn_fwd_kernel, per_step, q_width, kv_a...  27.5 us
  transfers between devices with their start and end apart: 11, of which 5 were waited for; matrix products, arithmetic and copies ran while one was open for 11% of the time, Pallas kernels for 33%

profile of v2, /device:TPU:0, one launch (start us, length us, event | category | flops | bytes accessed | tf_op | source)
XLA Modules:
  0.0 1029.1 jit_solution(2096123382731947733)
XLA Ops:
  39.0 211.4 %gather_weights.1 = (bf16[8,2,160,1056]{3,2,1,0:T(8,128)(2,1)}, bf16[896,1280]{1,0:T(8,128)(2,1)}, bf16[384,1280]{1,0:T(8,128)(2,1)}, bf16[2688,640]{1,0:T(8,128...) custom-call(bf16[160,1056]{1,0:T(8,128)(2,1)} %dynamic-slice_bitcast_fusion.refs_0_, ...), custom_call_target="tpu_custom_call" | custom-call | tf_op jit(solution)/shard_map/gather_weights/pallas_call | solution.py:224
  270.5 27.2 %collective-permute-done.1.refs_2_ = bf16[320,1152]{1,0:T(8,128)(2,1)S(1)} collective-permute-done((bf16[320,1152]{1,0:T(8,128)(2,1)S(1)}, bf16[320,1152]{1,0:T(8,128)(2,1)S(1)}, u32[]{:S(2)}, u32[]{:S(2)}) %collective-permute-start.1) | collective-permute-done | bytes 737312 | tf_op jit(solution)/shard_map/ppermute | solution.py:75
  317.6 18.4 %gather_latents.1.xl_ref = bf16[1024,1152]{1,0:T(8,128)(2,1)} custom-call(bf16[256,1152]{1,0:T(8,128)(2,1)} %concatenate.154.refs_0_), custom_call_target="tpu_custom_call" | custom-call | tf_op jit(solution)/shard_map/gather_latents/pallas_call | solution.py:224
  343.1 27.5 %attend.1 = (bf16[1024,1280]{1,0:T(8,128)(2,1)}, bf16[1024,1280]{1,0:T(8,128)(2,1)}, bf16[1024,640]{1,0:T(8,128)(2,1)}) custom-call(bf16[1024,1152]{1,0:T(8,128)(2,1)} %gather_latents.1.xl_ref, bf16[896,1280]{1,0:T(8,128)(2,1)} %get-tuple-element.51.wq_ref.refs_2_, bf16[384,1280]{1,0:T(8,128)(2,1)} %get-tuple-element.52.wkv_ref.refs_3_, ...), custom_call_target="tpu_custom_call" | custom-call | tf_op jit(solution)/shard_map/attend/pallas_call | solution.py:546
  372.9 38.8 %reduce_out.1 = f32[256,2688]{1,0:T(8,128)} custom-call(bf16[1024,640]{1,0:T(8,128)(2,1)} %get-tuple-element.55.refs_0_.o_ref, bf16[2688,640]{1,0:T(8,128)(2,1)} %get-tuple-element.56.refs_1_), custom_call_target="tpu_custom_call" | custom-call | tf_op jit(solution)/shard_map/reduce_out/pallas_call | solution.py:311
  420.7 21.5 %collective-permute-done.7.refs_2_ = bf16[4,320,1280]{2,1,0:T(8,128)(2,1)} collective-permute-done((bf16[4,320,1280]{2,1,0:T(8,128)(2,1)}, bf16[4,320,1280]{2,1,0:T(8,128)(2,1)}, u32[]{:S(2)}, u32[]{:S(2)}) %collective-permute-start.7) | collective-permute-done | bytes 3276832 | tf_op jit(solution)/shard_map/ppermute | solution.py:75
  442.2 53.8 %gather_rows.1.x_ref = bf16[2048,2688]{1,0:T(8,128)(2,1)} custom-call(bf16[256,2688]{1,0:T(8,128)(2,1)} %concatenate.162.refs_0_), custom_call_target="tpu_custom_call" | custom-call | tf_op jit(solution)/shard_map/gather_rows/pallas_call | solution.py:224
  496.0 5.9 place_ffn_1.1.w_ref.refs_3_
  501.8 28.2 %ffn_middle.3 = (bf16[2048,896]{1,0:T(8,128)(2,1)}, bf16[2048,512]{1,0:T(8,128)(2,1)}) custom-call(bf16[2048,2688]{1,0:T(8,128)(2,1)} %gather_rows.1.x_ref, bf16[2048,2688]{1,0:T(8,128)(2,1)} %get-tuple-element.61.g_ref, bf16[2688,1280]{1,0:T(8,128)(2,1)} %place_ffn_1.1.w_ref.refs_3_), custom_call_target="tpu_custom_call" | custom-call | tf_op jit(solution)/shard_map/ffn_middle/pallas_call | solution.py:635
  541.7 29.4 %ffn_middle.2 = (bf16[2048,768]{1,0:T(8,128)(2,1)}, bf16[2048,384]{1,0:T(8,128)(2,1)}) custom-call(bf16[2048,2688]{1,0:T(8,128)(2,1)} %gather_rows.1.x_ref, bf16[2048,2688]{1,0:T(8,128)(2,1)} %get-tuple-element.61.g_ref, bf16[2688,1152]{1,0:T(8,128)(2,1)} %place_ffn_0.1.w_ref.refs_2_), custom_call_target="tpu_custom_call" | custom-call | tf_op jit(solution)/shard_map/ffn_middle/pallas_call | solution.py:635
  571.1 61.1 %reduce_ffn_in.1 = f32[256,2688]{1,0:T(8,128)} custom-call(bf16[2048,768]{1,0:T(8,128)(2,1)} %get-tuple-element.71.refs_0_, bf16[2048,896]{1,0:T(8,128)(2,1)} %get-tuple-element.72.refs_1_, bf16[2688,1152]{1,0:T(8,128)(2,1)} %place_ffn_0.1.w_ref.refs_2_, bf16[2688,1280]{1,0:T(8,128)(2,1)} %place_ffn_1.1.w_ref.refs_3_), custom_call_target="tpu_custom_call" | custom-call | tf_op jit(solution)/shard_map/reduce_ffn_in/pallas_call | solution.py:311
  643.1 35.8 %gather_grad.1 = bf16[1024,2688]{1,0:T(8,128)(2,1)} custom-call(bf16[256,2688]{1,0:T(8,128)(2,1)} %concatenate.173.refs_0_), custom_call_target="tpu_custom_call" | custom-call | tf_op jit(solution)/shard_map/gather_grad/pallas_call | solution.py:224
  679.0 8.3 convolution_convert_fusion.2.do_ref
  688.6 27.0 %attend_back.1 = (bf16[1024,1280]{1,0:T(8,128)(2,1)}, bf16[1024,1280]{1,0:T(8,128)(2,1)}, f32[1024,128]{1,0:T(8,128)}) custom-call(bf16[1024,1280]{1,0:T(8,128)(2,1)} %get-tuple-element.73.qa_ref, bf16[1024,1280]{1,0:T(8,128)(2,1)} %get-tuple-element.74.kv_ref, bf16[1024,640]{1,0:T(8,128)(2,1)} %get-tuple-element.55.refs_0_.o_ref, ...), custom_call_target="tpu_custom_call" | custom-call | tf_op jit(solution)/shard_map/attend_back/pallas_call | solution.py:581
  722.2 22.7 %reduce_latents.1 = f32[256,1152]{1,0:T(8,128)} custom-call(bf16[1024,1280]{1,0:T(8,128)(2,1)} %get-tuple-element.75.refs_0_, bf16[1024,1280]{1,0:T(8,128)(2,1)} %get-tuple-element.76.refs_1_, bf16[896,1280]{1,0:T(8,128)(2,1)} %get-tuple-element.51.wq_ref.refs_2_, bf16[384,1280]{1,0:T(8,128)(2,1)} %get-tuple-element.52.wkv_ref.refs_3_, ...), custom_call_target="tpu_custom_call" | custom-call | tf_op jit(solution)/shard_map/reduce_latents/pallas_call | solution.py:311
  764.0 7.5 fusion.27
  771.6 8.9 add_convert_fusion
  786.4 38.7 %share_late.1 = (bf16[8,64,2560]{2,1,0:T(8,128)(2,1)}, bf16[8,16,3200]{2,1,0:T(8,128)(2,1)}) custom-call(bf16[64,2560]{1,0:T(8,128)(2,1)} %fusion.83.refs_0_, bf16[16,3200]{1,0:T(8,128)(2,1)} %pad_maximum_fusion.14.refs_1_), custom_call_target="tpu_custom_call" | custom-call | tf_op jit(solution)/shard_map/share_late/pallas_call | solution.py:385
  839.2 7.7 fusion.29
  846.9 12.3 %convert_add_fusion = f32[1024,2688]{1,0:T(8,128)} fusion(bf16[1024,2688]{1,0:T(8,128)(2,1)} %collective-permute-done.8, f32[1024,2688]{1,0:T(8,128)S(1)} %fusion.33, f32[1024,2688]{1,0:T(8,128)} %fusion.29, bf16[2688,1280]{1,0:T(8,128)(2,1)} %place_ffn_1.1.w_ref.refs_3_, bf16[1024,512]{1,0:T(8,128)(2,1)} %bitcast.237), kind=kOutput, calls=%fused_computation | convolution fusion | flops 715653120 | bytes 39485440 | tf_op jit(solution)/shard_map/dot_general | solution.py:42
  868.7 6.6 fusion.16
  877.1 47.2 %collective-permute-done.9 = bf16[2,256,2688]{2,1,0:T(8,128)(2,1)S(1)} collective-permute-done((bf16[2,256,2688]{2,1,0:T(8,128)(2,1)S(1)}, bf16[2,256,2688]{2,1,0:T(8,128)(2,1)S(1)}, u32[]{:S(2)}, u32[]{:S(2)}) %collective-permute-start.9) | collective-permute-done | bytes 2752544 | tf_op jit(solution)/shard_map/ppermute | solution.py:75
  951.1 9.1 collective-permute-done.10
  965.7 46.1 %share_early.1 = (bf16[8,64,2560]{2,1,0:T(8,128)(2,1)}, bf16[8,96,800]{2,1,0:T(8,128)(2,1)}) custom-call(bf16[64,2560]{1,0:T(8,128)(2,1)} %pad_maximum_fusion.7.refs_0_, bf16[96,800]{1,0:T(8,128)(2,1)} %constant_dynamic-update-slice_fusion.4.refs_1_), custom_call_target="tpu_custom_call" | custom-call | tf_op jit(solution)/shard_map/share_early/pallas_call | solution.py:385
  (484 shorter events, 223.1 us)
Async XLA Ops:
  0.6 411.0 %copy-start = (bf16[8,16,2560]{2,1,0:T(8,128)(2,1)S(1)}, bf16[8,16,2560]{2,1,0:T(8,128)(2,1)}, u32[]{:S(2)}) copy-start(bf16[8,16,2560]{2,1,0:T(8,128)(2,1)} %param.53) | copy-start | bytes 1966084
  13.3 288.7 %collective-permute-start.5 = (bf16[320,1280]{1,0:T(8,128)(2,1)}, bf16[320,1280]{1,0:T(8,128)(2,1)}, u32[]{:S(2)}, u32[]{:S(2)}) collective-permute-start(bf16[320,1280]{1,0:T(8,128)(2,1)} %get-tuple-element.183), channel_id=1, source_target_pairs={{0,24},{4,28},{8,16},{12,20},{16,8},{20,12},{24,0},{28,4},{1,25},{... | collective-permute-start | bytes 2457608 | tf_op jit(solution)/shard_map/ppermute | solution.py:75
  18.3 283.7 %collective-permute-start.3 = (bf16[320,1280]{1,0:T(8,128)(2,1)}, bf16[320,1280]{1,0:T(8,128)(2,1)}, u32[]{:S(2)}, u32[]{:S(2)}) collective-permute-start(bf16[320,1280]{1,0:T(8,128)(2,1)} %get-tuple-element.183), channel_id=1, source_target_pairs={{0,8},{4,12},{8,0},{12,4},{16,24},{20,28},{24,16},{28,20},{1,9},{5... | collective-permute-start | bytes 2457608 | tf_op jit(solution)/shard_map/ppermute | solution.py:75
  19.8 245.9 %collective-permute-start.2 = (bf16[320,1152]{1,0:T(8,128)(2,1)}, bf16[320,1152]{1,0:T(8,128)(2,1)}, u32[]{:S(2)}, u32[]{:S(2)}) collective-permute-start(bf16[320,1152]{1,0:T(8,128)(2,1)} %get-tuple-element.187), channel_id=1, source_target_pairs={{0,24},{4,28},{8,16},{12,20},{16,8},{20,12},{24,0},{28,4},{1,25},{... | collective-permute-start | bytes 2211848 | tf_op jit(solution)/shard_map/ppermute | solution.py:75
  20.6 249.8 %collective-permute-start = (bf16[320,1152]{1,0:T(8,128)(2,1)}, bf16[320,1152]{1,0:T(8,128)(2,1)}, u32[]{:S(2)}, u32[]{:S(2)}) collective-permute-start(bf16[320,1152]{1,0:T(8,128)(2,1)} %get-tuple-element.187), channel_id=1, source_target_pairs={{0,8},{4,12},{8,0},{12,4},{16,24},{20,28},{24,16},{28,20},{1,9},{5... | collective-permute-start | bytes 2211848 | tf_op jit(solution)/shard_map/ppermute | solution.py:75
  21.8 280.3 %collective-permute-start.4 = (bf16[320,1280]{1,0:T(8,128)(2,1)}, bf16[320,1280]{1,0:T(8,128)(2,1)}, u32[]{:S(2)}, u32[]{:S(2)}) collective-permute-start(bf16[320,1280]{1,0:T(8,128)(2,1)} %get-tuple-element.184.refs_0_), channel_id=1, source_target_pairs={{0,16},{4,20},{8,24},{12,28},{16,0},{20,4},{24,8},{28,12},{1,17},{... | collective-permute-start | bytes 2457608 | tf_op jit(solution)/shard_map/ppermute | solution.py:75
  36.4 216.6 %copy-start.44 = (bf16[2,8,16,1600]{3,2,1,0:T(8,128)(2,1)S(1)}, bf16[2,8,16,1600]{3,2,1,0:T(8,128)(2,1)}, u32[]{:S(2)}) copy-start(bf16[2,8,16,1600]{3,2,1,0:T(8,128)(2,1)} %param.55) | copy-start | bytes 2457604
  39.0 217.9 %copy-start.15 = (bf16[1,256,2560]{2,1,0:T(8,128)(2,1)S(1)}, bf16[1,256,2560]{2,1,0:T(8,128)(2,1)}, u32[]{:S(2)}) copy-start(bf16[1,256,2560]{2,1,0:T(8,128)(2,1)} %param.29) | copy-start | bytes 3932164
  263.7 38.3 %copy-start.82 = (bf16[256,32]{0,1:T(8,128)(2,1)}, bf16[256,32]{0,1:T(8,128)(2,1)S(1)}, u32[]{:S(2)}) copy-start(bf16[256,32]{0,1:T(8,128)(2,1)S(1)} %convolution_convert_fusion.5) | copy-start | bytes 49156
  265.6 32.1 %collective-permute-start.1 = (bf16[320,1152]{1,0:T(8,128)(2,1)S(1)}, bf16[320,1152]{1,0:T(8,128)(2,1)S(1)}, u32[]{:S(2)}, u32[]{:S(2)}) collective-permute-start(bf16[320,1152]{1,0:T(8,128)(2,1)S(1)} %copy-done.29), channel_id=1, source_target_pairs={{0,16},{4,20},{8,24},{12,28},{16,0},{20,4},{24,8},{28,12},{1,17},{... | collective-permute-start | bytes 2211848 | tf_op jit(solution)/shard_map/ppermute | solution.py:75
  270.5 144.8 %copy-start.57 = (bf16[16,2560]{1,0:T(8,128)(2,1)}, bf16[16,2560]{1,0:T(8,128)(2,1)S(1)}, u32[]{:S(2)}) copy-start(bf16[16,2560]{1,0:T(8,128)(2,1)S(1)} %get-tuple-element.263) | copy-start | bytes 245764
  305.8 67.1 %collective-permute-start.6 = (bf16[4,320,1152]{2,1,0:T(8,128)(2,1)}, bf16[4,320,1152]{2,1,0:T(8,128)(2,1)}, u32[]{:S(2)}, u32[]{:S(2)}) collective-permute-start(bf16[4,320,1152]{2,1,0:T(8,128)(2,1)} %place_column_0.1.refs_1_), channel_id=1, source_target_pairs={{0,4},{4,0},{8,12},{12,8},{16,20},{20,16},{24,28},{28,24},{1,5},{5... | collective-permute-start | bytes 8847368 | tf_op jit(solution)/shard_map/ppermute | solution.py:75
  306.3 135.9 %collective-permute-start.7 = (bf16[4,320,1280]{2,1,0:T(8,128)(2,1)}, bf16[4,320,1280]{2,1,0:T(8,128)(2,1)}, u32[]{:S(2)}, u32[]{:S(2)}) collective-permute-start(bf16[4,320,1280]{2,1,0:T(8,128)(2,1)} %place_column_1.1.refs_1_), channel_id=1, source_target_pairs={{0,4},{4,0},{8,12},{12,8},{16,20},{20,16},{24,28},{28,24},{1,5},{5... | collective-permute-start | bytes 9830408 | tf_op jit(solution)/shard_map/ppermute | solution.py:75
  372.9 38.8 %copy-start.16 = (bf16[1,256,2560]{2,1,0:T(8,128)(2,1)S(1)}, bf16[1,256,2560]{2,1,0:T(8,128)(2,1)}, u32[]{:S(2)}) copy-start(bf16[1,256,2560]{2,1,0:T(8,128)(2,1)} %param.29) | copy-start | bytes 3932164
  571.1 61.1 %copy-start.58 = (bf16[16,2560]{1,0:T(8,128)(2,1)S(1)}, bf16[16,2560]{1,0:T(8,128)(2,1)}, u32[]{:S(2)}) copy-start(bf16[16,2560]{1,0:T(8,128)(2,1)} %copy-done.57) | copy-start | bytes 245764
  571.1 61.1 %copy-start.60 = (bf16[16,2560]{1,0:T(8,128)(2,1)S(1)}, bf16[16,2560]{1,0:T(8,128)(2,1)}, u32[]{:S(2)}) copy-start(bf16[16,2560]{1,0:T(8,128)(2,1)} %get-tuple-element.264) | copy-start | bytes 245764
  571.1 61.1 %copy-start.73 = (f32[2560]{0:T(1024)S(1)}, f32[2560]{0:T(1024)}, u32[]{:S(2)}) copy-start(f32[2560]{0:T(1024)} %param.36) | copy-start | bytes 30724
  688.6 70.7 %copy-start.65 = (bf16[128,640]{1,0:T(8,128)(2,1)}, bf16[128,640]{1,0:T(8,128)(2,1)S(1)}, u32[]{:S(2)}) copy-start(bf16[128,640]{1,0:T(8,128)(2,1)S(1)} %fusion.88) | copy-start | bytes 491524
  780.5 66.5 %collective-permute-start.8 = (bf16[1024,2688]{1,0:T(8,128)(2,1)}, bf16[1024,2688]{1,0:T(8,128)(2,1)}, u32[]{:S(2)}, u32[]{:S(2)}) collective-permute-start(bf16[1024,2688]{1,0:T(8,128)(2,1)} %add_convert_fusion), channel_id=1, source_target_pairs={{0,1},{1,0},{2,3},{3,2},{4,5},{5,4},{6,7},{7,6},{8,9},{9,8},{10,11... | collective-permute-start | bytes 16515080 | tf_op jit(solution)/shard_map/ppermute | solution.py:75
  782.5 42.7 %copy-start.6 = (bf16[2048,768]{1,0:T(8,128)(2,1)S(1)}, bf16[2048,768]{1,0:T(8,128)(2,1)}, u32[]{:S(2)}) copy-start(bf16[2048,768]{1,0:T(8,128)(2,1)} %get-tuple-element.71.refs_0_) | copy-start | bytes 9437188
  786.4 40.6 %slice-start.6 = ((f32[128,896]{1,0:T(8,128)}), f32[128,416]{1,0:T(8,128)S(1)}, s32[]{:S(2)}) async-start(f32[128,896]{1,0:T(8,128)} %copy-done.32), calls=%async_computation.6 | async-start | bytes 524288 | tf_op jit(solution)/shard_map/slice | solution.py:1290
  862.2 62.0 %collective-permute-start.9 = (bf16[2,256,2688]{2,1,0:T(8,128)(2,1)S(1)}, bf16[2,256,2688]{2,1,0:T(8,128)(2,1)S(1)}, u32[]{:S(2)}, u32[]{:S(2)}) collective-permute-start(bf16[2,256,2688]{2,1,0:T(8,128)(2,1)S(1)} %bitcast.243), channel_id=1, source_target_pairs={{0,8},{4,12},{8,0},{12,4},{16,24},{20,28},{24,16},{28,20},{1,9},{5... | collective-permute-start | bytes 8257544 | tf_op jit(solution)/shard_map/ppermute | solution.py:75
  877.1 47.2 %slice-start = ((f32[1024,2688]{1,0:T(8,128)}), f32[512,2688]{1,0:T(8,128)S(1)}, s32[]{:S(2)}) async-start(f32[1024,2688]{1,0:T(8,128)} %convert_add_fusion), calls=%async_computation | async-start | bytes 11010048 | tf_op jit(solution)/shard_map/slice | solution.py:1205
  928.3 31.9 %collective-permute-start.10 = (bf16[1,256,2688]{2,1,0:T(8,128)(2,1)}, bf16[1,256,2688]{2,1,0:T(8,128)(2,1)}, u32[]{:S(2)}, u32[]{:S(2)}) collective-permute-start(bf16[1,256,2688]{2,1,0:T(8,128)(2,1)} %slice.849), channel_id=1, source_target_pairs={{0,2},{1,3},{2,0},{3,1},{4,6},{5,7},{6,4},{7,5},{8,10},{9,11},{10,... | collective-permute-start | bytes 4128776 | tf_op jit(solution)/shard_map/ppermute | solution.py:75
  (107 other events, 725.5 us)

commit v3 on v2

--- a/solution.py
+++ b/solution.py
@@ -24,7 +24,7 @@
 SCORE_SCALE = 1.0 / math.sqrt(PLAIN_HEAD_DIM + ROTARY_DIM)
 EXP2_SCALE = SCORE_SCALE * math.log2(math.e)
 BIG = 1e30
-VMEM_LIMIT = 56 * 1024 * 1024
+VMEM_LIMIT = 60 * 1024 * 1024
 FREE = pl.CostEstimate(flops=0, bytes_accessed=0, transcendentals=0)
 F32 = jnp.float32
 BF16 = jnp.bfloat16
@@ -73,36 +73,6 @@
 
 def swap(value, axis, bit, size):
     return lax.ppermute(value, axis, [(i, i ^ bit) for i in range(size)])
-
-
-def place_pieces(sources, copies, outs, name):
-    def kernel(*refs):
-        src_refs = refs[: len(sources)]
-        out_refs = refs[len(sources) : len(sources) + len(outs)]
-        sems = refs[-1]
-        d = lax.axis_index("dp")
-        t = lax.axis_index("tensor")
-        started = []
-        for n, (src, src_at, out, out_at) in enumerate(copies):
-            src_ref = src_refs[src] if src_at is None else src_refs[src].at[src_at]
-            copy = pltpu.make_async_copy(src_ref, out_refs[out].at[out_at(d, t)], sems.at[n])
-            copy.start()
-            started.append(copy)
-        for copy in started:
-            copy.wait()
-
-    any_spec = pl.BlockSpec(memory_space=pl.ANY)
-    moved = sum(s.size * s.dtype.itemsize for s in sources)
-    return pl.pallas_call(
-        kernel,
-        out_shape=[jax.ShapeDtypeStruct(o, BF16) for o in outs],
-        in_specs=[any_spec] * len(sources),
-        out_specs=[pl.BlockSpec(memory_space=pltpu.VMEM)] * len(outs),
-        scratch_shapes=[pltpu.SemaphoreType.DMA((len(copies),))],
-        compiler_params=pltpu.CompilerParams(vmem_limit_bytes=VMEM_LIMIT),
-        cost_estimate=FREE,
-        name=name,
-    )(*sources)
 
 
 class Links:
@@ -125,7 +95,7 @@
             )
         pl.semaphore_wait(barrier, len(steps))
 
-    def send(self, src, dst, step):
+    def prepare(self, src, dst, step):
         n = len(self.copies)
         copy = pltpu.make_async_remote_copy(
             src_ref=src,
@@ -135,8 +105,12 @@
             device_id=self.peer(step),
             device_id_type=pl.DeviceIdType.MESH,
         )
-        copy.start()
         self.copies.append(copy)
+        return n
+
+    def send(self, src, dst, step):
+        n = self.prepare(src, dst, step)
+        self.copies[n].start()
         return n
 
     def arrived(self, n):
@@ -150,6 +124,88 @@
             copy.wait_send()
 
 
+class Riders:
+    def __init__(self, links, riders, in_refs, out_refs):
+        self.links = links
+        self.rounds = []
+        d = links.place["dp"]
+        for rider in riders:
+            full = out_refs[rider["out"]]
+            if rider["kind"] == "plain":
+                src = in_refs[rider["src"]]
+                if rider["src_at"] is not None:
+                    src = src.at[rider["src_at"]]
+                self.add(0, src, full, rider["step"])
+                continue
+            count, pair, high = rider["count"], rider["pair"], rider["high"]
+            if rider["kind"] == "one":
+                begin, size = rider["rows"]
+                here = full.at[pl.ds(pl.multiple_of(d * count + begin, 16), size)]
+                for name, bit in (("other", pair), ("mine", high), ("other", high ^ pair)):
+                    src = in_refs[rider[name]].at[pl.ds(begin, size)]
+                    self.add(0, src, here, ("dp", bit))
+            else:
+                held = [0]
+                for k, step in enumerate(rider["steps"]):
+                    for key in list(held):
+                        low = jnp.bitwise_xor(lax.rem(d, pair), key)
+                        at = pl.multiple_of((rider["z"] * pair + low) * count, 16)
+                        here = full.at[pl.ds(at, count)]
+                        self.add(k, here, here, step)
+                        held.append(key ^ step[1])
+
+    def add(self, k, src, dst, step):
+        while len(self.rounds) <= k:
+            self.rounds.append([])
+        self.rounds[k].append(self.links.prepare(src, dst, step))
+
+    def start(self):
+        if self.rounds:
+            for n in self.rounds[0]:
+                self.links.copies[n].start()
+
+    def finish(self):
+        for k, numbers in enumerate(self.rounds):
+            if k:
+                for n in numbers:
+                    self.links.copies[n].start()
+            for n in numbers:
+                self.links.arrived(n)
+
+
+def rider_steps(riders):
+    steps = []
+    for rider in riders:
+        if rider["kind"] == "plain":
+            steps.append(rider["step"])
+        elif rider["kind"] == "one":
+            pair, high = rider["pair"], rider["high"]
+            steps += [("dp", pair), ("dp", high), ("dp", high ^ pair)]
+        else:
+            steps += rider["steps"]
+    return steps
+
+
+def rider_count(riders):
+    total = 0
+    for rider in riders:
+        if rider["kind"] == "plain":
+            total += 1
+        elif rider["kind"] == "one":
+            total += 3
+        else:
+            total += (1 << len(rider["steps"])) - 1
+    return total
+
+
+def distinct(steps):
+    out = []
+    for step in steps:
+        if step not in out:
+            out.append(step)
+    return out
+
+
 def flip(key, step):
     return (key[0] ^ step[1], key[1]) if step[0] == "dp" else (key[0], key[1] ^ step[1])
 
@@ -162,7 +218,7 @@
     return sum((1 << len(job["steps"])) - 1 for job in jobs)
 
 
-def run_gathers(links, src_refs, out_refs, jobs):
+def run_gathers(links, src_refs, out_refs, jobs, between=None):
     d, t = links.place["dp"], links.place["tensor"]
 
     def landing(job, key):
@@ -187,50 +243,64 @@
                 n = links.send(src, landing(job, key), step)
                 new = flip(key, step)
                 held[new] = (landing(job, new), n)
+        if between is not None:
+            between(k)
     return [landing(job, (0, 0)) for job in jobs]
 
 
-def remote_gather(sources, jobs, extra, outs, name, collective_id):
-    steps = []
-    for job in jobs:
-        steps += [s for s in job["steps"] if s not in steps]
-    count = gather_count(jobs)
+def remote_gather(
+    sources, jobs, extra, outs, name, collective_id, riders=(), aliases=(), distant=(), rider_round=0
+):
+    steps = distinct([s for job in jobs for s in job["steps"]] + rider_steps(riders))
+    count = gather_count(jobs) + rider_count(riders)
+    aliases = dict(aliases)
 
     def kernel(*refs):
         src_refs = refs[: len(sources)]
         out_refs = refs[len(sources) : len(sources) + len(outs)]
         send_sems, recv_sems, local_sems = refs[len(sources) + len(outs) :]
         links = Links(send_sems, recv_sems)
+        d, t = links.place["dp"], links.place["tensor"]
         links.greet(steps)
-        own = run_gathers(links, src_refs, out_refs, jobs)
+        ride = Riders(links, riders, src_refs, out_refs)
         local = []
-        for job, where in zip(jobs, own):
+        for job in jobs:
             src = src_refs[job["src"]]
             if job.get("src_at") is not None:
                 src = src.at[job["src_at"]]
-            local.append((src, where))
+            local.append((src, out_refs[job["out"]].at[job["out_at"](d, t)]))
         for src, out, at in extra:
-            local.append((src_refs[src], out_refs[out].at[at]))
+            local.append((src_refs[src], out_refs[out].at[at(d, t)]))
         started = []
         for n, (src, where) in enumerate(local):
             copy = pltpu.make_async_copy(src, where, local_sems.at[n])
             copy.start()
             started.append(copy)
+
+        def between(k):
+            if k == rider_round:
+                ride.start()
+
+        run_gathers(links, src_refs, out_refs, jobs, between)
+        ride.finish()
         links.close()
         for copy in started:
             copy.wait()
 
-    moved = sum(s.size * s.dtype.itemsize for s in sources)
     return pl.pallas_call(
         kernel,
         out_shape=[jax.ShapeDtypeStruct(o, BF16) for o in outs],
-        in_specs=[pl.BlockSpec(memory_space=pltpu.VMEM)] * len(sources),
+        in_specs=[
+            pl.BlockSpec(memory_space=pl.ANY if n in aliases or n in distant else pltpu.VMEM)
+            for n in range(len(sources))
+        ],
         out_specs=[pl.BlockSpec(memory_space=pl.ANY)] * len(outs),
         scratch_shapes=[
             pltpu.SemaphoreType.DMA((count,)),
             pltpu.SemaphoreType.DMA((count,)),
             pltpu.SemaphoreType.DMA((len(jobs) + len(extra),)),
         ],
+        input_output_aliases=aliases,
         compiler_params=pltpu.CompilerParams(
             collective_id=collective_id, has_side_effects=True, vmem_limit_bytes=VMEM_LIMIT
         ),
@@ -249,20 +319,26 @@
     return plan
 
 
-def remote_reduce(operands, fetched, term, keys, ways, rows, wide, name, collective_id, flops):
+def remote_reduce(
+    operands, fetched, term, keys, ways, rows, wide, name, collective_id, riders=(), ridden=(), carried=()
+):
     core_step = ("tensor", 1)
     part = rows // len(ways)
     plan = reduce_plan(keys, ways)
     slot = {entry: n for n, entry in enumerate(plan)}
-    steps = [core_step] + [s for s in ways[0]]
-    count = len(keys) + len(plan)
+    steps = distinct([core_step] + [s for s in ways[0]] + rider_steps(riders))
+    count = len(keys) + len(plan) + rider_count(riders)
     n_in = len(operands)
+    n_all = n_in + len(ridden) + len(carried)
 
     def kernel(*refs):
         in_refs = refs[:n_in]
-        out_ref = refs[n_in]
-        held = refs[n_in + 1 : 2 * n_in + 1]
-        core_out, core_in, chip, hop_out, hop_in, send_sems, recv_sems, in_sems = refs[2 * n_in + 1 :]
+        out_ref = refs[n_all]
+        ride_in = refs[n_in:n_all]
+        ride_out = refs[n_all + 1 : n_all + 1 + len(ridden)]
+        scratch = refs[n_all + 1 + len(ridden) :]
+        held = scratch[:n_in]
+        core_out, core_in, chip, hop_out, hop_in, send_sems, recv_sems, in_sems = scratch[n_in:]
         started = []
         for n in range(n_in):
             shape = fetched[n]
@@ -272,6 +348,8 @@
             started.append(copy)
         links = Links(send_sems, recv_sems)
         links.greet(steps)
+        ride = Riders(links, riders, ride_in, ride_out)
+        ride.start()
         for copy in started:
             copy.wait()
         came = {}
@@ -306,13 +384,17 @@
                         send_part(w, k, entry[2])
         for w in range(len(ways)):
             out_ref[w * part : (w + 1) * part, :] = so_far(w, len(ways[w]), (0, 0))
+        ride.finish()
         links.close()
 
+    any_spec = pl.BlockSpec(memory_space=pl.ANY)
     return pl.pallas_call(
         kernel,
-        out_shape=jax.ShapeDtypeStruct((rows, wide), F32),
-        in_specs=[pl.BlockSpec(memory_space=pl.ANY)] * n_in,
-        out_specs=pl.BlockSpec(memory_space=pltpu.VMEM),
+        out_shape=[jax.ShapeDtypeStruct((rows, wide), F32)]
+        + [jax.ShapeDtypeStruct(r.shape, r.dtype) for r in ridden],
+        in_specs=[any_spec] * n_all,
+        out_specs=[pl.BlockSpec(memory_space=pltpu.VMEM)] + [any_spec] * len(ridden),
+        input_output_aliases={n_in + n: 1 + n for n in range(len(ridden))},
         scratch_shapes=[pltpu.VMEM(s, o.dtype) for s, o in zip(fetched, operands)]
         + [
             pltpu.VMEM((len(keys), rows, wide), BF16),
@@ -329,7 +411,7 @@
         ),
         cost_estimate=FREE,
         name=name,
-    )(*operands)
+    )(*operands, *ridden, *carried)
 
 
 def remote_share(terms, parts, jobs_of, outs, n_t, t_steps, steps, name, collective_id):
@@ -536,17 +618,68 @@
         dpe_ref[...] += jnp.where(upper & (lane < 96), dk_all, 0.0)
 
 
-def attend(latents, w_q, w_kv, rope, pe_aug, doc_q, q_width, kv_at):
+def ridden_call(
+    kernel, grid, arrays, in_specs, out_shape, out_specs, scratch, riders, ridden, carried, fresh, name, collective_id
+):
+    steps = distinct(rider_steps(riders))
+    count = rider_count(riders)
+    n_in, n_out = len(arrays), len(out_shape)
+    n_ride_in = len(ridden) + len(carried)
+    n_ride_out = len(ridden) + len(fresh)
+
+    def body(*refs):
+        own_in, rest = refs[:n_in], refs[n_in:]
+        ride_in, rest = rest[:n_ride_in], rest[n_ride_in:]
+        own_out, rest = rest[:n_out], rest[n_out:]
+        ride_out, rest = rest[:n_ride_out], rest[n_ride_out:]
+        send_sems, recv_sems = rest[-2:]
+        own_scratch = rest[:-2]
+        links = Links(send_sems, recv_sems)
+        ride = Riders(links, riders, ride_in, ride_out)
+
+        @pl.when(pl.program_id(0) == 0)
+        def _():
+            links.greet(steps)
+            ride.start()
+
+        kernel(*own_in, *own_out, *own_scratch)
+
+        @pl.when(pl.program_id(0) == grid[0] - 1)
+        def _():
+            ride.finish()
+            links.close()
+
+    any_spec = pl.BlockSpec(memory_space=pl.ANY)
+    return pl.pallas_call(
+        body,
+        grid=grid,
+        in_specs=list(in_specs) + [any_spec] * n_ride_in,
+        out_specs=list(out_specs) + [any_spec] * n_ride_out,
+        out_shape=list(out_shape)
+        + [jax.ShapeDtypeStruct(r.shape, r.dtype) for r in ridden]
+        + [jax.ShapeDtypeStruct(f, BF16) for f in fresh],
+        scratch_shapes=list(scratch)
+        + [pltpu.SemaphoreType.DMA((count,)), pltpu.SemaphoreType.DMA((count,))],
+        input_output_aliases={n_in + n: n_out + n for n in range(len(ridden))},
+        compiler_params=pltpu.CompilerParams(
+            collective_id=collective_id, has_side_effects=True, vmem_limit_bytes=VMEM_LIMIT
+        ),
+        cost_estimate=FREE,
+        name=name,
+    )(*arrays, *ridden, *carried)
+
+
+def attend(latents, w_q, w_kv, rope, pe_aug, doc_q, q_width, kv_at, riders, ridden, carried):
     length = latents.shape[0]
     heads = w_q.shape[1] // HEAD_LANES
     per_step = 2 if heads % 2 == 0 else 1
     wide = per_step * HEAD_LANES
     whole = lambda a: pl.BlockSpec(a.shape, lambda h: (0,) * a.ndim)
-    flops = heads * length * (2 * q_width * 256 + length * 2 * 256)
-    return pl.pallas_call(
+    return ridden_call(
         functools.partial(attn_fwd_kernel, per_step, q_width, kv_at),
-        grid=(heads // per_step,),
-        in_specs=[
+        (heads // per_step,),
+        [latents, w_q, w_kv, rope, pe_aug, doc_q],
+        [
             whole(latents),
             pl.BlockSpec((w_q.shape[0], wide), lambda h: (0, h)),
             pl.BlockSpec((w_kv.shape[0], wide), lambda h: (0, h)),
@@ -554,23 +687,27 @@
             whole(pe_aug),
             whole(doc_q),
         ],
-        out_specs=[
+        [
+            jax.ShapeDtypeStruct((length, heads * HEAD_LANES), BF16),
+            jax.ShapeDtypeStruct((length, heads * HEAD_LANES), BF16),
+            jax.ShapeDtypeStruct((length, heads * VALUE_HEAD_DIM), BF16),
+        ],
+        [
             pl.BlockSpec((length, wide), lambda h: (0, h)),
             pl.BlockSpec((length, wide), lambda h: (0, h)),
             pl.BlockSpec((length, HEAD_LANES), lambda h: (0, h * per_step // 2)),
         ],
-        out_shape=[
-            jax.ShapeDtypeStruct((length, heads * HEAD_LANES), BF16),
-            jax.ShapeDtypeStruct((length, heads * HEAD_LANES), BF16),
-            jax.ShapeDtypeStruct((length, heads * VALUE_HEAD_DIM), BF16),
-        ],
-        compiler_params=pltpu.CompilerParams(vmem_limit_bytes=VMEM_LIMIT),
-        cost_estimate=FREE,
-        name="attend",
-    )(latents, w_q, w_kv, rope, pe_aug, doc_q)
-
-
-def attend_back(q_aug, kv, heads_out, heads_grad, rope, pe_aug):
+        [],
+        riders,
+        ridden,
+        carried,
+        [],
+        "attend",
+        10,
+    )
+
+
+def attend_back(q_aug, kv, heads_out, heads_grad, rope, pe_aug, riders, carried, fresh):
     length = q_aug.shape[0]
     heads = q_aug.shape[1] // HEAD_LANES
     per_step = 2 if heads % 2 == 0 else 1
@@ -578,80 +715,398 @@
     whole = lambda a: pl.BlockSpec(a.shape, lambda h: (0,) * a.ndim)
     columns = pl.BlockSpec((length, wide), lambda h: (0, h))
     packed = pl.BlockSpec((length, HEAD_LANES), lambda h: (0, h * per_step // 2))
+    arrays = [q_aug, kv, heads_out, heads_grad, rope, pe_aug]
+    in_specs = [columns, columns, packed, packed, whole(rope), whole(pe_aug)]
+    out_shape = [
+        jax.ShapeDtypeStruct((length, heads * HEAD_LANES), BF16),
+        jax.ShapeDtypeStruct((length, heads * HEAD_LANES), BF16),
+        jax.ShapeDtypeStruct((length, HEAD_LANES), F32),
+    ]
+    out_specs = [columns, columns, pl.BlockSpec((length, HEAD_LANES), lambda h: (0, 0))]
+    scratch = [pltpu.VMEM((length, HEAD_LANES), F32), pltpu.VMEM((length, HEAD_LANES), F32)]
+    kernel = functools.partial(attn_bwd_kernel, per_step)
+    grid = (heads // per_step,)
+    if riders:
+        return ridden_call(
+            kernel, grid, arrays, in_specs, out_shape, out_specs, scratch, riders, [], carried, fresh, "attend_back", 11
+        )
     return pl.pallas_call(
-        functools.partial(attn_bwd_kernel, per_step),
-        grid=(heads // per_step,),
-        in_specs=[columns, columns, packed, packed, whole(rope), whole(pe_aug)],
-        out_specs=[columns, columns, pl.BlockSpec((length, HEAD_LANES), lambda h: (0, 0))],
-        out_shape=[
-            jax.ShapeDtypeStruct((length, heads * HEAD_LANES), BF16),
-            jax.ShapeDtypeStruct((length, heads * HEAD_LANES), BF16),
-            jax.ShapeDtypeStruct((length, HEAD_LANES), F32),
-        ],
-        scratch_shapes=[
-            pltpu.VMEM((length, HEAD_LANES), F32),
-            pltpu.VMEM((length, HEAD_LANES), F32),
-        ],
+        kernel,
+        grid=grid,
+        in_specs=in_specs,
+        out_specs=out_specs,
+        out_shape=out_shape,
+        scratch_shapes=scratch,
         compiler_params=pltpu.CompilerParams(vmem_limit_bytes=VMEM_LIMIT),
         cost_estimate=FREE,
         name="attend_back",
-    )(q_aug, kv, heads_out, heads_grad, rope, pe_aug)
-
-
-def ffn_kernel(main, tail, tail_wide, x_ref, g_ref, w_ref, grad_ref, hid_ref):
-    gu_wide = 2 * main + tail_wide
-    pre = dot_nn(x_ref[...], w_ref[:, :gu_wide])
-    back = dot_nn(g_ref[...], w_ref[:, gu_wide:])
-
-    def middle(gate, up, hid_grad):
-        sig = 1.0 / (1.0 + jnp.exp(-gate))
-        silu = gate * sig
-        gate_grad = hid_grad * up * (sig * (1.0 + gate * (1.0 - sig)))
-        return silu * up, gate_grad, hid_grad * silu
-
-    hid, gate_grad, up_grad = middle(pre[:, :main], pre[:, main + tail_wide :], back)
-    hid_ref[:, :main] = narrow(hid)
-    grad_ref[:, :main] = narrow(gate_grad)
-    grad_ref[:, main + tail_wide :] = narrow(up_grad)
-    if tail_wide:
-        pre_tail = pre[:, main : main + tail_wide]
-        back_tail = dot_nn(g_ref[...], w_ref[:, main : main + tail_wide])
-        up_tail = pltpu.roll(pre_tail, tail_wide - tail, 1)
-        hid_tail = pltpu.roll(back_tail, tail_wide - 2 * tail, 1)
-        hid, gate_grad, up_grad = middle(pre_tail, up_tail, hid_tail)
-        lane = lax.broadcasted_iota(jnp.int32, pre_tail.shape, 1)
-        hid = pltpu.roll(hid, 2 * tail, 1)
-        hid = jnp.where((lane >= 2 * tail) & (lane < 3 * tail), hid, 0.0)
-        hid_ref[:, main:] = narrow(hid)
-        up_grad = pltpu.roll(up_grad, tail, 1)
-        both = jnp.where(lane < tail, gate_grad, jnp.where(lane < 2 * tail, up_grad, 0.0))
-        grad_ref[:, main : main + tail_wide] = narrow(both)
-
-
-def ffn_middle(x_rows, g_rows, weight, main, tail, tail_wide):
-    rows, depth = x_rows.shape
-    block = 256
-    width = weight.shape[1]
+    )(*arrays)
+
+
+def gate_middle(gate, up, hid_grad):
+    sig = 1.0 / (1.0 + jnp.exp(-gate))
+    silu = gate * sig
+    gate_grad = hid_grad * up * (sig * (1.0 + gate * (1.0 - sig)))
+    return silu * up, gate_grad, hid_grad * silu
+
+
+def tail_middle(pre, back, tail):
+    wide = pre.shape[1]
+    up = pltpu.roll(pre, wide - tail, 1)
+    hid_grad = pltpu.roll(back, wide - 2 * tail, 1)
+    hid, gate_grad, up_grad = gate_middle(pre, up, hid_grad)
+    lane = lax.broadcasted_iota(jnp.int32, pre.shape, 1)
+    hid = jnp.where((lane >= 2 * tail) & (lane < 3 * tail), pltpu.roll(hid, 2 * tail, 1), 0.0)
+    both = jnp.where(
+        lane < tail, gate_grad, jnp.where(lane < 2 * tail, pltpu.roll(up_grad, tail, 1), 0.0)
+    )
+    return hid, both
+
+
+def remote_ffn(x_own, g_all, weights, mains, tail, tail_wide, slow, block_of, riders, name, collective_id):
+    rows, aug = x_own.shape
+    total = g_all.shape[0]
+    blocks = total // rows
+    width = aug - CODE_LANES
+    chunks = len(mains)
+    tails = [0] * (chunks - 1) + [tail_wide]
+    gu = [2 * m + w for m, w in zip(mains, tails)]
+    core_step = ("tensor", 1)
+    keys = [(0, 0)]
+    for step in slow:
+        keys += [flip(key, step) for key in keys]
+    bits_of = {key: [s for s in slow if has_bit(key, s)] for key in keys}
+    keys.sort(key=lambda k: len(bits_of[k]))
+
+    def part_rows(key, step):
+        n = len(bits_of[key])
+        i = bits_of[key].index(step)
+        size = -(-rows // (16 * n)) * 16
+        begin = i * size
+        return begin, min(size, rows - begin)
+
+    count = len(keys) + sum(len(bits_of[k]) for k in keys) + rider_count(riders)
+    steps = distinct([core_step] + slow + rider_steps(riders))
+
+    def kernel(x_ref, g_ref, *refs):
+        refs = refs[chunks:]
+        codes_ref = refs[0]
+        grad_refs = refs[1 : 1 + chunks]
+        hid_refs = refs[1 + chunks : 1 + 2 * chunks]
+        w_refs = refs[1 + 2 * chunks : 1 + 3 * chunks]
+        x_held, back_held, g_held = refs[1 + 3 * chunks : 4 + 3 * chunks]
+        w_held = refs[4 + 3 * chunks : 4 + 4 * chunks]
+        send_sems, recv_sems, w_sems, g_sems = refs[4 + 4 * chunks :]
+        links = Links(send_sems, recv_sems)
+        place = links.place
+        fetch = [
+            pltpu.make_async_copy(w_refs[c], w_held[c], w_sems.at[c]) for c in range(chunks)
+        ]
+        fetch[0].start()
+        links.greet(steps)
+
+        def landing(key):
+            return x_held.at[block_of(key, place)]
+
+        arrivals = {key: [] for key in keys}
+
+        def pass_on(key, src):
+            for step in slow:
+                if has_bit(key, step):
+                    continue
+                there = flip(key, step)
+                begin, size = part_rows(there, step)
+                at = pl.ds(begin, size)
+                n = links.send(src.at[at], landing(key).at[at], step)
+                arrivals[there].append(n)
+
+        crossing = {}
+        pass_on((0, 0), x_ref)
+        crossing[(0, 0)] = links.send(x_ref, landing((0, 0)), core_step)
+        ride = Riders(links, riders, w_refs, w_refs)
+        ride.start()
+        x_held[block_of((0, 0), place)] = x_ref[...]
+
+        def g_copy(b, slot):
+            at = pl.ds(pl.multiple_of(b * rows, 16), rows)
+            return pltpu.make_async_copy(g_ref.at[at], g_held.at[slot], g_sems.at[slot])
+
+        def over_blocks(work):
+            g_copy(0, 0).start()
+
+            def one(b, carry):
+                slot = lax.rem(b, 2)
+
+                @pl.when(b + 1 < blocks)
+                def _():
+                    g_copy(b + 1, 1 - slot).start()
+
+                g_copy(b, slot).wait()
+                work(b, g_held[slot])
+                return carry
+
+            lax.fori_loop(0, blocks, one, 0)
+
+        fetch[0].wait()
+
+        def back_first(b, g_rows):
+            back_held[b] = dot_nn(g_rows, w_held[0][:, gu[0] :])
+
+        over_blocks(back_first)
+
+        def rows_at(b):
+            return pl.ds(pl.multiple_of(b * rows, 16), rows)
+
+        def forward(b, c, back):
+            main = mains[c]
+            x_rows = x_held[b]
+            pre = dot_nn(x_rows, w_held[c][:, : gu[c]])
+            hid, gate_grad, up_grad = gate_middle(pre[:, :main], pre[:, gu[c] - main :], back)
+            at = rows_at(b)
+            hid_refs[c][at, :main] = narrow(hid)
+            grad_refs[c][at, :main] = narrow(gate_grad)
+            grad_refs[c][at, gu[c] - main :] = narrow(up_grad)
+            return pre
+
+        def first_chunk(key):
+            def one(i, carry):
+                other = (key[0], key[1] + i)
+                b = block_of(other, place)
+                forward(b, 0, back_held[b])
+                return carry
+
+            lax.fori_loop(0, 2, one, 0)
+
+        links.arrived(crossing[(0, 0)])
+        first_chunk((0, 0))
+        for level in range(1, len(slow) + 1):
+            here = [key for key in keys if len(bits_of[key]) == level]
+            for key in here:
+                for n in arrivals[key]:
+                    links.arrived(n)
+                pass_on(key, landing(key))
+                crossing[key] = links.send(landing(key), landing(key), core_step)
+            for key in here:
+                links.arrived(crossing[key])
+                first_chunk(key)
+        ride.finish()
+        for c in range(1, chunks):
+            fetch[c].start()
+            fetch[c].wait()
+
+            def later(b, g_rows, c=c):
+                main = mains[c]
+                back = dot_nn(g_rows, w_held[c][:, gu[c] :])
+                pre = forward(b, c, back)
+                if tails[c]:
+                    at_tail = slice(main, main + tail_wide)
+                    hid, both = tail_middle(
+                        pre[:, at_tail], dot_nn(g_rows, w_held[c][:, at_tail]), tail
+                    )
+                    at = rows_at(b)
+                    hid_refs[c][at, main:] = narrow(hid)
+                    grad_refs[c][at, at_tail] = narrow(both)
+
+            over_blocks(later)
+        for b in range(blocks):
+            codes_ref[b * rows : (b + 1) * rows, :] = x_held[b, :, width:]
+        links.close()
+
+    any_spec = pl.BlockSpec(memory_space=pl.ANY)
+    vmem_spec = pl.BlockSpec(memory_space=pltpu.VMEM)
+    outs = pl.pallas_call(
+        kernel,
+        in_specs=[vmem_spec, any_spec] + [any_spec] * chunks,
+        out_specs=[vmem_spec] * (1 + 2 * chunks) + [any_spec] * chunks,
+        out_shape=[jax.ShapeDtypeStruct((total, CODE_LANES), BF16)]
+        + [jax.ShapeDtypeStruct((total, g), BF16) for g in gu]
+        + [jax.ShapeDtypeStruct((total, m + w), BF16) for m, w in zip(mains, tails)]
+        + [jax.ShapeDtypeStruct(w.shape, BF16) for w in weights],
+        scratch_shapes=[
+            pltpu.VMEM((blocks, rows, aug), BF16),
+            pltpu.VMEM((blocks, rows, mains[0]), F32),
+            pltpu.VMEM((2, rows, aug), BF16),
+        ]
+        + [pltpu.VMEM(w.shape, BF16) for w in weights]
+        + [
+            pltpu.SemaphoreType.DMA((count,)),
+            pltpu.SemaphoreType.DMA((count,)),
+            pltpu.SemaphoreType.DMA((chunks,)),
+            pltpu.SemaphoreType.DMA((2,)),
+        ],
+        input_output_aliases={2 + c: 1 + 2 * chunks + c for c in range(chunks)},
+        compiler_params=pltpu.CompilerParams(
+            collective_id=collective_id, has_side_effects=True, vmem_limit_bytes=VMEM_LIMIT
+        ),
+        cost_estimate=FREE,
+        name=name,
+    )(x_own, g_all, *weights)
+    return (
+        outs[0],
+        outs[1 : 1 + chunks],
+        outs[1 + chunks : 1 + 2 * chunks],
+        outs[1 + 2 * chunks :],
+    )
+
+
+def remote_ffn_back(grads, hids, weights, mains, tail_wide, keys, ways, block_of, rows, name, collective_id):
+    aug = weights[0].shape[0]
+    chunks = len(mains)
+    tails = [0] * (chunks - 1) + [tail_wide]
+    gu = [2 * m + w for m, w in zip(mains, tails)]
+    core_step = ("tensor", 1)
+    part = rows // len(ways)
+    plan = reduce_plan(keys, ways)
+    later = [entry for entry in plan if entry[1] > 0]
+    slot = {entry: n for n, entry in enumerate(plan)}
+    later_slot = {entry: n for n, entry in enumerate(later)}
+    steps = distinct([core_step] + ways[0])
+    count = 2 * len(keys) + len(plan)
+    operands = list(grads) + list(hids) + list(weights)
+
+    def kernel(*refs):
+        n_in = len(operands)
+        in_refs = refs[:n_in]
+        out_ref, terms_ref = refs[n_in : n_in + 2]
+        held = refs[n_in + 2 : 2 * n_in + 2]
+        rest = refs[2 * n_in + 2 :]
+        core_out, core_in, chip, hop_out, hop_in, stage, send_sems, recv_sems, in_sems, out_sems, free = rest
+        g_held, h_held, w_held = held[:chunks], held[chunks : 2 * chunks], held[2 * chunks :]
+        started = []
+        order = [n for c in range(chunks) for n in (c, 2 * chunks + c)] + list(range(chunks, 2 * chunks))
+        for n in order:
+            copy = pltpu.make_async_copy(in_refs[n], held[n], in_sems.at[n])
+            copy.start()
+            started.append(copy)
+        links = Links(send_sems, recv_sems)
+        place = links.place
+        links.greet(steps)
+        for copy in started:
+            copy.wait()
+        came = {}
+
+        def rows_of(key):
+            return pl.ds(pl.multiple_of(block_of(key, place) * rows, 16), rows)
+
+        def in_term(key):
+            at = rows_of(key)
+            out = dot_nt(g_held[0][at, :], w_held[0][:, : gu[0]])
+            for c in range(1, chunks):
+                out = out + dot_nt(g_held[c][at, :], w_held[c][:, : gu[c]])
+            return out
+
+        def down_term(key):
+            at = rows_of(key)
+            out = 0.0
+            for c in range(chunks):
+                out = out + dot_nt(h_held[c][at, : mains[c]], w_held[c][:, gu[c] :])
+                if tails[c]:
+                    out = out + dot_nt(
+                        h_held[c][at, mains[c] :], w_held[c][:, mains[c] : mains[c] + tails[c]]
+                    )
+            return out
+
+        def so_far(w, k, key):
+            if key == (0, 0):
+                total = out_ref[w * part : (w + 1) * part, :]
+            else:
+                total = chip[keys.index(key), w * part : (w + 1) * part, :].astype(F32)
+            for j in range(k):
+                entry = (w, j, flip(key, ways[w][j]))
+                links.arrived(came[entry])
+                total = total + hop_in[slot[entry]].astype(F32)
+            return total
+
+        crossings = []
+
+        def cross(i, value):
+            n = len(crossings)
+            if n >= 2:
+                links.copies[crossings[n - 2]].wait_send()
+            core_out[n % 2] = narrow(value)
+            crossings.append(links.send(core_out.at[n % 2], core_in.at[i], core_step))
+            return crossings[-1]
+
+        for i, key in enumerate(keys):
+            crossing = cross(i, in_term((key[0], key[1] ^ 1)))
+            mine = in_term(key)
+            links.arrived(crossing)
+            mine = mine + core_in[i].astype(F32)
+            if key == (0, 0):
+                out_ref[...] = mine
+            else:
+                chip[i] = narrow(mine)
+                for w, way in enumerate(ways):
+                    if has_bit(key, way[0]):
+                        at = slice(w * part, (w + 1) * part)
+                        entry = (w, 0, key)
+                        came[entry] = links.send(
+                            chip.at[i, pl.ds(w * part, part)], hop_in.at[slot[entry]], way[0]
+                        )
+        pl.semaphore_signal(
+            free, inc=1, device_id=links.peer(core_step), device_id_type=pl.DeviceIdType.MESH
+        )
+        pl.semaphore_wait(free, 1)
+        stored = []
+        for i, key in enumerate(keys):
+            crossing = cross(i, down_term((key[0], key[1] ^ 1)))
+            mine = down_term(key)
+            links.arrived(crossing)
+            if i >= 2:
+                stored[i - 2].wait()
+            stage[i % 2] = narrow(mine + core_in[i].astype(F32))
+            copy = pltpu.make_async_copy(stage.at[i % 2], terms_ref.at[i], out_sems.at[i])
+            copy.start()
+            stored.append(copy)
+            if i == len(keys) // 2 - 1:
+                for k in range(1, len(ways[0])):
+                    for w in range(len(ways)):
+                        for entry in plan:
+                            if entry[0] == w and entry[1] == k:
+                                hop_out[later_slot[entry]] = narrow(so_far(w, k, entry[2]))
+                                came[entry] = links.send(
+                                    hop_out.at[later_slot[entry]],
+                                    hop_in.at[slot[entry]],
+                                    ways[w][k],
+                                )
+        for w in range(len(ways)):
+            out_ref[w * part : (w + 1) * part, :] = so_far(w, len(ways[w]), (0, 0))
+        for copy in stored[max(0, len(keys) - 2) :]:
+            copy.wait()
+        for n, copy in enumerate(links.copies):
+            links.arrived(n)
+            if n not in crossings[:-2]:
+                copy.wait_send()
+
+    any_spec = pl.BlockSpec(memory_space=pl.ANY)
     return pl.pallas_call(
-        functools.partial(ffn_kernel, main, tail, tail_wide),
-        grid=(rows // block,),
-        in_specs=[
-            pl.BlockSpec((block, depth), lambda i: (i, 0)),
-            pl.BlockSpec((block, depth), lambda i: (i, 0)),
-            pl.BlockSpec((depth, width), lambda i: (0, 0)),
+        kernel,
+        out_shape=[
+            jax.ShapeDtypeStruct((rows, aug), F32),
+            jax.ShapeDtypeStruct((len(keys), rows, aug), BF16),
         ],
-        out_specs=[
-            pl.BlockSpec((block, 2 * main + tail_wide), lambda i: (i, 0)),
-            pl.BlockSpec((block, main + tail_wide), lambda i: (i, 0)),
+        in_specs=[any_spec] * len(operands),
+        out_specs=[pl.BlockSpec(memory_space=pltpu.VMEM), any_spec],
+        scratch_shapes=[pltpu.VMEM(o.shape, o.dtype) for o in operands]
+        + [
+            pltpu.VMEM((2, rows, aug), BF16),
+            pltpu.VMEM((len(keys), rows, aug), BF16),
+            pltpu.VMEM((len(keys) - 1, rows, aug), BF16),
+            pltpu.VMEM((max(len(later), 1), part, aug), BF16),
+            pltpu.VMEM((len(plan), part, aug), BF16),
+            pltpu.VMEM((2, rows, aug), BF16),
+            pltpu.SemaphoreType.DMA((count,)),
+            pltpu.SemaphoreType.DMA((count,)),
+            pltpu.SemaphoreType.DMA((len(operands),)),
+            pltpu.SemaphoreType.DMA((len(keys),)),
+            pltpu.SemaphoreType.REGULAR,
         ],
-        out_shape=[
-            jax.ShapeDtypeStruct((rows, 2 * main + tail_wide), BF16),
-            jax.ShapeDtypeStruct((rows, main + tail_wide), BF16),
-        ],
-        compiler_params=pltpu.CompilerParams(vmem_limit_bytes=VMEM_LIMIT),
+        compiler_params=pltpu.CompilerParams(
+            collective_id=collective_id, has_side_effects=True, vmem_limit_bytes=VMEM_LIMIT
+        ),
         cost_estimate=FREE,
-        name="ffn_middle",
-    )(x_rows, g_rows, weight)
+        name=name,
+    )(*operands)
 
 
 def per_device(
@@ -739,6 +1194,66 @@
     )
     down_out = pick(down_adapter_out, set_own)
 
+    hidden = down_matrix.shape[0]
+    half = hidden // 2
+    tiles = half // 128
+    main = tiles * 128
+    tail = half - main
+    tail_wide = -(-3 * tail // 128) * 128
+    first_tiles = (2 * tiles + 2) // 3
+    mains = [first_tiles * 128, main - first_tiles * 128]
+    chunks = len(mains)
+    tails = [0] * (chunks - 1) + [tail_wide]
+    gu_wide = [2 * m + w for m, w in zip(mains, tails)]
+
+    def columns(gate_part, up_part, down_part, chunk):
+        begin = sum(mains[:chunk])
+        at = slice(begin, begin + mains[chunk])
+        out = [gate_part[:, at]]
+        if tail and chunk == chunks - 1:
+            out += [gate_part[:, main:], up_part[:, main:], down_part[:, main:]]
+            if tail_wide > 3 * tail:
+                out.append(jnp.zeros((gate_part.shape[0], tail_wide - 3 * tail), BF16))
+        out += [up_part[:, at], down_part[:, at]]
+        return jnp.concatenate(out, axis=1)
+
+    def halves(value):
+        return value[:, :half], value[:, half:]
+
+    mats = [halves(gate_up_matrix[0]), halves(gate_up_matrix[1]), halves(down_matrix.T)]
+    ffn_mine, ffn_other = [], []
+    for chunk in range(chunks):
+        left = columns(mats[0][0], mats[1][0], mats[2][0], chunk)
+        right = columns(mats[0][1], mats[1][1], mats[2][1], chunk)
+        ffn_mine.append(jnp.where(first, left, right))
+        ffn_other.append(jnp.where(first, right, left))
+    ffn_rows_each = gate_up_matrix.shape[1]
+    z_count = n_dp // pair
+    ffn_wide = [m.shape[1] for m in ffn_mine]
+
+    def ride_one(out, mine, other, begin, size):
+        return dict(
+            kind="one",
+            out=out,
+            mine=mine,
+            other=other,
+            rows=(begin, size),
+            count=ffn_rows_each,
+            pair=pair,
+            high=high,
+        )
+
+    def ride_two(out, z):
+        return dict(
+            kind="two",
+            out=out,
+            z=z,
+            count=ffn_rows_each,
+            pair=pair,
+            high=high,
+            steps=[("dp", b) for b in reversed(low_bits)],
+        )
+
     def code_lanes(codes):
         none = jnp.zeros_like(codes)
         return jnp.concatenate(
@@ -763,12 +1278,12 @@
     )
 
     down_shard = query_down_matrix.shape[0]
-    core_rows = down_shard // 2
+    shares = n_t if down_shard % (16 * n_t) == 0 else 2
+    share_rows = down_shard // shares
     down_both = jnp.concatenate([query_down_matrix, keyvalue_down_matrix], axis=1)
     down_mine = lax.dynamic_index_in_dim(
-        down_both.reshape(2, core_rows, q_lat + kv_all), core, 0, keepdims=False
-    )
-    cut = -(-core_rows // 32) * 16
+        down_both.reshape(shares, share_rows, q_lat + kv_all), lax.rem(t, shares), 0, keepdims=False
+    )
     qb_rows, kvb_rows = query_up_matrix.shape[0], keyvalue_up_matrix.shape[0]
     head_q = PLAIN_HEAD_DIM + ROTARY_DIM
 
@@ -804,7 +1319,7 @@
     def group_block(dd, tt):
         return lax.rem(dd // pair, 2) * n_t + tt
 
-    def group_jobs(src, out):
+    def group_jobs(src, out, ways):
         return [
             dict(
                 src=src,
@@ -815,7 +1330,7 @@
                 ),
                 steps=steps + t_core,
             )
-            for at, steps in ((0, group_a), (half_rows, group_b))
+            for at, steps in zip((0, half_rows), ways)
         ]
 
     group_a = t_slow + [("dp", pair)]
@@ -823,14 +1338,9 @@
     jobs = [
         dict(
             src=0,
-            src_at=pl.ds(at, count),
             out=0,
-            out_at=lambda dd, tt, at=at, count=count: (dd, lax.rem(tt, 2), pl.ds(at, count)),
-            steps=steps + t_core,
-        )
-        for at, count, steps in (
-            (0, cut, outer_first),
-            (cut, core_rows - cut, inner_first),
+            out_at=lambda dd, tt: (dd, lax.rem(tt, shares)),
+            steps=outer_first + (t_slow if shares == n_t else []) + t_core,
         )
     ]
     jobs += [
@@ -838,10 +1348,10 @@
         dict(src=2, out=2, out_at=rows_at(CODE_LANES, kvb_rows, kvb_rows), steps=outer_first),
         dict(src=3, out=3, out_at=rows_at(0, out_rows, out_rows), steps=outer_first),
     ]
-    jobs += group_jobs(4, 4)
+    jobs += group_jobs(4, 4, (group_b, group_b))
     jobs.append(dict(src=8, out=5, out_at=lambda dd, tt: (dd,), steps=outer_first))
     set_mark = jnp.full((16, 128), sequence_adapter_index[0].astype(F32)).astype(BF16)
-    w_down, w_q, w_kv, w_out, g_all, set_marks = remote_gather(
+    w_down, w_q, w_kv, w_out, g_all, set_marks, w_ffn0, w_ffn1 = remote_gather(
         [
             down_mine,
             pad_heads(query_up_matrix),
@@ -852,53 +1362,38 @@
             kv_aug_rows,
             out_extra,
             set_mark,
+            ffn_mine[0],
+            ffn_other[0],
+            ffn_mine[1],
         ],
         jobs,
         [
-            (5, 1, (pl.ds(q_lat, CODE_LANES),)),
-            (6, 2, (pl.ds(0, CODE_LANES),)),
-            (7, 3, (pl.ds(width, CODE_LANES),)),
+            (5, 1, lambda dd, tt: (pl.ds(q_lat, CODE_LANES),)),
+            (6, 2, lambda dd, tt: (pl.ds(0, CODE_LANES),)),
+            (7, 3, lambda dd, tt: (pl.ds(width, CODE_LANES),)),
+            (9, 6, rows_at(0, ffn_rows_each, ffn_rows_each)),
+            (11, 7, rows_at(0, ffn_rows_each, ffn_rows_each)),
         ],
         [
-            (n_dp, 2, core_rows, q_lat + kv_all),
+            (n_dp, shares, share_rows, q_lat + kv_all),
             (q_lat + CODE_LANES, heads * HEAD_LANES),
             (CODE_LANES + kv_lat, heads * HEAD_LANES),
             (aug, heads * VALUE_HEAD_DIM),
             (2 * n_t * rows, aug),
             (n_dp, 16, 128),
+            (aug, ffn_wide[0]),
+            (aug, ffn_wide[1]),
         ],
         "gather_weights",
         1,
+        riders=[ride_one(6, 9, 10, 0, ffn_rows_each)],
+        rider_round=1,
     )
     set_all = set_marks[:, 0, 0].astype(jnp.int32)
     set_peer = lax.dynamic_index_in_dim(set_all, jnp.bitwise_xor(d, pair), 0, keepdims=False)
     set_even = jnp.where(first, set_own, set_peer)
     set_odd = jnp.where(first, set_peer, set_own)
     w_down = w_down.reshape(width, q_lat + kv_all)
-
-    hidden = down_matrix.shape[0]
-    half = hidden // 2
-    main = half // 128 * 128
-    tail = half - main
-    tail_wide = -(-3 * tail // 128) * 128
-    chunks = 2 if (main // 128) % 2 == 0 else 1
-    step_wide = main // chunks
-
-    def columns(gate_part, up_part, down_part, chunk):
-        at = slice(chunk * step_wide, (chunk + 1) * step_wide)
-        out = [gate_part[:, at]]
-        if tail and chunk == chunks - 1:
-            out += [gate_part[:, main:], up_part[:, main:], down_part[:, main:]]
-            if tail_wide > 3 * tail:
-                out.append(jnp.zeros((gate_part.shape[0], tail_wide - 3 * tail), BF16))
-        out += [up_part[:, at], down_part[:, at]]
-        return jnp.concatenate(out, axis=1)
-
-    def halves(value):
-        return value[:, :half], value[:, half:]
-
-    down_turned = down_matrix.T
-    mats = [halves(gate_up_matrix[0]), halves(gate_up_matrix[1]), halves(down_turned)]
     zero_codes = jnp.zeros((RANK, half), BF16)
 
     def half_of(value):
@@ -911,38 +1406,17 @@
         up_b = half_of(pick(gate_up_adapter_out[1], which)) * 2
         down_a_t = half_of(pick(turned(down_adapter_in), which))
         extra_parts.append((gate_b, up_b, down_a_t))
-
-    z_count = n_dp // pair
-    ffn_columns, ffn_known = [], []
+    ffn_extra = []
     for chunk in range(chunks):
-        left = columns(mats[0][0], mats[1][0], mats[2][0], chunk)
-        right = columns(mats[0][1], mats[1][1], mats[2][1], chunk)
-        mine = jnp.where(first, left, right)
-        other = jnp.where(first, right, left)
-        held = {
-            0: mine,
-            pair: hop(other, ("dp", pair)),
-            high: hop(mine, ("dp", high)),
-            high ^ pair: hop(other, ("dp", high ^ pair)),
-        }
-        count, wide = mine.shape
-        (column,) = place_pieces(
-            list(held.values()),
-            [
-                (n, None, 0, lambda dd, tt, r=r: (jnp.bitwise_xor(dd, r) // pair,))
-                for n, r in enumerate(held)
-            ],
-            [(z_count, count, wide)],
-            "place_column_" + str(chunk),
-        )
-        ffn_columns.append(column)
-    w_down, ffn_columns = lax.optimization_barrier((w_down, ffn_columns))
-    for column in ffn_columns:
-        known = {0: column}
-        for b in reversed(low_bits):
-            for r in list(known):
-                known[r ^ b] = hop(known[r], ("dp", b))
-        ffn_known.append(known)
+        extra = []
+        for gate_b, up_b, down_a_t in extra_parts:
+            extra.append(columns(gate_b, zero_codes, down_a_t, chunk))
+            extra.append(columns(zero_codes, up_b, zero_codes, chunk))
+        extra.append(jnp.zeros((CODE_LANES - 4 * RANK, extra[0].shape[1]), BF16))
+        ffn_extra.append(jnp.concatenate(extra, axis=0))
+    cut_a = ffn_rows_each // 64 * 16
+    cut_b = ffn_rows_each // 48 * 32
+
     cos_part, sin_part = rope_tables(document_numbers)
     zeros_l = jnp.zeros((length, PLAIN_HEAD_DIM), F32)
     zeros_r = jnp.zeros((length, HEAD_LANES - 96), F32)
@@ -1013,18 +1487,19 @@
             for n in range(parts)
         ]
 
-    def relative(value, name):
-        blocks = value.reshape(n_t, value.shape[0] // n_t, value.shape[1])
-        (full,) = place_pieces(
-            [blocks],
-            [(0, r, 0, lambda dd, tt, r=r: (jnp.bitwise_xor(tt, r),)) for r in range(n_t)],
-            [blocks.shape],
-            name,
-        )
-        return full
-
-    (lat_all,) = remote_gather(
-        [lat_own], token_jobs(0, 0, 2), [], [(length, lat_own.shape[1])], "gather_latents", 2
+    lat_all, w_ffn0, w_ffn1 = remote_gather(
+        [lat_own, ffn_extra[0], ffn_extra[1], w_ffn0, w_ffn1, ffn_mine[1], ffn_other[1]],
+        token_jobs(0, 0, 2),
+        [
+            (1, 1, lambda dd, tt: (pl.ds(width, CODE_LANES),)),
+            (2, 2, lambda dd, tt: (pl.ds(width, CODE_LANES),)),
+        ],
+        [(length, lat_own.shape[1]), (aug, ffn_wide[0]), (aug, ffn_wide[1])],
+        "gather_latents",
+        2,
+        riders=[ride_two(1, 0), ride_one(2, 5, 6, 0, cut_a)],
+        aliases={3: 1, 4: 2},
+        distant=(5, 6),
     )
     pe_rows = lat_all[:, pe_at : pe_at + ROTARY_DIM].astype(F32)
     pe_a, pe_b = pe_rows[:, : ROTARY_DIM // 2], pe_rows[:, ROTARY_DIM // 2 :]
@@ -1040,8 +1515,18 @@
         )
         + doc_k
     )
-    q_aug, kv, head_out = attend(
-        lat_all, w_q, w_kv, rope, pe_aug, doc_q, q_lat + CODE_LANES, q_lat
+    q_aug, kv, head_out, w_ffn0, w_ffn1 = attend(
+        lat_all,
+        w_q,
+        w_kv,
+        rope,
+        pe_aug,
+        doc_q,
+        q_lat + CODE_LANES,
+        q_lat,
+        [ride_two(0, 1), ride_one(1, 2, 3, cut_a, cut_b - cut_a)],
+        [w_ffn0, w_ffn1],
+        [ffn_mine[1], ffn_other[1]],
     )
     tensor_keys = [(0, r) for r in reversed(range(0, n_t, 2))]
 
@@ -1052,8 +1537,7 @@
     def out_term(held, place, key):
         return dot_nt(held[0][token_rows(key, place), :], held[1][...])
 
-    head_out, ffn_known[0] = lax.optimization_barrier((head_out, ffn_known[0]))
-    attn_sum = remote_reduce(
+    attn_sum, w_ffn0, w_ffn1 = remote_reduce(
         [head_out, w_out],
         [head_out.shape, w_out.shape],
         out_term,
@@ -1063,7 +1547,10 @@
         aug,
         "reduce_out",
         3,
-        2 * length * head_out.shape[1] * aug,
+        riders=[ride_two(0, z) for z in range(2, z_count)]
+        + [ride_one(1, 2, 3, cut_b, ffn_rows_each - cut_b)],
+        ridden=[w_ffn0, w_ffn1],
+        carried=[ffn_mine[1], ffn_other[1]],
     )
     out_codes = narrow(attn_sum[:, width : width + RANK])
     middle = residual + RESIDUAL * (
@@ -1074,92 +1561,39 @@
     ffn_rows = narrow(ffn_normed)
     gu_codes = narrow(dot_nt(ffn_rows, gu_in))
     x_own = jnp.concatenate([ffn_rows, code_lanes(gu_codes)], axis=1)
-    x_own, ffn_known = lax.optimization_barrier((x_own, ffn_known))
-    ffn_weights = []
-    for chunk, known in enumerate(ffn_known):
-        count, wide = known[0].shape[1:]
-        extra = []
-        for gate_b, up_b, down_a_t in extra_parts:
-            extra.append(columns(gate_b, zero_codes, down_a_t, chunk))
-            extra.append(columns(zero_codes, up_b, zero_codes, chunk))
-        extra.append(jnp.zeros((CODE_LANES - 4 * RANK, extra[0].shape[1]), BF16))
-        sources, copies = [jnp.concatenate(extra, axis=0)], [
-            (0, None, 0, lambda dd, tt: (pl.ds(width, CODE_LANES),))
-        ]
-        for r, piece in known.items():
-            for z in range(z_count):
-                copies.append(
-                    (
-                        len(sources),
-                        z,
-                        0,
-                        lambda dd, tt, r=r, z=z: (
-                            pl.ds(
-                                pl.multiple_of(
-                                    (z * pair + lax.rem(jnp.bitwise_xor(dd, r), pair)) * count, 16
-                                ),
-                                count,
-                            ),
-                        ),
-                    )
-                )
-            sources.append(piece)
-        (full,) = place_pieces(sources, copies, [(aug, wide)], "place_ffn_" + str(chunk))
-        ffn_weights.append(full)
-
-    (x_all,) = remote_gather(
-        [x_own], group_jobs(0, 0), [], [(2 * n_t * rows, aug)], "gather_rows", 4
-    )
-    grads, hids = [], []
-    for chunk in range(chunks):
-        last = chunk == chunks - 1
-        grad_c, hid_c = ffn_middle(
-            x_all, g_all, ffn_weights[chunk], step_wide, tail if last else 0, tail_wide if last else 0
-        )
-        grads.append(grad_c)
-        hids.append(hid_c)
-
-    def gu_columns(chunk):
-        return grads[chunk].shape[1]
-
-    group_keys = [
-        (p, r) for p in (pair, 0) for r in reversed(range(0, n_t, 2))
-    ]
-
-    def ffn_in_term(held, place, key):
-        block = group_block(
+
+    def group_block_of(key, place):
+        return group_block(
             jnp.bitwise_xor(place["dp"], key[0]), jnp.bitwise_xor(place["tensor"], key[1])
         )
-        at = pl.ds(pl.multiple_of(block * rows, 16), rows)
-        out = dot_nt(held[0][at, :], held[chunks][...])
-        for chunk in range(1, chunks):
-            out = out + dot_nt(held[chunk][at, :], held[chunks + chunk][...])
-        return out
-
-    ffn_in_sum = remote_reduce(
-        grads + ffn_weights,
-        [g.shape for g in grads] + [(aug, gu_columns(c)) for c in range(chunks)],
-        ffn_in_term,
+
+    x_codes, grads, hids, ffn_weights = remote_ffn(
+        x_own,
+        g_all,
+        [w_ffn0, w_ffn1],
+        mains,
+        tail,
+        tail_wide,
+        t_slow + [("dp", pair)],
+        group_block_of,
+        [ride_two(1, z) for z in range(z_count)],
+        "feed_forward",
+        4,
+    )
+    group_keys = [(p, r) for p in (pair, 0) for r in reversed(range(0, n_t, 2))]
+    ffn_in_sum, down_chip = remote_ffn_back(
+        grads,
+        hids,
+        ffn_weights,
+        mains,
+        tail_wide,
         group_keys,
         [group_a[::-1], group_b[::-1]],
+        group_block_of,
         rows,
-        aug,
-        "reduce_ffn_in",
+        "feed_forward_back",
         5,
-        2 * 2 * length * sum(g.shape[1] for g in grads) * aug,
-    )
-
-    def down_terms(hid_rows):
-        out = 0.0
-        for chunk, hid in enumerate(hid_rows):
-            weight = ffn_weights[chunk]
-            out = out + dot_nt(hid[:, :step_wide], weight[:, gu_columns(chunk) :])
-            if hid.shape[1] > step_wide:
-                out = out + dot_nt(
-                    hid[:, step_wide:], weight[:, step_wide : step_wide + tail_wide]
-                )
-        return out
-
+    )
     gu_code_grad = narrow(own_codes(ffn_in_sum))
     ffn_in_grad = ffn_in_sum[:, :width] + dot_nn(gu_code_grad, gu_in)
     middle_grad = out_grad + normalize_back(
@@ -1171,49 +1605,50 @@
         [attn_grad, out_code_grad, jnp.zeros((rows, CODE_LANES - RANK), BF16)], axis=1
     )
 
-    (grad_all,) = remote_gather(
-        [attn_grad_aug], token_jobs(0, 0, 2), [], [(length, aug)], "gather_grad", 6
-    )
+    ride_down = n_t == 4
+    sent = remote_gather(
+        [attn_grad_aug] + ([down_chip] if ride_down else []),
+        token_jobs(0, 0, 2),
+        [],
+        [(length, aug)] + ([(rows, aug)] if ride_down else []),
+        "gather_grad",
+        6,
+        riders=[dict(kind="plain", src=1, src_at=0, out=1, step=("dp", pair))] if ride_down else [],
+        distant=(1,),
+    )
+    grad_all = sent[0]
     heads_grad = narrow(dot_nn(grad_all, w_out))
     out_a = dot_tn(grad_all[:, width:], head_out)[:RANK]
-    dq, dkv, dpe = attend_back(q_aug, kv, head_out, heads_grad, rope, pe_aug)
-
-    hid_rel = place_pieces(
-        hids,
-        [
-            (
-                c,
-                pl.ds(b * rows, rows),
-                c,
-                lambda dd, tt, b=b: (
-                    jnp.bitwise_xor(lax.rem(dd // pair, 2), b // n_t) * n_t
-                    + jnp.bitwise_xor(tt, b % n_t),
-                ),
+    if ride_down:
+        down_far = narrow(down_chip[2].astype(F32) + sent[1].astype(F32))
+        dq, dkv, dpe, came_pair, came_y = attend_back(
+            q_aug,
+            kv,
+            head_out,
+            heads_grad,
+            rope,
+            pe_aug,
+            [
+                dict(kind="plain", src=0, src_at=1, out=0, step=("dp", pair)),
+                dict(kind="plain", src=1, src_at=None, out=1, step=("tensor", 2)),
+            ],
+            [down_chip, down_far],
+            [(rows, aug), (rows, aug)],
+        )
+        ffn_out = down_chip[3].astype(F32) + came_pair.astype(F32) + came_y.astype(F32)
+    else:
+        dq, dkv, dpe = attend_back(q_aug, kv, head_out, heads_grad, rope, pe_aug, [], [], [])
+        places = n_t // 2
+        ffn_out = down_chip[places:].astype(F32) + hop(down_chip[:places], ("dp", pair)).astype(F32)
+        while places > 1:
+            places //= 2
+            ffn_out = ffn_out[places:] + hop(narrow(ffn_out[:places]), ("tensor", 2 * places)).astype(
+                F32
             )
-            for c in range(chunks)
-            for b in range(2 * n_t)
-        ],
-        [(2 * n_t, rows, h.shape[1]) for h in hids],
-        "place_hidden",
-    )
-    hid_rel = [h.reshape(2, n_t // 2, 2, rows, h.shape[2]) for h in hid_rel]
-    hid_odd = [h[:, :, 1].reshape(n_t * rows, -1) for h in hid_rel]
-    hid_even = [h[:, :, 0].reshape(n_t * rows, -1) for h in hid_rel]
-    came = hop(narrow(down_terms(hid_odd)), t_core[0])
-    chip = down_terms(hid_even) + came.astype(F32)
-    chip = chip.reshape(2, n_t // 2, rows, aug)
-    ffn_out = chip[0] + hop(narrow(chip[1]), ("dp", pair)).astype(F32)
-    left = n_t // 2
-    while left > 1:
-        ffn_out = ffn_out[: left // 2] + hop(
-            narrow(ffn_out[left // 2 :]), ("tensor", left)
-        ).astype(F32)
-        left //= 2
-    ffn_out = ffn_out[0]
+        ffn_out = ffn_out[0]
     down_codes = narrow(own_codes(ffn_out)[:, :RANK])
     outputs = narrow(
-        middle
-        + RESIDUAL * (ffn_out[:, :width] + ADAPT_SCALE * dot_nn(down_codes, down_out))
+        middle + RESIDUAL * (ffn_out[:, :width] + ADAPT_SCALE * dot_nn(down_codes, down_out))
     )
 
     pe_g = dpe[:, PLAIN_HEAD_DIM : PLAIN_HEAD_DIM + ROTARY_DIM]
@@ -1238,7 +1673,7 @@
         )
 
     operands = [dq, dkv, w_q, w_kv, pe_padded]
-    lat_sum = remote_reduce(
+    (lat_sum,) = remote_reduce(
         operands,
         [o.shape for o in operands],
         latent_term,
@@ -1248,7 +1683,6 @@
         lat_wide,
         "reduce_latents",
         7,
-        2 * length * dq.shape[1] * lat_wide,
     )
     qb_code_grad = narrow(lat_sum[:, q_lat : q_lat + RANK])
     kvb_code_grad = narrow(lat_sum[:, q_lat + RANK : q_lat + 2 * RANK])
@@ -1287,16 +1721,17 @@
     early_terms = jnp.concatenate([gu_a, out_b, down_b], axis=0)
 
     def uncolumn(parts, at_tail, first_at):
-        out = [parts[c][:, first_at(c) : first_at(c) + step_wide] for c in range(chunks)]
+        out = [parts[c][:, first_at(c) : first_at(c) + mains[c]] for c in range(chunks)]
         if tail:
-            out.append(parts[-1][:, step_wide + at_tail * tail : step_wide + (at_tail + 1) * tail])
+            at = mains[-1] + at_tail * tail
+            out.append(parts[-1][:, at : at + tail])
         return jnp.concatenate(out, axis=1)
 
-    x_codes, g_codes = x_all[:, width:], g_all[:, width:]
+    g_codes = g_all[:, width:]
     gu_b = [dot_tn(x_codes, g) for g in grads]
     down_at = [dot_tn(g_codes, h) for h in hids]
     gate_b_all = ADAPT_SCALE * uncolumn(gu_b, 0, lambda c: 0)
-    up_b_all = ADAPT_SCALE * uncolumn(gu_b, 1, lambda c: gu_columns(c) - step_wide)
+    up_b_all = ADAPT_SCALE * uncolumn(gu_b, 1, lambda c: gu_wide[c] - mains[c])
     down_a_all = uncolumn(down_at, 2, lambda c: 0)
     packed = []
     for p in range(2):

time: 1040 us -> 782 us (0.75)
  waiting for transfers between devices: 107 us -> 0 us
  Pallas kernels: 661 us -> 608 us
  matrix products: 110 us -> 58.7 us
  local copies, waits for them, and re-layouts: 93.6 us -> 63 us
  starting transfers between devices: 14.2 us -> 0 us
    ppermute x11 -> x0, waiting for transfers between devices: 107 us -> none  [swap(): return lax.ppermute(value, axis, [(i, i ^ bit) for i in range(size)])]
    pallas_call x4 -> x3, Pallas kernels: 319 us -> 225 us  [remote_gather(): pl.pallas_call(kernel, out_shape=[jax.ShapeDtypeStruct(o, BF16) for o in...]
    dot_general x14 -> x8, matrix products: 58.7 us -> 10.1 us  [dot_nt(): lax.dot_general(a, b, (((1,), (1,)), ((), ())), preferred_element_type=F32)]
    pallas_call x12 -> x6, Pallas kernels: 257 us -> 296 us  [the longest x1 79.6 us: remote_ffn(): pl.pallas_call(kernel, in_specs=[vmem_spec, any_spec] + [any_spec] * chun...]
    ppermute x11 -> x0, starting transfers between devices: 14.2 us -> none  [swap(): return lax.ppermute(value, axis, [(i, i ^ bit) for i in range(size)])]
    unnamed x257 -> x173, local copies, waits for them, and re-layouts: 35.2 us -> 30 us
  transfers between devices with their start and end apart: 11 -> 0, of which waited for: 5 -> 0; matrix products, arithmetic and copies ran while one was open for 11% -> 0% of each run, Pallas kernels for 33% -> 0%
where the time goes in v3:
time: 782 us; the launch traced here: 771 us
  Pallas kernels  608 us (78%)
  local copies, waits for them, and re-layouts  63 us (8%)
  matrix products  58.7 us (8%)
  other arithmetic  36.7 us (5%)
    pallas_call x3, Pallas kernels, remote_gather(): pl.pallas_call(kernel, out_shape=[jax.ShapeDtypeStruct(o, BF16) for o in...  225 us
    pallas_call x2, Pallas kernels, remote_share(): pl.pallas_call(kernel, out_shape=[jax.ShapeDtypeStruct(o, BF16) for o in...  87 us
    pallas_call x1, Pallas kernels, remote_ffn(): pl.pallas_call(kernel, in_specs=[vmem_spec, any_spec] + [any_spec] * chun...  79.6 us
    pallas_call x2, Pallas kernels, ridden_call(): pl.pallas_call(body, grid=grid, in_specs=list(in_specs) + [any_spec] * n_...  78 us
    pallas_call x2, Pallas kernels, remote_reduce(): pl.pallas_call(kernel, out_shape=[jax.ShapeDtypeStruct((rows, wide), F32)...  69 us
    pallas_call x1, Pallas kernels, remote_ffn_back(): pl.pallas_call(kernel, out_shape=[jax.ShapeDtypeStruct((rows, aug), F32),...  68.9 us
    unnamed x173, local copies, waits for them, and re-layouts  30 us
    dot_general x9, matrix products, dot_nn(): lax.dot_general(a, b, (((1,), (0,)), ((), ())), preferred_element_type=F32)  25.7 us

profile of v3, /device:TPU:0, one launch (start us, length us, event | category | flops | bytes accessed | tf_op | source)
XLA Modules:
  0.0 770.9 jit_solution(16373446689749189875)
XLA Ops:
  23.5 163.7 %gather_weights.1 = (bf16[8,4,80,1056]{3,2,1,0:T(8,128)(2,1)}, bf16[896,1280]{1,0:T(8,128)(2,1)}, bf16[384,1280]{1,0:T(8,128)(2,1)}, bf16[2688,640]{1,0:T(8,128)...) custom-call(bf16[80,1056]{1,0:T(8,128)(2,1)} %dynamic-slice_bitcast_, ...), custom_call_target="tpu_custom_call" | custom-call | tf_op jit(solution)/shard_map/gather_weights/pallas_call | solution.py:290
  188.2 4.6 fusion.44
  207.2 26.2 %gather_latents.1 = (bf16[1024,1152]{1,0:T(8,128)(2,1)}, bf16[2688,1536]{1,0:T(8,128)(2,1)}, bf16[2688,896]{1,0:T(8,128)(2,1)}) custom-call(bf16[256,1152]{1,0:T(8,128)(2,1)} %concatenate.154.refs_0_, bf16[128,1536]{1,0:T(8,128)(2,1)} %copy-done.34, bf16[128,896]{1,0:T(8,128)(2,1)} %copy-done.41, ...), custom_call_target="tpu_custom_call", output_to_operand_aliasing={{1}: (3, {}), {2}: (4, {})} | custom-call | tf_op jit(solution)/shard_map/gather_latents/pallas_call | solution.py:290
  241.3 41.8 %attend.1 = (bf16[1024,1280]{1,0:T(8,128)(2,1)}, bf16[1024,1280]{1,0:T(8,128)(2,1)}, bf16[1024,640]{1,0:T(8,128)(2,1)}, bf16[2688,1536]{1,0:T(8,128)(2,1)}, bf16[2688,896]{1,0:T(8,128)(2,1)}) custom-call(bf16[1024,1152]{1,0:T(8,128)(2,1)} %get-tuple-element.59.refs_0_, ...), custom_call_target="tpu_custom_call", output_to_operand_aliasing={{3}: (6, {}), {4}: (7, {})} | custom-call | tf_op jit(solution)/shard_map/attend/pallas_call | solution.py:653
  283.1 46.2 %reduce_out.1 = (f32[256,2688]{1,0:T(8,128)}, bf16[2688,1536]{1,0:T(8,128)(2,1)}, bf16[2688,896]{1,0:T(8,128)(2,1)}) custom-call(bf16[1024,640]{1,0:T(8,128)(2,1)} %get-tuple-element.64.refs_0_.refs_2_, bf16[2688,640]{1,0:T(8,128)(2,1)} %get-tuple-element.65.refs_1_, ...), custom_call_target="tpu_custom_call", output_to_operand_aliasing={{1}: (2, {}), {2}: (3, {})} | custom-call | tf_op jit(solution)/shard_map/reduce_out/pallas_call | solution.py:391
  329.3 3.1 multiply_reduce_fusion.1
  335.6 3.3 concatenate.172.x_ref
  338.9 79.6 %feed_forward.1 = (bf16[2048,128]{1,0:T(8,128)(2,1)}, bf16[2048,1024]{1,0:T(8,128)(2,1)}, bf16[2048,640]{1,0:T(8,128)(2,1)}, bf16[2048,512]{1,0:T(8,128)(2,1)}, ...) custom-call(bf16[256,2688]{1,0:T(8,128)(2,1)} %concatenate.172.x_ref, ...), custom_call_target="tpu_custom_call", output_to_operand_aliasing={{5}: (2, {}), {6}: (3, {})} | custom-call | tf_op jit(solution)/shard_map/feed_forward/pallas_call | solution.py:917
  418.5 68.9 %feed_forward_back.1 = (f32[256,2688]{1,0:T(8,128)}, bf16[4,256,2688]{2,1,0:T(8,128)(2,1)}) custom-call(bf16[2048,1024]{1,0:T(8,128)(2,1)} %get-tuple-element.72.refs_0_, bf16[2048,640]{1,0:T(8,128)(2,1)} %get-tuple-element.73.refs_1_, bf16[2048,512]{1,0:T(8,128)(2,1)} %get-tuple-element.74.refs_2_, bf16[2048,384]{1,0:T(8,128)(2,1)} %get-tuple-element.75.refs_3_, ...), custom_call_target="tpu_custom_call" | custom-call | tf_op jit(solution)/shard_map/feed_forward_back/pallas_call | solution.py:1082
  487.5 2.6 multiply_reduce_fusion
  494.1 3.3 concatenate.173.refs_0_
  497.3 35.4 %gather_grad.1 = (bf16[1024,2688]{1,0:T(8,128)(2,1)}, bf16[256,2688]{1,0:T(8,128)(2,1)}) custom-call(bf16[256,2688]{1,0:T(8,128)(2,1)} %concatenate.173.refs_0_, bf16[4,256,2688]{2,1,0:T(8,128)(2,1)} %get-tuple-element.78.refs_1_.refs_6_), custom_call_target="tpu_custom_call" | custom-call | tf_op jit(solution)/shard_map/gather_grad/pallas_call | solution.py:290
  532.7 9.3 %convolution_convert_fusion.2.refs_3_ = bf16[1024,640]{1,0:T(8,128)(2,1)} fusion(bf16[1024,2688]{1,0:T(8,128)(2,1)} %get-tuple-element.82, bf16[2688,640]{1,0:T(8,128)(2,1)} %get-tuple-element.65.refs_1_), kind=kOutput, calls=%fused_computation.64 | convolution fusion | flops 3523870720 | bytes 10256384 | tf_op jit(solution)/shard_map/dot_general | solution.py:38
  542.0 2.8 fusion.19.refs_7_
  544.8 36.2 %attend_back.1 = (bf16[1024,1280]{1,0:T(8,128)(2,1)}, bf16[1024,1280]{1,0:T(8,128)(2,1)}, f32[1024,128]{1,0:T(8,128)}, bf16[256,2688]{1,0:T(8,128)(2,1)}, bf16[256,2688]{1,0:T(8,128)(2,1)}) custom-call(bf16[1024,1280]{1,0:T(8,128)(2,1)} %get-tuple-element.79.refs_0_, bf16[1024,1280]{1,0:T(8,128)(2,1)} %get-tuple-element.80.refs_1_, ...), custom_call_target="tpu_custom_call" | custom-call | tf_op jit(solution)/shard_map/attend_back/pallas_call | solution.py:653
  581.0 2.6 fusion.20
  583.7 2.7 fusion.9
  590.1 22.8 %reduce_latents.1 = f32[256,1152]{1,0:T(8,128)} custom-call(bf16[1024,1280]{1,0:T(8,128)(2,1)} %get-tuple-element.86.refs_0_, bf16[1024,1280]{1,0:T(8,128)(2,1)} %get-tuple-element.87.refs_1_, bf16[896,1280]{1,0:T(8,128)(2,1)} %get-tuple-element.60.refs_1_.refs_2_, bf16[384,1280]{1,0:T(8,128)(2,1)} %get-tuple-element.61.refs_2_.refs_3_, ...), custom_call_target="tpu_custom_call" | custom-call | tf_op jit(solution)/shard_map/reduce_latents/pallas_call | solution.py:391
  617.4 4.6 fusion.160
  634.7 41.2 %share_late.1 = (bf16[8,64,2560]{2,1,0:T(8,128)(2,1)}, bf16[8,16,3200]{2,1,0:T(8,128)(2,1)}) custom-call(bf16[64,2560]{1,0:T(8,128)(2,1)} %fusion.86.refs_0_, bf16[16,3200]{1,0:T(8,128)(2,1)} %pad_maximum_fusion.14.refs_1_), custom_call_target="tpu_custom_call" | custom-call | tf_op jit(solution)/shard_map/share_late/pallas_call | solution.py:467
  676.8 3.8 fusion.35
  705.8 45.9 %share_early.1 = (bf16[8,64,2560]{2,1,0:T(8,128)(2,1)}, bf16[8,96,800]{2,1,0:T(8,128)(2,1)}) custom-call(bf16[64,2560]{1,0:T(8,128)(2,1)} %pad_maximum_fusion.7.refs_0_, bf16[96,800]{1,0:T(8,128)(2,1)} %copy-done.42), custom_call_target="tpu_custom_call" | custom-call | tf_op jit(solution)/shard_map/share_early/pallas_call | solution.py:467
  751.6 3.6 fusion.33
  757.7 3.2 copy.203
  (363 shorter events, 108.9 us)
Async XLA Ops:
  0.6 328.6 %copy-start = (bf16[8,16,2560]{2,1,0:T(8,128)(2,1)S(1)}, bf16[8,16,2560]{2,1,0:T(8,128)(2,1)}, u32[]{:S(2)}) copy-start(bf16[8,16,2560]{2,1,0:T(8,128)(2,1)} %param.53) | copy-start | bytes 1966084
  0.7 5.8 copy-start.7
  10.1 6.8 copy-start.26
  23.5 163.8 %copy-start.14 = (bf16[1,256,2560]{2,1,0:T(8,128)(2,1)S(1)}, bf16[1,256,2560]{2,1,0:T(8,128)(2,1)}, u32[]{:S(2)}) copy-start(bf16[1,256,2560]{2,1,0:T(8,128)(2,1)} %param.29) | copy-start | bytes 3932164
  23.5 164.7 %copy-start.56 = (f32[2560]{0:T(1024)S(1)}, f32[2560]{0:T(1024)}, u32[]{:S(2)}) copy-start(f32[2560]{0:T(1024)} %param.33) | copy-start | bytes 30724
  188.2 5.6 copy-start.69
  196.2 9.1 %copy-start.2 = (f32[256,1056]{1,0:T(8,128)}, f32[256,1056]{1,0:T(8,128)S(1)}, u32[]{:S(2)}) copy-start(f32[256,1056]{1,0:T(8,128)S(1)} %fusion.18) | copy-start | bytes 3244036
  196.2 9.1 %copy-start.32 = (bf16[2,8,16,1600]{3,2,1,0:T(8,128)(2,1)S(1)}, bf16[2,8,16,1600]{3,2,1,0:T(8,128)(2,1)}, u32[]{:S(2)}) copy-start(bf16[2,8,16,1600]{3,2,1,0:T(8,128)(2,1)} %param.55) | copy-start | bytes 2457604
  197.5 8.0 %copy-start.24 = (bf16[256,768]{1,0:T(8,128)(2,1)}, bf16[256,768]{1,0:T(8,128)(2,1)S(1)}, u32[]{:S(2)}) copy-start(bf16[256,768]{1,0:T(8,128)(2,1)S(1)} %multiply_convert_fusion.2) | copy-start | bytes 1179652
  207.2 27.5 %copy-start.51 = (s32[1,1024]{1,0:T(1,128)S(1)}, s32[1,1024]{1,0:T(1,128)}, u32[]{:S(2)}) copy-start(s32[1,1024]{1,0:T(1,128)} %param.31) | copy-start | bytes 12292
  418.5 68.9 %copy-start.40 = (bf16[16,2560]{1,0:T(8,128)(2,1)S(1)}, bf16[16,2560]{1,0:T(8,128)(2,1)}, u32[]{:S(2)}) copy-start(bf16[16,2560]{1,0:T(8,128)(2,1)} %copy-done.39) | copy-start | bytes 245764
  418.5 68.9 %copy-start.48 = (f32[2560]{0:T(1024)S(1)}, f32[2560]{0:T(1024)}, u32[]{:S(2)}) copy-start(f32[2560]{0:T(1024)} %param.36) | copy-start | bytes 30724
  532.7 9.3 %copy-start.30 = (bf16[256,2688]{1,0:T(8,128)(2,1)S(1)}, bf16[256,2688]{1,0:T(8,128)(2,1)}, u32[]{:S(2)}) copy-start(bf16[256,2688]{1,0:T(8,128)(2,1)} %get-tuple-element.83) | copy-start | bytes 4128772
  590.1 24.4 %copy-start.3 = (f32[256,1056]{1,0:T(8,128)S(1)}, f32[256,1056]{1,0:T(8,128)}, u32[]{:S(2)}) copy-start(f32[256,1056]{1,0:T(8,128)} %copy-done.2) | copy-start | bytes 3244036
  590.1 24.4 %copy-start.65 = (f32[256]{0:T(256)S(1)}, f32[256]{0:T(256)}, u32[]{:S(2)}) copy-start(f32[256]{0:T(256)} %param.35) | copy-start | bytes 3076
  617.3 4.7 copy-start.44
  617.4 4.7 copy-start.46
  617.4 5.0 copy-start.36
  617.4 5.0 copy-start.38
  617.4 5.0 copy-start.57
  680.6 5.3 copy-start.5
  689.2 5.8 copy-start.9
  690.4 5.0 copy-start.13
  692.2 4.6 copy-start.11
  (50 other events, 122.0 us)

commit v4 on v3

--- a/solution.py
+++ b/solution.py
@@ -148,8 +148,8 @@
                 held = [0]
                 for k, step in enumerate(rider["steps"]):
                     for key in list(held):
-                        low = jnp.bitwise_xor(lax.rem(d, pair), key)
-                        at = pl.multiple_of((rider["z"] * pair + low) * count, 16)
+                        place = jnp.bitwise_xor(d, rider["z"] * pair + key)
+                        at = pl.multiple_of(place * count, 16)
                         here = full.at[pl.ds(at, count)]
                         self.add(k, here, here, step)
                         held.append(key ^ step[1])
@@ -218,7 +218,7 @@
     return sum((1 << len(job["steps"])) - 1 for job in jobs)
 
 
-def run_gathers(links, src_refs, out_refs, jobs, between=None):
+def gather_rounds(links, src_refs, out_refs, jobs):
     d, t = links.place["dp"], links.place["tensor"]
 
     def landing(job, key):
@@ -243,62 +243,110 @@
                 n = links.send(src, landing(job, key), step)
                 new = flip(key, step)
                 held[new] = (landing(job, new), n)
-        if between is not None:
-            between(k)
-    return [landing(job, (0, 0)) for job in jobs]
+        yield k
 
 
 def remote_gather(
-    sources, jobs, extra, outs, name, collective_id, riders=(), aliases=(), distant=(), rider_round=0
+    sources,
+    jobs,
+    extra,
+    outs,
+    name,
+    collective_id,
+    riders=(),
+    aliases=(),
+    distant=(),
+    order=(),
+    near_outs=(),
+    scratch=(),
+    work=None,
+    late=(),
 ):
     steps = distinct([s for job in jobs for s in job["steps"]] + rider_steps(riders))
     count = gather_count(jobs) + rider_count(riders)
     aliases = dict(aliases)
+    n_src, n_out, n_near = len(sources), len(outs), len(near_outs)
 
     def kernel(*refs):
-        src_refs = refs[: len(sources)]
-        out_refs = refs[len(sources) : len(sources) + len(outs)]
-        send_sems, recv_sems, local_sems = refs[len(sources) + len(outs) :]
+        src_refs, refs = refs[:n_src], refs[n_src:]
+        out_refs, refs = refs[:n_out], refs[n_out:]
+        near, refs = refs[: n_near + len(scratch)], refs[n_near + len(scratch) :]
+        send_sems, recv_sems, local_sems = refs
+        all_src, all_out = list(src_refs) + list(near), list(out_refs) + list(near)
         links = Links(send_sems, recv_sems)
         d, t = links.place["dp"], links.place["tensor"]
         links.greet(steps)
         ride = Riders(links, riders, src_refs, out_refs)
         local = []
+
+        def keep(src, where):
+            copy = pltpu.make_async_copy(src, where, local_sems.at[len(local)])
+            copy.start()
+            local.append(copy)
+            return copy
+
+        for src, out, at in extra:
+            keep(all_src[src], all_out[out].at[at(d, t)])
+        groups = {}
         for job in jobs:
-            src = src_refs[job["src"]]
-            if job.get("src_at") is not None:
-                src = src.at[job["src_at"]]
-            local.append((src, out_refs[job["out"]].at[job["out_at"](d, t)]))
-        for src, out, at in extra:
-            local.append((src_refs[src], out_refs[out].at[at(d, t)]))
-        started = []
-        for n, (src, where) in enumerate(local):
-            copy = pltpu.make_async_copy(src, where, local_sems.at[n])
-            copy.start()
-            started.append(copy)
-
-        def between(k):
-            if k == rider_round:
+            groups.setdefault(job.get("group", 0), []).append(job)
+        turns = {}
+        sent = {g: [] for g in groups}
+        kept = {g: [] for g in groups}
+
+        def advance(group):
+            before = len(links.copies)
+            if group not in turns:
+                turns[group] = gather_rounds(links, all_src, all_out, groups[group])
+                for job in groups[group]:
+                    src = all_src[job["src"]]
+                    if job.get("src_at") is not None:
+                        src = src.at[job["src_at"]]
+                    kept[group].append(keep(src, all_out[job["out"]].at[job["out_at"](d, t)]))
+            going = next(turns[group], None) is not None
+            sent[group] += range(before, len(links.copies))
+            return going
+
+        waited = set()
+        if "ride" not in order:
+            ride.start()
+        for turn in order:
+            if turn == "ride":
                 ride.start()
-
-        run_gathers(links, src_refs, out_refs, jobs, between)
+            elif turn == "work":
+                work(all_src)
+                for src, out in late:
+                    keep(all_src[src], all_out[out])
+            elif isinstance(turn, tuple):
+                for n in sent[turn[1]]:
+                    links.arrived(n)
+                for copy in kept[turn[1]]:
+                    copy.wait()
+                waited.add(turn[1])
+            else:
+                advance(turn)
+        for group in groups:
+            while advance(group):
+                pass
         ride.finish()
         links.close()
-        for copy in started:
-            copy.wait()
-
+        done = [copy for group in waited for copy in kept[group]]
+        for copy in local:
+            if not any(copy is other for other in done):
+                copy.wait()
+
+    vmem = pl.BlockSpec(memory_space=pltpu.VMEM)
+    far = pl.BlockSpec(memory_space=pl.ANY)
     return pl.pallas_call(
         kernel,
-        out_shape=[jax.ShapeDtypeStruct(o, BF16) for o in outs],
-        in_specs=[
-            pl.BlockSpec(memory_space=pl.ANY if n in aliases or n in distant else pltpu.VMEM)
-            for n in range(len(sources))
-        ],
-        out_specs=[pl.BlockSpec(memory_space=pl.ANY)] * len(outs),
-        scratch_shapes=[
+        out_shape=[jax.ShapeDtypeStruct(o, BF16) for o in outs] + list(near_outs),
+        in_specs=[far if n in aliases or n in distant else vmem for n in range(n_src)],
+        out_specs=[far] * n_out + [vmem] * n_near,
+        scratch_shapes=[pltpu.VMEM(o.shape, o.dtype) for o in scratch]
+        + [
             pltpu.SemaphoreType.DMA((count,)),
             pltpu.SemaphoreType.DMA((count,)),
-            pltpu.SemaphoreType.DMA((len(jobs) + len(extra),)),
+            pltpu.SemaphoreType.DMA((len(jobs) + len(extra) + len(late),)),
         ],
         input_output_aliases=aliases,
         compiler_params=pltpu.CompilerParams(
@@ -320,25 +368,36 @@
 
 
 def remote_reduce(
-    operands, fetched, term, keys, ways, rows, wide, name, collective_id, riders=(), ridden=(), carried=()
+    operands, fetched, term, keys, ways, rows, wide, name, collective_id, riders=(), ridden=(), carried=(), jobs=(), job_sources=(), job_outs=()
 ):
     core_step = ("tensor", 1)
     part = rows // len(ways)
     plan = reduce_plan(keys, ways)
     slot = {entry: n for n, entry in enumerate(plan)}
-    steps = distinct([core_step] + [s for s in ways[0]] + rider_steps(riders))
-    count = len(keys) + len(plan) + rider_count(riders)
+    steps = distinct(
+        [core_step]
+        + [s for s in ways[0]]
+        + rider_steps(riders)
+        + [s for job in jobs for s in job["steps"]]
+    )
+    count = len(keys) + len(plan) + rider_count(riders) + gather_count(jobs)
     n_in = len(operands)
-    n_all = n_in + len(ridden) + len(carried)
+    n_ride = n_in + len(ridden) + len(carried)
+    n_all = n_ride + len(job_sources)
+    n_jobs = len(job_outs)
 
     def kernel(*refs):
         in_refs = refs[:n_in]
         out_ref = refs[n_all]
-        ride_in = refs[n_in:n_all]
+        ride_in = refs[n_in:n_ride]
+        job_in = refs[n_ride:n_all]
         ride_out = refs[n_all + 1 : n_all + 1 + len(ridden)]
-        scratch = refs[n_all + 1 + len(ridden) :]
+        job_out = refs[n_all + 1 + len(ridden) : n_all + 1 + len(ridden) + n_jobs]
+        scratch = refs[n_all + 1 + len(ridden) + n_jobs :]
         held = scratch[:n_in]
-        core_out, core_in, chip, hop_out, hop_in, send_sems, recv_sems, in_sems = scratch[n_in:]
+        core_out, core_in, chip, hop_out, hop_in, send_sems, recv_sems, in_sems, job_sems = scratch[
+            n_in:
+        ]
         started = []
         for n in range(n_in):
             shape = fetched[n]
@@ -350,6 +409,16 @@
         links.greet(steps)
         ride = Riders(links, riders, ride_in, ride_out)
         ride.start()
+        rounds = gather_rounds(links, job_in, job_out, jobs) if jobs else iter(())
+        next(rounds, None)
+        placed = []
+        for n, job in enumerate(jobs):
+            at = job["out_at"](links.place["dp"], links.place["tensor"])
+            copy = pltpu.make_async_copy(
+                job_in[job["src"]], job_out[job["out"]].at[at], job_sems.at[n]
+            )
+            copy.start()
+            placed.append(copy)
         for copy in started:
             copy.wait()
         came = {}
@@ -376,6 +445,7 @@
                 if way and has_bit(key, way[0]):
                     hop_out[slot[(w, 0, key)]] = narrow(chip[i, w * part : (w + 1) * part, :])
                     send_part(w, 0, key)
+            next(rounds, None)
         for k in range(1, len(ways[0])):
             for w in range(len(ways)):
                 for entry in plan:
@@ -384,16 +454,21 @@
                         send_part(w, k, entry[2])
         for w in range(len(ways)):
             out_ref[w * part : (w + 1) * part, :] = so_far(w, len(ways[w]), (0, 0))
+        for _ in rounds:
+            pass
         ride.finish()
         links.close()
+        for copy in placed:
+            copy.wait()
 
     any_spec = pl.BlockSpec(memory_space=pl.ANY)
     return pl.pallas_call(
         kernel,
         out_shape=[jax.ShapeDtypeStruct((rows, wide), F32)]
-        + [jax.ShapeDtypeStruct(r.shape, r.dtype) for r in ridden],
-        in_specs=[any_spec] * n_all,
-        out_specs=[pl.BlockSpec(memory_space=pltpu.VMEM)] + [any_spec] * len(ridden),
+        + [jax.ShapeDtypeStruct(r.shape, r.dtype) for r in ridden]
+        + [jax.ShapeDtypeStruct(o, BF16) for o in job_outs],
+        in_specs=[any_spec] * n_ride + [pl.BlockSpec(memory_space=pltpu.VMEM)] * len(job_sources),
+        out_specs=[pl.BlockSpec(memory_space=pltpu.VMEM)] + [any_spec] * (len(ridden) + n_jobs),
         input_output_aliases={n_in + n: 1 + n for n in range(len(ridden))},
         scratch_shapes=[pltpu.VMEM(s, o.dtype) for s, o in zip(fetched, operands)]
         + [
@@ -405,84 +480,191 @@
             pltpu.SemaphoreType.DMA((count,)),
             pltpu.SemaphoreType.DMA((count,)),
             pltpu.SemaphoreType.DMA((n_in,)),
+            pltpu.SemaphoreType.DMA((max(len(jobs), 1),)),
         ],
         compiler_params=pltpu.CompilerParams(
             collective_id=collective_id, has_side_effects=True, vmem_limit_bytes=VMEM_LIMIT
         ),
         cost_estimate=FREE,
         name=name,
-    )(*operands, *ridden, *carried)
-
-
-def remote_share(terms, parts, jobs_of, outs, n_t, t_steps, steps, name, collective_id):
-    count, wide = terms.shape[0] // n_t, terms.shape[1]
-    job = dict(
-        src=0,
-        out=0,
-        out_at=lambda dd, tt: (dd, pl.ds(pl.multiple_of(tt * count, 16), count)),
-        steps=steps + t_steps[::-1],
-    )
-    jobs = [job] + jobs_of
-    copies = n_t - 1 + gather_count(jobs)
-    n_in = 1 + len(parts)
-    needed = list(job["steps"])
-
-    def kernel(*refs):
-        in_refs, out_refs = refs[:n_in], refs[n_in : n_in + len(outs)]
-        own, came_in, went_out, send_sems, recv_sems, local_sems = refs[n_in + len(outs) :]
-        links = Links(send_sems, recv_sems)
-        links.greet(needed)
-        t = links.place["tensor"]
-        live = list(range(n_t))
-        sums = {
-            r: in_refs[0][pl.ds(pl.multiple_of(jnp.bitwise_xor(t, r) * count, 16), count), :].astype(
-                F32
-            )
-            for r in live
-        }
-        slot = 0
-        for step in t_steps:
+    )(*operands, *ridden, *carried, *job_sources)
+
+
+class Share:
+    def __init__(self, links, n_t, orders, source, out, own, sums, came, went, terms, fetch_sem):
+        self.links, self.terms, self.own = links, terms, own
+        self.fetch = pltpu.make_async_copy(source, terms, fetch_sem.at[0])
+        self.sums, self.came, self.went = sums, came, went
+        self.count = terms.shape[0] // n_t
+        self.wide = terms.shape[1] // len(orders)
+        count = self.count
+        t_steps = [("tensor", 1 << b) for b in range(n_t.bit_length() - 1)]
+        self.rounds = []
+        live, slot = list(range(n_t)), 0
+        before = []
+        for k, step in enumerate(t_steps):
             sent = []
             for r in live:
                 if r & step[1]:
-                    went_out[slot] = narrow(sums[r])
-                    sent.append((r, slot, links.send(went_out.at[slot], came_in.at[slot], step)))
+                    src = terms.at[self.block(r)] if k == 0 else went.at[slot]
+                    sent.append((r, slot, links.prepare(src, came.at[slot], step)))
                     slot += 1
             live = [r for r in live if not r & step[1]]
-            for r, at, n in sent:
-                links.arrived(n)
-                sums[r ^ step[1]] = sums[r ^ step[1]] + came_in[at].astype(F32)
-        own[...] = narrow(sums[0])
-        sources = [own] + list(in_refs[1:])
-        places = run_gathers(links, sources, out_refs, jobs)
-        started = []
-        for n, (one, where) in enumerate(zip(jobs, places)):
-            copy = pltpu.make_async_copy(sources[one["src"]], where, local_sems.at[n])
+            self.rounds.append(functools.partial(self.scatter, k, list(live), before, sent, step))
+            before = [(r ^ step[1], at, n) for r, at, n in sent]
+        d, t = links.place["dp"], links.place["tensor"]
+
+        def landing(p, key):
+            rows = pl.ds(pl.multiple_of(jnp.bitwise_xor(t, key[1]) * count, 16), count)
+            return out.at[p, jnp.bitwise_xor(d, key[0]), rows]
+
+        self.places = [landing(p, (0, 0)) for p in range(len(orders))]
+        held = [{(0, 0): (own.at[p], None)} for p in range(len(orders))]
+        seen = set()
+        for k in range(len(orders[0])):
+            work = []
+            for p, order in enumerate(orders):
+                step = order[k]
+                for key in list(held[p]):
+                    src, needs = held[p][key]
+                    n = links.prepare(src, landing(p, key), step)
+                    work.append((None if needs in seen else needs, n))
+                    seen.add(needs)
+                    new = flip(key, step)
+                    held[p][new] = (landing(p, new), n)
+            self.rounds.append(functools.partial(self.gather, k, before, work))
+
+    def block(self, r):
+        at = jnp.bitwise_xor(self.links.place["tensor"], r) * self.count
+        return pl.ds(pl.multiple_of(at, 16), self.count)
+
+    def scatter(self, k, live, before, sent, step):
+        if k == 0:
+            self.fetch.start()
+            self.fetch.wait()
+            for r in live:
+                self.sums[r] = self.terms[self.block(r), :].astype(F32)
+        self.add(before)
+        for r, at, n in sent:
+            if k:
+                self.went[at] = narrow(self.sums[r])
+            self.links.copies[n].start()
+
+    def add(self, before):
+        for r, at, n in before:
+            self.links.arrived(n)
+            self.sums[r] = self.sums[r] + self.came[at].astype(F32)
+
+    def gather(self, k, before, work):
+        if k == 0:
+            self.add(before)
+            for p in range(self.own.shape[0]):
+                self.own[p] = narrow(self.sums[0, :, p * self.wide : (p + 1) * self.wide])
+        for needs, n in work:
+            if needs is not None:
+                self.links.copies[needs].wait_recv()
+                self.links.waited.add(needs)
+            self.links.copies[n].start()
+
+    def keep(self, sems):
+        return [
+            pltpu.make_async_copy(self.own.at[p], where, sems.at[p])
+            for p, where in enumerate(self.places)
+        ]
+
+
+def share_shapes(shape, n_t, orders):
+    count, parts = shape[0] // n_t, len(orders)
+    copies = n_t - 1 + parts * ((1 << len(orders[0])) - 1)
+    scratch = [
+        pltpu.VMEM((parts, count, shape[1] // parts), BF16),
+        pltpu.VMEM((n_t, count, shape[1]), F32),
+        pltpu.VMEM((n_t - 1, count, shape[1]), BF16),
+        pltpu.VMEM((n_t - 1, count, shape[1]), BF16),
+        pltpu.VMEM(shape, BF16),
+        pltpu.SemaphoreType.DMA((1,)),
+        pltpu.SemaphoreType.DMA((parts,)),
+    ]
+    return scratch, copies
+
+
+def remote_share(terms, n_dp, n_t, orders, name, collective_id):
+    scratch, copies = share_shapes(terms.shape, n_t, orders)
+    parts = len(orders)
+
+    def kernel(source, out_ref, *refs):
+        own_sems, send_sems, recv_sems = refs[-3:]
+        links = Links(send_sems, recv_sems)
+        links.greet(orders[0])
+        share = Share(links, n_t, orders, source, out_ref, *refs[:-3])
+        for one in share.rounds:
+            one()
+        kept = share.keep(own_sems)
+        for copy in kept:
             copy.start()
-            started.append(copy)
         links.close()
-        for copy in started:
+        for copy in kept:
             copy.wait()
 
     return pl.pallas_call(
         kernel,
-        out_shape=[jax.ShapeDtypeStruct(o, BF16) for o in outs],
-        in_specs=[pl.BlockSpec(memory_space=pltpu.VMEM)] * n_in,
-        out_specs=[pl.BlockSpec(memory_space=pl.ANY)] * len(outs),
-        scratch_shapes=[
-            pltpu.VMEM((count, wide), BF16),
-            pltpu.VMEM((n_t - 1, count, wide), BF16),
-            pltpu.VMEM((n_t - 1, count, wide), BF16),
-            pltpu.SemaphoreType.DMA((copies,)),
-            pltpu.SemaphoreType.DMA((copies,)),
-            pltpu.SemaphoreType.DMA((len(jobs),)),
-        ],
+        out_shape=jax.ShapeDtypeStruct((parts, n_dp, terms.shape[0], terms.shape[1] // parts), BF16),
+        in_specs=[pl.BlockSpec(memory_space=pl.ANY)],
+        out_specs=pl.BlockSpec(memory_space=pl.ANY),
+        scratch_shapes=scratch
+        + [pltpu.SemaphoreType.DMA((copies,)), pltpu.SemaphoreType.DMA((copies,))],
         compiler_params=pltpu.CompilerParams(
             collective_id=collective_id, has_side_effects=True, vmem_limit_bytes=VMEM_LIMIT
         ),
         cost_estimate=FREE,
         name=name,
-    )(terms, *parts)
+    )(terms)
+
+
+def set_sums(set_ids, sources, acc_shape, add, outs, put, groups, name):
+    n_src = len(sources)
+    count = set_ids.shape[0]
+
+    def kernel(ids_ref, *refs):
+        src_refs, out_refs, acc = refs[:n_src], refs[n_src:-1], refs[-1]
+        k = pl.program_id(0)
+        acc[...] = jnp.zeros_like(acc)
+        for s in range(count):
+
+            @pl.when(ids_ref[s] == k)
+            def _(s=s):
+                add(s, src_refs, acc)
+
+        put(acc, out_refs)
+
+    out_specs = []
+    for before, after in outs:
+        lead = len(before)
+        block = tuple(before) + (1,) + tuple(after)
+        out_specs.append(
+            pl.BlockSpec(
+                block, lambda k, ids, lead=lead, n=len(after): (0,) * lead + (k,) + (0,) * n
+            )
+        )
+    return pl.pallas_call(
+        kernel,
+        grid_spec=pltpu.PrefetchScalarGridSpec(
+            num_scalar_prefetch=1,
+            grid=(groups,),
+            in_specs=[
+                pl.BlockSpec(a.shape, lambda k, ids, n=a.ndim: (0,) * n) for a in sources
+            ],
+            out_specs=out_specs,
+            scratch_shapes=[pltpu.VMEM(acc_shape, F32)],
+        ),
+        out_shape=[
+            jax.ShapeDtypeStruct(tuple(before) + (groups,) + tuple(after), F32)
+            for before, after in outs
+        ],
+        compiler_params=pltpu.CompilerParams(vmem_limit_bytes=VMEM_LIMIT),
+        cost_estimate=FREE,
+        name=name,
+    )(set_ids, *sources)
 
 
 def split_three(value):
@@ -619,21 +801,31 @@
 
 
 def ridden_call(
-    kernel, grid, arrays, in_specs, out_shape, out_specs, scratch, riders, ridden, carried, fresh, name, collective_id
+    kernel,
+    grid,
+    arrays,
+    in_specs,
+    out_shape,
+    out_specs,
+    scratch,
+    riders,
+    ridden,
+    carried,
+    fresh,
+    name,
+    collective_id,
 ):
     steps = distinct(rider_steps(riders))
     count = rider_count(riders)
     n_in, n_out = len(arrays), len(out_shape)
     n_ride_in = len(ridden) + len(carried)
     n_ride_out = len(ridden) + len(fresh)
-
     def body(*refs):
         own_in, rest = refs[:n_in], refs[n_in:]
         ride_in, rest = rest[:n_ride_in], rest[n_ride_in:]
         own_out, rest = rest[:n_out], rest[n_out:]
         ride_out, rest = rest[:n_ride_out], rest[n_ride_out:]
         send_sems, recv_sems = rest[-2:]
-        own_scratch = rest[:-2]
         links = Links(send_sems, recv_sems)
         ride = Riders(links, riders, ride_in, ride_out)
 
@@ -642,7 +834,7 @@
             links.greet(steps)
             ride.start()
 
-        kernel(*own_in, *own_out, *own_scratch)
+        kernel(*own_in, *own_out, *rest[:-2])
 
         @pl.when(pl.program_id(0) == grid[0] - 1)
         def _():
@@ -707,7 +899,7 @@
     )
 
 
-def attend_back(q_aug, kv, heads_out, heads_grad, rope, pe_aug, riders, carried, fresh):
+def attend_back(q_aug, kv, heads_out, heads_grad, rope, pe_aug, riders, ridden, carried, fresh):
     length = q_aug.shape[0]
     heads = q_aug.shape[1] // HEAD_LANES
     per_step = 2 if heads % 2 == 0 else 1
@@ -724,23 +916,21 @@
     ]
     out_specs = [columns, columns, pl.BlockSpec((length, HEAD_LANES), lambda h: (0, 0))]
     scratch = [pltpu.VMEM((length, HEAD_LANES), F32), pltpu.VMEM((length, HEAD_LANES), F32)]
-    kernel = functools.partial(attn_bwd_kernel, per_step)
-    grid = (heads // per_step,)
-    if riders:
-        return ridden_call(
-            kernel, grid, arrays, in_specs, out_shape, out_specs, scratch, riders, [], carried, fresh, "attend_back", 11
-        )
-    return pl.pallas_call(
-        kernel,
-        grid=grid,
-        in_specs=in_specs,
-        out_specs=out_specs,
-        out_shape=out_shape,
-        scratch_shapes=scratch,
-        compiler_params=pltpu.CompilerParams(vmem_limit_bytes=VMEM_LIMIT),
-        cost_estimate=FREE,
-        name="attend_back",
-    )(*arrays)
+    return ridden_call(
+        functools.partial(attn_bwd_kernel, per_step),
+        (heads // per_step,),
+        arrays,
+        in_specs,
+        out_shape,
+        out_specs,
+        scratch,
+        riders,
+        ridden,
+        carried,
+        fresh,
+        "attend_back",
+        11,
+    )
 
 
 def gate_middle(gate, up, hid_grad):
@@ -763,7 +953,7 @@
     return hid, both
 
 
-def remote_ffn(x_own, g_all, weights, mains, tail, tail_wide, slow, block_of, riders, name, collective_id):
+def remote_ffn(x_own, g_all, weights, extras, mains, tail, tail_wide, slow, block_of, riders, name, collective_id):
     rows, aug = x_own.shape
     total = g_all.shape[0]
     blocks = total // rows
@@ -789,7 +979,8 @@
     steps = distinct([core_step] + slow + rider_steps(riders))
 
     def kernel(x_ref, g_ref, *refs):
-        refs = refs[chunks:]
+        e_refs = refs[chunks : 2 * chunks]
+        refs = refs[2 * chunks :]
         codes_ref = refs[0]
         grad_refs = refs[1 : 1 + chunks]
         hid_refs = refs[1 + chunks : 1 + 2 * chunks]
@@ -800,9 +991,18 @@
         links = Links(send_sems, recv_sems)
         place = links.place
         fetch = [
-            pltpu.make_async_copy(w_refs[c], w_held[c], w_sems.at[c]) for c in range(chunks)
+            pltpu.make_async_copy(w_refs[c], w_held[c].at[pl.ds(0, width)], w_sems.at[c])
+            for c in range(chunks)
+        ]
+        fetch_extra = [
+            pltpu.make_async_copy(
+                e_refs[c], w_held[c].at[pl.ds(width, CODE_LANES)], w_sems.at[chunks + c]
+            )
+            for c in range(chunks)
         ]
         fetch[0].start()
+        for copy in fetch_extra:
+            copy.start()
         links.greet(steps)
 
         def landing(key):
@@ -848,6 +1048,8 @@
             lax.fori_loop(0, blocks, one, 0)
 
         fetch[0].wait()
+        for copy in fetch_extra:
+            copy.wait()
 
         def back_first(b, g_rows):
             back_held[b] = dot_nn(g_rows, w_held[0][:, gu[0] :])
@@ -916,7 +1118,7 @@
     vmem_spec = pl.BlockSpec(memory_space=pltpu.VMEM)
     outs = pl.pallas_call(
         kernel,
-        in_specs=[vmem_spec, any_spec] + [any_spec] * chunks,
+        in_specs=[vmem_spec, any_spec] + [any_spec] * (2 * chunks),
         out_specs=[vmem_spec] * (1 + 2 * chunks) + [any_spec] * chunks,
         out_shape=[jax.ShapeDtypeStruct((total, CODE_LANES), BF16)]
         + [jax.ShapeDtypeStruct((total, g), BF16) for g in gu]
@@ -927,11 +1129,11 @@
             pltpu.VMEM((blocks, rows, mains[0]), F32),
             pltpu.VMEM((2, rows, aug), BF16),
         ]
-        + [pltpu.VMEM(w.shape, BF16) for w in weights]
+        + [pltpu.VMEM((aug, w.shape[1]), BF16) for w in weights]
         + [
             pltpu.SemaphoreType.DMA((count,)),
             pltpu.SemaphoreType.DMA((count,)),
-            pltpu.SemaphoreType.DMA((chunks,)),
+            pltpu.SemaphoreType.DMA((2 * chunks,)),
             pltpu.SemaphoreType.DMA((2,)),
         ],
         input_output_aliases={2 + c: 1 + 2 * chunks + c for c in range(chunks)},
@@ -940,7 +1142,7 @@
         ),
         cost_estimate=FREE,
         name=name,
-    )(x_own, g_all, *weights)
+    )(x_own, g_all, *weights, *extras)
     return (
         outs[0],
         outs[1 : 1 + chunks],
@@ -949,8 +1151,11 @@
     )
 
 
-def remote_ffn_back(grads, hids, weights, mains, tail_wide, keys, ways, block_of, rows, name, collective_id):
-    aug = weights[0].shape[0]
+def remote_ffn_back(
+    grads, hids, weights, extras, x_codes, g_codes, mains, tail_wide, keys, ways, block_of, rows, name, collective_id
+):
+    width = weights[0].shape[0]
+    aug = width + CODE_LANES
     chunks = len(mains)
     tails = [0] * (chunks - 1) + [tail_wide]
     gu = [2 * m + w for m, w in zip(mains, tails)]
@@ -962,26 +1167,42 @@
     later_slot = {entry: n for n, entry in enumerate(later)}
     steps = distinct([core_step] + ways[0])
     count = 2 * len(keys) + len(plan)
-    operands = list(grads) + list(hids) + list(weights)
+    operands = list(grads) + list(hids) + list(weights) + [x_codes, g_codes]
+    shapes = [o.shape for o in operands]
+    for c in range(chunks):
+        shapes[2 * chunks + c] = (aug, weights[c].shape[1])
 
     def kernel(*refs):
         n_in = len(operands)
-        in_refs = refs[:n_in]
+        in_refs, e_refs, refs = refs[:n_in], refs[n_in : n_in + chunks], refs[n_in + chunks :]
+        refs = in_refs + refs
         out_ref, terms_ref = refs[n_in : n_in + 2]
-        held = refs[n_in + 2 : 2 * n_in + 2]
-        rest = refs[2 * n_in + 2 :]
+        gu_refs = refs[n_in + 2 : n_in + 2 + chunks]
+        down_refs = refs[n_in + 2 + chunks : n_in + 2 + 2 * chunks]
+        held = refs[n_in + 2 + 2 * chunks : 2 * n_in + 2 + 2 * chunks]
+        rest = refs[2 * n_in + 2 + 2 * chunks :]
         core_out, core_in, chip, hop_out, hop_in, stage, send_sems, recv_sems, in_sems, out_sems, free = rest
-        g_held, h_held, w_held = held[:chunks], held[chunks : 2 * chunks], held[2 * chunks :]
+        g_held, h_held = held[:chunks], held[chunks : 2 * chunks]
+        w_held = held[2 * chunks : 3 * chunks]
         started = []
-        order = [n for c in range(chunks) for n in (c, 2 * chunks + c)] + list(range(chunks, 2 * chunks))
+        order = [n for c in range(chunks) for n in (2 * chunks + c, c)]
+        order += list(range(chunks, 2 * chunks)) + [3 * chunks, 3 * chunks + 1]
         for n in order:
-            copy = pltpu.make_async_copy(in_refs[n], held[n], in_sems.at[n])
+            is_weight = 2 * chunks <= n < 3 * chunks
+            to = held[n].at[pl.ds(0, width)] if is_weight else held[n]
+            copy = pltpu.make_async_copy(in_refs[n], to, in_sems.at[n])
+            copy.start()
+            started.append(copy)
+        for c in range(chunks):
+            copy = pltpu.make_async_copy(
+                e_refs[c], w_held[c].at[pl.ds(width, CODE_LANES)], in_sems.at[n_in + c]
+            )
             copy.start()
             started.append(copy)
         links = Links(send_sems, recv_sems)
         place = links.place
         links.greet(steps)
-        for copy in started:
+        for copy in started[: 2 * chunks] + started[n_in:]:
             copy.wait()
         came = {}
 
@@ -1047,6 +1268,8 @@
             free, inc=1, device_id=links.peer(core_step), device_id_type=pl.DeviceIdType.MESH
         )
         pl.semaphore_wait(free, 1)
+        for copy in started[2 * chunks : n_in]:
+            copy.wait()
         stored = []
         for i, key in enumerate(keys):
             crossing = cross(i, down_term((key[0], key[1] ^ 1)))
@@ -1069,6 +1292,10 @@
                                     hop_in.at[slot[entry]],
                                     ways[w][k],
                                 )
+        x_held, gc_held = held[3 * chunks :]
+        for c in range(chunks):
+            gu_refs[c][...] = dot_tn(x_held[...], g_held[c][...])
+            down_refs[c][...] = dot_tn(gc_held[...], h_held[c][...])
         for w in range(len(ways)):
             out_ref[w * part : (w + 1) * part, :] = so_far(w, len(ways[w]), (0, 0))
         for copy in stored[max(0, len(keys) - 2) :]:
@@ -1084,10 +1311,13 @@
         out_shape=[
             jax.ShapeDtypeStruct((rows, aug), F32),
             jax.ShapeDtypeStruct((len(keys), rows, aug), BF16),
-        ],
-        in_specs=[any_spec] * len(operands),
-        out_specs=[pl.BlockSpec(memory_space=pltpu.VMEM), any_spec],
-        scratch_shapes=[pltpu.VMEM(o.shape, o.dtype) for o in operands]
+        ]
+        + [jax.ShapeDtypeStruct((CODE_LANES, g.shape[1]), F32) for g in grads]
+        + [jax.ShapeDtypeStruct((CODE_LANES, h.shape[1]), F32) for h in hids],
+        in_specs=[any_spec] * (len(operands) + chunks),
+        out_specs=[pl.BlockSpec(memory_space=pltpu.VMEM), any_spec]
+        + [pl.BlockSpec(memory_space=pltpu.VMEM)] * (2 * chunks),
+        scratch_shapes=[pltpu.VMEM(n, o.dtype) for n, o in zip(shapes, operands)]
         + [
             pltpu.VMEM((2, rows, aug), BF16),
             pltpu.VMEM((len(keys), rows, aug), BF16),
@@ -1097,7 +1327,7 @@
             pltpu.VMEM((2, rows, aug), BF16),
             pltpu.SemaphoreType.DMA((count,)),
             pltpu.SemaphoreType.DMA((count,)),
-            pltpu.SemaphoreType.DMA((len(operands),)),
+            pltpu.SemaphoreType.DMA((len(operands) + chunks,)),
             pltpu.SemaphoreType.DMA((len(keys),)),
             pltpu.SemaphoreType.REGULAR,
         ],
@@ -1106,7 +1336,59 @@
         ),
         cost_estimate=FREE,
         name=name,
-    )(*operands)
+    )(*operands, *extras)
+
+
+def ffn_extras(places, gate_up_out, down_in, mains, tail, tail_wide):
+    half = down_in.shape[2] // 2
+    chunks = len(mains)
+    tails = [0] * (chunks - 1) + [tail_wide]
+    wide = [3 * m + w for m, w in zip(mains, tails)]
+
+    def kernel(places_ref, gu_ref, down_ref, *outs):
+        for out in outs:
+            out[...] = jnp.zeros_like(out)
+        lower = places_ref[2] == 0
+        for p in range(2):
+            which = places_ref[p]
+
+            def half_of(value):
+                return jnp.where(lower, value[:, :half], value[:, half:])
+
+            parts = [
+                half_of(gu_ref[0, which]) * 2,
+                half_of(gu_ref[1, which]) * 2,
+                half_of(down_ref[which]),
+            ]
+            for kind, value in enumerate(parts):
+                top = 2 * RANK * p + (RANK if kind == 1 else 0)
+                at_rows = slice(top, top + RANK)
+                begin = 0
+                for c in range(chunks):
+                    main = mains[c]
+                    at = [0, main + tails[c], 2 * main + tails[c]][kind]
+                    outs[c][at_rows, at : at + main] = value[:, begin : begin + main]
+                    begin += main
+                if tail:
+                    at = mains[-1] + kind * tail
+                    outs[-1][at_rows, at : at + tail] = value[:, begin:]
+
+    return pl.pallas_call(
+        kernel,
+        grid_spec=pltpu.PrefetchScalarGridSpec(
+            num_scalar_prefetch=1,
+            grid=(1,),
+            in_specs=[
+                pl.BlockSpec(a.shape, lambda i, ids, n=a.ndim: (0,) * n)
+                for a in (gate_up_out, down_in)
+            ],
+            out_specs=[pl.BlockSpec((CODE_LANES, w), lambda i, ids: (0, 0)) for w in wide],
+        ),
+        out_shape=[jax.ShapeDtypeStruct((CODE_LANES, w), BF16) for w in wide],
+        compiler_params=pltpu.CompilerParams(vmem_limit_bytes=VMEM_LIMIT),
+        cost_estimate=FREE,
+        name="ffn_extras",
+    )(places, gate_up_out, down_in)
 
 
 def per_device(
@@ -1280,10 +1562,24 @@
     down_shard = query_down_matrix.shape[0]
     shares = n_t if down_shard % (16 * n_t) == 0 else 2
     share_rows = down_shard // shares
-    down_both = jnp.concatenate([query_down_matrix, keyvalue_down_matrix], axis=1)
+    down_wide = -(-(q_lat + kv_all) // 128) * 128
+    down_pad = down_wide - q_lat - kv_all
+    down_both = jnp.concatenate(
+        [query_down_matrix, keyvalue_down_matrix, jnp.zeros((down_shard, down_pad), BF16)], axis=1
+    )
     down_mine = lax.dynamic_index_in_dim(
-        down_both.reshape(shares, share_rows, q_lat + kv_all), lax.rem(t, shares), 0, keepdims=False
-    )
+        down_both.reshape(shares, share_rows, down_wide), lax.rem(t, shares), 0, keepdims=False
+    )
+    down_in = jnp.concatenate([qa_in, kva_in], axis=0)
+    down_b_rows = jnp.concatenate(
+        [
+            jnp.pad(qa_out, ((0, 0), (0, down_wide - q_lat))),
+            jnp.pad(kva_out, ((0, 0), (q_lat, down_pad))),
+        ],
+        axis=0,
+    )
+    qb_in_wide = jnp.pad(qb_in, ((0, CODE_LANES - RANK), (0, 0)))
+    kvb_in_wide = jnp.pad(kvb_in, ((RANK, CODE_LANES - 2 * RANK), (0, 0)))
     qb_rows, kvb_rows = query_up_matrix.shape[0], keyvalue_up_matrix.shape[0]
     head_q = PLAIN_HEAD_DIM + ROTARY_DIM
 
@@ -1329,93 +1625,167 @@
                     pl.ds(pl.multiple_of(group_block(dd, tt) * rows + at, 16), half_rows),
                 ),
                 steps=steps + t_core,
+                group="rows",
             )
             for at, steps in zip((0, half_rows), ways)
         ]
 
     group_a = t_slow + [("dp", pair)]
     group_b = [("dp", pair)] + t_slow
+    pe_at = q_lat + 2 * RANK
+    lat_wide = q_lat + CODE_LANES + kv_lat
+
+    def token_jobs(src, out, parts, group=0):
+        count = rows // parts
+        return [
+            dict(
+                src=src,
+                src_at=pl.ds(n * count, count),
+                out=out,
+                out_at=lambda dd, tt, n=n: (
+                    pl.ds(pl.multiple_of(tt * rows + n * count, 16), count),
+                ),
+                steps=t_slow + t_core,
+                group=group,
+            )
+            for n in range(parts)
+        ]
+
+    def latent_work(refs):
+        x_ref, norm_ref, q_norm_ref, kv_norm_ref, in_ref, b_ref, qb_ref, kvb_ref = refs[12:20]
+        latent_ref, codes_ref, w_ref, own_ref = refs[20:24]
+        x_f = x_ref[...].astype(F32)
+        scale = lax.rsqrt(jnp.mean(x_f * x_f, axis=-1, keepdims=True) + NORM_EPS)
+        h_rows = narrow(x_f * scale * norm_ref[...])
+        codes = narrow(dot_nt(h_rows, in_ref[...]))
+        latent = dot_nn(h_rows, w_ref[...]) + ADAPT_SCALE * dot_nn(codes, b_ref[...])
+        latent_ref[...] = latent
+        codes_ref[...] = codes
+        q_part = latent[:, :q_lat]
+        kv_part = latent[:, q_lat : q_lat + kv_lat]
+        q_scale = lax.rsqrt(jnp.mean(q_part * q_part, axis=-1, keepdims=True) + NORM_EPS)
+        kv_scale = lax.rsqrt(jnp.mean(kv_part * kv_part, axis=-1, keepdims=True) + NORM_EPS)
+        q_in = narrow(q_part * q_scale * q_norm_ref[...])
+        kv_in = narrow(kv_part * kv_scale * kv_norm_ref[...])
+        own_ref[:, :q_lat] = q_in
+        own_ref[:, q_lat + CODE_LANES :] = kv_in
+        code_block = dot_nt(q_in, qb_ref[...]) + dot_nt(kv_in, kvb_ref[...])
+        pe_block = pltpu.roll(latent[:, q_lat + kv_lat :], 2 * RANK, 1)
+        lane = lax.broadcasted_iota(jnp.int32, code_block.shape, 1)
+        own_ref[:, q_lat : q_lat + CODE_LANES] = narrow(
+            jnp.where(lane < 2 * RANK, code_block, pe_block)
+        )
+
+    down_steps = outer_first + (t_slow if shares == n_t else []) + t_core
+    n_start_outs = 9
+    latent_at, w_at, lat_own_at = n_start_outs, n_start_outs + 2, n_start_outs + 3
+    n_start_sources = 20
     jobs = [
         dict(
             src=0,
-            out=0,
-            out_at=lambda dd, tt: (dd, lax.rem(tt, shares)),
-            steps=outer_first + (t_slow if shares == n_t else []) + t_core,
+            out=w_at,
+            out_at=lambda dd, tt: (
+                pl.ds(
+                    pl.multiple_of(dd * down_shard + lax.rem(tt, shares) * share_rows, 16), share_rows
+                ),
+            ),
+            steps=down_steps,
+            group="down",
+        ),
+        dict(src=1, out=1, out_at=rows_at(0, qb_rows, qb_rows), steps=outer_first, group="up"),
+        dict(src=2, out=2, out_at=rows_at(CODE_LANES, kvb_rows, kvb_rows), steps=outer_first, group="up"),
+        dict(src=8, out=5, out_at=lambda dd, tt: (dd,), steps=outer_first, group="up"),
+        dict(src=3, out=3, out_at=rows_at(0, out_rows, out_rows), steps=outer_first, group="out"),
+    ]
+    low_steps = [("dp", b) for b in reversed(low_bits)]
+    for src, out in ((9, 6), (11, 7)):
+        jobs.append(
+            dict(
+                src=src,
+                out=out,
+                out_at=rows_at(0, ffn_rows_each, ffn_rows_each),
+                steps=low_steps,
+                group="own",
+            )
         )
-    ]
-    jobs += [
-        dict(src=1, out=1, out_at=rows_at(0, qb_rows, qb_rows), steps=outer_first),
-        dict(src=2, out=2, out_at=rows_at(CODE_LANES, kvb_rows, kvb_rows), steps=outer_first),
-        dict(src=3, out=3, out_at=rows_at(0, out_rows, out_rows), steps=outer_first),
-    ]
     jobs += group_jobs(4, 4, (group_b, group_b))
-    jobs.append(dict(src=8, out=5, out_at=lambda dd, tt: (dd,), steps=outer_first))
+    jobs += token_jobs(n_start_sources + 3, 8, 2, "latents")
     set_mark = jnp.full((16, 128), sequence_adapter_index[0].astype(F32)).astype(BF16)
-    w_down, w_q, w_kv, w_out, g_all, set_marks, w_ffn0, w_ffn1 = remote_gather(
-        [
-            down_mine,
-            pad_heads(query_up_matrix),
-            keyvalue_up_matrix,
-            output_matrix.T,
-            g_own,
-            q_aug_rows,
-            kv_aug_rows,
-            out_extra,
-            set_mark,
-            ffn_mine[0],
-            ffn_other[0],
-            ffn_mine[1],
-        ],
-        jobs,
-        [
-            (5, 1, lambda dd, tt: (pl.ds(q_lat, CODE_LANES),)),
-            (6, 2, lambda dd, tt: (pl.ds(0, CODE_LANES),)),
-            (7, 3, lambda dd, tt: (pl.ds(width, CODE_LANES),)),
-            (9, 6, rows_at(0, ffn_rows_each, ffn_rows_each)),
-            (11, 7, rows_at(0, ffn_rows_each, ffn_rows_each)),
-        ],
-        [
-            (n_dp, shares, share_rows, q_lat + kv_all),
-            (q_lat + CODE_LANES, heads * HEAD_LANES),
-            (CODE_LANES + kv_lat, heads * HEAD_LANES),
-            (aug, heads * VALUE_HEAD_DIM),
-            (2 * n_t * rows, aug),
-            (n_dp, 16, 128),
-            (aug, ffn_wide[0]),
-            (aug, ffn_wide[1]),
-        ],
-        "gather_weights",
-        1,
-        riders=[ride_one(6, 9, 10, 0, ffn_rows_each)],
-        rider_round=1,
+    w_down, w_q, w_kv, w_out, g_all, set_marks, w_ffn0, w_ffn1, lat_all, latent, down_codes_in = (
+        remote_gather(
+            [
+                down_mine,
+                pad_heads(query_up_matrix),
+                keyvalue_up_matrix,
+                output_matrix.T,
+                g_own,
+                q_aug_rows,
+                kv_aug_rows,
+                out_extra,
+                set_mark,
+                ffn_mine[0],
+                ffn_other[0],
+                ffn_mine[1],
+                inputs[0],
+                attention_norm_gain[None],
+                query_latent_gain[None],
+                keyvalue_latent_gain[None],
+                down_in,
+                down_b_rows,
+                qb_in_wide,
+                kvb_in_wide,
+            ],
+            jobs,
+            [
+                (5, 1, lambda dd, tt: (pl.ds(q_lat, CODE_LANES),)),
+                (6, 2, lambda dd, tt: (pl.ds(0, CODE_LANES),)),
+                (7, 3, lambda dd, tt: (pl.ds(width, CODE_LANES),)),
+            ],
+            [
+                (width, down_wide),
+                (q_lat + CODE_LANES, heads * HEAD_LANES),
+                (CODE_LANES + kv_lat, heads * HEAD_LANES),
+                (aug, heads * VALUE_HEAD_DIM),
+                (2 * n_t * rows, aug),
+                (n_dp, 16, 128),
+                (width, ffn_wide[0]),
+                (width, ffn_wide[1]),
+                (length, lat_wide),
+            ],
+            "gather_start",
+            1,
+            riders=[ride_one(6, 9, 10, 0, ffn_rows_each)],
+            order=["down", "up", "out", "down", "up", "down", "own", "out", "rows", "down"]
+            + ["up", "out", "ride"]
+            + ["down"] * (len(down_steps) - 4)
+            + [("all", "down"), "work", "latents", "rows"]
+            + ["latents"] * len(t_slow)
+            + ["rows"],
+            near_outs=[
+                jax.ShapeDtypeStruct((rows, down_wide), F32),
+                jax.ShapeDtypeStruct((rows, 2 * RANK), BF16),
+            ],
+            scratch=[
+                jax.ShapeDtypeStruct((width, down_wide), BF16),
+                jax.ShapeDtypeStruct((rows, lat_wide), BF16),
+            ],
+            work=latent_work,
+            late=[(n_start_sources + 2, 0)],
+        )
     )
     set_all = set_marks[:, 0, 0].astype(jnp.int32)
     set_peer = lax.dynamic_index_in_dim(set_all, jnp.bitwise_xor(d, pair), 0, keepdims=False)
     set_even = jnp.where(first, set_own, set_peer)
     set_odd = jnp.where(first, set_peer, set_own)
-    w_down = w_down.reshape(width, q_lat + kv_all)
-    zero_codes = jnp.zeros((RANK, half), BF16)
-
-    def half_of(value):
-        left, right = halves(value)
-        return jnp.where(first, left, right)
-
-    extra_parts = []
-    for which in (set_even, set_odd):
-        gate_b = half_of(pick(gate_up_adapter_out[0], which)) * 2
-        up_b = half_of(pick(gate_up_adapter_out[1], which)) * 2
-        down_a_t = half_of(pick(turned(down_adapter_in), which))
-        extra_parts.append((gate_b, up_b, down_a_t))
-    ffn_extra = []
-    for chunk in range(chunks):
-        extra = []
-        for gate_b, up_b, down_a_t in extra_parts:
-            extra.append(columns(gate_b, zero_codes, down_a_t, chunk))
-            extra.append(columns(zero_codes, up_b, zero_codes, chunk))
-        extra.append(jnp.zeros((CODE_LANES - 4 * RANK, extra[0].shape[1]), BF16))
-        ffn_extra.append(jnp.concatenate(extra, axis=0))
-    cut_a = ffn_rows_each // 64 * 16
-    cut_b = ffn_rows_each // 48 * 32
+    ffn_extra = ffn_extras(
+        jnp.stack([set_even, set_odd, zl]).astype(jnp.int32),
+        gate_up_adapter_out,
+        turned(down_adapter_in),
+        mains,
+        tail,
+        tail_wide,
+    )
+    cut_a = ffn_rows_each // 48 * 16
 
     cos_part, sin_part = rope_tables(document_numbers)
     zeros_l = jnp.zeros((length, PLAIN_HEAD_DIM), F32)
@@ -1440,67 +1810,12 @@
     residual = inputs[0].astype(F32)
     attn_normed, attn_scale = normalize(residual, attention_norm_gain)
     attn_rows = narrow(attn_normed)
-    down_in = jnp.concatenate([qa_in, kva_in], axis=0)
-    down_codes_in = narrow(dot_nt(attn_rows, down_in))
-    down_b_rows = jnp.concatenate(
-        [
-            jnp.pad(qa_out, ((0, 0), (0, kv_all))),
-            jnp.pad(kva_out, ((0, 0), (q_lat, 0))),
-        ],
-        axis=0,
-    )
-    latent = dot_nn(attn_rows, w_down) + ADAPT_SCALE * dot_nn(down_codes_in, down_b_rows)
     q_latent = latent[:, :q_lat]
     kv_latent = latent[:, q_lat : q_lat + kv_lat]
     q_normed, q_scale = normalize(q_latent, query_latent_gain)
     kv_normed, kv_scale = normalize(kv_latent, keyvalue_latent_gain)
     q_input = narrow(q_normed)
     kv_input = narrow(kv_normed)
-    pe_input = narrow(latent[:, q_lat + kv_lat :])
-    qb_codes = narrow(dot_nt(q_input, qb_in))
-    kvb_codes = narrow(dot_nt(kv_input, kvb_in))
-    pe_at = q_lat + 2 * RANK
-    lat_own = jnp.concatenate(
-        [
-            q_input,
-            qb_codes,
-            kvb_codes,
-            pe_input,
-            jnp.zeros((rows, CODE_LANES - 2 * RANK - ROTARY_DIM), BF16),
-            kv_input,
-        ],
-        axis=1,
-    )
-
-    def token_jobs(src, out, parts):
-        count = rows // parts
-        return [
-            dict(
-                src=src,
-                src_at=pl.ds(n * count, count),
-                out=out,
-                out_at=lambda dd, tt, n=n: (
-                    pl.ds(pl.multiple_of(tt * rows + n * count, 16), count),
-                ),
-                steps=t_slow + t_core,
-            )
-            for n in range(parts)
-        ]
-
-    lat_all, w_ffn0, w_ffn1 = remote_gather(
-        [lat_own, ffn_extra[0], ffn_extra[1], w_ffn0, w_ffn1, ffn_mine[1], ffn_other[1]],
-        token_jobs(0, 0, 2),
-        [
-            (1, 1, lambda dd, tt: (pl.ds(width, CODE_LANES),)),
-            (2, 2, lambda dd, tt: (pl.ds(width, CODE_LANES),)),
-        ],
-        [(length, lat_own.shape[1]), (aug, ffn_wide[0]), (aug, ffn_wide[1])],
-        "gather_latents",
-        2,
-        riders=[ride_two(1, 0), ride_one(2, 5, 6, 0, cut_a)],
-        aliases={3: 1, 4: 2},
-        distant=(5, 6),
-    )
     pe_rows = lat_all[:, pe_at : pe_at + ROTARY_DIM].astype(F32)
     pe_a, pe_b = pe_rows[:, : ROTARY_DIM // 2], pe_rows[:, ROTARY_DIM // 2 :]
     pe_aug = narrow(
@@ -1524,7 +1839,7 @@
         doc_q,
         q_lat + CODE_LANES,
         q_lat,
-        [ride_two(0, 1), ride_one(1, 2, 3, cut_a, cut_b - cut_a)],
+        [ride_two(0, 1), ride_one(1, 2, 3, 0, cut_a)],
         [w_ffn0, w_ffn1],
         [ffn_mine[1], ffn_other[1]],
     )
@@ -1548,7 +1863,7 @@
         "reduce_out",
         3,
         riders=[ride_two(0, z) for z in range(2, z_count)]
-        + [ride_one(1, 2, 3, cut_b, ffn_rows_each - cut_b)],
+        + [ride_one(1, 2, 3, cut_a, ffn_rows_each - cut_a)],
         ridden=[w_ffn0, w_ffn1],
         carried=[ffn_mine[1], ffn_other[1]],
     )
@@ -1571,20 +1886,24 @@
         x_own,
         g_all,
         [w_ffn0, w_ffn1],
+        ffn_extra,
         mains,
         tail,
         tail_wide,
         t_slow + [("dp", pair)],
         group_block_of,
-        [ride_two(1, z) for z in range(z_count)],
+        [ride_two(1, z) for z in range(1, z_count)],
         "feed_forward",
         4,
     )
     group_keys = [(p, r) for p in (pair, 0) for r in reversed(range(0, n_t, 2))]
-    ffn_in_sum, down_chip = remote_ffn_back(
+    ffn_in_sum, down_chip, *code_terms = remote_ffn_back(
         grads,
         hids,
         ffn_weights,
+        ffn_extra,
+        x_codes,
+        g_all[:, width:],
         mains,
         tail_wide,
         group_keys,
@@ -1605,23 +1924,70 @@
         [attn_grad, out_code_grad, jnp.zeros((rows, CODE_LANES - RANK), BF16)], axis=1
     )
 
+    def uncolumn(parts, at_tail, first_at):
+        out = [parts[c][:, first_at(c) : first_at(c) + mains[c]] for c in range(chunks)]
+        if tail:
+            at = mains[-1] + at_tail * tail
+            out.append(parts[-1][:, at : at + tail])
+        return jnp.concatenate(out, axis=1)
+
+    gu_b, down_at = code_terms[:chunks], code_terms[chunks:]
+    gate_b_all = ADAPT_SCALE * uncolumn(gu_b, 0, lambda c: 0)
+    up_b_all = ADAPT_SCALE * uncolumn(gu_b, 1, lambda c: gu_wide[c] - mains[c])
+    down_a_all = uncolumn(down_at, 2, lambda c: 0)
+    packed = []
+    for p in range(2):
+        at = 2 * RANK * p
+        packed += [
+            gate_b_all[at : at + RANK],
+            up_b_all[at + RANK : at + 2 * RANK],
+            down_a_all[at : at + RANK],
+        ]
+    hidden_own = narrow(jnp.concatenate(packed, axis=0))
+
+    def dp_job(src, out):
+        return dict(src=src, out=out, out_at=lambda dd, tt: (dd,), steps=outer_first)
+
     ride_down = n_t == 4
     sent = remote_gather(
-        [attn_grad_aug] + ([down_chip] if ride_down else []),
-        token_jobs(0, 0, 2),
+        [attn_grad_aug, hidden_own] + ([down_chip] if ride_down else []),
+        token_jobs(0, 0, 2)
+        + [
+            dict(
+                src=1,
+                out=1,
+                out_at=rows_at(0, hidden_own.shape[0], hidden_own.shape[0]),
+                steps=[("dp", high), ("dp", pair)],
+                group="hidden",
+            )
+        ],
         [],
-        [(length, aug)] + ([(rows, aug)] if ride_down else []),
+        [(length, aug), (n_dp * hidden_own.shape[0], hidden_own.shape[1])] + ([(rows, aug)] if ride_down else []),
         "gather_grad",
         6,
-        riders=[dict(kind="plain", src=1, src_at=0, out=1, step=("dp", pair))] if ride_down else [],
-        distant=(1,),
-    )
+        riders=[dict(kind="plain", src=2, src_at=0, out=2, step=("dp", pair))] if ride_down else [],
+        distant=(2,),
+        order=[0, "hidden", "hidden", "ride"],
+    )
+    hidden_terms = sent[1]
     grad_all = sent[0]
     heads_grad = narrow(dot_nn(grad_all, w_out))
     out_a = dot_tn(grad_all[:, width:], head_out)[:RANK]
+    hidden_ride = [
+        dict(
+            kind="two",
+            out=0,
+            z=z,
+            count=hidden_own.shape[0],
+            pair=pair,
+            high=high,
+            steps=[("dp", b) for b in reversed(low_bits)],
+        )
+        for z in range(z_count)
+    ]
     if ride_down:
-        down_far = narrow(down_chip[2].astype(F32) + sent[1].astype(F32))
-        dq, dkv, dpe, came_pair, came_y = attend_back(
+        down_far = narrow(down_chip[2].astype(F32) + sent[2].astype(F32))
+        dq, dkv, dpe, hidden_terms, came_pair, came_y = attend_back(
             q_aug,
             kv,
             head_out,
@@ -1629,15 +1995,18 @@
             rope,
             pe_aug,
             [
-                dict(kind="plain", src=0, src_at=1, out=0, step=("dp", pair)),
-                dict(kind="plain", src=1, src_at=None, out=1, step=("tensor", 2)),
-            ],
+                dict(kind="plain", src=1, src_at=1, out=1, step=("dp", pair)),
+                dict(kind="plain", src=2, src_at=None, out=2, step=("tensor", 2)),
+            ]
+            + hidden_ride,
+            [hidden_terms],
             [down_chip, down_far],
             [(rows, aug), (rows, aug)],
         )
-        ffn_out = down_chip[3].astype(F32) + came_pair.astype(F32) + came_y.astype(F32)
     else:
-        dq, dkv, dpe = attend_back(q_aug, kv, head_out, heads_grad, rope, pe_aug, [], [], [])
+        dq, dkv, dpe, hidden_terms = attend_back(
+            q_aug, kv, head_out, heads_grad, rope, pe_aug, hidden_ride, [hidden_terms], [], []
+        )
         places = n_t // 2
         ffn_out = down_chip[places:].astype(F32) + hop(down_chip[:places], ("dp", pair)).astype(F32)
         while places > 1:
@@ -1646,19 +2015,12 @@
                 F32
             )
         ffn_out = ffn_out[0]
-    down_codes = narrow(own_codes(ffn_out)[:, :RANK])
-    outputs = narrow(
-        middle + RESIDUAL * (ffn_out[:, :width] + ADAPT_SCALE * dot_nn(down_codes, down_out))
-    )
-
     pe_g = dpe[:, PLAIN_HEAD_DIM : PLAIN_HEAD_DIM + ROTARY_DIM]
     pe_ga, pe_gb = pe_g[:, : ROTARY_DIM // 2], pe_g[:, ROTARY_DIM // 2 :]
     pe_grad = jnp.concatenate(
         [pe_ga * cos_part + pe_gb * sin_part, pe_gb * cos_part - pe_ga * sin_part], axis=1
     )
     pe_padded = jnp.pad(pe_grad, ((0, 0), (2 * RANK, CODE_LANES - 2 * RANK - ROTARY_DIM)))
-    lat_wide = q_lat + CODE_LANES + kv_lat
-
     def latent_term(held, place, key):
         at = token_rows(key, place)
         from_q = dot_nt(held[0][at, :], held[2][...])
@@ -1672,8 +2034,12 @@
             axis=1,
         )
 
+    lat_codes = lat_all[:, q_lat : q_lat + CODE_LANES]
+    qb_b = ADAPT_SCALE * dot_tn(lat_codes, dq)[:RANK]
+    kvb_b = ADAPT_SCALE * dot_tn(lat_codes, dkv)[RANK : 2 * RANK]
+    head_own = narrow(jnp.concatenate([qb_b, kvb_b, out_a], axis=1))
     operands = [dq, dkv, w_q, w_kv, pe_padded]
-    (lat_sum,) = remote_reduce(
+    lat_sum, head_terms = remote_reduce(
         operands,
         [o.shape for o in operands],
         latent_term,
@@ -1683,6 +2049,19 @@
         lat_wide,
         "reduce_latents",
         7,
+        jobs=[dp_job(0, 0)],
+        job_sources=[head_own],
+        job_outs=[(n_dp,) + head_own.shape],
+    )
+    if ride_down:
+        ffn_out = (
+            down_chip[3].astype(F32)
+            + came_pair.astype(F32)
+            + came_y.astype(F32)
+        )
+    down_codes = narrow(own_codes(ffn_out)[:, :RANK])
+    outputs = narrow(
+        middle + RESIDUAL * (ffn_out[:, :width] + ADAPT_SCALE * dot_nn(down_codes, down_out))
     )
     qb_code_grad = narrow(lat_sum[:, q_lat : q_lat + RANK])
     kvb_code_grad = narrow(lat_sum[:, q_lat + RANK : q_lat + 2 * RANK])
@@ -1695,6 +2074,7 @@
                 normalize_back(q_latent, q_scale, query_latent_gain, q_norm_grad),
                 normalize_back(kv_latent, kv_scale, keyvalue_latent_gain, kv_norm_grad),
                 pe_sum,
+                jnp.zeros((rows, down_pad), F32),
             ],
             axis=1,
         )
@@ -1705,113 +2085,121 @@
         residual, attn_scale, attention_norm_gain, attn_in_grad
     )
 
-    onehot = narrow(set_all[:, None] == jnp.arange(group_count, dtype=jnp.int32)[None, :])
-
-    def to_sets(terms):
-        return jnp.einsum("sk,srn->krn", onehot, terms, preferred_element_type=F32)
-
-    def dp_job(src, out):
-        return dict(src=src, out=out, out_at=lambda dd, tt: (dd,), steps=outer_first)
-
-    t_steps = t_core + t_slow[::-1]
-
     gu_a = dot_tn(gu_code_grad, ffn_rows)
     out_b = ADAPT_SCALE * dot_tn(out_codes, attn_grad)
     down_b = ADAPT_SCALE * dot_tn(down_codes, ffn_grad)
-    early_terms = jnp.concatenate([gu_a, out_b, down_b], axis=0)
-
-    def uncolumn(parts, at_tail, first_at):
-        out = [parts[c][:, first_at(c) : first_at(c) + mains[c]] for c in range(chunks)]
-        if tail:
-            at = mains[-1] + at_tail * tail
-            out.append(parts[-1][:, at : at + tail])
-        return jnp.concatenate(out, axis=1)
-
-    g_codes = g_all[:, width:]
-    gu_b = [dot_tn(x_codes, g) for g in grads]
-    down_at = [dot_tn(g_codes, h) for h in hids]
-    gate_b_all = ADAPT_SCALE * uncolumn(gu_b, 0, lambda c: 0)
-    up_b_all = ADAPT_SCALE * uncolumn(gu_b, 1, lambda c: gu_wide[c] - mains[c])
-    down_a_all = uncolumn(down_at, 2, lambda c: 0)
-    packed = []
-    for p in range(2):
-        at = 2 * RANK * p
-        packed += [
-            gate_b_all[at : at + RANK],
-            up_b_all[at + RANK : at + 2 * RANK],
-            down_a_all[at : at + RANK],
-        ]
-    hidden_own = narrow(jnp.concatenate(packed, axis=0))
-    early, hidden_terms = remote_share(
-        narrow(early_terms),
-        [hidden_own],
-        [dp_job(1, 1)],
-        [(n_dp,) + early_terms.shape, (n_dp,) + hidden_own.shape],
-        n_t,
-        t_steps,
-        outer_first,
-        "share_early",
-        8,
-    )
-    hidden_terms = hidden_terms.reshape(2, 2, pair, 2, 3 * RANK, half)
-    hidden_terms = jnp.concatenate([hidden_terms[:, 0], hidden_terms[:, 1]], axis=-1)
-    hidden_terms = jnp.moveaxis(hidden_terms, 2, 1).reshape(n_dp, 3 * RANK, hidden)
-    hidden_sets = to_sets(hidden_terms)
-
-    lat_codes = lat_all[:, q_lat : q_lat + CODE_LANES]
-    qb_b = ADAPT_SCALE * dot_tn(lat_codes, dq)[:RANK]
-    kvb_b = ADAPT_SCALE * dot_tn(lat_codes, dkv)[RANK : 2 * RANK]
-    head_own = narrow(jnp.concatenate([qb_b, kvb_b, out_a], axis=1))
+    table_orders = [outer_first + t_slow + t_core, t_slow + outer_first + t_core]
     down_in_terms = dot_tn(code_grad, attn_rows)
     b_terms = ADAPT_SCALE * dot_tn(down_codes_in, latent_grad)
     qb_a = dot_tn(qb_code_grad, q_input)
     kvb_a = dot_tn(kvb_code_grad, kv_input)
-    small = jnp.concatenate([b_terms[:RANK, :q_lat], b_terms[RANK:, q_lat:], qb_a, kvb_a], axis=1)
-    small_wide = small.shape[1]
-    small = jnp.pad(small, ((0, RANK), (0, width - small_wide)))
-    late_terms = jnp.concatenate([down_in_terms, small], axis=0)
-    late, head_terms = remote_share(
-        narrow(late_terms),
-        [head_own],
-        [dp_job(1, 1)],
-        [(n_dp,) + late_terms.shape, (n_dp,) + head_own.shape],
+    small = [b_terms[:RANK, :q_lat], b_terms[RANK:, q_lat : q_lat + kv_all], qb_a, kvb_a]
+    small_at = [0]
+    padded = []
+    for value in small:
+        wide = -(-value.shape[1] // 128) * 128
+        padded.append(jnp.pad(value, ((0, 0), (0, wide - value.shape[1]))))
+        small_at.append(small_at[-1] + wide)
+    small_rows = jnp.pad(
+        jnp.concatenate(padded, axis=1), ((0, 0), (0, width - small_at[-1]))
+    )
+    shared = jnp.concatenate([gu_a, out_b, down_b, down_in_terms, small_rows], axis=0)
+    shared = jnp.pad(shared, ((0, -shared.shape[0] % (16 * n_t)), (0, 0)))
+    shared_terms = remote_share(
+        narrow(shared),
+        n_dp,
         n_t,
-        t_steps,
-        outer_first,
-        "share_late",
-        9,
-    )
-    head_sets = to_sets(head_terms)
+        table_orders,
+        "share",
+        8,
+    )
+    part_wide = width // 2
+
+    def add_shared(s, refs, acc):
+        for p in range(2):
+            at = slice(p * part_wide, (p + 1) * part_wide)
+            acc[:, at] += refs[0][p, s].astype(F32)
+
+    def put_shared(acc, outs):
+        outs[0][0, 0] = acc[:RANK, :]
+        outs[0][1, 0] = acc[RANK : 2 * RANK, :]
+        for n in range(4):
+            outs[1 + n][0] = acc[(2 + n) * RANK : (3 + n) * RANK, :]
+        for n, value in enumerate(small):
+            at = small_at[n]
+            outs[5 + n][0] = acc[6 * RANK : 7 * RANK, at : at + value.shape[1]]
+
+    shared_sets = set_sums(
+        set_all,
+        [shared_terms],
+        (shared.shape[0], width),
+        add_shared,
+        [((2,), (RANK, width))]
+        + [((), (RANK, width))] * 4
+        + [((), (RANK, value.shape[1])) for value in small],
+        put_shared,
+        group_count,
+        "sum_shared",
+    )
+    gu_a_t, out_b_grad, down_b_grad, qa_a_t, kva_a_t, qa_b_grad, kva_b_grad, qb_a_t, kvb_a_t = (
+        shared_sets
+    )
     wide = heads * HEAD_LANES
-    qb_b_grad = head_sets[:, :, :wide].reshape(group_count, RANK, heads, HEAD_LANES)[..., :head_q]
-    qb_b_grad = qb_b_grad.reshape(group_count, RANK, heads * head_q)
-    kvb_b_grad = head_sets[:, :, wide : 2 * wide]
-    out_a_grad = turned(head_sets[:, :, 2 * wide :])
-
-    early_sets = to_sets(early)
-    late_sets = to_sets(late)
-    gu_a_grad = jnp.stack(
-        [turned(early_sets[:, :RANK]), turned(early_sets[:, RANK : 2 * RANK])], axis=0
-    )
-    late_small = late_sets[:, 2 * RANK : 3 * RANK]
-    at = [0, q_lat, q_lat + kv_all, 2 * q_lat + kv_all, small_wide]
+    head_wide = head_own.shape[1]
+
+    def add_split(s, refs, acc):
+        which = (s // pair) % 2
+        base = s - which * pair
+        for h in range(2):
+            acc[: 3 * RANK, h * half : (h + 1) * half] += refs[0][
+                base + h * pair, which * 3 * RANK : (which + 1) * 3 * RANK, :
+            ].astype(F32)
+        acc[3 * RANK :, :head_wide] += refs[1][s].astype(F32)
+
+    def put_split(acc, outs):
+        outs[0][0, 0] = acc[:RANK, :hidden]
+        outs[0][1, 0] = acc[RANK : 2 * RANK, :hidden]
+        outs[1][0] = acc[2 * RANK : 3 * RANK, :hidden]
+        for h in range(heads):
+            outs[2][0, :, h * head_q : (h + 1) * head_q] = acc[
+                3 * RANK :, h * HEAD_LANES : h * HEAD_LANES + head_q
+            ]
+        outs[3][0] = acc[3 * RANK :, wide : 2 * wide]
+        outs[4][0] = acc[3 * RANK :, 2 * wide : head_wide]
+
+    gu_b_grad, down_a_t, qb_b_grad, kvb_b_grad, out_a_t = set_sums(
+        set_all,
+        [hidden_terms.reshape((n_dp,) + hidden_own.shape), head_terms],
+        (4 * RANK, max(hidden, -(-head_wide // 128) * 128)),
+        add_split,
+        [
+            ((2,), (RANK, hidden)),
+            ((), (RANK, hidden)),
+            ((), (RANK, heads * head_q)),
+            ((), (RANK, wide)),
+            ((), (RANK, head_wide - 2 * wide)),
+        ],
+        put_split,
+        group_count,
+        "sum_split",
+    )
     return (
         outputs[None],
         input_grad[None],
-        turned(late_sets[:, :RANK]),
-        late_small[:, :, at[0] : at[1]],
-        turned(late_sets[:, RANK : 2 * RANK]),
-        late_small[:, :, at[1] : at[2]],
-        turned(late_small[:, :, at[2] : at[3]]),
+        turned(qa_a_t),
+        qa_b_grad,
+        turned(kva_a_t),
+        kva_b_grad,
+        turned(qb_a_t),
         qb_b_grad,
-        turned(late_small[:, :, at[3] : at[4]]),
+        turned(kvb_a_t),
         kvb_b_grad,
-        out_a_grad,
-        early_sets[:, 2 * RANK : 3 * RANK],
-        gu_a_grad,
-        jnp.stack([hidden_sets[:, :RANK], hidden_sets[:, RANK : 2 * RANK]], axis=0),
-        turned(hidden_sets[:, 2 * RANK :]),
-        early_sets[:, 3 * RANK :],
+        turned(out_a_t),
+        out_b_grad,
+        turned(gu_a_t),
+        gu_b_grad,
+        turned(down_a_t),
+        down_b_grad,
     )
 
 

time: 782 us -> 702 us (0.90)
  Pallas kernels: 608 us -> 576 us
  local copies, waits for them, and re-layouts: 63 us -> 40.8 us
  matrix products: 58.7 us -> 37.9 us
    unnamed x173 -> x101, local copies, waits for them, and re-layouts: 30 us -> 5.73 us
    pallas_call x3 -> x5, Pallas kernels: 167 us -> 148 us  [the longest x1 87.3 us: remote_ffn(): pl.pallas_call(kernel, in_specs=[vmem_spec, any_spec] + [any_spec] * (2 *...]
    pallas_call x2, Pallas kernels: 78 us -> 67.7 us  [ridden_call(): pl.pallas_call(body, grid=grid, in_specs=list(in_specs) + [any_spec] * n_...]
    dot_general x4 -> x0, matrix products: 9.52 us -> none  [to_sets(): return jnp.einsum('sk,srn->krn', onehot, terms, preferred_element_type=F32)]
    pallas_call x3 -> x2, Pallas kernels: 225 us -> 219 us  [remote_gather(): pl.pallas_call(kernel, out_shape=[jax.ShapeDtypeStruct(o, BF16) for o in...]
    dot_general x9 -> x7, matrix products: 25.7 us -> 21.4 us  [dot_nn(): lax.dot_general(a, b, (((1,), (0,)), ((), ())), preferred_element_type=F32)]
where the time goes in v4:
time: 702 us; the launch traced here: 692 us
  Pallas kernels  576 us (82%)
  local copies, waits for them, and re-layouts  40.8 us (6%)
  matrix products  37.9 us (5%)
  other arithmetic  33.1 us (5%)
    pallas_call x2, Pallas kernels, remote_gather(): pl.pallas_call(kernel, out_shape=[jax.ShapeDtypeStruct(o, BF16) for o in...  219 us
    pallas_call x1, Pallas kernels, remote_ffn(): pl.pallas_call(kernel, in_specs=[vmem_spec, any_spec] + [any_spec] * (2 *...  87.3 us
    pallas_call x2, Pallas kernels, remote_reduce(): pl.pallas_call(kernel, out_shape=[jax.ShapeDtypeStruct((rows, wide), F32)...  71.7 us
    pallas_call x1, Pallas kernels, remote_ffn_back(): pl.pallas_call(kernel, out_shape=[jax.ShapeDtypeStruct((rows, aug), F32),...  70 us
    pallas_call x2, Pallas kernels, ridden_call(): pl.pallas_call(body, grid=grid, in_specs=list(in_specs) + [any_spec] * n_...  67.7 us
    pallas_call x1, Pallas kernels, remote_share(): pl.pallas_call(kernel, out_shape=jax.ShapeDtypeStruct((parts, n_dp, terms...  41.9 us
    dot_general x7, matrix products, dot_nn(): lax.dot_general(a, b, (((1,), (0,)), ((), ())), preferred_element_type=F32)  21.4 us
    pallas_call x2, Pallas kernels, set_sums(): pl.pallas_call(kernel, grid_spec=pltpu.PrefetchScalarGridSpec(num_scalar_...  15.5 us

profile of v4, /device:TPU:0, one launch (start us, length us, event | category | flops | bytes accessed | tf_op | source)
XLA Modules:
  0.0 691.7 jit_solution(3235753271913520465)
XLA Ops:
  31.0 171.1 %gather_start.1 = (bf16[2560,1152]{1,0:T(8,128)(2,1)}, bf16[896,1280]{1,0:T(8,128)(2,1)}, bf16[384,1280]{1,0:T(8,128)(2,1)}, bf16[2688,640]{1,0:T(8,128)(2,1)}, ...) custom-call(bf16[80,1152]{1,0:T(8,128)(2,1)} %dynamic-slice_bitcast_, ...), custom_call_target="tpu_custom_call" | custom-call | tf_op jit(solution)/shard_map/gather_start/pallas_call | solution.py:340
  204.2 2.3 fusion.58
  209.9 31.6 %attend.1 = (bf16[1024,1280]{1,0:T(8,128)(2,1)}, bf16[1024,1280]{1,0:T(8,128)(2,1)}, bf16[1024,640]{1,0:T(8,128)(2,1)}, bf16[2560,1536]{1,0:T(8,128)(2,1)}, bf16[2560,896]{1,0:T(8,128)(2,1)}) custom-call(bf16[1024,1152]{1,0:T(8,128)(2,1)} %get-tuple-element.75.refs_0_, ...), custom_call_target="tpu_custom_call", output_to_operand_aliasing={{3}: (6, {}), {4}: (7, {})} | custom-call | tf_op jit(solution)/shard_map/attend/pallas_call | solution.py:845
  241.5 47.6 %reduce_out.1 = (f32[256,2688]{1,0:T(8,128)}, bf16[2560,1536]{1,0:T(8,128)(2,1)}, bf16[2560,896]{1,0:T(8,128)(2,1)}) custom-call(bf16[1024,640]{1,0:T(8,128)(2,1)} %get-tuple-element.80.refs_0_.refs_2_, bf16[2688,640]{1,0:T(8,128)(2,1)} %get-tuple-element.81.refs_1_, ...), custom_call_target="tpu_custom_call", output_to_operand_aliasing={{1}: (2, {}), {2}: (3, {})} | custom-call | tf_op jit(solution)/shard_map/reduce_out/pallas_call | solution.py:465
  289.1 3.1 multiply_reduce_fusion.1
  295.4 3.3 concatenate.119.x_ref
  301.8 2.9 ffn_extras.1
  304.7 87.3 %feed_forward.1 = (bf16[2048,128]{1,0:T(8,128)(2,1)}, bf16[2048,1024]{1,0:T(8,128)(2,1)}, bf16[2048,640]{1,0:T(8,128)(2,1)}, bf16[2048,512]{1,0:T(8,128)(2,1)}, ...) custom-call(bf16[256,2688]{1,0:T(8,128)(2,1)} %concatenate.119.x_ref, ...), custom_call_target="tpu_custom_call", output_to_operand_aliasing={{5}: (2, {}), {6}: (3, {})} | custom-call | tf_op jit(solution)/shard_map/feed_forward/pallas_call | solution.py:1119
  393.9 70.0 %feed_forward_back.1 = (f32[256,2688]{1,0:T(8,128)}, bf16[4,256,2688]{2,1,0:T(8,128)(2,1)}, f32[128,1024]{1,0:T(8,128)}, f32[128,640]{1,0:T(8,128)}, f32[128,512]{1,0:T(8,128)}, /*index=5*/f32[128,384]{1,0:T(8,128)}) custom-call(bf16[2048,1024]{1,0:T(8,128)(2,1)} %get-tuple-element.91.refs_0_, bf16[2048,640]{1,0:T(8,128)(2,1)} %get-tuple-element.92.refs_1_, ...), custom_call_target="tpu_custom_call" | custom-call | tf_op jit(solution)/shard_map/feed_forward_back/pallas_call | solution.py:1309
  463.9 2.6 multiply_reduce_fusion
  466.6 2.4 multiply_convert_fusion
  470.5 3.5 concatenate.120.refs_0_
  478.8 47.7 %gather_grad.1 = (bf16[1024,2688]{1,0:T(8,128)(2,1)}, bf16[768,800]{1,0:T(8,128)(2,1)}, bf16[256,2688]{1,0:T(8,128)(2,1)}) custom-call(bf16[256,2688]{1,0:T(8,128)(2,1)} %concatenate.120.refs_0_, bf16[96,800]{1,0:T(8,128)(2,1)} %copy-done.24, bf16[4,256,2688]{2,1,0:T(8,128)(2,1)} %get-tuple-element.98.refs_2_.refs_7_), custom_call_target="tpu_custom_call" | custom-call | tf_op jit(solution)/shard_map/gather_grad/pallas_call | solution.py:340
  526.5 9.3 %convolution_convert_fusion.2.refs_3_ = bf16[1024,640]{1,0:T(8,128)(2,1)} fusion(bf16[1024,2688]{1,0:T(8,128)(2,1)} %get-tuple-element.106, bf16[2688,640]{1,0:T(8,128)(2,1)} %get-tuple-element.81.refs_1_), kind=kOutput, calls=%fused_computation.56 | convolution fusion | flops 3523870720 | bytes 10256384 | tf_op jit(solution)/shard_map/dot_general | solution.py:38
  535.8 2.8 fusion.17.refs_8_
  538.6 36.1 %attend_back.1 = (bf16[1024,1280]{1,0:T(8,128)(2,1)}, bf16[1024,1280]{1,0:T(8,128)(2,1)}, f32[1024,128]{1,0:T(8,128)}, bf16[768,800]{1,0:T(8,128)(2,1)}, bf16[25...) custom-call(bf16[1024,1280]{1,0:T(8,128)(2,1)} %get-tuple-element.99.refs_0_, ...), custom_call_target="tpu_custom_call", output_to_operand_aliasing={{3}: (6, {})} | custom-call | tf_op jit(solution)/shard_map/attend_back/pallas_call | solution.py:845
  574.7 2.6 fusion.18
  577.5 2.7 fusion.8
  580.2 2.4 fusion.60
  588.9 24.1 %reduce_latents.1 = (f32[256,1152]{1,0:T(8,128)}, bf16[8,16,3200]{2,1,0:T(8,128)(2,1)}) custom-call(bf16[1024,1280]{1,0:T(8,128)(2,1)} %get-tuple-element.112.refs_0_, bf16[1024,1280]{1,0:T(8,128)(2,1)} %get-tuple-element.113.refs_1_, bf16[896,1280]{1,0:T(8,128)(2,1)} %get-tuple-element.76.refs_1_.refs_2_, ...), custom_call_target="tpu_custom_call" | custom-call | tf_op jit(solution)/shard_map/reduce_latents/pallas_call | solution.py:465
  618.0 4.7 fusion.126
  633.8 41.9 %share.1.refs_0_ = bf16[2,8,128,1280]{3,2,1,0:T(8,128)(2,1)} custom-call(bf16[128,2560]{1,0:T(8,128)(2,1)} %pad.55.source), custom_call_target="tpu_custom_call" | custom-call | tf_op jit(solution)/shard_map/share/pallas_call | solution.py:609
  675.7 8.8 %sum_shared.1 = (f32[2,8,16,2560]{3,2,1,0:T(8,128)}, f32[8,16,2560]{2,1,0:T(8,128)}, f32[8,16,2560]{2,1,0:T(8,128)}, f32[8,16,2560]{2,1,0:T(8,128)}, f32[8,16,25...) custom-call(s32[8]{0:T(128)} %fusion.109.ids_ref, ...), custom_call_target="tpu_custom_call" | custom-call | tf_op jit(solution)/shard_map/sum_shared/pallas_call | solution.py:649
  684.5 6.7 sum_split.1
  (228 shorter events, 70.2 us)
Async XLA Ops:
  0.6 288.4 %copy-start = (bf16[8,16,2560]{2,1,0:T(8,128)(2,1)S(1)}, bf16[8,16,2560]{2,1,0:T(8,128)(2,1)}, u32[]{:S(2)}) copy-start(bf16[8,16,2560]{2,1,0:T(8,128)(2,1)} %param.53) | copy-start | bytes 1966084
  0.7 3.9 copy-start.25
  0.7 5.0 copy-start.3
  9.4 6.8 copy-start.15
  31.0 172.3 %copy-start.40 = (s32[1,1024]{1,0:T(1,128)S(1)}, s32[1,1024]{1,0:T(1,128)}, u32[]{:S(2)}) copy-start(s32[1,1024]{1,0:T(1,128)} %param.31) | copy-start | bytes 12292
  204.2 4.4 copy-start.38
  204.2 4.4 copy-start.45
  393.9 70.0 %copy-start.21 = (bf16[16,2560]{1,0:T(8,128)(2,1)S(1)}, bf16[16,2560]{1,0:T(8,128)(2,1)}, u32[]{:S(2)}) copy-start(bf16[16,2560]{1,0:T(8,128)(2,1)} %copy-done.20) | copy-start | bytes 245764
  393.9 70.0 %copy-start.23 = (bf16[16,2560]{1,0:T(8,128)(2,1)S(1)}, bf16[16,2560]{1,0:T(8,128)(2,1)}, u32[]{:S(2)}) copy-start(bf16[16,2560]{1,0:T(8,128)(2,1)} %copy-done.22) | copy-start | bytes 245764
  393.9 70.0 %copy-start.33 = (f32[2560]{0:T(1024)S(1)}, f32[2560]{0:T(1024)}, u32[]{:S(2)}) copy-start(f32[2560]{0:T(1024)} %param.36) | copy-start | bytes 30724
  470.5 7.6 %copy-start.19 = (f32[128,512]{1,0:T(8,128)S(1)}, f32[128,512]{1,0:T(8,128)}, u32[]{:S(2)}) copy-start(f32[128,512]{1,0:T(8,128)} %get-tuple-element.104) | copy-start | bytes 786436
  474.0 4.0 copy-start.31
  526.5 9.3 %copy-start.17 = (bf16[256,2688]{1,0:T(8,128)(2,1)S(1)}, bf16[256,2688]{1,0:T(8,128)(2,1)}, u32[]{:S(2)}) copy-start(bf16[256,2688]{1,0:T(8,128)(2,1)} %get-tuple-element.108) | copy-start | bytes 4128772
  580.2 3.6 copy-start.2
  580.2 5.1 copy-start.12
  588.9 25.5 %copy-start.14 = (f32[256,1152]{1,0:T(8,128)S(1)}, f32[256,1152]{1,0:T(8,128)}, u32[]{:S(2)}) copy-start(f32[256,1152]{1,0:T(8,128)} %get-tuple-element.111) | copy-start | bytes 3538948
  588.9 25.5 %copy-start.37 = (f32[768]{0:T(1024)S(1)}, f32[768]{0:T(1024)}, u32[]{:S(2)}) copy-start(f32[768]{0:T(1024)} %param.34) | copy-start | bytes 9220
  618.0 4.7 copy-start.30
  618.0 5.0 copy-start.10
  618.0 5.0 copy-start.35
  624.7 3.8 copy-start.7
  624.7 5.2 copy-start.9
  626.9 4.3 copy-start.5
  633.8 57.4 %copy-start.1 = (bf16[8,16,2560]{2,1,0:T(8,128)(2,1)S(1)}, bf16[8,16,2560]{2,1,0:T(8,128)(2,1)}, u32[]{:S(2)}) copy-start(bf16[8,16,2560]{2,1,0:T(8,128)(2,1)} %param.53) | copy-start | bytes 1966084
  (23 other events, 47.6 us)

commit v5 on v4

--- a/solution.py
+++ b/solution.py
@@ -149,8 +149,9 @@
                 for k, step in enumerate(rider["steps"]):
                     for key in list(held):
                         place = jnp.bitwise_xor(d, rider["z"] * pair + key)
-                        at = pl.multiple_of(place * count, 16)
-                        here = full.at[pl.ds(at, count)]
+                        begin, size = rider.get("rows", (0, count))
+                        at = pl.multiple_of(place * count + begin, 16)
+                        here = full.at[pl.ds(at, size)]
                         self.add(k, here, here, step)
                         held.append(key ^ step[1])
 
@@ -313,6 +314,8 @@
         for turn in order:
             if turn == "ride":
                 ride.start()
+            elif callable(turn):
+                turn(all_src)
             elif turn == "work":
                 work(all_src)
                 for src, out in late:
@@ -368,7 +371,7 @@
 
 
 def remote_reduce(
-    operands, fetched, term, keys, ways, rows, wide, name, collective_id, riders=(), ridden=(), carried=(), jobs=(), job_sources=(), job_outs=()
+    operands, fetched, term, keys, ways, rows, wide, name, collective_id, riders=(), ridden=(), carried=(), jobs=(), job_sources=(), job_outs=(), after=None, after_in=(), after_out=()
 ):
     core_step = ("tensor", 1)
     part = rows // len(ways)
@@ -385,10 +388,14 @@
     n_ride = n_in + len(ridden) + len(carried)
     n_all = n_ride + len(job_sources)
     n_jobs = len(job_outs)
+    after_out = list(after_out) or [jax.ShapeDtypeStruct((rows, wide), F32)]
+    n_own = len(after_out)
 
     def kernel(*refs):
         in_refs = refs[:n_in]
-        out_ref = refs[n_all]
+        own_out = refs[n_all + len(after_in) : n_all + len(after_in) + n_own]
+        extra_in = refs[n_all : n_all + len(after_in)]
+        refs = refs[:n_all] + refs[n_all + len(after_in) + n_own - 1 :]
         ride_in = refs[n_in:n_ride]
         job_in = refs[n_ride:n_all]
         ride_out = refs[n_all + 1 : n_all + 1 + len(ridden)]
@@ -453,7 +460,11 @@
                         hop_out[slot[entry]] = narrow(so_far(w, k, entry[2]))
                         send_part(w, k, entry[2])
         for w in range(len(ways)):
-            out_ref[w * part : (w + 1) * part, :] = so_far(w, len(ways[w]), (0, 0))
+            total = so_far(w, len(ways[w]), (0, 0))
+            if after is None:
+                own_out[0][w * part : (w + 1) * part, :] = total
+            else:
+                after(slice(w * part, (w + 1) * part), total, extra_in, own_out)
         for _ in rounds:
             pass
         ride.finish()
@@ -464,12 +475,14 @@
     any_spec = pl.BlockSpec(memory_space=pl.ANY)
     return pl.pallas_call(
         kernel,
-        out_shape=[jax.ShapeDtypeStruct((rows, wide), F32)]
+        out_shape=after_out
         + [jax.ShapeDtypeStruct(r.shape, r.dtype) for r in ridden]
         + [jax.ShapeDtypeStruct(o, BF16) for o in job_outs],
-        in_specs=[any_spec] * n_ride + [pl.BlockSpec(memory_space=pltpu.VMEM)] * len(job_sources),
-        out_specs=[pl.BlockSpec(memory_space=pltpu.VMEM)] + [any_spec] * (len(ridden) + n_jobs),
-        input_output_aliases={n_in + n: 1 + n for n in range(len(ridden))},
+        in_specs=[any_spec] * n_ride
+        + [pl.BlockSpec(memory_space=pltpu.VMEM)] * (len(job_sources) + len(after_in)),
+        out_specs=[pl.BlockSpec(memory_space=pltpu.VMEM)] * n_own
+        + [any_spec] * (len(ridden) + n_jobs),
+        input_output_aliases={n_in + n: n_own + n for n in range(len(ridden))},
         scratch_shapes=[pltpu.VMEM(s, o.dtype) for s, o in zip(fetched, operands)]
         + [
             pltpu.VMEM((len(keys), rows, wide), BF16),
@@ -487,7 +500,7 @@
         ),
         cost_estimate=FREE,
         name=name,
-    )(*operands, *ridden, *carried, *job_sources)
+    )(*operands, *ridden, *carried, *job_sources, *after_in)
 
 
 class Share:
@@ -588,17 +601,24 @@
     return scratch, copies
 
 
-def remote_share(terms, n_dp, n_t, orders, name, collective_id):
+def remote_share(terms, n_dp, n_t, orders, name, collective_id, work_in, work_out, work):
     scratch, copies = share_shapes(terms.shape, n_t, orders)
     parts = len(orders)
 
-    def kernel(source, out_ref, *refs):
+    n_in, n_work = len(work_in), len(work_out)
+
+    def kernel(source, *refs):
+        work_refs = refs[:n_in] + refs[n_in + 1 : n_in + 1 + n_work]
+        out_ref = refs[n_in]
+        refs = refs[n_in + 1 + n_work :]
         own_sems, send_sems, recv_sems = refs[-3:]
         links = Links(send_sems, recv_sems)
         links.greet(orders[0])
         share = Share(links, n_t, orders, source, out_ref, *refs[:-3])
-        for one in share.rounds:
+        for k, one in enumerate(share.rounds):
             one()
+            if k == len(share.rounds) - 2:
+                work(work_refs)
         kept = share.keep(own_sems)
         for copy in kept:
             copy.start()
@@ -608,9 +628,14 @@
 
     return pl.pallas_call(
         kernel,
-        out_shape=jax.ShapeDtypeStruct((parts, n_dp, terms.shape[0], terms.shape[1] // parts), BF16),
-        in_specs=[pl.BlockSpec(memory_space=pl.ANY)],
-        out_specs=pl.BlockSpec(memory_space=pl.ANY),
+        out_shape=[
+            jax.ShapeDtypeStruct((parts, n_dp, terms.shape[0], terms.shape[1] // parts), BF16)
+        ]
+        + list(work_out),
+        in_specs=[pl.BlockSpec(memory_space=pl.ANY)]
+        + [pl.BlockSpec(memory_space=pltpu.VMEM)] * n_in,
+        out_specs=[pl.BlockSpec(memory_space=pl.ANY)]
+        + [pl.BlockSpec(memory_space=pltpu.VMEM)] * n_work,
         scratch_shapes=scratch
         + [pltpu.SemaphoreType.DMA((copies,)), pltpu.SemaphoreType.DMA((copies,))],
         compiler_params=pltpu.CompilerParams(
@@ -618,7 +643,7 @@
         ),
         cost_estimate=FREE,
         name=name,
-    )(terms)
+    )(terms, *work_in)
 
 
 def set_sums(set_ids, sources, acc_shape, add, outs, put, groups, name):
@@ -957,6 +982,7 @@
     rows, aug = x_own.shape
     total = g_all.shape[0]
     blocks = total // rows
+    both = 2 * rows
     width = aug - CODE_LANES
     chunks = len(mains)
     tails = [0] * (chunks - 1) + [tail_wide]
@@ -1006,7 +1032,8 @@
         links.greet(steps)
 
         def landing(key):
-            return x_held.at[block_of(key, place)]
+            at = pl.multiple_of(block_of(key, place) * rows, 16)
+            return x_held.at[pl.ds(at, rows)]
 
         arrivals = {key: [] for key in keys}
 
@@ -1025,10 +1052,10 @@
         crossing[(0, 0)] = links.send(x_ref, landing((0, 0)), core_step)
         ride = Riders(links, riders, w_refs, w_refs)
         ride.start()
-        x_held[block_of((0, 0), place)] = x_ref[...]
+        x_held[pl.ds(pl.multiple_of(block_of((0, 0), place) * rows, 16), rows), :] = x_ref[...]
 
         def g_copy(b, slot):
-            at = pl.ds(pl.multiple_of(b * rows, 16), rows)
+            at = pl.ds(pl.multiple_of(b * both, 16), both)
             return pltpu.make_async_copy(g_ref.at[at], g_held.at[slot], g_sems.at[slot])
 
         def over_blocks(work):
@@ -1037,7 +1064,7 @@
             def one(b, carry):
                 slot = lax.rem(b, 2)
 
-                @pl.when(b + 1 < blocks)
+                @pl.when(b + 1 < blocks // 2)
                 def _():
                     g_copy(b + 1, 1 - slot).start()
 
@@ -1045,7 +1072,7 @@
                 work(b, g_held[slot])
                 return carry
 
-            lax.fori_loop(0, blocks, one, 0)
+            lax.fori_loop(0, blocks // 2, one, 0)
 
         fetch[0].wait()
         for copy in fetch_extra:
@@ -1056,28 +1083,19 @@
 
         over_blocks(back_first)
 
-        def rows_at(b):
-            return pl.ds(pl.multiple_of(b * rows, 16), rows)
-
         def forward(b, c, back):
             main = mains[c]
-            x_rows = x_held[b]
-            pre = dot_nn(x_rows, w_held[c][:, : gu[c]])
+            at = pl.ds(pl.multiple_of(b * both, 16), both)
+            pre = dot_nn(x_held[at, :], w_held[c][:, : gu[c]])
             hid, gate_grad, up_grad = gate_middle(pre[:, :main], pre[:, gu[c] - main :], back)
-            at = rows_at(b)
             hid_refs[c][at, :main] = narrow(hid)
             grad_refs[c][at, :main] = narrow(gate_grad)
             grad_refs[c][at, gu[c] - main :] = narrow(up_grad)
-            return pre
+            return pre, at
 
         def first_chunk(key):
-            def one(i, carry):
-                other = (key[0], key[1] + i)
-                b = block_of(other, place)
-                forward(b, 0, back_held[b])
-                return carry
-
-            lax.fori_loop(0, 2, one, 0)
+            b = block_of(key, place) // 2
+            forward(b, 0, back_held[b])
 
         links.arrived(crossing[(0, 0)])
         first_chunk((0, 0))
@@ -1099,19 +1117,17 @@
             def later(b, g_rows, c=c):
                 main = mains[c]
                 back = dot_nn(g_rows, w_held[c][:, gu[c] :])
-                pre = forward(b, c, back)
+                pre, at = forward(b, c, back)
                 if tails[c]:
                     at_tail = slice(main, main + tail_wide)
                     hid, both = tail_middle(
                         pre[:, at_tail], dot_nn(g_rows, w_held[c][:, at_tail]), tail
                     )
-                    at = rows_at(b)
                     hid_refs[c][at, main:] = narrow(hid)
                     grad_refs[c][at, at_tail] = narrow(both)
 
             over_blocks(later)
-        for b in range(blocks):
-            codes_ref[b * rows : (b + 1) * rows, :] = x_held[b, :, width:]
+        codes_ref[...] = x_held[:, width:]
         links.close()
 
     any_spec = pl.BlockSpec(memory_space=pl.ANY)
@@ -1125,9 +1141,9 @@
         + [jax.ShapeDtypeStruct((total, m + w), BF16) for m, w in zip(mains, tails)]
         + [jax.ShapeDtypeStruct(w.shape, BF16) for w in weights],
         scratch_shapes=[
-            pltpu.VMEM((blocks, rows, aug), BF16),
-            pltpu.VMEM((blocks, rows, mains[0]), F32),
-            pltpu.VMEM((2, rows, aug), BF16),
+            pltpu.VMEM((total, aug), BF16),
+            pltpu.VMEM((blocks // 2, both, mains[0]), F32),
+            pltpu.VMEM((2, both, aug), BF16),
         ]
         + [pltpu.VMEM((aug, w.shape[1]), BF16) for w in weights]
         + [
@@ -1391,6 +1407,131 @@
     )(places, gate_up_out, down_in)
 
 
+def chunk_places(mains, tail, tail_wide):
+    out = []
+    begin = 0
+    for c, main in enumerate(mains):
+        wide = tail_wide if c == len(mains) - 1 else 0
+        for kind, at in enumerate((0, main + wide, 2 * main + wide)):
+            out.append((kind, c, at, begin, main))
+        begin += main
+    if tail:
+        for kind in range(3):
+            out.append((kind, len(mains) - 1, mains[-1] + kind * tail, begin, tail))
+    return out
+
+
+def prepare(places, tables, shards, sizes, mains, tail, tail_wide):
+    heads, head_q, shares, down_wide = sizes
+    qa_in, kva_in, qb_in, kvb_in, out_in, gu_in, qa_out, kva_out, qb_out, kvb_out, out_out, down_out = (
+        tables
+    )
+    q_down, kv_down, q_up, gate_up, down_t, cotangent = shards
+    width, q_lat, kv_all = qa_in.shape[2], q_down.shape[1], kv_down.shape[1]
+    rows = cotangent.shape[0]
+    share_rows = q_down.shape[0] // shares
+    wide = heads * HEAD_LANES
+    half = down_t.shape[1] // 2
+    wides = [3 * m for m in mains[:-1]] + [3 * mains[-1] + tail_wide]
+
+    def kernel(places_ref, *refs):
+        ins, outs = refs[: len(tables) + len(shards)], refs[len(tables) + len(shards) :]
+        qa_i, kva_i, qb_i, kvb_i, out_i, gu_i, qa_o, kva_o, qb_o, kvb_o, out_o, down_o = ins[
+            : len(tables)
+        ]
+        qd, kvd, qu, gu_w, down_w, cot = ins[len(tables) :]
+        down_in_o, down_b_o, qb_w, kvb_w, q_aug, kv_aug, out_x, gu_lanes, out_p, down_p, gu_p = outs[:11]
+        mine_d, q_pad, g_own = outs[11:14]
+        pieces = outs[14:]
+        first = places_ref[1] == 0
+        for out in (down_b_o, qb_w, kvb_w, q_aug, kv_aug, out_x, gu_lanes, out_p, gu_p, mine_d, q_pad):
+            out[...] = jnp.zeros_like(out)
+        for out in pieces:
+            out[...] = jnp.zeros_like(out)
+        down_in_o[:RANK, :] = qa_i[0]
+        down_in_o[RANK:, :] = kva_i[0]
+        down_b_o[:RANK, :q_lat] = qa_o[0]
+        down_b_o[RANK:, q_lat : q_lat + kv_all] = kva_o[0]
+        qb_w[:RANK, :] = qb_i[0]
+        kvb_w[RANK : 2 * RANK, :] = kvb_i[0]
+        out_x[:RANK, :] = out_i[0]
+        kv_aug[RANK : 2 * RANK, :] = narrow(kvb_o[0].astype(F32) * ADAPT_SCALE)
+        q_out = narrow(qb_o[0].astype(F32) * ADAPT_SCALE)
+        q_up_all = qu[...]
+        for h in range(heads):
+            at = slice(h * HEAD_LANES, h * HEAD_LANES + head_q)
+            q_aug[:RANK, at] = q_out[:, h * head_q : (h + 1) * head_q]
+            q_pad[:, at] = q_up_all[:, h * head_q : (h + 1) * head_q]
+        for n in range(2):
+            both = gu_i[n, 0]
+            none = jnp.zeros_like(both)
+            gu_p[n * RANK : (n + 1) * RANK, :] = both
+            gu_lanes[n * RANK : (n + 1) * RANK, :] = jnp.where(first, both, none)
+            gu_lanes[(2 + n) * RANK : (3 + n) * RANK, :] = jnp.where(first, none, both)
+        out_p[:RANK, :] = out_o[0]
+        down_p[...] = down_o[0]
+        mine_d[:, :q_lat] = qd[...]
+        mine_d[:, q_lat : q_lat + kv_all] = kvd[...]
+        grad = narrow(RESIDUAL * cot[...].astype(F32))
+        g_own[:, :width] = grad
+        codes = dot_nt(grad, jnp.concatenate([down_o[0]] * 8, axis=0)) * ADAPT_SCALE
+        lane = lax.broadcasted_iota(jnp.int32, codes.shape, 1)
+        begin = jnp.where(first, 0, 2 * RANK)
+        g_own[:, width:] = narrow(jnp.where((lane >= begin) & (lane < begin + RANK), codes, 0.0))
+        sources = [gu_w[0], gu_w[1], down_w[...]]
+        sides = [(v[:, :half], v[:, half:]) for v in sources]
+        for kind, c, at, begin, count in chunk_places(mains, tail, tail_wide):
+            left = sides[kind][0][:, begin : begin + count]
+            right = sides[kind][1][:, begin : begin + count]
+            pieces[2 * c][:, at : at + count] = jnp.where(first, left, right)
+            pieces[2 * c + 1][:, at : at + count] = jnp.where(first, right, left)
+
+    def picked(table):
+        if table.ndim == 4:
+            return pl.BlockSpec((2, 1) + table.shape[2:], lambda i, ids: (0, ids[0], 0, 0))
+        return pl.BlockSpec((1,) + table.shape[1:], lambda i, ids: (ids[0], 0, 0))
+
+    def shared(shard):
+        return pl.BlockSpec((share_rows, shard.shape[1]), lambda i, ids: (ids[2], 0))
+
+    def whole(shape):
+        return pl.BlockSpec(shape, lambda i, ids: (0,) * len(shape))
+
+    out_shapes = [
+        (2 * RANK, width),
+        (2 * RANK, down_wide),
+        (CODE_LANES, qb_in.shape[2]),
+        (CODE_LANES, kvb_in.shape[2]),
+        (CODE_LANES, wide),
+        (CODE_LANES, wide),
+        (CODE_LANES, out_in.shape[2]),
+        (CODE_LANES, width),
+        (CODE_LANES, width),
+        (RANK, width),
+        (CODE_LANES, width),
+        (share_rows, down_wide),
+        (q_up.shape[0], wide),
+        (rows, width + CODE_LANES),
+    ]
+    for w in wides:
+        out_shapes += [(down_t.shape[0], w)] * 2
+    return pl.pallas_call(
+        kernel,
+        grid_spec=pltpu.PrefetchScalarGridSpec(
+            num_scalar_prefetch=1,
+            grid=(1,),
+            in_specs=[picked(a) for a in tables]
+            + [shared(q_down), shared(kv_down)]
+            + [whole(a.shape) for a in shards[2:]],
+            out_specs=[whole(o) for o in out_shapes],
+        ),
+        out_shape=[jax.ShapeDtypeStruct(o, BF16) for o in out_shapes],
+        compiler_params=pltpu.CompilerParams(vmem_limit_bytes=VMEM_LIMIT),
+        cost_estimate=FREE,
+        name="prepare",
+    )(places, *tables, *shards)
+
+
 def per_device(
     n_dp,
     n_t,
@@ -1461,21 +1602,6 @@
     def turned(table):
         return jnp.swapaxes(table, -1, -2)
 
-    qa_in, kva_in = pick(turned(query_down_adapter_in), set_own), pick(
-        turned(keyvalue_down_adapter_in), set_own
-    )
-    qa_out, kva_out = pick(query_down_adapter_out, set_own), pick(keyvalue_down_adapter_out, set_own)
-    qb_in, kvb_in = pick(turned(query_up_adapter_in), set_own), pick(
-        turned(keyvalue_up_adapter_in), set_own
-    )
-    qb_out, kvb_out = pick(query_up_adapter_out, set_own), pick(keyvalue_up_adapter_out, set_own)
-    out_in, out_out = pick(turned(output_adapter_in), set_own), pick(output_adapter_out, set_own)
-    gu_in = jnp.concatenate(
-        [pick(turned(gate_up_adapter_in[0]), set_own), pick(turned(gate_up_adapter_in[1]), set_own)],
-        axis=0,
-    )
-    down_out = pick(down_adapter_out, set_own)
-
     hidden = down_matrix.shape[0]
     half = hidden // 2
     tiles = half // 128
@@ -1488,27 +1614,60 @@
     tails = [0] * (chunks - 1) + [tail_wide]
     gu_wide = [2 * m + w for m, w in zip(mains, tails)]
 
-    def columns(gate_part, up_part, down_part, chunk):
-        begin = sum(mains[:chunk])
-        at = slice(begin, begin + mains[chunk])
-        out = [gate_part[:, at]]
-        if tail and chunk == chunks - 1:
-            out += [gate_part[:, main:], up_part[:, main:], down_part[:, main:]]
-            if tail_wide > 3 * tail:
-                out.append(jnp.zeros((gate_part.shape[0], tail_wide - 3 * tail), BF16))
-        out += [up_part[:, at], down_part[:, at]]
-        return jnp.concatenate(out, axis=1)
-
-    def halves(value):
-        return value[:, :half], value[:, half:]
-
-    mats = [halves(gate_up_matrix[0]), halves(gate_up_matrix[1]), halves(down_matrix.T)]
-    ffn_mine, ffn_other = [], []
-    for chunk in range(chunks):
-        left = columns(mats[0][0], mats[1][0], mats[2][0], chunk)
-        right = columns(mats[0][1], mats[1][1], mats[2][1], chunk)
-        ffn_mine.append(jnp.where(first, left, right))
-        ffn_other.append(jnp.where(first, right, left))
+    head_q = PLAIN_HEAD_DIM + ROTARY_DIM
+    down_shard = query_down_matrix.shape[0]
+    shares = n_t if down_shard % (16 * n_t) == 0 else 2
+    share_rows = down_shard // shares
+    down_wide = -(-(q_lat + kv_all) // 128) * 128
+    down_pad = down_wide - q_lat - kv_all
+    (
+        down_in,
+        down_b_rows,
+        qb_in_wide,
+        kvb_in_wide,
+        q_aug_rows,
+        kv_aug_rows,
+        out_extra,
+        gu_in_lanes,
+        out_out_wide,
+        down_out,
+        gu_in_wide,
+        down_mine,
+        q_up_mine,
+        g_own,
+        *ffn_pieces,
+    ) = prepare(
+        jnp.stack([set_own, zl, lax.rem(t, shares)]).astype(jnp.int32),
+        [
+            turned(query_down_adapter_in),
+            turned(keyvalue_down_adapter_in),
+            turned(query_up_adapter_in),
+            turned(keyvalue_up_adapter_in),
+            turned(output_adapter_in),
+            turned(gate_up_adapter_in),
+            query_down_adapter_out,
+            keyvalue_down_adapter_out,
+            query_up_adapter_out,
+            keyvalue_up_adapter_out,
+            output_adapter_out,
+            down_adapter_out,
+        ],
+        [
+            query_down_matrix,
+            keyvalue_down_matrix,
+            query_up_matrix,
+            gate_up_matrix,
+            down_matrix.T,
+            cotangent[0],
+        ],
+        (heads, head_q, shares, down_wide),
+        mains,
+        tail,
+        tail_wide,
+    )
+    qb_in, kvb_in = qb_in_wide[:RANK], kvb_in_wide[RANK : 2 * RANK]
+    out_out, gu_in = out_out_wide[:RANK], gu_in_wide[: 2 * RANK]
+    ffn_mine, ffn_other = ffn_pieces[::2], ffn_pieces[1::2]
     ffn_rows_each = gate_up_matrix.shape[1]
     z_count = n_dp // pair
     ffn_wide = [m.shape[1] for m in ffn_mine]
@@ -1525,88 +1684,23 @@
             high=high,
         )
 
-    def ride_two(out, z):
+    def ride_two(out, z, begin=0, size=None):
         return dict(
             kind="two",
             out=out,
             z=z,
+            rows=(begin, ffn_rows_each if size is None else size),
             count=ffn_rows_each,
             pair=pair,
             high=high,
             steps=[("dp", b) for b in reversed(low_bits)],
         )
 
-    def code_lanes(codes):
-        none = jnp.zeros_like(codes)
-        return jnp.concatenate(
-            [
-                jnp.where(first, codes, none),
-                jnp.where(first, none, codes),
-                jnp.zeros((codes.shape[0], CODE_LANES - 4 * RANK), codes.dtype),
-            ],
-            axis=1,
-        )
-
     def own_codes(value):
         lanes = value[:, width:]
         return jnp.where(first, lanes[:, : 2 * RANK], lanes[:, 2 * RANK : 4 * RANK])
 
-    out_grad = cotangent[0].astype(F32)
-    ffn_grad = narrow(RESIDUAL * out_grad)
-    down_code_grad = narrow(ADAPT_SCALE * dot_nt(ffn_grad, down_out))
-    none16 = jnp.zeros((rows, RANK), BF16)
-    g_own = jnp.concatenate(
-        [ffn_grad, code_lanes(jnp.concatenate([down_code_grad, none16], axis=1))], axis=1
-    )
-
-    down_shard = query_down_matrix.shape[0]
-    shares = n_t if down_shard % (16 * n_t) == 0 else 2
-    share_rows = down_shard // shares
-    down_wide = -(-(q_lat + kv_all) // 128) * 128
-    down_pad = down_wide - q_lat - kv_all
-    down_both = jnp.concatenate(
-        [query_down_matrix, keyvalue_down_matrix, jnp.zeros((down_shard, down_pad), BF16)], axis=1
-    )
-    down_mine = lax.dynamic_index_in_dim(
-        down_both.reshape(shares, share_rows, down_wide), lax.rem(t, shares), 0, keepdims=False
-    )
-    down_in = jnp.concatenate([qa_in, kva_in], axis=0)
-    down_b_rows = jnp.concatenate(
-        [
-            jnp.pad(qa_out, ((0, 0), (0, down_wide - q_lat))),
-            jnp.pad(kva_out, ((0, 0), (q_lat, down_pad))),
-        ],
-        axis=0,
-    )
-    qb_in_wide = jnp.pad(qb_in, ((0, CODE_LANES - RANK), (0, 0)))
-    kvb_in_wide = jnp.pad(kvb_in, ((RANK, CODE_LANES - 2 * RANK), (0, 0)))
     qb_rows, kvb_rows = query_up_matrix.shape[0], keyvalue_up_matrix.shape[0]
-    head_q = PLAIN_HEAD_DIM + ROTARY_DIM
-
-    def pad_heads(value):
-        split = value.reshape(value.shape[0], heads, head_q)
-        return jnp.pad(split, ((0, 0), (0, 0), (0, HEAD_LANES - head_q))).reshape(
-            value.shape[0], heads * HEAD_LANES
-        )
-
-    q_aug_rows = jnp.concatenate(
-        [
-            narrow(ADAPT_SCALE * pad_heads(qb_out)),
-            jnp.zeros((CODE_LANES - RANK, heads * HEAD_LANES), BF16),
-        ],
-        axis=0,
-    )
-    kv_aug_rows = jnp.concatenate(
-        [
-            jnp.zeros((RANK, heads * HEAD_LANES), BF16),
-            narrow(ADAPT_SCALE * kvb_out),
-            jnp.zeros((CODE_LANES - 2 * RANK, heads * HEAD_LANES), BF16),
-        ],
-        axis=0,
-    )
-    out_extra = jnp.concatenate(
-        [out_in, jnp.zeros((CODE_LANES - RANK, out_in.shape[1]), BF16)], axis=0
-    )
     out_rows = output_matrix.shape[1]
 
     def rows_at(start, step, count):
@@ -1715,7 +1809,7 @@
         remote_gather(
             [
                 down_mine,
-                pad_heads(query_up_matrix),
+                q_up_mine,
                 keyvalue_up_matrix,
                 output_matrix.T,
                 g_own,
@@ -1839,7 +1933,7 @@
         doc_q,
         q_lat + CODE_LANES,
         q_lat,
-        [ride_two(0, 1), ride_one(1, 2, 3, 0, cut_a)],
+        [ride_two(0, 1), ride_two(0, 2, 0, cut_a), ride_one(1, 2, 3, 0, cut_a)],
         [w_ffn0, w_ffn1],
         [ffn_mine[1], ffn_other[1]],
     )
@@ -1852,7 +1946,21 @@
     def out_term(held, place, key):
         return dot_nt(held[0][token_rows(key, place), :], held[1][...])
 
-    attn_sum, w_ffn0, w_ffn1 = remote_reduce(
+    def middle_work(at, total, extra, outs):
+        x_ref, out_b_ref, norm_ref, lanes_ref = extra
+        middle_ref, codes_ref, own_ref = outs
+        codes = narrow(total[:, width : width + RANK])
+        mid = x_ref[at, :].astype(F32) + RESIDUAL * (
+            total[:, :width] + ADAPT_SCALE * dot_nn(codes, out_b_ref[...])
+        )
+        middle_ref[at, :] = mid
+        codes_ref[at, :] = codes
+        scale = lax.rsqrt(jnp.mean(mid * mid, axis=-1, keepdims=True) + NORM_EPS)
+        normed = narrow(mid * scale * norm_ref[...])
+        own_ref[at, :width] = normed
+        own_ref[at, width:] = narrow(dot_nt(normed, lanes_ref[...]))
+
+    middle, out_codes, x_own, w_ffn0, w_ffn1 = remote_reduce(
         [head_out, w_out],
         [head_out.shape, w_out.shape],
         out_term,
@@ -1862,20 +1970,21 @@
         aug,
         "reduce_out",
         3,
-        riders=[ride_two(0, z) for z in range(2, z_count)]
+        riders=[ride_two(0, 2, cut_a, ffn_rows_each - cut_a)]
+        + [ride_two(0, z) for z in range(3, z_count)]
         + [ride_one(1, 2, 3, cut_a, ffn_rows_each - cut_a)],
         ridden=[w_ffn0, w_ffn1],
         carried=[ffn_mine[1], ffn_other[1]],
-    )
-    out_codes = narrow(attn_sum[:, width : width + RANK])
-    middle = residual + RESIDUAL * (
-        attn_sum[:, :width] + ADAPT_SCALE * dot_nn(out_codes, out_out)
-    )
-
-    ffn_normed, ffn_scale = normalize(middle, feedforward_norm_gain)
-    ffn_rows = narrow(ffn_normed)
-    gu_codes = narrow(dot_nt(ffn_rows, gu_in))
-    x_own = jnp.concatenate([ffn_rows, code_lanes(gu_codes)], axis=1)
+        after=middle_work,
+        after_in=[inputs[0], out_out, feedforward_norm_gain[None], gu_in_lanes],
+        after_out=[
+            jax.ShapeDtypeStruct((rows, width), F32),
+            jax.ShapeDtypeStruct((rows, RANK), BF16),
+            jax.ShapeDtypeStruct((rows, aug), BF16),
+        ],
+    )
+    ffn_rows = x_own[:, :width]
+    ffn_scale = lax.rsqrt(jnp.mean(middle * middle, axis=-1, keepdims=True) + NORM_EPS)
 
     def group_block_of(key, place):
         return group_block(
@@ -1913,72 +2022,126 @@
         "feed_forward_back",
         5,
     )
-    gu_code_grad = narrow(own_codes(ffn_in_sum))
-    ffn_in_grad = ffn_in_sum[:, :width] + dot_nn(gu_code_grad, gu_in)
-    middle_grad = out_grad + normalize_back(
-        middle, ffn_scale, feedforward_norm_gain, ffn_in_grad
-    )
-    attn_grad = narrow(RESIDUAL * middle_grad)
-    out_code_grad = narrow(ADAPT_SCALE * dot_nt(attn_grad, out_out))
-    attn_grad_aug = jnp.concatenate(
-        [attn_grad, out_code_grad, jnp.zeros((rows, CODE_LANES - RANK), BF16)], axis=1
-    )
-
-    def uncolumn(parts, at_tail, first_at):
-        out = [parts[c][:, first_at(c) : first_at(c) + mains[c]] for c in range(chunks)]
-        if tail:
-            at = mains[-1] + at_tail * tail
-            out.append(parts[-1][:, at : at + tail])
-        return jnp.concatenate(out, axis=1)
-
-    gu_b, down_at = code_terms[:chunks], code_terms[chunks:]
-    gate_b_all = ADAPT_SCALE * uncolumn(gu_b, 0, lambda c: 0)
-    up_b_all = ADAPT_SCALE * uncolumn(gu_b, 1, lambda c: gu_wide[c] - mains[c])
-    down_a_all = uncolumn(down_at, 2, lambda c: 0)
-    packed = []
-    for p in range(2):
-        at = 2 * RANK * p
-        packed += [
-            gate_b_all[at : at + RANK],
-            up_b_all[at + RANK : at + 2 * RANK],
-            down_a_all[at : at + RANK],
-        ]
-    hidden_own = narrow(jnp.concatenate(packed, axis=0))
+    def grad_work(part, refs):
+        at = slice(part * half_rows, (part + 1) * half_rows)
+        sum_ref, mid_ref, cot_ref, norm_ref, gu_ref, out_ref = refs[0:6]
+        middle_ref, codes_ref, aug_ref = refs[n_grad : n_grad + 3]
+        lanes = sum_ref[at, width:]
+        lanes = jnp.where(zl_of() == 0, lanes, pltpu.roll(lanes, CODE_LANES - 2 * RANK, 1))
+        lane = lax.broadcasted_iota(jnp.int32, lanes.shape, 1)
+        codes = narrow(jnp.where(lane < 2 * RANK, lanes, 0.0))
+        codes_ref[at, :] = codes
+        weighted = (sum_ref[at, :width] + dot_nn(codes, gu_ref[...])) * norm_ref[...]
+        mid = mid_ref[at, :]
+        scale = lax.rsqrt(jnp.mean(mid * mid, axis=-1, keepdims=True) + NORM_EPS)
+        inner = jnp.mean(mid * weighted, axis=-1, keepdims=True)
+        grad = cot_ref[at, :].astype(F32) + scale * weighted - mid * (scale * scale * scale * inner)
+        middle_ref[at, :] = grad
+        scaled = narrow(RESIDUAL * grad)
+        aug_ref[at, :width] = scaled
+        aug_ref[at, width:] = narrow(ADAPT_SCALE * dot_nt(scaled, out_ref[...]))
+
+    def zl_of():
+        return lax.rem(lax.axis_index("dp") // pair, 2)
+
+    hidden_shape = (6 * RANK, half)
+
+    def hidden_work(refs):
+        gu_refs, down_refs = refs[6 : 6 + chunks], refs[6 + chunks : 6 + 2 * chunks]
+        own_ref = refs[n_grad + 6]
+        for kind, c, at, begin, count in chunk_places(mains, tail, tail_wide):
+            for p in range(2):
+                to = slice((3 * p + kind) * RANK, (3 * p + kind + 1) * RANK)
+                if kind < 2:
+                    top = 2 * RANK * p + kind * RANK
+                    value = gu_refs[c][top : top + RANK, at : at + count] * ADAPT_SCALE
+                else:
+                    here = at - 2 * mains[c] - tails[c] if count == mains[c] else at
+                    value = down_refs[c][2 * RANK * p : 2 * RANK * p + RANK, here : here + count]
+                own_ref[to, begin : begin + count] = narrow(value)
 
     def dp_job(src, out):
         return dict(src=src, out=out, out_at=lambda dd, tt: (dd,), steps=outer_first)
 
+    n_grad = 7 + 2 * chunks + (1 if n_t == 4 else 0)
+
+    def heads_work(refs):
+        w_ref, heads_ref, lanes_ref, all_ref = refs[6 + 2 * chunks], *refs[n_grad + 3 : n_grad + 6]
+        for n in range(2):
+            at = slice(n * length // 2, (n + 1) * length // 2)
+            heads_ref[at, :] = narrow(dot_nn(all_ref[at, :], w_ref[...]))
+        lanes_ref[...] = all_ref[:, width:]
+
     ride_down = n_t == 4
+    n_far = 2 if ride_down else 1
     sent = remote_gather(
-        [attn_grad_aug, hidden_own] + ([down_chip] if ride_down else []),
-        token_jobs(0, 0, 2)
+        [
+            ffn_in_sum,
+            middle,
+            cotangent[0],
+            feedforward_norm_gain[None],
+            gu_in_wide,
+            out_out_wide,
+            *code_terms,
+            w_out,
+        ]
+        + ([down_chip] if ride_down else []),
+        token_jobs(n_grad + 2, n_far + 5, 2, "top")[:1]
+        + token_jobs(n_grad + 2, n_far + 5, 2, "bottom")[1:]
         + [
             dict(
-                src=1,
-                out=1,
-                out_at=rows_at(0, hidden_own.shape[0], hidden_own.shape[0]),
+                src=n_grad + 6,
+                out=0,
+                out_at=rows_at(0, hidden_shape[0], hidden_shape[0]),
                 steps=[("dp", high), ("dp", pair)],
                 group="hidden",
             )
         ],
         [],
-        [(length, aug), (n_dp * hidden_own.shape[0], hidden_own.shape[1])] + ([(rows, aug)] if ride_down else []),
+        [(n_dp * hidden_shape[0], half)] + ([(rows, aug)] if ride_down else []),
         "gather_grad",
         6,
-        riders=[dict(kind="plain", src=2, src_at=0, out=2, step=("dp", pair))] if ride_down else [],
-        distant=(2,),
-        order=[0, "hidden", "hidden", "ride"],
-    )
-    hidden_terms = sent[1]
-    grad_all = sent[0]
-    heads_grad = narrow(dot_nn(grad_all, w_out))
-    out_a = dot_tn(grad_all[:, width:], head_out)[:RANK]
+        riders=[dict(kind="plain", src=n_grad - 1, src_at=0, out=1, step=("dp", pair))]
+        if ride_down
+        else [],
+        distant=(n_grad - 1,) if ride_down else (),
+        order=[
+            functools.partial(grad_work, 0),
+            "top",
+            functools.partial(grad_work, 1),
+            "bottom",
+            hidden_work,
+            "hidden",
+            "hidden",
+            "ride",
+            "top",
+            "bottom",
+        ]
+        + ["top", "bottom"] * (len(t_slow) - 1)
+        + [("all", "top"), ("all", "bottom"), heads_work],
+        near_outs=[
+            jax.ShapeDtypeStruct((rows, width), F32),
+            jax.ShapeDtypeStruct((rows, CODE_LANES), BF16),
+            jax.ShapeDtypeStruct((rows, aug), BF16),
+            jax.ShapeDtypeStruct((length, w_out.shape[1]), BF16),
+            jax.ShapeDtypeStruct((length, CODE_LANES), BF16),
+        ],
+        scratch=[
+            jax.ShapeDtypeStruct((length, aug), BF16),
+            jax.ShapeDtypeStruct(hidden_shape, BF16),
+        ],
+    )
+    middle_grad, gu_code_grad, attn_grad_aug, heads_grad, grad_lanes = sent[n_far:]
+    gu_code_grad = gu_code_grad[:, : 2 * RANK]
+    attn_grad = attn_grad_aug[:, :width]
+    hidden_terms = sent[0]
+    out_a = dot_tn(grad_lanes, head_out)[:RANK]
     hidden_ride = [
         dict(
             kind="two",
             out=0,
             z=z,
-            count=hidden_own.shape[0],
+            count=hidden_shape[0],
             pair=pair,
             high=high,
             steps=[("dp", b) for b in reversed(low_bits)],
@@ -1986,7 +2149,7 @@
         for z in range(z_count)
     ]
     if ride_down:
-        down_far = narrow(down_chip[2].astype(F32) + sent[2].astype(F32))
+        down_far = narrow(down_chip[2].astype(F32) + sent[1].astype(F32))
         dq, dkv, dpe, hidden_terms, came_pair, came_y = attend_back(
             q_aug,
             kv,
@@ -2039,7 +2202,53 @@
     kvb_b = ADAPT_SCALE * dot_tn(lat_codes, dkv)[RANK : 2 * RANK]
     head_own = narrow(jnp.concatenate([qb_b, kvb_b, out_a], axis=1))
     operands = [dq, dkv, w_q, w_kv, pe_padded]
-    lat_sum, head_terms = remote_reduce(
+    small_at, small_wide = [0], []
+    for value in (q_lat, kv_all, q_lat, kv_lat):
+        small_wide.append(value)
+        small_at.append(small_at[-1] + -(-value // 128) * 128)
+
+    def latent_back(at, total, extra, outs):
+        latent_ref, q_norm, kv_norm, qb_ref, kvb_ref, b_ref, rows_ref, codes_ref = extra
+        grad_ref, code_ref, terms_ref = outs
+        block = total[:, q_lat : q_lat + CODE_LANES]
+        lane = lax.broadcasted_iota(jnp.int32, block.shape, 1)
+        codes = narrow(jnp.where(lane < 2 * RANK, block, 0.0))
+        latent_f = latent_ref[...]
+        parts = []
+        inputs_in = []
+        for begin, size, grad, norm_ref, in_ref in (
+            (0, q_lat, total[:, :q_lat], q_norm, qb_ref),
+            (q_lat, kv_lat, total[:, q_lat + CODE_LANES :], kv_norm, kvb_ref),
+        ):
+            value = latent_f[:, begin : begin + size]
+            scale = lax.rsqrt(jnp.mean(value * value, axis=-1, keepdims=True) + NORM_EPS)
+            inputs_in.append(narrow(value * scale * norm_ref[...]))
+            weighted = (grad + dot_nn(codes, in_ref[...])) * norm_ref[...]
+            inner = jnp.mean(value * weighted, axis=-1, keepdims=True)
+            parts.append(scale * weighted - value * (scale * scale * scale * inner))
+        grad_ref[:, :q_lat] = narrow(parts[0])
+        grad_ref[:, q_lat : q_lat + kv_lat] = narrow(parts[1])
+        pe_block = pltpu.roll(block, CODE_LANES - 2 * RANK, 1)
+        pe_block = jnp.where(lane < ROTARY_DIM, pe_block, 0.0)
+        grad_ref[:, q_lat + kv_lat :] = narrow(pe_block[:, : down_wide - q_lat - kv_lat])
+        grad_rows = grad_ref[...]
+        code_grad = narrow(ADAPT_SCALE * dot_nt(grad_rows, b_ref[...]))
+        code_ref[...] = code_grad
+        terms_ref[...] = jnp.zeros_like(terms_ref)
+        terms_ref[: 2 * RANK, :] = narrow(dot_tn(code_grad, rows_ref[...]))
+        b_terms = ADAPT_SCALE * dot_tn(codes_ref[...], grad_rows)
+        qb_a = dot_tn(codes, inputs_in[0])
+        kvb_a = dot_tn(codes, inputs_in[1])
+        small_values = (
+            b_terms[:RANK, :q_lat],
+            b_terms[RANK:, q_lat : q_lat + kv_all],
+            qb_a[:RANK, :],
+            kvb_a[RANK : 2 * RANK, :],
+        )
+        for value, begin, size in zip(small_values, small_at, small_wide):
+            terms_ref[2 * RANK :, begin : begin + size] = narrow(value)
+
+    latent_grad, code_grad, late_terms, head_terms = remote_reduce(
         operands,
         [o.shape for o in operands],
         latent_term,
@@ -2052,6 +2261,22 @@
         jobs=[dp_job(0, 0)],
         job_sources=[head_own],
         job_outs=[(n_dp,) + head_own.shape],
+        after=latent_back,
+        after_in=[
+            latent,
+            query_latent_gain[None],
+            keyvalue_latent_gain[None],
+            qb_in_wide,
+            kvb_in_wide,
+            down_b_rows,
+            attn_rows,
+            down_codes_in,
+        ],
+        after_out=[
+            jax.ShapeDtypeStruct((rows, down_wide), BF16),
+            jax.ShapeDtypeStruct((rows, 2 * RANK), BF16),
+            jax.ShapeDtypeStruct((3 * RANK, width), BF16),
+        ],
     )
     if ride_down:
         ffn_out = (
@@ -2063,55 +2288,42 @@
     outputs = narrow(
         middle + RESIDUAL * (ffn_out[:, :width] + ADAPT_SCALE * dot_nn(down_codes, down_out))
     )
-    qb_code_grad = narrow(lat_sum[:, q_lat : q_lat + RANK])
-    kvb_code_grad = narrow(lat_sum[:, q_lat + RANK : q_lat + 2 * RANK])
-    pe_sum = lat_sum[:, pe_at : pe_at + ROTARY_DIM]
-    q_norm_grad = lat_sum[:, :q_lat] + dot_nn(qb_code_grad, qb_in)
-    kv_norm_grad = lat_sum[:, q_lat + CODE_LANES :] + dot_nn(kvb_code_grad, kvb_in)
-    latent_grad = narrow(
-        jnp.concatenate(
-            [
-                normalize_back(q_latent, q_scale, query_latent_gain, q_norm_grad),
-                normalize_back(kv_latent, kv_scale, keyvalue_latent_gain, kv_norm_grad),
-                pe_sum,
-                jnp.zeros((rows, down_pad), F32),
-            ],
-            axis=1,
-        )
-    )
-    code_grad = narrow(ADAPT_SCALE * dot_nt(latent_grad, down_b_rows))
-    attn_in_grad = dot_nt(latent_grad, w_down) + dot_nn(code_grad, down_in)
-    input_grad = middle_grad + normalize_back(
-        residual, attn_scale, attention_norm_gain, attn_in_grad
-    )
-
     gu_a = dot_tn(gu_code_grad, ffn_rows)
     out_b = ADAPT_SCALE * dot_tn(out_codes, attn_grad)
-    down_b = ADAPT_SCALE * dot_tn(down_codes, ffn_grad)
+    down_b = ADAPT_SCALE * dot_tn(down_codes, g_own[:, :width])
     table_orders = [outer_first + t_slow + t_core, t_slow + outer_first + t_core]
-    down_in_terms = dot_tn(code_grad, attn_rows)
-    b_terms = ADAPT_SCALE * dot_tn(down_codes_in, latent_grad)
-    qb_a = dot_tn(qb_code_grad, q_input)
-    kvb_a = dot_tn(kvb_code_grad, kv_input)
-    small = [b_terms[:RANK, :q_lat], b_terms[RANK:, q_lat : q_lat + kv_all], qb_a, kvb_a]
-    small_at = [0]
-    padded = []
-    for value in small:
-        wide = -(-value.shape[1] // 128) * 128
-        padded.append(jnp.pad(value, ((0, 0), (0, wide - value.shape[1]))))
-        small_at.append(small_at[-1] + wide)
-    small_rows = jnp.pad(
-        jnp.concatenate(padded, axis=1), ((0, 0), (0, width - small_at[-1]))
-    )
-    shared = jnp.concatenate([gu_a, out_b, down_b, down_in_terms, small_rows], axis=0)
+    shared = jnp.concatenate([narrow(gu_a), narrow(out_b), narrow(down_b), late_terms], axis=0)
     shared = jnp.pad(shared, ((0, -shared.shape[0] % (16 * n_t)), (0, 0)))
-    shared_terms = remote_share(
-        narrow(shared),
+
+    def input_work(refs):
+        grad_ref, code_ref, w_ref, in_ref, x_ref, norm_ref, mid_ref, out_ref = refs
+        back = dot_nt(grad_ref[...], w_ref[...]) + dot_nn(code_ref[...], in_ref[...])
+        value = x_ref[...].astype(F32)
+        scale = lax.rsqrt(jnp.mean(value * value, axis=-1, keepdims=True) + NORM_EPS)
+        weighted = back * norm_ref[...]
+        inner = jnp.mean(value * weighted, axis=-1, keepdims=True)
+        out_ref[...] = (
+            mid_ref[...] + scale * weighted - value * (scale * scale * scale * inner)
+        )
+
+    shared_terms, input_grad = remote_share(
+        shared,
         n_dp,
         n_t,
         table_orders,
         "share",
         8,
+        [
+            latent_grad,
+            code_grad,
+            w_down,
+            down_in,
+            inputs[0],
+            attention_norm_gain[None],
+            middle_grad,
+        ],
+        [jax.ShapeDtypeStruct((rows, width), F32)],
+        input_work,
     )
     part_wide = width // 2
 
@@ -2125,9 +2337,9 @@
         outs[0][1, 0] = acc[RANK : 2 * RANK, :]
         for n in range(4):
             outs[1 + n][0] = acc[(2 + n) * RANK : (3 + n) * RANK, :]
-        for n, value in enumerate(small):
+        for n, size in enumerate(small_wide):
             at = small_at[n]
-            outs[5 + n][0] = acc[6 * RANK : 7 * RANK, at : at + value.shape[1]]
+            outs[5 + n][0] = acc[6 * RANK : 7 * RANK, at : at + size]
 
     shared_sets = set_sums(
         set_all,
@@ -2136,7 +2348,7 @@
         add_shared,
         [((2,), (RANK, width))]
         + [((), (RANK, width))] * 4
-        + [((), (RANK, value.shape[1])) for value in small],
+        + [((), (RANK, size)) for size in small_wide],
         put_shared,
         group_count,
         "sum_shared",
@@ -2169,7 +2381,7 @@
 
     gu_b_grad, down_a_t, qb_b_grad, kvb_b_grad, out_a_t = set_sums(
         set_all,
-        [hidden_terms.reshape((n_dp,) + hidden_own.shape), head_terms],
+        [hidden_terms.reshape((n_dp,) + hidden_shape), head_terms],
         (4 * RANK, max(hidden, -(-head_wide // 128) * 128)),
         add_split,
         [

time: 702 us -> 642 us (0.915)
  matrix products: 37.9 us -> 6.24 us
  local copies, waits for them, and re-layouts: 40.8 us -> 10.9 us
  Pallas kernels: 576 us -> 594 us
  other arithmetic: 33.1 us -> 23.5 us
    dot_general x7 -> x1, matrix products: 21.4 us -> 1.66 us  [dot_nn(): lax.dot_general(a, b, (((1,), (0,)), ((), ())), preferred_element_type=F32)]
    concatenate x12 -> x0, local copies, waits for them, and re-layouts: 12.5 us -> none  [the longest x1 3.49 us: per_device(): jnp.concatenate([attn_grad, out_code_grad, jnp.zeros((rows, CODE_LANES -...]
    pallas_call x3 -> x4, Pallas kernels: 114 us -> 125 us  [the longest x2 69.6 us: remote_reduce(): pl.pallas_call(kernel, out_shape=after_out + [jax.ShapeDtypeStruct(r.shap...]
    pallas_call x2, Pallas kernels: 219 us -> 227 us  [remote_gather(): pl.pallas_call(kernel, out_shape=[jax.ShapeDtypeStruct(o, BF16) for o in...]
    dot_general x5 -> x0, matrix products: 7.86 us -> none  [dot_nt(): lax.dot_general(a, b, (((1,), (1,)), ((), ())), preferred_element_type=F32)]
where the time goes in v5:
time: 642 us; the launch traced here: 638 us
  Pallas kernels  594 us (93%)
  other arithmetic  23.5 us (4%)
  local copies, waits for them, and re-layouts  10.9 us (2%)
    pallas_call x2, Pallas kernels, remote_gather(): pl.pallas_call(kernel, out_shape=[jax.ShapeDtypeStruct(o, BF16) for o in...  227 us
    pallas_call x1, Pallas kernels, remote_ffn(): pl.pallas_call(kernel, in_specs=[vmem_spec, any_spec] + [any_spec] * (2 *...  80.7 us
    pallas_call x2, Pallas kernels, ridden_call(): pl.pallas_call(body, grid=grid, in_specs=list(in_specs) + [any_spec] * n_...  73.6 us
    pallas_call x2, Pallas kernels, remote_reduce(): pl.pallas_call(kernel, out_shape=after_out + [jax.ShapeDtypeStruct(r.shap...  69.6 us
    pallas_call x1, Pallas kernels, remote_ffn_back(): pl.pallas_call(kernel, out_shape=[jax.ShapeDtypeStruct((rows, aug), F32),...  69.4 us
    pallas_call x1, Pallas kernels, remote_share(): pl.pallas_call(kernel, out_shape=[jax.ShapeDtypeStruct((parts, n_dp, term...  46.7 us
    pallas_call x2, Pallas kernels, set_sums(): pl.pallas_call(kernel, grid_spec=pltpu.PrefetchScalarGridSpec(num_scalar_...  15.5 us

profile of v5, /device:TPU:0, one launch (start us, length us, event | category | flops | bytes accessed | tf_op | source)
XLA Modules:
  0.0 638.2 jit_solution(15054875658132858146)
XLA Ops:
  1.9 1.8 copy.59.refs_13_
  3.7 8.9 %prepare.1 = (bf16[32,2560]{1,0:T(8,128)(2,1)}, bf16[32,1152]{1,0:T(8,128)(2,1)}, bf16[128,768]{1,0:T(8,128)(2,1)}, bf16[128,256]{1,0:T(8,128)(2,1)}, bf16[128,1...) custom-call(s32[3]{0:T(128)} %pad_add_fusion.places_ref, ...), custom_call_target="tpu_custom_call" | custom-call | tf_op jit(solution)/shard_map/prepare/pallas_call | solution.py:1518
  14.4 171.3 %gather_start.1 = (bf16[2560,1152]{1,0:T(8,128)(2,1)}, bf16[896,1280]{1,0:T(8,128)(2,1)}, bf16[384,1280]{1,0:T(8,128)(2,1)}, bf16[2688,640]{1,0:T(8,128)(2,1)}, ...) custom-call(bf16[80,1152]{1,0:T(8,128)(2,1)} %get-tuple-element.103., ...), custom_call_target="tpu_custom_call" | custom-call | tf_op jit(solution)/shard_map/gather_start/pallas_call | solution.py:343
  187.9 2.3 fusion.33
  190.3 2.0 select_convert_fusion
  193.6 37.6 %attend.1 = (bf16[1024,1280]{1,0:T(8,128)(2,1)}, bf16[1024,1280]{1,0:T(8,128)(2,1)}, bf16[1024,640]{1,0:T(8,128)(2,1)}, bf16[2560,1536]{1,0:T(8,128)(2,1)}, bf16[2560,896]{1,0:T(8,128)(2,1)}) custom-call(bf16[1024,1152]{1,0:T(8,128)(2,1)} %get-tuple-element.116.refs_0_, ...), custom_call_target="tpu_custom_call", output_to_operand_aliasing={{3}: (6, {}), {4}: (7, {})} | custom-call | tf_op jit(solution)/shard_map/attend/pallas_call | solution.py:870
  231.2 1.5 slice.93.refs_7_
  233.3 43.1 %reduce_out.1 = (f32[256,2560]{1,0:T(8,128)}, bf16[256,16]{1,0:T(8,128)(2,1)}, bf16[256,2688]{1,0:T(8,128)(2,1)}, bf16[2560,1536]{1,0:T(8,128)(2,1)}, bf16[2560,896]{1,0:T(8,128)(2,1)}) custom-call(bf16[1024,640]{1,0:T(8,128)(2,1)} %get-tuple-element.122.refs_0_.refs_2_, ...), custom_call_target="tpu_custom_call", output_to_operand_aliasing={{3}: (2, {}), {4}: (3, {})} | custom-call | tf_op jit(solution)/shard_map/reduce_out/pallas_call | solution.py:476
  279.6 2.9 ffn_extras.1
  282.4 80.7 %feed_forward.1 = (bf16[2048,128]{1,0:T(8,128)(2,1)}, bf16[2048,1024]{1,0:T(8,128)(2,1)}, bf16[2048,640]{1,0:T(8,128)(2,1)}, bf16[2048,512]{1,0:T(8,128)(2,1)}, ...) custom-call(bf16[256,2688]{1,0:T(8,128)(2,1)} %get-tuple-element.129, ...), custom_call_target="tpu_custom_call", output_to_operand_aliasing={{5}: (2, {}), {6}: (3, {})} | custom-call | tf_op jit(solution)/shard_map/feed_forward/pallas_call | solution.py:1135
  363.2 1.9 slice.95.refs_7_
  365.0 69.4 %feed_forward_back.1 = (f32[256,2688]{1,0:T(8,128)}, bf16[4,256,2688]{2,1,0:T(8,128)(2,1)}, f32[128,1024]{1,0:T(8,128)}, f32[128,640]{1,0:T(8,128)}, f32[128,512]{1,0:T(8,128)}, /*index=5*/f32[128,384]{1,0:T(8,128)}) custom-call(bf16[2048,1024]{1,0:T(8,128)(2,1)} %get-tuple-element.136.refs_0_, bf16[2048,640]{1,0:T(8,128)(2,1)} %get-tuple-element.137.refs_1_, ...), custom_call_target="tpu_custom_call" | custom-call | tf_op jit(solution)/shard_map/feed_forward_back/pallas_call | solution.py:1325
  434.5 55.6 %gather_grad.1 = (bf16[768,800]{1,0:T(8,128)(2,1)}, bf16[256,2688]{1,0:T(8,128)(2,1)}, f32[256,2560]{1,0:T(8,128)}, bf16[256,128]{1,0:T(8,128)(2,1)}, bf16[256,2...) custom-call(f32[256,2688]{1,0:T(8,128)} %get-tuple-element.146.refs_0_, ...), custom_call_target="tpu_custom_call" | custom-call | tf_op jit(solution)/shard_map/gather_grad/pallas_call | solution.py:343
  490.1 3.1 fusion.7.refs_8_
  493.2 36.0 %attend_back.1 = (bf16[1024,1280]{1,0:T(8,128)(2,1)}, bf16[1024,1280]{1,0:T(8,128)(2,1)}, f32[1024,128]{1,0:T(8,128)}, bf16[768,800]{1,0:T(8,128)(2,1)}, bf16[25...) custom-call(bf16[1024,1280]{1,0:T(8,128)(2,1)} %get-tuple-element.144.refs_0_, ...), custom_call_target="tpu_custom_call", output_to_operand_aliasing={{3}: (6, {})} | custom-call | tf_op jit(solution)/shard_map/attend_back/pallas_call | solution.py:870
  529.3 2.8 fusion.8
  532.2 1.7 fusion.4
  533.9 2.4 fusion.35
  537.9 1.7 fusion.13
  539.6 1.5 fusion.12
  543.6 26.5 %reduce_latents.1 = (bf16[256,1152]{1,0:T(8,128)(2,1)}, bf16[256,32]{1,0:T(8,128)(2,1)}, bf16[48,2560]{1,0:T(8,128)(2,1)}, bf16[8,16,3200]{2,1,0:T(8,128)(2,1)}) custom-call(bf16[1024,1280]{1,0:T(8,128)(2,1)} %get-tuple-element.161.refs_0_, bf16[1024,1280]{1,0:T(8,128)(2,1)} %get-tuple-element.162.refs_1_, ...), custom_call_target="tpu_custom_call" | custom-call | tf_op jit(solution)/shard_map/reduce_latents/pallas_call | solution.py:476
  572.7 46.7 %share.1 = (bf16[2,8,128,1280]{3,2,1,0:T(8,128)(2,1)}, f32[256,2560]{1,0:T(8,128)}) custom-call(bf16[128,2560]{1,0:T(8,128)(2,1)} %fusion.32.source, bf16[256,1152]{1,0:T(8,128)(2,1)} %get-tuple-element.168.refs_0_, bf16[256,32]{1,0:T(8,128)(2,1)} %get-tuple-element.169.refs_1_, bf16[2560,1152]{1,0:T(8,128)(2,1)} %get-tuple-element.170.refs_2_, ...), custom_call_target="tpu_custom_call" | custom-call | tf_op jit(solution)/shard_map/share/pallas_call | solution.py:629
  620.8 8.8 %sum_shared.1 = (f32[2,8,16,2560]{3,2,1,0:T(8,128)}, f32[8,16,2560]{2,1,0:T(8,128)}, f32[8,16,2560]{2,1,0:T(8,128)}, f32[8,16,2560]{2,1,0:T(8,128)}, f32[8,16,25...) custom-call(s32[8]{0:T(128)} %fusion.46.ids_ref, ...), custom_call_target="tpu_custom_call" | custom-call | tf_op jit(solution)/shard_map/sum_shared/pallas_call | solution.py:674
  629.7 6.7 %sum_split.1 = (f32[2,8,16,1600]{3,2,1,0:T(8,128)}, f32[8,16,1600]{2,1,0:T(8,128)}, f32[8,16,960]{2,1,0:T(8,128)}, f32[8,16,1280]{2,1,0:T(8,128)}, f32[8,16,640]{2,1,0:T(8,128)}) custom-call(s32[8]{0:T(128)} %fusion.46.ids_ref, bf16[8,96,800]{2,1,0:T(8,128)(2,1)} %bitcast.68, bf16[8,16,3200]{2,1,0:T(8,128)(2,1)} %get-tuple-element.180.refs_1_), custom_call_target="tpu_custom_call" | custom-call | tf_op jit(solution)/shard_map/sum_split/pallas_call | solution.py:674
  (82 shorter events, 17.9 us)
Async XLA Ops:
  3.7 9.5 %copy-start.15 = (f32[2560]{0:T(1024)S(1)}, f32[2560]{0:T(1024)}, u32[]{:S(2)}) copy-start(f32[2560]{0:T(1024)} %param.33) | copy-start | bytes 30724
  3.7 10.1 %copy-start.18 = (f32[768]{0:T(1024)S(1)}, f32[768]{0:T(1024)}, u32[]{:S(2)}) copy-start(f32[768]{0:T(1024)} %param.34) | copy-start | bytes 9220
  14.4 172.6 %copy-start.16 = (s32[1,1024]{1,0:T(1,128)S(1)}, s32[1,1024]{1,0:T(1,128)}, u32[]{:S(2)}) copy-start(s32[1,1024]{1,0:T(1,128)} %param.31) | copy-start | bytes 12292
  193.6 39.2 %copy-start.17 = (f32[2560]{0:T(1024)S(1)}, f32[2560]{0:T(1024)}, u32[]{:S(2)}) copy-start(f32[2560]{0:T(1024)} %param.36) | copy-start | bytes 30724
  529.2 3.0 copy-start.2
  529.3 3.0 copy-start.12
  532.2 1.7 copy-start.8
  533.9 3.6 copy-start.1
  533.9 3.6 copy-start.10
  533.9 4.0 copy-start.4
  537.5 2.1 copy-start.3
  539.6 2.2 copy-start
  543.6 26.5 %copy-start.5 = (bf16[256,2688]{1,0:T(8,128)(2,1)S(1)}, bf16[256,2688]{1,0:T(8,128)(2,1)}, u32[]{:S(2)}) copy-start(bf16[256,2688]{1,0:T(8,128)(2,1)} %get-tuple-element.105.refs_4_) | copy-start | bytes 4128772
  543.6 26.8 %copy-start.9 = (bf16[256,2688]{1,0:T(8,128)(2,1)S(1)}, bf16[256,2688]{1,0:T(8,128)(2,1)}, u32[]{:S(2)}) copy-start(bf16[256,2688]{1,0:T(8,128)(2,1)} %get-tuple-element.160) | copy-start | bytes 4128772
  543.6 26.8 %copy-start.13 = (bf16[256,16]{1,0:T(8,128)(2,1)S(1)}, bf16[256,16]{1,0:T(8,128)(2,1)}, u32[]{:S(2)}) copy-start(bf16[256,16]{1,0:T(8,128)(2,1)} %get-tuple-element.159) | copy-start | bytes 24580
  570.1 1.3 copy-start.6
  570.1 1.3 copy-start.14
  570.1 1.7 copy-start.11
  620.8 15.5 %copy-start.7 = (f32[256,2560]{1,0:T(8,128)S(1)}, f32[256,2560]{1,0:T(8,128)}, u32[]{:S(2)}) copy-start(f32[256,2560]{1,0:T(8,128)} %get-tuple-element.172) | copy-start | bytes 7864324

commit v6 on v5

--- a/solution.py
+++ b/solution.py
@@ -136,6 +136,19 @@
                 if rider["src_at"] is not None:
                     src = src.at[rider["src_at"]]
                 self.add(0, src, full, rider["step"])
+                continue
+            if rider["kind"] == "block":
+                held = [0]
+                for k, step in enumerate(rider["steps"]):
+                    for key in list(held):
+                        here = full.at[rider["at"](links.place, key)]
+                        self.add(k, here, here, step)
+                        held.append(key ^ step[1])
+                continue
+            if rider["kind"] == "blocks":
+                for key in rider["keys"]:
+                    here = full.at[rider["at"](links.place, key)]
+                    self.add(0, here, here, rider["step"])
                 continue
             count, pair, high = rider["count"], rider["pair"], rider["high"]
             if rider["kind"] == "one":
@@ -177,7 +190,7 @@
 def rider_steps(riders):
     steps = []
     for rider in riders:
-        if rider["kind"] == "plain":
+        if rider["kind"] in ("plain", "blocks"):
             steps.append(rider["step"])
         elif rider["kind"] == "one":
             pair, high = rider["pair"], rider["high"]
@@ -192,6 +205,8 @@
     for rider in riders:
         if rider["kind"] == "plain":
             total += 1
+        elif rider["kind"] == "blocks":
+            total += len(rider["keys"])
         elif rider["kind"] == "one":
             total += 3
         else:
@@ -300,6 +315,8 @@
             if group not in turns:
                 turns[group] = gather_rounds(links, all_src, all_out, groups[group])
                 for job in groups[group]:
+                    if not job.get("keep", True):
+                        continue
                     src = all_src[job["src"]]
                     if job.get("src_at") is not None:
                         src = src.at[job["src_at"]]
@@ -611,14 +628,22 @@
         work_refs = refs[:n_in] + refs[n_in + 1 : n_in + 1 + n_work]
         out_ref = refs[n_in]
         refs = refs[n_in + 1 + n_work :]
-        own_sems, send_sems, recv_sems = refs[-3:]
+        held, refs = refs[:n_in], refs[n_in:]
+        own_sems, send_sems, recv_sems, in_sems = refs[-4:]
+        fetched = [
+            pltpu.make_async_copy(work_refs[n], held[n], in_sems.at[n]) for n in range(n_in)
+        ]
+        for copy in fetched:
+            copy.start()
         links = Links(send_sems, recv_sems)
         links.greet(orders[0])
-        share = Share(links, n_t, orders, source, out_ref, *refs[:-3])
+        share = Share(links, n_t, orders, source, out_ref, *refs[:-4])
         for k, one in enumerate(share.rounds):
             one()
             if k == len(share.rounds) - 2:
-                work(work_refs)
+                for copy in fetched:
+                    copy.wait()
+                work(list(held) + list(work_refs[n_in:]))
         kept = share.keep(own_sems)
         for copy in kept:
             copy.start()
@@ -633,11 +658,16 @@
         ]
         + list(work_out),
         in_specs=[pl.BlockSpec(memory_space=pl.ANY)]
-        + [pl.BlockSpec(memory_space=pltpu.VMEM)] * n_in,
+        + [pl.BlockSpec(memory_space=pl.ANY)] * n_in,
         out_specs=[pl.BlockSpec(memory_space=pl.ANY)]
         + [pl.BlockSpec(memory_space=pltpu.VMEM)] * n_work,
-        scratch_shapes=scratch
-        + [pltpu.SemaphoreType.DMA((copies,)), pltpu.SemaphoreType.DMA((copies,))],
+        scratch_shapes=[pltpu.VMEM(a.shape, a.dtype) for a in work_in]
+        + scratch
+        + [
+            pltpu.SemaphoreType.DMA((copies,)),
+            pltpu.SemaphoreType.DMA((copies,)),
+            pltpu.SemaphoreType.DMA((n_in,)),
+        ],
         compiler_params=pltpu.CompilerParams(
             collective_id=collective_id, has_side_effects=True, vmem_limit_bytes=VMEM_LIMIT
         ),
@@ -759,7 +789,21 @@
 
 
 def attn_bwd_kernel(
-    per_step, qa_ref, kv_ref, o_ref, do_ref, rope_ref, pe_ref, dq_ref, dkv_ref, dpe_ref, dk_acc, dv_acc
+    per_step,
+    qa_ref,
+    kv_ref,
+    o_ref,
+    do_ref,
+    rope_ref,
+    pe_ref,
+    codes_ref,
+    dq_ref,
+    dkv_ref,
+    dpe_ref,
+    cq_ref,
+    ckv_ref,
+    dk_acc,
+    dv_acc,
 ):
     length = qa_ref.shape[0]
     step = pl.program_id(0)
@@ -823,6 +867,13 @@
         dk_all = dk_acc[...] * SCORE_SCALE
         dkv_ref[:, span] = narrow(jnp.where(upper, dv_acc[...], dk_all))
         dpe_ref[...] += jnp.where(upper & (lane < 96), dk_all, 0.0)
+    cq_ref[...] = dot_tn(codes_ref[...], dq_ref[...])
+    ckv_ref[...] = dot_tn(codes_ref[...], dkv_ref[...])
+
+    @pl.when(step == pl.num_programs(0) - 1)
+    def _():
+        turned_back = rope_mix(dpe_ref[...], rope_ref[0], -rope_ref[1], -rope_ref[2])
+        dpe_ref[...] = pltpu.roll(turned_back, PLAIN_HEAD_DIM + 2 * RANK, 1)
 
 
 def ridden_call(
@@ -924,7 +975,7 @@
     )
 
 
-def attend_back(q_aug, kv, heads_out, heads_grad, rope, pe_aug, riders, ridden, carried, fresh):
+def attend_back(q_aug, kv, heads_out, heads_grad, rope, pe_aug, codes, riders, ridden, carried, fresh):
     length = q_aug.shape[0]
     heads = q_aug.shape[1] // HEAD_LANES
     per_step = 2 if heads % 2 == 0 else 1
@@ -932,14 +983,17 @@
     whole = lambda a: pl.BlockSpec(a.shape, lambda h: (0,) * a.ndim)
     columns = pl.BlockSpec((length, wide), lambda h: (0, h))
     packed = pl.BlockSpec((length, HEAD_LANES), lambda h: (0, h * per_step // 2))
-    arrays = [q_aug, kv, heads_out, heads_grad, rope, pe_aug]
+    rows_in, lane_block = codes
+    arrays = [q_aug, kv, heads_out, heads_grad, rope, pe_aug, rows_in]
     in_specs = [columns, columns, packed, packed, whole(rope), whole(pe_aug)]
+    in_specs.append(pl.BlockSpec((length, CODE_LANES), lambda h: (0, lane_block)))
     out_shape = [
         jax.ShapeDtypeStruct((length, heads * HEAD_LANES), BF16),
         jax.ShapeDtypeStruct((length, heads * HEAD_LANES), BF16),
         jax.ShapeDtypeStruct((length, HEAD_LANES), F32),
-    ]
+    ] + [jax.ShapeDtypeStruct((CODE_LANES, heads * HEAD_LANES), F32)] * 2
     out_specs = [columns, columns, pl.BlockSpec((length, HEAD_LANES), lambda h: (0, 0))]
+    out_specs += [pl.BlockSpec((CODE_LANES, wide), lambda h: (0, h))] * 2
     scratch = [pltpu.VMEM((length, HEAD_LANES), F32), pltpu.VMEM((length, HEAD_LANES), F32)]
     return ridden_call(
         functools.partial(attn_bwd_kernel, per_step),
@@ -1099,6 +1153,30 @@
 
         links.arrived(crossing[(0, 0)])
         first_chunk((0, 0))
+
+        def later(b, g_rows, c):
+            main = mains[c]
+            back = dot_nn(g_rows, w_held[c][:, gu[c] :])
+            pre, at = forward(b, c, back)
+            if tails[c]:
+                at_tail = slice(main, main + tail_wide)
+                hid, both_grads = tail_middle(
+                    pre[:, at_tail], dot_nn(g_rows, w_held[c][:, at_tail]), tail
+                )
+                hid_refs[c][at, main:] = narrow(hid)
+                grad_refs[c][at, at_tail] = narrow(both_grads)
+
+        def later_chunks(pairs):
+            places = [block_of(key, place) // 2 for key in pairs]
+            g_copy(places[0], 0).start()
+            for n, b in enumerate(places):
+                if n + 1 < len(places):
+                    g_copy(places[n + 1], (n + 1) % 2).start()
+                g_copy(b, n % 2).wait()
+                for c in range(1, chunks):
+                    later(b, g_held[n % 2], c)
+
+        waiting = [(0, 0)]
         for level in range(1, len(slow) + 1):
             here = [key for key in keys if len(bits_of[key]) == level]
             for key in here:
@@ -1109,24 +1187,15 @@
             for key in here:
                 links.arrived(crossing[key])
                 first_chunk(key)
-        ride.finish()
-        for c in range(1, chunks):
-            fetch[c].start()
-            fetch[c].wait()
-
-            def later(b, g_rows, c=c):
-                main = mains[c]
-                back = dot_nn(g_rows, w_held[c][:, gu[c] :])
-                pre, at = forward(b, c, back)
-                if tails[c]:
-                    at_tail = slice(main, main + tail_wide)
-                    hid, both = tail_middle(
-                        pre[:, at_tail], dot_nn(g_rows, w_held[c][:, at_tail]), tail
-                    )
-                    hid_refs[c][at, main:] = narrow(hid)
-                    grad_refs[c][at, at_tail] = narrow(both)
-
-            over_blocks(later)
+            waiting += here
+            if level == len(slow) - 1:
+                ride.finish()
+                for c in range(1, chunks):
+                    fetch[c].start()
+                    fetch[c].wait()
+                later_chunks(waiting)
+                waiting = []
+        later_chunks(waiting)
         codes_ref[...] = x_held[:, width:]
         links.close()
 
@@ -1168,7 +1237,7 @@
 
 
 def remote_ffn_back(
-    grads, hids, weights, extras, x_codes, g_codes, mains, tail_wide, keys, ways, block_of, rows, name, collective_id
+    grads, hids, weights, extras, x_codes, g_all, mains, tail_wide, keys, ways, block_of, rows, name, collective_id
 ):
     width = weights[0].shape[0]
     aug = width + CODE_LANES
@@ -1183,10 +1252,11 @@
     later_slot = {entry: n for n, entry in enumerate(later)}
     steps = distinct([core_step] + ways[0])
     count = 2 * len(keys) + len(plan)
-    operands = list(grads) + list(hids) + list(weights) + [x_codes, g_codes]
+    operands = list(grads) + list(hids) + list(weights) + [x_codes, g_all]
     shapes = [o.shape for o in operands]
     for c in range(chunks):
         shapes[2 * chunks + c] = (aug, weights[c].shape[1])
+    shapes[3 * chunks + 1] = x_codes.shape
 
     def kernel(*refs):
         n_in = len(operands)
@@ -1206,7 +1276,10 @@
         for n in order:
             is_weight = 2 * chunks <= n < 3 * chunks
             to = held[n].at[pl.ds(0, width)] if is_weight else held[n]
-            copy = pltpu.make_async_copy(in_refs[n], to, in_sems.at[n])
+            src = in_refs[n]
+            if n == 3 * chunks + 1:
+                src = src.at[:, pl.ds(width, CODE_LANES)]
+            copy = pltpu.make_async_copy(src, to, in_sems.at[n])
             copy.start()
             started.append(copy)
         for c in range(chunks):
@@ -1747,10 +1820,11 @@
 
     def latent_work(refs):
         x_ref, norm_ref, q_norm_ref, kv_norm_ref, in_ref, b_ref, qb_ref, kvb_ref = refs[12:20]
-        latent_ref, codes_ref, w_ref, own_ref = refs[20:24]
+        latent_ref, codes_ref, rows_ref, w_ref, own_ref = refs[20:25]
         x_f = x_ref[...].astype(F32)
         scale = lax.rsqrt(jnp.mean(x_f * x_f, axis=-1, keepdims=True) + NORM_EPS)
         h_rows = narrow(x_f * scale * norm_ref[...])
+        rows_ref[...] = h_rows
         codes = narrow(dot_nt(h_rows, in_ref[...]))
         latent = dot_nn(h_rows, w_ref[...]) + ADAPT_SCALE * dot_nn(codes, b_ref[...])
         latent_ref[...] = latent
@@ -1772,7 +1846,7 @@
 
     down_steps = outer_first + (t_slow if shares == n_t else []) + t_core
     n_start_outs = 9
-    latent_at, w_at, lat_own_at = n_start_outs, n_start_outs + 2, n_start_outs + 3
+    w_at, lat_own_at = n_start_outs + 3, n_start_outs + 4
     n_start_sources = 20
     jobs = [
         dict(
@@ -1802,10 +1876,16 @@
                 group="own",
             )
         )
-    jobs += group_jobs(4, 4, (group_b, group_b))
-    jobs += token_jobs(n_start_sources + 3, 8, 2, "latents")
+    def own_block(dd, tt):
+        return (pl.ds(pl.multiple_of(group_block(dd, tt) * rows, 16), rows),)
+
+    jobs.append(dict(src=4, out=4, out_at=own_block, steps=t_slow + t_core, group="rows"))
+    jobs.append(
+        dict(src=4, out=4, out_at=own_block, steps=[("dp", pair)], group="pair", keep=False)
+    )
+    jobs += token_jobs(n_start_sources + 4, 8, 2, "latents")
     set_mark = jnp.full((16, 128), sequence_adapter_index[0].astype(F32)).astype(BF16)
-    w_down, w_q, w_kv, w_out, g_all, set_marks, w_ffn0, w_ffn1, lat_all, latent, down_codes_in = (
+    start = (
         remote_gather(
             [
                 down_mine,
@@ -1849,24 +1929,27 @@
             "gather_start",
             1,
             riders=[ride_one(6, 9, 10, 0, ffn_rows_each)],
-            order=["down", "up", "out", "down", "up", "down", "own", "out", "rows", "down"]
-            + ["up", "out", "ride"]
+            order=["down", "up", "out", "rows", "down", "up", "down", "own", "out", "pair"]
+            + ["down", "up", "out", "ride"]
             + ["down"] * (len(down_steps) - 4)
-            + [("all", "down"), "work", "latents", "rows"]
+            + [("all", "down"), "work", "latents"]
             + ["latents"] * len(t_slow)
             + ["rows"],
             near_outs=[
                 jax.ShapeDtypeStruct((rows, down_wide), F32),
                 jax.ShapeDtypeStruct((rows, 2 * RANK), BF16),
+                jax.ShapeDtypeStruct((rows, width), BF16),
             ],
             scratch=[
                 jax.ShapeDtypeStruct((width, down_wide), BF16),
                 jax.ShapeDtypeStruct((rows, lat_wide), BF16),
             ],
             work=latent_work,
-            late=[(n_start_sources + 2, 0)],
+            late=[(n_start_sources + 3, 0)],
         )
     )
+    w_down, w_q, w_kv, w_out, g_all, set_marks, w_ffn0, w_ffn1, lat_all = start[:9]
+    latent, down_codes_in, attn_rows = start[9:]
     set_all = set_marks[:, 0, 0].astype(jnp.int32)
     set_peer = lax.dynamic_index_in_dim(set_all, jnp.bitwise_xor(d, pair), 0, keepdims=False)
     set_even = jnp.where(first, set_own, set_peer)
@@ -1901,15 +1984,6 @@
         doc_lane & ~is_doc, -BIG, jnp.where((lane_ids >= 96) & (lane_ids < 99), 1.0, 0.0)
     )
 
-    residual = inputs[0].astype(F32)
-    attn_normed, attn_scale = normalize(residual, attention_norm_gain)
-    attn_rows = narrow(attn_normed)
-    q_latent = latent[:, :q_lat]
-    kv_latent = latent[:, q_lat : q_lat + kv_lat]
-    q_normed, q_scale = normalize(q_latent, query_latent_gain)
-    kv_normed, kv_scale = normalize(kv_latent, keyvalue_latent_gain)
-    q_input = narrow(q_normed)
-    kv_input = narrow(kv_normed)
     pe_rows = lat_all[:, pe_at : pe_at + ROTARY_DIM].astype(F32)
     pe_a, pe_b = pe_rows[:, : ROTARY_DIM // 2], pe_rows[:, ROTARY_DIM // 2 :]
     pe_aug = narrow(
@@ -1924,7 +1998,11 @@
         )
         + doc_k
     )
-    q_aug, kv, head_out, w_ffn0, w_ffn1 = attend(
+    def pair_rows(place, key):
+        block = group_block(jnp.bitwise_xor(place["dp"], pair), jnp.bitwise_xor(place["tensor"], key))
+        return pl.ds(pl.multiple_of(block * rows, 16), rows)
+
+    q_aug, kv, head_out, w_ffn0, w_ffn1, g_all = attend(
         lat_all,
         w_q,
         w_kv,
@@ -1933,8 +2011,13 @@
         doc_q,
         q_lat + CODE_LANES,
         q_lat,
-        [ride_two(0, 1), ride_two(0, 2, 0, cut_a), ride_one(1, 2, 3, 0, cut_a)],
-        [w_ffn0, w_ffn1],
+        [
+            ride_two(0, 1),
+            ride_two(0, 2, 0, cut_a),
+            ride_one(1, 3, 4, 0, cut_a),
+            dict(kind="block", out=2, at=pair_rows, steps=t_slow),
+        ],
+        [w_ffn0, w_ffn1, g_all],
         [ffn_mine[1], ffn_other[1]],
     )
     tensor_keys = [(0, r) for r in reversed(range(0, n_t, 2))]
@@ -1960,7 +2043,7 @@
         own_ref[at, :width] = normed
         own_ref[at, width:] = narrow(dot_nt(normed, lanes_ref[...]))
 
-    middle, out_codes, x_own, w_ffn0, w_ffn1 = remote_reduce(
+    middle, out_codes, x_own, w_ffn0, w_ffn1, g_all = remote_reduce(
         [head_out, w_out],
         [head_out.shape, w_out.shape],
         out_term,
@@ -1972,8 +2055,17 @@
         3,
         riders=[ride_two(0, 2, cut_a, ffn_rows_each - cut_a)]
         + [ride_two(0, z) for z in range(3, z_count)]
-        + [ride_one(1, 2, 3, cut_a, ffn_rows_each - cut_a)],
-        ridden=[w_ffn0, w_ffn1],
+        + [
+            ride_one(1, 3, 4, cut_a, ffn_rows_each - cut_a),
+            dict(
+                kind="blocks",
+                out=2,
+                at=pair_rows,
+                keys=list(range(0, n_t, 2)),
+                step=t_core[0],
+            ),
+        ],
+        ridden=[w_ffn0, w_ffn1, g_all],
         carried=[ffn_mine[1], ffn_other[1]],
         after=middle_work,
         after_in=[inputs[0], out_out, feedforward_norm_gain[None], gu_in_lanes],
@@ -1983,8 +2075,6 @@
             jax.ShapeDtypeStruct((rows, aug), BF16),
         ],
     )
-    ffn_rows = x_own[:, :width]
-    ffn_scale = lax.rsqrt(jnp.mean(middle * middle, axis=-1, keepdims=True) + NORM_EPS)
 
     def group_block_of(key, place):
         return group_block(
@@ -2012,7 +2102,7 @@
         ffn_weights,
         ffn_extra,
         x_codes,
-        g_all[:, width:],
+        g_all,
         mains,
         tail_wide,
         group_keys,
@@ -2106,14 +2196,14 @@
         else [],
         distant=(n_grad - 1,) if ride_down else (),
         order=[
+            hidden_work,
+            "hidden",
             functools.partial(grad_work, 0),
             "top",
+            "ride",
             functools.partial(grad_work, 1),
             "bottom",
-            hidden_work,
             "hidden",
-            "hidden",
-            "ride",
             "top",
             "bottom",
         ]
@@ -2133,7 +2223,6 @@
     )
     middle_grad, gu_code_grad, attn_grad_aug, heads_grad, grad_lanes = sent[n_far:]
     gu_code_grad = gu_code_grad[:, : 2 * RANK]
-    attn_grad = attn_grad_aug[:, :width]
     hidden_terms = sent[0]
     out_a = dot_tn(grad_lanes, head_out)[:RANK]
     hidden_ride = [
@@ -2150,13 +2239,14 @@
     ]
     if ride_down:
         down_far = narrow(down_chip[2].astype(F32) + sent[1].astype(F32))
-        dq, dkv, dpe, hidden_terms, came_pair, came_y = attend_back(
+        dq, dkv, pe_padded, cq, ckv, hidden_terms, came_pair, came_y = attend_back(
             q_aug,
             kv,
             head_out,
             heads_grad,
             rope,
             pe_aug,
+            (lat_all, q_lat // CODE_LANES),
             [
                 dict(kind="plain", src=1, src_at=1, out=1, step=("dp", pair)),
                 dict(kind="plain", src=2, src_at=None, out=2, step=("tensor", 2)),
@@ -2167,8 +2257,8 @@
             [(rows, aug), (rows, aug)],
         )
     else:
-        dq, dkv, dpe, hidden_terms = attend_back(
-            q_aug, kv, head_out, heads_grad, rope, pe_aug, hidden_ride, [hidden_terms], [], []
+        dq, dkv, pe_padded, cq, ckv, hidden_terms = attend_back(
+            q_aug, kv, head_out, heads_grad, rope, pe_aug, (lat_all, q_lat // CODE_LANES), hidden_ride, [hidden_terms], [], []
         )
         places = n_t // 2
         ffn_out = down_chip[places:].astype(F32) + hop(down_chip[:places], ("dp", pair)).astype(F32)
@@ -2178,12 +2268,6 @@
                 F32
             )
         ffn_out = ffn_out[0]
-    pe_g = dpe[:, PLAIN_HEAD_DIM : PLAIN_HEAD_DIM + ROTARY_DIM]
-    pe_ga, pe_gb = pe_g[:, : ROTARY_DIM // 2], pe_g[:, ROTARY_DIM // 2 :]
-    pe_grad = jnp.concatenate(
-        [pe_ga * cos_part + pe_gb * sin_part, pe_gb * cos_part - pe_ga * sin_part], axis=1
-    )
-    pe_padded = jnp.pad(pe_grad, ((0, 0), (2 * RANK, CODE_LANES - 2 * RANK - ROTARY_DIM)))
     def latent_term(held, place, key):
         at = token_rows(key, place)
         from_q = dot_nt(held[0][at, :], held[2][...])
@@ -2197,9 +2281,8 @@
             axis=1,
         )
 
-    lat_codes = lat_all[:, q_lat : q_lat + CODE_LANES]
-    qb_b = ADAPT_SCALE * dot_tn(lat_codes, dq)[:RANK]
-    kvb_b = ADAPT_SCALE * dot_tn(lat_codes, dkv)[RANK : 2 * RANK]
+    qb_b = ADAPT_SCALE * cq[:RANK]
+    kvb_b = ADAPT_SCALE * ckv[RANK : 2 * RANK]
     head_own = narrow(jnp.concatenate([qb_b, kvb_b, out_a], axis=1))
     operands = [dq, dkv, w_q, w_kv, pe_padded]
     small_at, small_wide = [0], []
@@ -2288,9 +2371,9 @@
     outputs = narrow(
         middle + RESIDUAL * (ffn_out[:, :width] + ADAPT_SCALE * dot_nn(down_codes, down_out))
     )
-    gu_a = dot_tn(gu_code_grad, ffn_rows)
-    out_b = ADAPT_SCALE * dot_tn(out_codes, attn_grad)
-    down_b = ADAPT_SCALE * dot_tn(down_codes, g_own[:, :width])
+    gu_a = dot_tn(gu_code_grad, x_own)[:, :width]
+    out_b = ADAPT_SCALE * dot_tn(out_codes, attn_grad_aug)[:, :width]
+    down_b = ADAPT_SCALE * dot_tn(down_codes, g_own)[:, :width]
     table_orders = [outer_first + t_slow + t_core, t_slow + outer_first + t_core]
     shared = jnp.concatenate([narrow(gu_a), narrow(out_b), narrow(down_b), late_terms], axis=0)
     shared = jnp.pad(shared, ((0, -shared.shape[0] % (16 * n_t)), (0, 0)))

time: 642 us -> 622 us (0.969)
  Pallas kernels: 594 us -> 582 us
    pallas_call x2, Pallas kernels: 227 us -> 220 us  [remote_gather(): pl.pallas_call(kernel, out_shape=[jax.ShapeDtypeStruct(o, BF16) for o in...]
where the time goes in v6:
time: 622 us; the launch traced here: 618 us
  Pallas kernels  582 us (94%)
  other arithmetic  18.5 us (3%)
  local copies, waits for them, and re-layouts  10 us (2%)
    pallas_call x2, Pallas kernels, remote_gather(): pl.pallas_call(kernel, out_shape=[jax.ShapeDtypeStruct(o, BF16) for o in...  220 us
    pallas_call x1, Pallas kernels, remote_ffn(): pl.pallas_call(kernel, in_specs=[vmem_spec, any_spec] + [any_spec] * (2 *...  80.5 us
    pallas_call x2, Pallas kernels, ridden_call(): pl.pallas_call(body, grid=grid, in_specs=list(in_specs) + [any_spec] * n_...  70.4 us
    pallas_call x2, Pallas kernels, remote_reduce(): pl.pallas_call(kernel, out_shape=after_out + [jax.ShapeDtypeStruct(r.shap...  69.8 us
    pallas_call x1, Pallas kernels, remote_ffn_back(): pl.pallas_call(kernel, out_shape=[jax.ShapeDtypeStruct((rows, aug), F32),...  68.2 us
    pallas_call x1, Pallas kernels, remote_share(): pl.pallas_call(kernel, out_shape=[jax.ShapeDtypeStruct((parts, n_dp, term...  44.8 us
    pallas_call x2, Pallas kernels, set_sums(): pl.pallas_call(kernel, grid_spec=pltpu.PrefetchScalarGridSpec(num_scalar_...  16 us

profile of v6, /device:TPU:0, one launch (start us, length us, event | category | flops | bytes accessed | tf_op | source)
XLA Modules:
  0.0 618.3 jit_solution(1245784239364274636)
XLA Ops:
  1.9 1.8 copy.56.refs_13_
  3.7 8.9 %prepare.1 = (bf16[32,2560]{1,0:T(8,128)(2,1)}, bf16[32,1152]{1,0:T(8,128)(2,1)}, bf16[128,768]{1,0:T(8,128)(2,1)}, bf16[128,256]{1,0:T(8,128)(2,1)}, bf16[128,1...) custom-call(s32[3]{0:T(128)} %pad_add_fusion.places_ref, ...), custom_call_target="tpu_custom_call" | custom-call | tf_op jit(solution)/shard_map/prepare/pallas_call | solution.py:1591
  14.4 167.6 %gather_start.1 = (bf16[2560,1152]{1,0:T(8,128)(2,1)}, bf16[896,1280]{1,0:T(8,128)(2,1)}, bf16[384,1280]{1,0:T(8,128)(2,1)}, bf16[2688,640]{1,0:T(8,128)(2,1)}, ...) custom-call(bf16[80,1152]{1,0:T(8,128)(2,1)} %get-tuple-element.108., ...), custom_call_target="tpu_custom_call" | custom-call | tf_op jit(solution)/shard_map/gather_start/pallas_call | solution.py:360
  182.1 1.1 slice_convert_fusion.1
  184.1 2.3 fusion.21
  186.6 2.0 select_convert_fusion
  188.6 1.2 pad_maximum_fusion.refs_3_.refs_4_
  189.8 34.6 %attend.1 = (bf16[1024,1280]{1,0:T(8,128)(2,1)}, bf16[1024,1280]{1,0:T(8,128)(2,1)}, bf16[1024,640]{1,0:T(8,128)(2,1)}, bf16[2560,1536]{1,0:T(8,128)(2,1)}, bf16...) custom-call(bf16[1024,1152]{1,0:T(8,128)(2,1)} %get-tuple-element.12, ...), custom_call_target="tpu_custom_call", output_to_operand_aliasing={{3}: (6, {}), {4}: (7, {}), {5}: (8, {})} | custom-call | tf_op jit(solution)/shard_map/attend/pallas_call | solution.py:921
  224.5 1.5 slice.79.refs_8_
  226.6 44.7 %reduce_out.1 = (f32[256,2560]{1,0:T(8,128)}, bf16[256,16]{1,0:T(8,128)(2,1)}, bf16[256,2688]{1,0:T(8,128)(2,1)}, bf16[2560,1536]{1,0:T(8,128)(2,1)}, bf16[2560,...) custom-call(bf16[1024,640]{1,0:T(8,128)(2,1)} %get-tuple-element.128.refs_, ...), custom_call_target="tpu_custom_call", output_to_operand_aliasing={{3}: (2, {}), {4}: (3, {}), {5}: (4, {})} | custom-call | tf_op jit(solution)/shard_map/reduce_out/pallas_call | solution.py:493
  274.5 2.9 ffn_extras.1
  277.4 80.5 %feed_forward.1 = (bf16[2048,128]{1,0:T(8,128)(2,1)}, bf16[2048,1024]{1,0:T(8,128)(2,1)}, bf16[2048,640]{1,0:T(8,128)(2,1)}, bf16[2048,512]{1,0:T(8,128)(2,1)}, ...) custom-call(bf16[256,2688]{1,0:T(8,128)(2,1)} %get-tuple-element.136, ...), custom_call_target="tpu_custom_call", output_to_operand_aliasing={{5}: (2, {}), {6}: (3, {})} | custom-call | tf_op jit(solution)/shard_map/feed_forward/pallas_call | solution.py:1204
  357.9 68.2 %feed_forward_back.1 = (f32[256,2688]{1,0:T(8,128)}, bf16[4,256,2688]{2,1,0:T(8,128)(2,1)}, f32[128,1024]{1,0:T(8,128)}, f32[128,640]{1,0:T(8,128)}, f32[128,512]{1,0:T(8,128)}, /*index=5*/f32[128,384]{1,0:T(8,128)}) custom-call(bf16[2048,1024]{1,0:T(8,128)(2,1)} %get-tuple-element.143.refs_0_, bf16[2048,640]{1,0:T(8,128)(2,1)} %get-tuple-element.144.refs_1_, ...), custom_call_target="tpu_custom_call" | custom-call | tf_op jit(solution)/shard_map/feed_forward_back/pallas_call | solution.py:1398
  426.1 52.6 %gather_grad.1 = (bf16[768,800]{1,0:T(8,128)(2,1)}, bf16[256,2688]{1,0:T(8,128)(2,1)}, f32[256,2560]{1,0:T(8,128)}, bf16[256,128]{1,0:T(8,128)(2,1)}, bf16[256,2...) custom-call(f32[256,2688]{1,0:T(8,128)} %get-tuple-element.153.refs_0_, ...), custom_call_target="tpu_custom_call" | custom-call | tf_op jit(solution)/shard_map/gather_grad/pallas_call | solution.py:360
  478.7 3.1 fusion.7.refs_9_
  481.8 35.8 %attend_back.1 = (bf16[1024,1280]{1,0:T(8,128)(2,1)}, bf16[1024,1280]{1,0:T(8,128)(2,1)}, f32[1024,128]{1,0:T(8,128)}, f32[128,1280]{1,0:T(8,128)}, f32[128,1280...) custom-call(bf16[1024,1280]{1,0:T(8,128)(2,1)} %get-tuple-element.15, ...), custom_call_target="tpu_custom_call", output_to_operand_aliasing={{5}: (7, {})} | custom-call | tf_op jit(solution)/shard_map/attend_back/pallas_call | solution.py:921
  519.6 25.1 %reduce_latents.1 = (bf16[256,1152]{1,0:T(8,128)(2,1)}, bf16[256,32]{1,0:T(8,128)(2,1)}, bf16[48,2560]{1,0:T(8,128)(2,1)}, bf16[8,16,3200]{2,1,0:T(8,128)(2,1)}) custom-call(bf16[1024,1280]{1,0:T(8,128)(2,1)} %get-tuple-element.168.refs_0_, bf16[1024,1280]{1,0:T(8,128)(2,1)} %get-tuple-element.169.refs_1_, ...), custom_call_target="tpu_custom_call" | custom-call | tf_op jit(solution)/shard_map/reduce_latents/pallas_call | solution.py:493
  544.7 1.6 fusion.30.ids_ref
  546.3 7.1 %sum_split.1 = (f32[2,8,16,1600]{3,2,1,0:T(8,128)}, f32[8,16,1600]{2,1,0:T(8,128)}, f32[8,16,960]{2,1,0:T(8,128)}, f32[8,16,1280]{2,1,0:T(8,128)}, f32[8,16,640]{2,1,0:T(8,128)}) custom-call(s32[8]{0:T(128)} %fusion.30.ids_ref, bf16[8,96,800]{2,1,0:T(8,128)(2,1)} %bitcast.65, bf16[8,16,3200]{2,1,0:T(8,128)(2,1)} %get-tuple-element.190.refs_1_), custom_call_target="tpu_custom_call" | custom-call | tf_op jit(solution)/shard_map/sum_split/pallas_call | solution.py:704
  555.3 2.1 fusion.8
  559.3 44.8 %share.1 = (bf16[2,8,128,1280]{3,2,1,0:T(8,128)(2,1)}, f32[256,2560]{1,0:T(8,128)}) custom-call(bf16[128,2560]{1,0:T(8,128)(2,1)} %fusion.17.source, bf16[256,1152]{1,0:T(8,128)(2,1)} %get-tuple-element.178.refs_0_, bf16[256,32]{1,0:T(8,128)(2,1)} %get-tuple-element.179.refs_1_, bf16[2560,1152]{1,0:T(8,128)(2,1)} %get-tuple-element.180.refs_2_, ...), custom_call_target="tpu_custom_call" | custom-call | tf_op jit(solution)/shard_map/share/pallas_call | solution.py:654
  604.0 8.9 %sum_shared.1 = (f32[2,8,16,2560]{3,2,1,0:T(8,128)}, f32[8,16,2560]{2,1,0:T(8,128)}, f32[8,16,2560]{2,1,0:T(8,128)}, f32[8,16,2560]{2,1,0:T(8,128)}, f32[8,16,25...) custom-call(s32[8]{0:T(128)} %fusion.30.ids_ref, ...), custom_call_target="tpu_custom_call" | custom-call | tf_op jit(solution)/shard_map/sum_shared/pallas_call | solution.py:704
  613.0 3.5 fusion.4
  616.5 1.5 copy.69
  (73 shorter events, 11.7 us)
Async XLA Ops:
  3.7 9.5 %copy-start.14 = (f32[2560]{0:T(1024)S(1)}, f32[2560]{0:T(1024)}, u32[]{:S(2)}) copy-start(f32[2560]{0:T(1024)} %param.33) | copy-start | bytes 30724
  3.7 10.1 %copy-start.16 = (f32[768]{0:T(1024)S(1)}, f32[768]{0:T(1024)}, u32[]{:S(2)}) copy-start(f32[768]{0:T(1024)} %param.34) | copy-start | bytes 9220
  14.4 168.7 %copy-start.13 = (s32[1,1024]{1,0:T(1,128)S(1)}, s32[1,1024]{1,0:T(1,128)}, u32[]{:S(2)}) copy-start(s32[1,1024]{1,0:T(1,128)} %param.31) | copy-start | bytes 12292
  189.8 36.2 %copy-start.15 = (f32[2560]{0:T(1024)S(1)}, f32[2560]{0:T(1024)}, u32[]{:S(2)}) copy-start(f32[2560]{0:T(1024)} %param.36) | copy-start | bytes 30724
  481.8 36.7 %copy-start = (bf16[1024,640]{1,0:T(8,128)(2,1)S(1)}, bf16[1024,640]{1,0:T(8,128)(2,1)}, u32[]{:S(2)}) copy-start(bf16[1024,640]{1,0:T(8,128)(2,1)} %get-tuple-element.128.refs_0_.refs_2_) | copy-start | bytes 3932164
  481.8 36.7 %copy-start.8 = (bf16[1024,128]{1,0:T(8,128)(2,1)S(1)}, bf16[1024,128]{1,0:T(8,128)(2,1)}, u32[]{:S(2)}) copy-start(bf16[1024,128]{1,0:T(8,128)(2,1)} %get-tuple-element.173) | copy-start | bytes 786436
  519.6 33.8 %copy-start.12 = (bf16[256,128]{1,0:T(8,128)(2,1)S(1)}, bf16[256,128]{1,0:T(8,128)(2,1)}, u32[]{:S(2)}) copy-start(bf16[256,128]{1,0:T(8,128)(2,1)} %get-tuple-element.165) | copy-start | bytes 196612
  544.7 8.7 %copy-start.1 = (bf16[256,2688]{1,0:T(8,128)(2,1)S(1)}, bf16[256,2688]{1,0:T(8,128)(2,1)}, u32[]{:S(2)}) copy-start(bf16[256,2688]{1,0:T(8,128)(2,1)} %get-tuple-element.136.x_ref) | copy-start | bytes 4128772
  546.3 7.5 %copy-start.6 = (bf16[256,2688]{1,0:T(8,128)(2,1)S(1)}, bf16[256,2688]{1,0:T(8,128)(2,1)}, u32[]{:S(2)}) copy-start(bf16[256,2688]{1,0:T(8,128)(2,1)} %get-tuple-element.167) | copy-start | bytes 4128772
  546.3 7.5 %copy-start.11 = (bf16[256,16]{1,0:T(8,128)(2,1)S(1)}, bf16[256,16]{1,0:T(8,128)(2,1)}, u32[]{:S(2)}) copy-start(bf16[256,16]{1,0:T(8,128)(2,1)} %get-tuple-element.166) | copy-start | bytes 24580
  553.4 1.3 copy-start.4
  553.4 1.8 copy-start.5
  553.8 3.5 copy-start.7
  555.3 2.2 copy-start.2
  557.3 0.9 copy-start.9
  557.4 1.0 slice-start
  604.0 8.9 %copy-start.10 = (bf16[16,2560]{1,0:T(8,128)(2,1)S(1)}, bf16[16,2560]{1,0:T(8,128)(2,1)}, u32[]{:S(2)}) copy-start(bf16[16,2560]{1,0:T(8,128)(2,1)} %get-tuple-element.164) | copy-start | bytes 245764
  613.0 3.5 copy-start.3

commit v7 on v6

--- a/solution.py
+++ b/solution.py
@@ -1845,6 +1845,7 @@
         )
 
     down_steps = outer_first + (t_slow if shares == n_t else []) + t_core
+    cut_c = ffn_rows_each * 4 // 5 // 16 * 16
     n_start_outs = 9
     w_at, lat_own_at = n_start_outs + 3, n_start_outs + 4
     n_start_sources = 20
@@ -1928,7 +1929,7 @@
             ],
             "gather_start",
             1,
-            riders=[ride_one(6, 9, 10, 0, ffn_rows_each)],
+            riders=[ride_one(6, 9, 10, 0, cut_c)],
             order=["down", "up", "out", "rows", "down", "up", "down", "own", "out", "pair"]
             + ["down", "up", "out", "ride"]
             + ["down"] * (len(down_steps) - 4)
@@ -1963,6 +1964,7 @@
         tail_wide,
     )
     cut_a = ffn_rows_each // 48 * 16
+    cut_d = ffn_rows_each // 32 * 16
 
     cos_part, sin_part = rope_tables(document_numbers)
     zeros_l = jnp.zeros((length, PLAIN_HEAD_DIM), F32)
@@ -2012,13 +2014,14 @@
         q_lat + CODE_LANES,
         q_lat,
         [
-            ride_two(0, 1),
-            ride_two(0, 2, 0, cut_a),
+            ride_two(0, 1, 0, cut_c),
+            ride_two(0, 2, 0, cut_d),
+            ride_one(0, 5, 6, cut_c, ffn_rows_each - cut_c),
             ride_one(1, 3, 4, 0, cut_a),
             dict(kind="block", out=2, at=pair_rows, steps=t_slow),
         ],
         [w_ffn0, w_ffn1, g_all],
-        [ffn_mine[1], ffn_other[1]],
+        [ffn_mine[1], ffn_other[1], ffn_mine[0], ffn_other[0]],
     )
     tensor_keys = [(0, r) for r in reversed(range(0, n_t, 2))]
 
@@ -2034,7 +2037,7 @@
         middle_ref, codes_ref, own_ref = outs
         codes = narrow(total[:, width : width + RANK])
         mid = x_ref[at, :].astype(F32) + RESIDUAL * (
-            total[:, :width] + ADAPT_SCALE * dot_nn(codes, out_b_ref[...])
+            total[:, :width] + ADAPT_SCALE * dot_nn(codes, out_b_ref[:RANK, :])
         )
         middle_ref[at, :] = mid
         codes_ref[at, :] = codes
@@ -2053,8 +2056,9 @@
         aug,
         "reduce_out",
         3,
-        riders=[ride_two(0, 2, cut_a, ffn_rows_each - cut_a)]
-        + [ride_two(0, z) for z in range(3, z_count)]
+        riders=[ride_two(0, 2, cut_d, cut_c - cut_d)]
+        + [ride_two(0, z, 0, cut_c) for z in range(3, z_count)]
+        + [ride_two(0, z, cut_c, ffn_rows_each - cut_c) for z in range(1, z_count)]
         + [
             ride_one(1, 3, 4, cut_a, ffn_rows_each - cut_a),
             dict(
@@ -2068,7 +2072,7 @@
         ridden=[w_ffn0, w_ffn1, g_all],
         carried=[ffn_mine[1], ffn_other[1]],
         after=middle_work,
-        after_in=[inputs[0], out_out, feedforward_norm_gain[None], gu_in_lanes],
+        after_in=[inputs[0], out_out_wide, feedforward_norm_gain[None], gu_in_lanes],
         after_out=[
             jax.ShapeDtypeStruct((rows, width), F32),
             jax.ShapeDtypeStruct((rows, RANK), BF16),

time: 622 us -> 614 us (0.987)
  Pallas kernels: 582 us -> 575 us
    pallas_call x2, Pallas kernels: 220 us -> 210 us  [remote_gather(): pl.pallas_call(kernel, out_shape=[jax.ShapeDtypeStruct(o, BF16) for o in...]
where the time goes in v7:
time: 614 us; the launch traced here: 610 us
  Pallas kernels  575 us (94%)
  other arithmetic  18.5 us (3%)
  local copies, waits for them, and re-layouts  8.47 us (1%)
    pallas_call x2, Pallas kernels, remote_gather(): pl.pallas_call(kernel, out_shape=[jax.ShapeDtypeStruct(o, BF16) for o in...  210 us
    pallas_call x1, Pallas kernels, remote_ffn(): pl.pallas_call(kernel, in_specs=[vmem_spec, any_spec] + [any_spec] * (2 *...  77.6 us
    pallas_call x2, Pallas kernels, ridden_call(): pl.pallas_call(body, grid=grid, in_specs=list(in_specs) + [any_spec] * n_...  72.2 us
    pallas_call x2, Pallas kernels, remote_reduce(): pl.pallas_call(kernel, out_shape=after_out + [jax.ShapeDtypeStruct(r.shap...  72.1 us
    pallas_call x1, Pallas kernels, remote_ffn_back(): pl.pallas_call(kernel, out_shape=[jax.ShapeDtypeStruct((rows, aug), F32),...  70.2 us
    pallas_call x1, Pallas kernels, remote_share(): pl.pallas_call(kernel, out_shape=[jax.ShapeDtypeStruct((parts, n_dp, term...  45.7 us
    pallas_call x2, Pallas kernels, set_sums(): pl.pallas_call(kernel, grid_spec=pltpu.PrefetchScalarGridSpec(num_scalar_...  16.2 us

profile of v7, /device:TPU:0, one launch (start us, length us, event | category | flops | bytes accessed | tf_op | source)
XLA Modules:
  0.0 610.4 jit_solution(9956543832237259599)
XLA Ops:
  1.9 1.8 copy.56.refs_13_
  3.7 8.9 %prepare.1 = (bf16[32,2560]{1,0:T(8,128)(2,1)}, bf16[32,1152]{1,0:T(8,128)(2,1)}, bf16[128,768]{1,0:T(8,128)(2,1)}, bf16[128,256]{1,0:T(8,128)(2,1)}, bf16[128,1...) custom-call(s32[3]{0:T(128)} %pad_add_fusion.places_ref, ...), custom_call_target="tpu_custom_call" | custom-call | tf_op jit(solution)/shard_map/prepare/pallas_call | solution.py:1591
  14.4 158.1 %gather_start.1 = (bf16[2560,1152]{1,0:T(8,128)(2,1)}, bf16[896,1280]{1,0:T(8,128)(2,1)}, bf16[384,1280]{1,0:T(8,128)(2,1)}, bf16[2688,640]{1,0:T(8,128)(2,1)}, ...) custom-call(bf16[80,1152]{1,0:T(8,128)(2,1)} %get-tuple-element.108., ...), custom_call_target="tpu_custom_call" | custom-call | tf_op jit(solution)/shard_map/gather_start/pallas_call | solution.py:360
  172.6 1.1 slice_convert_fusion.1
  174.6 2.3 fusion.21
  177.1 2.0 select_convert_fusion
  179.1 1.2 pad_maximum_fusion.refs_3_.refs_4_
  180.4 35.7 %attend.1 = (bf16[1024,1280]{1,0:T(8,128)(2,1)}, bf16[1024,1280]{1,0:T(8,128)(2,1)}, bf16[1024,640]{1,0:T(8,128)(2,1)}, bf16[2560,1536]{1,0:T(8,128)(2,1)}, bf16...) custom-call(bf16[1024,1152]{1,0:T(8,128)(2,1)} %get-tuple-element.12, ...), custom_call_target="tpu_custom_call", output_to_operand_aliasing={{3}: (6, {}), {4}: (7, {}), {5}: (8, {})} | custom-call | tf_op jit(solution)/shard_map/attend/pallas_call | solution.py:921
  216.6 45.8 %reduce_out.1 = (f32[256,2560]{1,0:T(8,128)}, bf16[256,16]{1,0:T(8,128)(2,1)}, bf16[256,2688]{1,0:T(8,128)(2,1)}, bf16[2560,1536]{1,0:T(8,128)(2,1)}, bf16[2560,...) custom-call(bf16[1024,640]{1,0:T(8,128)(2,1)} %get-tuple-element.128.refs_, ...), custom_call_target="tpu_custom_call", output_to_operand_aliasing={{3}: (2, {}), {4}: (3, {}), {5}: (4, {})} | custom-call | tf_op jit(solution)/shard_map/reduce_out/pallas_call | solution.py:493
  265.6 2.9 ffn_extras.1
  268.4 77.6 %feed_forward.1 = (bf16[2048,128]{1,0:T(8,128)(2,1)}, bf16[2048,1024]{1,0:T(8,128)(2,1)}, bf16[2048,640]{1,0:T(8,128)(2,1)}, bf16[2048,512]{1,0:T(8,128)(2,1)}, ...) custom-call(bf16[256,2688]{1,0:T(8,128)(2,1)} %get-tuple-element.136, ...), custom_call_target="tpu_custom_call", output_to_operand_aliasing={{5}: (2, {}), {6}: (3, {})} | custom-call | tf_op jit(solution)/shard_map/feed_forward/pallas_call | solution.py:1204
  346.0 70.2 %feed_forward_back.1 = (f32[256,2688]{1,0:T(8,128)}, bf16[4,256,2688]{2,1,0:T(8,128)(2,1)}, f32[128,1024]{1,0:T(8,128)}, f32[128,640]{1,0:T(8,128)}, f32[128,512]{1,0:T(8,128)}, /*index=5*/f32[128,384]{1,0:T(8,128)}) custom-call(bf16[2048,1024]{1,0:T(8,128)(2,1)} %get-tuple-element.143.refs_0_, bf16[2048,640]{1,0:T(8,128)(2,1)} %get-tuple-element.144.refs_1_, ...), custom_call_target="tpu_custom_call" | custom-call | tf_op jit(solution)/shard_map/feed_forward_back/pallas_call | solution.py:1398
  416.2 51.5 %gather_grad.1 = (bf16[768,800]{1,0:T(8,128)(2,1)}, bf16[256,2688]{1,0:T(8,128)(2,1)}, f32[256,2560]{1,0:T(8,128)}, bf16[256,128]{1,0:T(8,128)(2,1)}, bf16[256,2...) custom-call(f32[256,2688]{1,0:T(8,128)} %get-tuple-element.153.refs_0_, ...), custom_call_target="tpu_custom_call" | custom-call | tf_op jit(solution)/shard_map/gather_grad/pallas_call | solution.py:360
  467.6 3.1 fusion.7.refs_9_
  470.8 36.5 %attend_back.1 = (bf16[1024,1280]{1,0:T(8,128)(2,1)}, bf16[1024,1280]{1,0:T(8,128)(2,1)}, f32[1024,128]{1,0:T(8,128)}, f32[128,1280]{1,0:T(8,128)}, f32[128,1280...) custom-call(bf16[1024,1280]{1,0:T(8,128)(2,1)} %get-tuple-element.15, ...), custom_call_target="tpu_custom_call", output_to_operand_aliasing={{5}: (7, {})} | custom-call | tf_op jit(solution)/shard_map/attend_back/pallas_call | solution.py:921
  507.3 0.9 multiply_convert_fusion
  509.4 26.4 %reduce_latents.1 = (bf16[256,1152]{1,0:T(8,128)(2,1)}, bf16[256,32]{1,0:T(8,128)(2,1)}, bf16[48,2560]{1,0:T(8,128)(2,1)}, bf16[8,16,3200]{2,1,0:T(8,128)(2,1)}) custom-call(bf16[1024,1280]{1,0:T(8,128)(2,1)} %get-tuple-element.168.refs_0_, bf16[1024,1280]{1,0:T(8,128)(2,1)} %get-tuple-element.169.refs_1_, ...), custom_call_target="tpu_custom_call" | custom-call | tf_op jit(solution)/shard_map/reduce_latents/pallas_call | solution.py:493
  535.7 1.6 fusion.30.ids_ref
  537.3 7.2 %sum_split.1 = (f32[2,8,16,1600]{3,2,1,0:T(8,128)}, f32[8,16,1600]{2,1,0:T(8,128)}, f32[8,16,960]{2,1,0:T(8,128)}, f32[8,16,1280]{2,1,0:T(8,128)}, f32[8,16,640]{2,1,0:T(8,128)}) custom-call(s32[8]{0:T(128)} %fusion.30.ids_ref, bf16[8,96,800]{2,1,0:T(8,128)(2,1)} %bitcast.65, bf16[8,16,3200]{2,1,0:T(8,128)(2,1)} %get-tuple-element.190.refs_1_), custom_call_target="tpu_custom_call" | custom-call | tf_op jit(solution)/shard_map/sum_split/pallas_call | solution.py:704
  546.4 2.1 fusion.8
  550.4 45.7 %share.1 = (bf16[2,8,128,1280]{3,2,1,0:T(8,128)(2,1)}, f32[256,2560]{1,0:T(8,128)}) custom-call(bf16[128,2560]{1,0:T(8,128)(2,1)} %fusion.17.source, bf16[256,1152]{1,0:T(8,128)(2,1)} %get-tuple-element.178.refs_0_, bf16[256,32]{1,0:T(8,128)(2,1)} %get-tuple-element.179.refs_1_, bf16[2560,1152]{1,0:T(8,128)(2,1)} %get-tuple-element.180.refs_2_, ...), custom_call_target="tpu_custom_call" | custom-call | tf_op jit(solution)/shard_map/share/pallas_call | solution.py:654
  596.1 9.0 %sum_shared.1 = (f32[2,8,16,2560]{3,2,1,0:T(8,128)}, f32[8,16,2560]{2,1,0:T(8,128)}, f32[8,16,2560]{2,1,0:T(8,128)}, f32[8,16,2560]{2,1,0:T(8,128)}, f32[8,16,25...) custom-call(s32[8]{0:T(128)} %fusion.30.ids_ref, ...), custom_call_target="tpu_custom_call" | custom-call | tf_op jit(solution)/shard_map/sum_shared/pallas_call | solution.py:704
  605.1 3.5 fusion.4
  608.7 1.5 copy.69
  (72 shorter events, 10.7 us)
Async XLA Ops:
  3.7 9.5 %copy-start.14 = (f32[2560]{0:T(1024)S(1)}, f32[2560]{0:T(1024)}, u32[]{:S(2)}) copy-start(f32[2560]{0:T(1024)} %param.33) | copy-start | bytes 30724
  3.7 10.1 %copy-start.16 = (f32[768]{0:T(1024)S(1)}, f32[768]{0:T(1024)}, u32[]{:S(2)}) copy-start(f32[768]{0:T(1024)} %param.34) | copy-start | bytes 9220
  14.4 159.2 %copy-start.13 = (s32[1,1024]{1,0:T(1,128)S(1)}, s32[1,1024]{1,0:T(1,128)}, u32[]{:S(2)}) copy-start(s32[1,1024]{1,0:T(1,128)} %param.31) | copy-start | bytes 12292
  180.4 35.7 %copy-start.15 = (f32[2560]{0:T(1024)S(1)}, f32[2560]{0:T(1024)}, u32[]{:S(2)}) copy-start(f32[2560]{0:T(1024)} %param.36) | copy-start | bytes 30724
  470.8 37.5 %copy-start = (bf16[1024,640]{1,0:T(8,128)(2,1)S(1)}, bf16[1024,640]{1,0:T(8,128)(2,1)}, u32[]{:S(2)}) copy-start(bf16[1024,640]{1,0:T(8,128)(2,1)} %get-tuple-element.128.refs_0_.refs_2_) | copy-start | bytes 3932164
  470.8 37.5 %copy-start.8 = (bf16[1024,128]{1,0:T(8,128)(2,1)S(1)}, bf16[1024,128]{1,0:T(8,128)(2,1)}, u32[]{:S(2)}) copy-start(bf16[1024,128]{1,0:T(8,128)(2,1)} %get-tuple-element.173) | copy-start | bytes 786436
  509.4 35.2 %copy-start.12 = (bf16[256,128]{1,0:T(8,128)(2,1)S(1)}, bf16[256,128]{1,0:T(8,128)(2,1)}, u32[]{:S(2)}) copy-start(bf16[256,128]{1,0:T(8,128)(2,1)} %get-tuple-element.165) | copy-start | bytes 196612
  535.7 8.8 %copy-start.1 = (bf16[256,2688]{1,0:T(8,128)(2,1)S(1)}, bf16[256,2688]{1,0:T(8,128)(2,1)}, u32[]{:S(2)}) copy-start(bf16[256,2688]{1,0:T(8,128)(2,1)} %get-tuple-element.136.x_ref) | copy-start | bytes 4128772
  537.3 7.6 %copy-start.6 = (bf16[256,2688]{1,0:T(8,128)(2,1)S(1)}, bf16[256,2688]{1,0:T(8,128)(2,1)}, u32[]{:S(2)}) copy-start(bf16[256,2688]{1,0:T(8,128)(2,1)} %get-tuple-element.167) | copy-start | bytes 4128772
  537.3 7.6 %copy-start.11 = (bf16[256,16]{1,0:T(8,128)(2,1)S(1)}, bf16[256,16]{1,0:T(8,128)(2,1)}, u32[]{:S(2)}) copy-start(bf16[256,16]{1,0:T(8,128)(2,1)} %get-tuple-element.166) | copy-start | bytes 24580
  544.5 1.3 copy-start.4
  544.5 1.8 copy-start.5
  544.9 3.5 copy-start.7
  546.4 2.2 copy-start.2
  548.4 0.9 copy-start.9
  548.5 1.0 slice-start
  596.1 9.0 %copy-start.10 = (bf16[16,2560]{1,0:T(8,128)(2,1)S(1)}, bf16[16,2560]{1,0:T(8,128)(2,1)}, u32[]{:S(2)}) copy-start(bf16[16,2560]{1,0:T(8,128)(2,1)} %get-tuple-element.164) | copy-start | bytes 245764
  605.1 3.5 copy-start.3

commit v8 on v7

--- a/solution.py
+++ b/solution.py
@@ -1845,7 +1845,7 @@
         )
 
     down_steps = outer_first + (t_slow if shares == n_t else []) + t_core
-    cut_c = ffn_rows_each * 4 // 5 // 16 * 16
+    cut_c = ffn_rows_each * 3 // 4 // 16 * 16
     n_start_outs = 9
     w_at, lat_own_at = n_start_outs + 3, n_start_outs + 4
     n_start_sources = 20

time: 614 us -> 618 us (level)
  no operation moved by 1% of the time
where the time goes in v8:
time: 618 us; the launch traced here: 615 us
  Pallas kernels  579 us (94%)
  other arithmetic  18.5 us (3%)
  local copies, waits for them, and re-layouts  8.47 us (1%)
    pallas_call x2, Pallas kernels, remote_gather(): pl.pallas_call(kernel, out_shape=[jax.ShapeDtypeStruct(o, BF16) for o in...  210 us
    pallas_call x1, Pallas kernels, remote_ffn(): pl.pallas_call(kernel, in_specs=[vmem_spec, any_spec] + [any_spec] * (2 *...  77.6 us
    pallas_call x2, Pallas kernels, ridden_call(): pl.pallas_call(body, grid=grid, in_specs=list(in_specs) + [any_spec] * n_...  75.7 us
    pallas_call x2, Pallas kernels, remote_reduce(): pl.pallas_call(kernel, out_shape=after_out + [jax.ShapeDtypeStruct(r.shap...  72.8 us
    pallas_call x1, Pallas kernels, remote_ffn_back(): pl.pallas_call(kernel, out_shape=[jax.ShapeDtypeStruct((rows, aug), F32),...  70.1 us
    pallas_call x1, Pallas kernels, remote_share(): pl.pallas_call(kernel, out_shape=[jax.ShapeDtypeStruct((parts, n_dp, term...  45.7 us
    pallas_call x2, Pallas kernels, set_sums(): pl.pallas_call(kernel, grid_spec=pltpu.PrefetchScalarGridSpec(num_scalar_...  16.2 us

profile of v8, /device:TPU:0, one launch (start us, length us, event | category | flops | bytes accessed | tf_op | source)
XLA Modules:
  0.0 614.6 jit_solution(3269845927463636324)
XLA Ops:
  1.9 1.8 copy.56.refs_13_
  3.7 8.9 %prepare.1 = (bf16[32,2560]{1,0:T(8,128)(2,1)}, bf16[32,1152]{1,0:T(8,128)(2,1)}, bf16[128,768]{1,0:T(8,128)(2,1)}, bf16[128,256]{1,0:T(8,128)(2,1)}, bf16[128,1...) custom-call(s32[3]{0:T(128)} %pad_add_fusion.places_ref, ...), custom_call_target="tpu_custom_call" | custom-call | tf_op jit(solution)/shard_map/prepare/pallas_call | solution.py:1591
  14.4 158.1 %gather_start.1 = (bf16[2560,1152]{1,0:T(8,128)(2,1)}, bf16[896,1280]{1,0:T(8,128)(2,1)}, bf16[384,1280]{1,0:T(8,128)(2,1)}, bf16[2688,640]{1,0:T(8,128)(2,1)}, ...) custom-call(bf16[80,1152]{1,0:T(8,128)(2,1)} %get-tuple-element.108., ...), custom_call_target="tpu_custom_call" | custom-call | tf_op jit(solution)/shard_map/gather_start/pallas_call | solution.py:360
  172.6 1.1 slice_convert_fusion.1
  174.6 2.3 fusion.21
  177.1 2.0 select_convert_fusion
  179.1 1.2 pad_maximum_fusion.refs_3_.refs_4_
  180.4 39.2 %attend.1 = (bf16[1024,1280]{1,0:T(8,128)(2,1)}, bf16[1024,1280]{1,0:T(8,128)(2,1)}, bf16[1024,640]{1,0:T(8,128)(2,1)}, bf16[2560,1536]{1,0:T(8,128)(2,1)}, bf16...) custom-call(bf16[1024,1152]{1,0:T(8,128)(2,1)} %get-tuple-element.12, ...), custom_call_target="tpu_custom_call", output_to_operand_aliasing={{3}: (6, {}), {4}: (7, {}), {5}: (8, {})} | custom-call | tf_op jit(solution)/shard_map/attend/pallas_call | solution.py:921
  220.2 46.4 %reduce_out.1 = (f32[256,2560]{1,0:T(8,128)}, bf16[256,16]{1,0:T(8,128)(2,1)}, bf16[256,2688]{1,0:T(8,128)(2,1)}, bf16[2560,1536]{1,0:T(8,128)(2,1)}, bf16[2560,...) custom-call(bf16[1024,640]{1,0:T(8,128)(2,1)} %get-tuple-element.128.refs_, ...), custom_call_target="tpu_custom_call", output_to_operand_aliasing={{3}: (2, {}), {4}: (3, {}), {5}: (4, {})} | custom-call | tf_op jit(solution)/shard_map/reduce_out/pallas_call | solution.py:493
  269.8 2.9 ffn_extras.1
  272.6 77.6 %feed_forward.1 = (bf16[2048,128]{1,0:T(8,128)(2,1)}, bf16[2048,1024]{1,0:T(8,128)(2,1)}, bf16[2048,640]{1,0:T(8,128)(2,1)}, bf16[2048,512]{1,0:T(8,128)(2,1)}, ...) custom-call(bf16[256,2688]{1,0:T(8,128)(2,1)} %get-tuple-element.136, ...), custom_call_target="tpu_custom_call", output_to_operand_aliasing={{5}: (2, {}), {6}: (3, {})} | custom-call | tf_op jit(solution)/shard_map/feed_forward/pallas_call | solution.py:1204
  350.2 70.1 %feed_forward_back.1 = (f32[256,2688]{1,0:T(8,128)}, bf16[4,256,2688]{2,1,0:T(8,128)(2,1)}, f32[128,1024]{1,0:T(8,128)}, f32[128,640]{1,0:T(8,128)}, f32[128,512]{1,0:T(8,128)}, /*index=5*/f32[128,384]{1,0:T(8,128)}) custom-call(bf16[2048,1024]{1,0:T(8,128)(2,1)} %get-tuple-element.143.refs_0_, bf16[2048,640]{1,0:T(8,128)(2,1)} %get-tuple-element.144.refs_1_, ...), custom_call_target="tpu_custom_call" | custom-call | tf_op jit(solution)/shard_map/feed_forward_back/pallas_call | solution.py:1398
  420.4 51.5 %gather_grad.1 = (bf16[768,800]{1,0:T(8,128)(2,1)}, bf16[256,2688]{1,0:T(8,128)(2,1)}, f32[256,2560]{1,0:T(8,128)}, bf16[256,128]{1,0:T(8,128)(2,1)}, bf16[256,2...) custom-call(f32[256,2688]{1,0:T(8,128)} %get-tuple-element.153.refs_0_, ...), custom_call_target="tpu_custom_call" | custom-call | tf_op jit(solution)/shard_map/gather_grad/pallas_call | solution.py:360
  471.8 3.1 fusion.7.refs_9_
  475.0 36.5 %attend_back.1 = (bf16[1024,1280]{1,0:T(8,128)(2,1)}, bf16[1024,1280]{1,0:T(8,128)(2,1)}, f32[1024,128]{1,0:T(8,128)}, f32[128,1280]{1,0:T(8,128)}, f32[128,1280...) custom-call(bf16[1024,1280]{1,0:T(8,128)(2,1)} %get-tuple-element.15, ...), custom_call_target="tpu_custom_call", output_to_operand_aliasing={{5}: (7, {})} | custom-call | tf_op jit(solution)/shard_map/attend_back/pallas_call | solution.py:921
  511.5 0.9 multiply_convert_fusion
  513.5 26.4 %reduce_latents.1 = (bf16[256,1152]{1,0:T(8,128)(2,1)}, bf16[256,32]{1,0:T(8,128)(2,1)}, bf16[48,2560]{1,0:T(8,128)(2,1)}, bf16[8,16,3200]{2,1,0:T(8,128)(2,1)}) custom-call(bf16[1024,1280]{1,0:T(8,128)(2,1)} %get-tuple-element.168.refs_0_, bf16[1024,1280]{1,0:T(8,128)(2,1)} %get-tuple-element.169.refs_1_, ...), custom_call_target="tpu_custom_call" | custom-call | tf_op jit(solution)/shard_map/reduce_latents/pallas_call | solution.py:493
  539.9 1.6 fusion.30.ids_ref
  541.5 7.2 %sum_split.1 = (f32[2,8,16,1600]{3,2,1,0:T(8,128)}, f32[8,16,1600]{2,1,0:T(8,128)}, f32[8,16,960]{2,1,0:T(8,128)}, f32[8,16,1280]{2,1,0:T(8,128)}, f32[8,16,640]{2,1,0:T(8,128)}) custom-call(s32[8]{0:T(128)} %fusion.30.ids_ref, bf16[8,96,800]{2,1,0:T(8,128)(2,1)} %bitcast.65, bf16[8,16,3200]{2,1,0:T(8,128)(2,1)} %get-tuple-element.190.refs_1_), custom_call_target="tpu_custom_call" | custom-call | tf_op jit(solution)/shard_map/sum_split/pallas_call | solution.py:704
  550.5 2.1 fusion.8
  554.6 45.7 %share.1 = (bf16[2,8,128,1280]{3,2,1,0:T(8,128)(2,1)}, f32[256,2560]{1,0:T(8,128)}) custom-call(bf16[128,2560]{1,0:T(8,128)(2,1)} %fusion.17.source, bf16[256,1152]{1,0:T(8,128)(2,1)} %get-tuple-element.178.refs_0_, bf16[256,32]{1,0:T(8,128)(2,1)} %get-tuple-element.179.refs_1_, bf16[2560,1152]{1,0:T(8,128)(2,1)} %get-tuple-element.180.refs_2_, ...), custom_call_target="tpu_custom_call" | custom-call | tf_op jit(solution)/shard_map/share/pallas_call | solution.py:654
  600.3 9.0 %sum_shared.1 = (f32[2,8,16,2560]{3,2,1,0:T(8,128)}, f32[8,16,2560]{2,1,0:T(8,128)}, f32[8,16,2560]{2,1,0:T(8,128)}, f32[8,16,2560]{2,1,0:T(8,128)}, f32[8,16,25...) custom-call(s32[8]{0:T(128)} %fusion.30.ids_ref, ...), custom_call_target="tpu_custom_call" | custom-call | tf_op jit(solution)/shard_map/sum_shared/pallas_call | solution.py:704
  609.3 3.5 fusion.4
  612.8 1.5 copy.69
  (72 shorter events, 10.7 us)
Async XLA Ops:
  3.7 9.5 %copy-start.14 = (f32[2560]{0:T(1024)S(1)}, f32[2560]{0:T(1024)}, u32[]{:S(2)}) copy-start(f32[2560]{0:T(1024)} %param.33) | copy-start | bytes 30724
  3.7 10.1 %copy-start.16 = (f32[768]{0:T(1024)S(1)}, f32[768]{0:T(1024)}, u32[]{:S(2)}) copy-start(f32[768]{0:T(1024)} %param.34) | copy-start | bytes 9220
  14.4 159.2 %copy-start.13 = (s32[1,1024]{1,0:T(1,128)S(1)}, s32[1,1024]{1,0:T(1,128)}, u32[]{:S(2)}) copy-start(s32[1,1024]{1,0:T(1,128)} %param.31) | copy-start | bytes 12292
  180.4 39.2 %copy-start.15 = (f32[2560]{0:T(1024)S(1)}, f32[2560]{0:T(1024)}, u32[]{:S(2)}) copy-start(f32[2560]{0:T(1024)} %param.36) | copy-start | bytes 30724
  475.0 37.4 %copy-start = (bf16[1024,640]{1,0:T(8,128)(2,1)S(1)}, bf16[1024,640]{1,0:T(8,128)(2,1)}, u32[]{:S(2)}) copy-start(bf16[1024,640]{1,0:T(8,128)(2,1)} %get-tuple-element.128.refs_0_.refs_2_) | copy-start | bytes 3932164
  475.0 37.4 %copy-start.8 = (bf16[1024,128]{1,0:T(8,128)(2,1)S(1)}, bf16[1024,128]{1,0:T(8,128)(2,1)}, u32[]{:S(2)}) copy-start(bf16[1024,128]{1,0:T(8,128)(2,1)} %get-tuple-element.173) | copy-start | bytes 786436
  513.5 35.2 %copy-start.12 = (bf16[256,128]{1,0:T(8,128)(2,1)S(1)}, bf16[256,128]{1,0:T(8,128)(2,1)}, u32[]{:S(2)}) copy-start(bf16[256,128]{1,0:T(8,128)(2,1)} %get-tuple-element.165) | copy-start | bytes 196612
  539.9 8.8 %copy-start.1 = (bf16[256,2688]{1,0:T(8,128)(2,1)S(1)}, bf16[256,2688]{1,0:T(8,128)(2,1)}, u32[]{:S(2)}) copy-start(bf16[256,2688]{1,0:T(8,128)(2,1)} %get-tuple-element.136.x_ref) | copy-start | bytes 4128772
  541.5 7.6 %copy-start.6 = (bf16[256,2688]{1,0:T(8,128)(2,1)S(1)}, bf16[256,2688]{1,0:T(8,128)(2,1)}, u32[]{:S(2)}) copy-start(bf16[256,2688]{1,0:T(8,128)(2,1)} %get-tuple-element.167) | copy-start | bytes 4128772
  541.5 7.6 %copy-start.11 = (bf16[256,16]{1,0:T(8,128)(2,1)S(1)}, bf16[256,16]{1,0:T(8,128)(2,1)}, u32[]{:S(2)}) copy-start(bf16[256,16]{1,0:T(8,128)(2,1)} %get-tuple-element.166) | copy-start | bytes 24580
  548.7 1.3 copy-start.4
  548.7 1.8 copy-start.5
  549.1 3.5 copy-start.7
  550.5 2.2 copy-start.2
  552.6 0.9 copy-start.9
  552.7 1.0 slice-start
  600.2 9.0 %copy-start.10 = (bf16[16,2560]{1,0:T(8,128)(2,1)S(1)}, bf16[16,2560]{1,0:T(8,128)(2,1)}, u32[]{:S(2)}) copy-start(bf16[16,2560]{1,0:T(8,128)(2,1)} %get-tuple-element.164) | copy-start | bytes 245764
  609.3 3.5 copy-start.3
